TPU v7x, 32 devices: a whole 2x2x4 slice. The times are simulated.
32 devices in a mesh: blk: 16 (over z, x, core), node: 2 (over y).
Axes of the slice: x: 2, y: 2, z: 4, core: 2. Of those that a mesh axis runs over, the one named last changes fastest.
Arguments:
- image_embeds: bfloat16 [5120, 1152], P(('blk', 'node')), may hold values from -0.1796875 to 0.1796875
- text_embeds: bfloat16 [5120, 1152], P(('blk', 'node')), may hold values from -0.1796875 to 0.1796875
- pair_text: int32 [5120], replicated, may hold values from 0 to 5119, as said below
- similarity_scale: float32 [1], replicated, may hold values from 5 to 15
- logit_bias: float32 [1], replicated, may hold values from -6 to -2
Outputs:
- image_grads: float32 [5120, 1152], P(('blk', 'node'))
- text_grads: float32 [5120, 1152], P(('blk', 'node'))
Inputs may be any that keep to these rules, and one draw needn't show every extreme that they name: pair_text is a permutation that maps each image to a report of its own group of 320 consecutive pairs.
All inputs are finite; a program needn't handle non-finite values.
Results may differ from a plain program's by a relative error of at most 0.0043.
Values may be sent and summed in bfloat16 or wider, within the bound.
No kernel may reach another device: no remote copies, remote signals or barrier semaphores. Data moves between devices by JAX's collectives and lax.ppermute only.
A program may use at most 64 MiB of HBM per device.

v0:
```python
import jax
import jax.numpy as jnp
from jax import lax
from jax.sharding import PartitionSpec as P

TURNS = 3


def passed_along(block, axis, distance):
    devices = range(lax.axis_size(axis))
    route = [((i - distance) % len(devices), i) for i in devices]
    return lax.ppermute(block, axis, route)


def unit_rows(raw_rows):
    values = raw_rows.astype(jnp.float32)
    inverse = lax.rsqrt(jnp.sum(values * values, axis=1, keepdims=True) + 1e-06)
    return (values * inverse, inverse)


def tangent_part(gradient, unit_rows_f, inverse):
    return (
        gradient - unit_rows_f * jnp.sum(unit_rows_f * gradient, axis=1, keepdims=True)
    ) * inverse


def pass_images(visitor):
    return passed_along(visitor, "blk", 1)


def carry_grads(partial_value):
    return passed_along(partial_value, "blk", 1)


def local(image_embeds, text_embeds, pair_text, similarity_scale, logit_bias):
    rows_here = image_embeds.shape[0]
    node_count = lax.axis_size("node")
    cycle_count = lax.axis_size("blk")
    node_index = lax.axis_index("node")
    cycle_index = lax.axis_index("blk")
    text_span = rows_here * node_count
    softness_factor = similarity_scale[0]
    shift_amount_value = logit_bias[0]
    image_unit, image_inv = unit_rows(image_embeds)
    text_unit, text_inv = unit_rows(text_embeds)
    image_half = image_unit.astype(jnp.bfloat16)
    text_half = text_unit.astype(jnp.bfloat16)
    text_block = lax.all_gather(text_half, "node", axis=0, tiled=True)
    text_start = cycle_index * text_span
    text_columns = jnp.arange(text_span, dtype=jnp.int32)
    visitor = image_half
    seen_list = []
    tile_list = []
    partial_value = jnp.zeros((rows_here, image_embeds.shape[1]), jnp.float32)
    for turn in range(TURNS):
        if turn > 0:
            visitor = pass_images(visitor)
            partial_value = carry_grads(partial_value)
        source = (cycle_index - turn + cycle_count) % cycle_count
        pair_logit_matrix = (
            softness_factor
            * lax.dot_general(
                visitor, text_block, (((1,), (1,)), ((), ())), preferred_element_type=jnp.float32
            )
            + shift_amount_value
        )
        targets = (
            lax.dynamic_slice_in_dim(
                pair_text, (source * node_count + node_index) * rows_here, rows_here, 0
            )
            - text_start
        )
        pair_label_polarity = jnp.where(
            targets[:, None] == text_columns[None, :], 1.0, -1.0
        ).astype(jnp.float32)
        weight_panel = (
            -pair_label_polarity
            * softness_factor
            * jax.nn.sigmoid(-pair_label_polarity * pair_logit_matrix)
        ).astype(jnp.bfloat16)
        term = jnp.dot(weight_panel, text_block, preferred_element_type=jnp.float32)
        partial_value = partial_value + term
        seen_list.append(visitor)
        tile_list.append(weight_panel)
    image_dir = passed_along(partial_value, "blk", -(TURNS - 1))
    seen = jnp.stack(seen_list, axis=0)
    tile_stack = jnp.stack(tile_list, axis=0)
    text_terms = jnp.einsum("sit,sid->td", tile_stack, seen, preferred_element_type=jnp.float32)
    text_dir = lax.psum_scatter(text_terms, "node", scatter_dimension=0, tiled=True)
    image_grads = tangent_part(image_dir, image_unit, image_inv)
    text_grads = tangent_part(text_dir, text_unit, text_inv)
    return (image_grads, text_grads)


def solution(mesh):
    return jax.shard_map(
        local,
        mesh=mesh,
        in_specs=(P(("blk", "node"), None), P(("blk", "node"), None), P(), P(), P()),
        out_specs=(P(("blk", "node"), None), P(("blk", "node"), None)),
        check_vma=False,
    )
```

profile of v0, /device:TPU:0, one launch (start us, length us, event | category | flops | bytes accessed | tf_op | source)
XLA Modules:
  0.0 86.6 jit_solution(3503993171313645257)
XLA Ops:
  7.2 1.2 %fusion.38 = f32[160]{0:T(256)S(1)} fusion(bf16[160,1152]{1,0:T(8,128)(2,1)} %param.5), kind=kLoop, calls=%fused_computation.47 | loop fusion | flops 552800 | bytes 369280 | tf_op jit(solution)/shard_map/reduce_sum | solution.py:17
  8.4 1.1 %fusion.34 = bf16[160,1152]{1,0:T(8,128)(2,1)S(1)} fusion(bf16[160,1152]{1,0:T(8,128)(2,1)} %param.5, f32[160]{0:T(256)S(1)} %add_rsqrt_fusion.1), kind=kLoop, calls=%fused_computation.43 | loop fusion | flops 552960 | bytes 737920 | tf_op jit(solution)/shard_map/convert_element_type | solution.py:46
  9.5 0.5 collective-permute-start.1
  10.0 0.2 fusion.42
  10.2 0.1 fusion.31
  10.3 11.7 %all_gather.3 = bf16[320,1152]{1,0:T(8,128)(2,1)S(1)} all-gather(bf16[160,1152]{1,0:T(8,128)(2,1)S(1)} %fusion.31), channel_id=1, replica_groups=mesh['blk'=16,'node'=2] {'node'}, dimensions={0}, use_global_device_ids=true | all-gather | bytes 1105920 | tf_op jit(solution)/shard_map/all_gather | solution.py:48
  23.4 0.9 dynamic-slice_subtract_fusion
  24.3 0.5 fusion.21
  24.8 0.4 fusion.49
  25.1 0.8 collective-permute-start
  26.0 1.8 %collective-permute-start.3 = (bf16[160,1152]{1,0:T(8,128)(2,1)}, bf16[160,1152]{1,0:T(8,128)(2,1)S(1)}, u32[]{:S(2)}, u32[]{:S(2)}) collective-permute-start(bf16[160,1152]{1,0:T(8,128)(2,1)} %collective-permute-done.1), channel_id=1, source_target_pairs={{30,0},{0,2},{2,4},{4,6},{6,8},{8,10},{10,12},{12,14},{14,16},{16,... | collective-permute-start | bytes 1105928 | tf_op jit(solution)/shard_map/ppermute | solution.py:12
  27.8 0.1 fusion.63
  27.9 1.5 %fusion.22 = bf16[160,320]{1,0:T(8,128)(2,1)S(1)} fusion(bf16[160,1152]{1,0:T(8,128)(2,1)} %collective-permute-done.1, bf16[320,1152]{1,0:T(8,128)(2,1)S(1)} %all_gather.3, s32[160]{0:T(256)S(1)} %get-tuple-element.4, f32[]{:T(128)} %bitcast.28, f32[]{:T(128)} %bitcast.23), kind=kOutput, calls=%fused_computation.27 | convolution fusion | flops 118579200 | bytes 1208968 | tf_op jit(solution)/shard_map/dot_general | solution.py:62
  29.4 13.4 %collective-permute-done.3 = bf16[160,1152]{1,0:T(8,128)(2,1)S(1)} collective-permute-done((bf16[160,1152]{1,0:T(8,128)(2,1)}, bf16[160,1152]{1,0:T(8,128)(2,1)S(1)}, u32[]{:S(2)}, u32[]{:S(2)}) %collective-permute-start.3) | collective-permute-done | bytes 368672 | tf_op jit(solution)/shard_map/ppermute | solution.py:12
  42.7 0.5 fusion.23
  43.2 2.8 %convolution_bitcast_fusion = f32[320,1152]{1,0:T(8,128)} fusion(bf16[1,160,1152]{2,1,0:T(8,128)(2,1)S(1)} %bitcast.32, bf16[1,160,1152]{2,1,0:T(8,128)(2,1)} %bitcast.6, bf16[1,160,1152]{2,1,0:T(8,128)(2,1)S(1)} %fusion.63, bf16[1,160,320]{2,1,0:T(8,128)(2,1)S(1)} %bitcast.29, bf16[1,160,320]{2,1,0:T(8,128)(2,1)S(1)} %bitcast.30, ...), kind=kOutput, calls=%fused_computation | convolution fusion | flops 355307520 | bytes 2887680 | tf_op jit(solution)/shard_map/sit,sid->td/dot_general | solution.py:88
  46.1 0.4 convolution_add_fusion
  46.5 0.4 fusion.50
  46.9 13.3 %collective-permute-done.2 = f32[160,1152]{1,0:T(8,128)S(1)} collective-permute-done((f32[160,1152]{1,0:T(8,128)S(1)}, f32[160,1152]{1,0:T(8,128)S(1)}, u32[]{:S(2)}, u32[]{:S(2)}) %collective-permute-start.2) | collective-permute-done | bytes 737312 | tf_op jit(solution)/shard_map/ppermute | solution.py:12
  60.3 15.5 %collective-permute-done.4 = f32[160,1152]{1,0:T(8,128)S(1)} collective-permute-done((f32[160,1152]{1,0:T(8,128)S(1)}, f32[160,1152]{1,0:T(8,128)S(1)}, u32[]{:S(2)}, u32[]{:S(2)}) %collective-permute-start.4) | collective-permute-done | bytes 737312 | tf_op jit(solution)/shard_map/ppermute | solution.py:12
  75.9 0.2 fusion.35
  76.1 1.1 %fusion.37 = f32[160,1152]{1,0:T(8,128)} fusion(f32[160,1152]{1,0:T(8,128)S(1)} %collective-permute-done.4, bf16[160,1152]{1,0:T(8,128)(2,1)S(1)} %copy-done, f32[160]{0:T(256)S(1)} %fusion.35, f32[160]{0:T(256)S(1)} %add_rsqrt_fusion.1), kind=kLoop, calls=%fused_computation.46 | loop fusion | flops 921600 | bytes 1844480 | tf_op jit(solution)/shard_map/mul | solution.py:22
  77.2 1.4 %fusion.39 = f32[160]{0:T(256)S(1)} fusion(f32[160,1152]{1,0:T(8,128)} %reduce-scatter.2.cloned.1.call-done, bf16[160,1152]{1,0:T(8,128)(2,1)S(1)} %copy-done.1, f32[160]{0:T(256)S(1)} %add_rsqrt_fusion), kind=kLoop, calls=%fused_computation.48 | loop fusion | flops 737120 | bytes 1107200 | tf_op jit(solution)/shard_map/reduce_sum | solution.py:23
  78.7 1.1 %fusion.41 = f32[160,1152]{1,0:T(8,128)} fusion(f32[160,1152]{1,0:T(8,128)S(1)} %copy-done.2, bf16[160,1152]{1,0:T(8,128)(2,1)S(1)} %copy-done.1, f32[160]{0:T(256)S(1)} %fusion.39, f32[160]{0:T(256)S(1)} %add_rsqrt_fusion), kind=kLoop, calls=%fused_computation.50 | loop fusion | flops 921600 | bytes 1844480 | tf_op jit(solution)/shard_map/mul | solution.py:22
  (16 shorter events, 0.3 us)
Async XLA Ops:
  7.2 2.9 %copy-start.1 = (bf16[160,1152]{1,0:T(8,128)(2,1)S(1)}, bf16[160,1152]{1,0:T(8,128)(2,1)}, u32[]{:S(2)}) copy-start(bf16[160,1152]{1,0:T(8,128)(2,1)} %param.6) | copy-start | bytes 1105924
  7.2 70.1 %reduce-scatter.2.cloned.1.call-start = ((), (), s32[]{:S(2)}) async-start(), calls=%async_computation.1 | async-start | bytes 2211840 | tf_op jit(solution)/shard_map/reduce_scatter | solution.py:89
  9.5 16.5 %collective-permute-start.1 = (bf16[160,1152]{1,0:T(8,128)(2,1)S(1)}, bf16[160,1152]{1,0:T(8,128)(2,1)}, u32[]{:S(2)}, u32[]{:S(2)}) collective-permute-start(bf16[160,1152]{1,0:T(8,128)(2,1)S(1)} %fusion.34), channel_id=1, source_target_pairs={{30,0},{0,2},{2,4},{4,6},{6,8},{8,10},{10,12},{12,14},{14,16},{16,... | collective-permute-start | bytes 1105928 | tf_op jit(solution)/shard_map/ppermute | solution.py:12
  24.8 3.0 %copy-start = (bf16[160,1152]{1,0:T(8,128)(2,1)S(1)}, bf16[160,1152]{1,0:T(8,128)(2,1)}, u32[]{:S(2)}) copy-start(bf16[160,1152]{1,0:T(8,128)(2,1)} %param.5) | copy-start | bytes 1105924
  25.1 20.9 %collective-permute-start = (f32[160,1152]{1,0:T(8,128)S(1)}, f32[160,1152]{1,0:T(8,128)S(1)}, u32[]{:S(2)}, u32[]{:S(2)}) collective-permute-start(f32[160,1152]{1,0:T(8,128)S(1)} %fusion.49), channel_id=1, source_target_pairs={{30,0},{0,2},{2,4},{4,6},{6,8},{8,10},{10,12},{12,14},{14,16},{16,... | collective-permute-start | bytes 2211848 | tf_op jit(solution)/shard_map/ppermute | solution.py:12
  26.0 16.7 %collective-permute-start.3 = (bf16[160,1152]{1,0:T(8,128)(2,1)}, bf16[160,1152]{1,0:T(8,128)(2,1)S(1)}, u32[]{:S(2)}, u32[]{:S(2)}) collective-permute-start(bf16[160,1152]{1,0:T(8,128)(2,1)} %collective-permute-done.1), channel_id=1, source_target_pairs={{30,0},{0,2},{2,4},{4,6},{6,8},{8,10},{10,12},{12,14},{14,16},{16,... | collective-permute-start | bytes 1105928 | tf_op jit(solution)/shard_map/ppermute | solution.py:12
  46.4 13.7 %collective-permute-start.2 = (f32[160,1152]{1,0:T(8,128)S(1)}, f32[160,1152]{1,0:T(8,128)S(1)}, u32[]{:S(2)}, u32[]{:S(2)}) collective-permute-start(f32[160,1152]{1,0:T(8,128)S(1)} %convolution_add_fusion), channel_id=1, source_target_pairs={{30,0},{0,2},{2,4},{4,6},{6,8},{8,10},{10,12},{12,14},{14,16},{16,... | collective-permute-start | bytes 2211848 | tf_op jit(solution)/shard_map/ppermute | solution.py:12
  60.3 15.6 %collective-permute-start.4 = (f32[160,1152]{1,0:T(8,128)S(1)}, f32[160,1152]{1,0:T(8,128)S(1)}, u32[]{:S(2)}, u32[]{:S(2)}) collective-permute-start(f32[160,1152]{1,0:T(8,128)S(1)} %add.112), channel_id=1, source_target_pairs={{4,0},{6,2},{8,4},{10,6},{12,8},{14,10},{16,12},{18,14},{20,16},{2... | collective-permute-start | bytes 2211848 | tf_op jit(solution)/shard_map/ppermute | solution.py:12
  77.2 1.4 %copy-start.2 = (f32[160,1152]{1,0:T(8,128)S(1)}, f32[160,1152]{1,0:T(8,128)}, u32[]{:S(2)}) copy-start(f32[160,1152]{1,0:T(8,128)} %reduce-scatter.2.cloned.1.call-done) | copy-start | bytes 2211844
Sparse Core Ops, SparseCore 0:
  46.2 24.5 reduce-scatter.1
where the time goes:
time: 87.1 us; the launch traced here: 86.6 us
  waiting for transfers between devices  42.2 us (48%)
  between operations  15.5 us (18%)
  blocking collectives  11.7 us (13%)
  other arithmetic  7.59 us (9%)
  matrix products  6.35 us (7%)
  starting transfers between devices  3.26 us (4%)
    ppermute x5, waiting for transfers between devices, passed_along(): return lax.ppermute(block, axis, route)  42.2 us
    all_gather x1, blocking collectives, local(): text_block = lax.all_gather(text_half, 'node', axis=0, tiled=True)  11.7 us
    ppermute x5, starting transfers between devices, passed_along(): return lax.ppermute(block, axis, route)  3.22 us
    dot_general x1, matrix products, local(): jnp.einsum('sit,sid->td', tile_stack, seen, preferred_element_type=jnp.fl...  2.79 us
    dot_general x3, matrix products, local(): lax.dot_general(visitor, text_block, (((1,), (1,)), ((), ())), preferred_...  2.45 us
    mul x2, other arithmetic, tangent_part(): (gradient - unit_rows_f * jnp.sum(unit_rows_f * gradient, axis=1, keepdim...  2.25 us
  transfers between devices with their start and end apart: 6, of which 3 were waited for; matrix products, arithmetic and copies ran while one was open for 10% of the time, Pallas kernels for 0%

commit v1 on v0

v1 whole, which is shorter than its diff:
```python
import jax
import jax.numpy as jnp
from jax import lax
from jax.sharding import PartitionSpec as P

TURNS = 3


def shifted(block, axis, distance):
    count = lax.axis_size(axis)
    route = [(i, (i + distance) % count) for i in range(count)]
    return lax.ppermute(block, axis, route)


def unit_rows(raw_rows):
    values = raw_rows.astype(jnp.float32)
    inverse = lax.rsqrt(jnp.sum(values * values, axis=1, keepdims=True) + 1e-06)
    return (values * inverse, inverse)


def tangent_part(gradient, unit_rows_f, inverse):
    return (
        gradient - unit_rows_f * jnp.sum(unit_rows_f * gradient, axis=1, keepdims=True)
    ) * inverse


def local(image_embeds, text_embeds, pair_text, similarity_scale, logit_bias):
    rows = image_embeds.shape[0]
    node_count = lax.axis_size("node")
    node_index = lax.axis_index("node")
    cycle_index = lax.axis_index("blk")
    scale = similarity_scale[0]
    bias = logit_bias[0]

    visitors = [image_embeds] + [shifted(image_embeds, "blk", t) for t in range(1, TURNS)]
    texts = [text_embeds] + [shifted(text_embeds, "node", -k) for k in range(1, node_count)]

    image_unit, image_inv = unit_rows(image_embeds)
    text_unit, text_inv = unit_rows(text_embeds)
    image_halves = [image_unit.astype(jnp.bfloat16)] + [
        unit_rows(v)[0].astype(jnp.bfloat16) for v in visitors[1:]
    ]
    text_halves = [text_unit.astype(jnp.bfloat16)] + [
        unit_rows(v)[0].astype(jnp.bfloat16) for v in texts[1:]
    ]
    text_all = jnp.concatenate(text_halves, axis=0)

    targets = lax.dynamic_slice_in_dim(
        pair_text, (cycle_index * node_count + node_index) * rows, rows, 0
    )
    columns = jnp.concatenate(
        [
            (cycle_index * node_count + (node_index + k) % node_count) * rows
            + jnp.arange(rows, dtype=jnp.int32)
            for k in range(node_count)
        ]
    )
    paired = targets[:, None] == columns[None, :]

    image_dir = None
    back = []
    text_terms = 0.0
    for t in range(TURNS):
        logits = (
            scale
            * lax.dot_general(
                image_halves[t],
                text_all,
                (((1,), (1,)), ((), ())),
                preferred_element_type=jnp.float32,
            )
            + bias
        )
        if t == 0:
            weights = jnp.where(paired, -scale, scale) * jax.nn.sigmoid(
                jnp.where(paired, -logits, logits)
            )
        else:
            weights = scale * jax.nn.sigmoid(logits)
        weights = weights.astype(jnp.bfloat16)
        term = jnp.dot(weights, text_all, preferred_element_type=jnp.float32)
        if t == 0:
            image_dir = term
        else:
            back.append(shifted(term.astype(jnp.bfloat16), "blk", -t))
        text_terms = text_terms + lax.dot_general(
            weights,
            image_halves[t],
            (((0,), (0,)), ((), ())),
            preferred_element_type=jnp.float32,
        )
    text_dir = text_terms[:rows]
    for k in range(1, node_count):
        part = text_terms[k * rows : (k + 1) * rows].astype(jnp.bfloat16)
        text_dir = text_dir + shifted(part, "node", k).astype(jnp.float32)
    for part in back:
        image_dir = image_dir + part.astype(jnp.float32)
    image_grads = tangent_part(image_dir, image_unit, image_inv)
    text_grads = tangent_part(text_dir, text_unit, text_inv)
    return (image_grads, text_grads)


def solution(mesh):
    return jax.shard_map(
        local,
        mesh=mesh,
        in_specs=(P(("blk", "node"), None), P(("blk", "node"), None), P(), P(), P()),
        out_specs=(P(("blk", "node"), None), P(("blk", "node"), None)),
        check_vma=False,
    )
```

time: 87.1 us -> 38.1 us (0.44)
  waiting for transfers between devices: 42.2 us -> 16.1 us
  between operations: 15.5 us -> 2.08 us
  blocking collectives: 11.7 us -> 0 us
  starting transfers between devices: 3.26 us -> 7.95 us
  matrix products: 6.35 us -> 4.13 us
    ppermute x5 -> x6, waiting for transfers between devices: 42.2 us -> 16.1 us  [shifted(): return lax.ppermute(block, axis, route)]
    all_gather x1 -> x0, blocking collectives: 11.7 us -> none  [local(): text_block = lax.all_gather(text_half, 'node', axis=0, tiled=True)]
    ppermute x5 -> x6, starting transfers between devices: 3.22 us -> 7.95 us  [shifted(): return lax.ppermute(block, axis, route)]
    dot_general x7 -> x9, matrix products: 6.35 us -> 4.13 us  [the longest x3 1.46 us: local(): lax.dot_general(image_halves[t], text_all, (((1,), (1,)), ((), ())), pref...]
    reduce_sum x2 -> x5, other arithmetic: 1.34 us -> 2.85 us  [unit_rows(): inverse = lax.rsqrt(jnp.sum(values * values, axis=1, keepdims=True) + 1e-06)]
    reduce_sum x2 -> x1, other arithmetic: 1.68 us -> 0.27 us  [tangent_part(): jnp.sum(unit_rows_f * gradient, axis=1, keepdims=True)]
  transfers between devices with their start and end apart: 6 -> 6, of which waited for: 3 -> 6; matrix products, arithmetic and copies ran while one was open for 10% -> 18% of each run, Pallas kernels for 0% -> 0%
where the time goes in v1:
time: 38.1 us; the launch traced here: 37.8 us
  waiting for transfers between devices  16.1 us (42%)
  starting transfers between devices  7.95 us (21%)
  other arithmetic  6.79 us (18%)
  matrix products  4.13 us (11%)
  between operations  2.08 us (5%)
  local copies, waits for them, and re-layouts  0.83 us (2%)
    ppermute x6, waiting for transfers between devices, shifted(): return lax.ppermute(block, axis, route)  16.1 us
    ppermute x6, starting transfers between devices, shifted(): return lax.ppermute(block, axis, route)  7.95 us
    reduce_sum x5, other arithmetic, unit_rows(): inverse = lax.rsqrt(jnp.sum(values * values, axis=1, keepdims=True) + 1e-06)  2.85 us
    mul x2, other arithmetic, tangent_part(): (gradient - unit_rows_f * jnp.sum(unit_rows_f * gradient, axis=1, keepdim...  2.31 us
    dot_general x3, matrix products, local(): lax.dot_general(image_halves[t], text_all, (((1,), (1,)), ((), ())), pref...  1.46 us
    dot_general x3, matrix products, local(): lax.dot_general(weights, image_halves[t], (((0,), (0,)), ((), ())), prefe...  1.41 us
    dot_general x3, matrix products, local(): term = jnp.dot(weights, text_all, preferred_element_type=jnp.float32)  1.25 us
    convert_element_type x1, other arithmetic, local(): text_unit.astype(jnp.bfloat16)  1.12 us
  transfers between devices with their start and end apart: 6, of which 6 were waited for; matrix products, arithmetic and copies ran while one was open for 18% of the time, Pallas kernels for 0%

profile of v1, /device:TPU:0, one launch (start us, length us, event | category | flops | bytes accessed | tf_op | source)
XLA Modules:
  0.0 37.8 jit_solution(11207004689298216189)
XLA Ops:
  0.6 3.0 %collective-permute-start.3 = (bf16[160,1152]{1,0:T(8,128)(2,1)}, bf16[160,1152]{1,0:T(8,128)(2,1)S(1)}, u32[]{:S(2)}, u32[]{:S(2)}) collective-permute-start(bf16[160,1152]{1,0:T(8,128)(2,1)} %param.5), channel_id=1, source_target_pairs={{0,4},{2,6},{4,8},{6,10},{8,12},{10,14},{12,16},{14,18},{16,20},{1... | collective-permute-start | bytes 1105928 | tf_op jit(solution)/shard_map/ppermute | solution.py:12
  3.6 1.5 %collective-permute-start = (bf16[160,1152]{1,0:T(8,128)(2,1)}, bf16[160,1152]{1,0:T(8,128)(2,1)S(1)}, u32[]{:S(2)}, u32[]{:S(2)}) collective-permute-start(bf16[160,1152]{1,0:T(8,128)(2,1)} %param.6), channel_id=1, source_target_pairs={{0,1},{1,0},{2,3},{3,2},{4,5},{5,4},{6,7},{7,6},{8,9},{9,8},{10,11... | collective-permute-start | bytes 1105928 | tf_op jit(solution)/shard_map/ppermute | solution.py:12
  5.1 1.2 %fusion.28 = f32[160]{0:T(256)S(1)} fusion(bf16[160,1152]{1,0:T(8,128)(2,1)} %param.6), kind=kLoop, calls=%fused_computation.45 | loop fusion | flops 552800 | bytes 369280 | tf_op jit(solution)/shard_map/reduce_sum | solution.py:17
  6.3 1.2 %fusion.24 = f32[160]{0:T(256)S(1)} fusion(bf16[160,1152]{1,0:T(8,128)(2,1)} %param.5), kind=kLoop, calls=%fused_computation.41 | loop fusion | flops 552800 | bytes 369280 | tf_op jit(solution)/shard_map/reduce_sum | solution.py:17
  7.6 1.1 %fusion.17 = bf16[160,1152]{1,0:T(8,128)(2,1)S(1)} fusion(bf16[160,1152]{1,0:T(8,128)(2,1)} %param.6, f32[160]{0:T(256)S(1)} %add_rsqrt_fusion.3), kind=kLoop, calls=%fused_computation.32 | loop fusion | flops 552960 | bytes 737920 | tf_op jit(solution)/shard_map/convert_element_type | solution.py:43
  10.1 0.8 %dynamic_slice.3 = s32[160]{0:T(256)S(1)} dynamic-slice(s32[5120]{0:T(1024)} %param.7, s32[]{:T(128)S(6)} %select_n.22), dynamic_slice_sizes={160} | dynamic-slice | bytes 1284 | tf_op jit(solution)/shard_map/dynamic_slice | solution.py:48
  10.9 3.8 %collective-permute-done = bf16[160,1152]{1,0:T(8,128)(2,1)S(1)} collective-permute-done((bf16[160,1152]{1,0:T(8,128)(2,1)}, bf16[160,1152]{1,0:T(8,128)(2,1)S(1)}, u32[]{:S(2)}, u32[]{:S(2)}) %collective-permute-start) | collective-permute-done | bytes 368672 | tf_op jit(solution)/shard_map/ppermute | solution.py:12
  14.8 1.5 %collective-permute-done.3 = bf16[160,1152]{1,0:T(8,128)(2,1)S(1)} collective-permute-done((bf16[160,1152]{1,0:T(8,128)(2,1)}, bf16[160,1152]{1,0:T(8,128)(2,1)S(1)}, u32[]{:S(2)}, u32[]{:S(2)}) %collective-permute-start.3) | collective-permute-done | bytes 368672 | tf_op jit(solution)/shard_map/ppermute | solution.py:12
  16.4 3.0 %collective-permute-done.1 = bf16[160,1152]{1,0:T(8,128)(2,1)S(1)} collective-permute-done((bf16[160,1152]{1,0:T(8,128)(2,1)}, bf16[160,1152]{1,0:T(8,128)(2,1)S(1)}, u32[]{:S(2)}, u32[]{:S(2)}) %collective-permute-start.1) | collective-permute-done | bytes 368672 | tf_op jit(solution)/shard_map/ppermute | solution.py:12
  19.7 0.5 %fusion.40 = bf16[160,320]{1,0:T(8,128)(2,1)S(1)} fusion(bf16[160,1152]{1,0:T(8,128)(2,1)S(1)} %copy-done.1, f32[160]{0:T(256)S(1)} %add_rsqrt_fusion.4, f32[]{:T(128)} %bitcast.12, f32[]{:T(128)} %bitcast.11, f32[]{:T(128)S(6)} %neg.15, s32[320]{0:T(512)S(1)} %pad_add_fusion, s32[160]{0:T(256)S(1)} %dynamic_slice.3, bf16[160,1152]{1,0:T(8,128)(2,1)S(1)} %fusion.30, ...), kind=kOutput, calls=%fused_computation.62 | convolution fusion | flops 120555520 | bytes 1210892 | tf_op jit(solution)/shard_map/dot_general | solution.py:66
  20.2 0.5 %fusion.45 = f32[320,1152]{1,0:T(8,128)S(1)} fusion(bf16[160,320]{1,0:T(8,128)(2,1)S(1)} %fusion.40, bf16[160,1152]{1,0:T(8,128)(2,1)S(1)} %copy-done.1, f32[160]{0:T(256)S(1)} %add_rsqrt_fusion.4), kind=kOutput, calls=%fused_computation.64 | convolution fusion | flops 118517760 | bytes 1946240 | tf_op jit(solution)/shard_map/dot_general | solution.py:86
  20.7 0.5 %fusion.13 = bf16[160,320]{1,0:T(8,128)(2,1)S(1)} fusion(bf16[160,1152]{1,0:T(8,128)(2,1)S(1)} %collective-permute-done.1, f32[160]{0:T(256)S(1)} %add_rsqrt_fusion.1, f32[]{:T(128)} %bitcast.14, f32[]{:T(128)} %bitcast.9, bf16[160,1152]{1,0:T(8,128)(2,1)S(1)} %fusion.30, bf16[160,1152]{1,0:T(8,128)(2,1)S(1)} %fusion.17), kind=kOutput, calls=%fused_computation.20 | convolution fusion | flops 120350720 | bytes 1208968 | tf_op jit(solution)/shard_map/dot_general | solution.py:66
  21.2 0.5 %convolution_add_fusion.1 = f32[320,1152]{1,0:T(8,128)S(1)} fusion(f32[320,1152]{1,0:T(8,128)S(1)} %fusion.45, bf16[160,320]{1,0:T(8,128)(2,1)S(1)} %fusion.13, bf16[160,1152]{1,0:T(8,128)(2,1)S(1)} %collective-permute-done.1, f32[160]{0:T(256)S(1)} %add_rsqrt_fusion.1), kind=kOutput, calls=%fused_computation.1 | convolution fusion | flops 118886400 | bytes 3420800 | tf_op jit(solution)/shard_map/dot_general | solution.py:86
  21.7 0.5 %fusion.14 = bf16[160,320]{1,0:T(8,128)(2,1)S(1)} fusion(bf16[160,1152]{1,0:T(8,128)(2,1)S(1)} %collective-permute-done.3, f32[160]{0:T(256)S(1)} %add_rsqrt_fusion, f32[]{:T(128)} %bitcast.13, f32[]{:T(128)} %bitcast.10, bf16[160,1152]{1,0:T(8,128)(2,1)S(1)} %fusion.30, bf16[160,1152]{1,0:T(8,128)(2,1)S(1)} %fusion.17), kind=kOutput, calls=%fused_computation.21 | convolution fusion | flops 120350720 | bytes 1208968 | tf_op jit(solution)/shard_map/dot_general | solution.py:66
  22.2 0.5 %convolution_add_fusion = f32[320,1152]{1,0:T(8,128)S(1)} fusion(f32[320,1152]{1,0:T(8,128)S(1)} %convolution_add_fusion.1, bf16[160,320]{1,0:T(8,128)(2,1)S(1)} %fusion.14, bf16[160,1152]{1,0:T(8,128)(2,1)S(1)} %collective-permute-done.3, f32[160]{0:T(256)S(1)} %add_rsqrt_fusion), kind=kOutput, calls=%fused_computation | convolution fusion | flops 118886400 | bytes 3420800 | tf_op jit(solution)/shard_map/dot_general | solution.py:86
  22.7 1.6 %collective-permute-start.5 = (bf16[160,1152]{1,0:T(8,128)(2,1)S(1)}, bf16[160,1152]{1,0:T(8,128)(2,1)S(1)}, u32[]{:S(2)}, u32[]{:S(2)}) collective-permute-start(bf16[160,1152]{1,0:T(8,128)(2,1)S(1)} %slice.17), channel_id=1, source_target_pairs={{0,1},{1,0},{2,3},{3,2},{4,5},{5,4},{6,7},{7,6},{8,9},{9,8},{10,11... | collective-permute-start | bytes 1105928 | tf_op jit(solution)/shard_map/ppermute | solution.py:12
  24.3 0.4 convolution_convert_fusion
  24.7 1.8 %collective-permute-start.4 = (bf16[160,1152]{1,0:T(8,128)(2,1)S(1)}, bf16[160,1152]{1,0:T(8,128)(2,1)S(1)}, u32[]{:S(2)}, u32[]{:S(2)}) collective-permute-start(bf16[160,1152]{1,0:T(8,128)(2,1)S(1)} %convolution_convert_fusion), channel_id=1, source_target_pairs={{0,28},{2,30},{4,0},{6,2},{8,4},{10,6},{12,8},{14,10},{16,12},{18,... | collective-permute-start | bytes 1105928 | tf_op jit(solution)/shard_map/ppermute | solution.py:12
  26.9 3.4 %collective-permute-done.5 = bf16[160,1152]{1,0:T(8,128)(2,1)S(1)} collective-permute-done((bf16[160,1152]{1,0:T(8,128)(2,1)S(1)}, bf16[160,1152]{1,0:T(8,128)(2,1)S(1)}, u32[]{:S(2)}, u32[]{:S(2)}) %collective-permute-start.5) | collective-permute-done | bytes 368672 | tf_op jit(solution)/shard_map/ppermute | solution.py:12
  30.5 1.2 %fusion.27 = f32[160,1152]{1,0:T(8,128)} fusion(bf16[160,1152]{1,0:T(8,128)(2,1)S(1)} %copy-done, bf16[160,1152]{1,0:T(8,128)(2,1)S(1)} %collective-permute-done.5, f32[320,1152]{1,0:T(8,128)S(1)} %convolution_add_fusion, f32[160]{0:T(256)S(1)} %fusion.25, f32[160]{0:T(256)S(1)} %add_rsqrt_fusion.3), kind=kLoop, calls=%fused_computation.44 | loop fusion | flops 1290240 | bytes 2213120 | tf_op jit(solution)/shard_map/mul | solution.py:22
  31.7 0.5 %collective-permute-done.4 = bf16[160,1152]{1,0:T(8,128)(2,1)S(1)} collective-permute-done((bf16[160,1152]{1,0:T(8,128)(2,1)S(1)}, bf16[160,1152]{1,0:T(8,128)(2,1)S(1)}, u32[]{:S(2)}, u32[]{:S(2)}) %collective-permute-start.4) | collective-permute-done | bytes 368672 | tf_op jit(solution)/shard_map/ppermute | solution.py:12
  32.2 3.9 %collective-permute-done.2 = bf16[160,1152]{1,0:T(8,128)(2,1)S(1)} collective-permute-done((bf16[160,1152]{1,0:T(8,128)(2,1)S(1)}, bf16[160,1152]{1,0:T(8,128)(2,1)S(1)}, u32[]{:S(2)}, u32[]{:S(2)}) %collective-permute-start.2) | collective-permute-done | bytes 368672 | tf_op jit(solution)/shard_map/ppermute | solution.py:12
  36.2 0.5 %fusion.21 = (f32[160]{0:T(256)S(1)}, f32[160,1152]{1,0:T(8,128)S(1)}) fusion(bf16[160,1152]{1,0:T(8,128)(2,1)S(1)} %copy-done.1, f32[160]{0:T(256)S(1)} %add_rsqrt_fusion.4, bf16[160,1152]{1,0:T(8,128)(2,1)S(1)} %collective-permute-done.4, bf16[160,1152]{1,0:T(8,128)(2,1)S(1)} %collective-permute-done.2, bf16[160,320]{1,0:T(8,128)(2,1)S(1)} %fusion.40, ...), kind=kOutput, calls=%fused_computation.38 | convolution fusion | flops 120913760 | bytes 2684160 | tf_op jit(solution)/shard_map/dot_general | solution.py:81
  36.7 1.2 %fusion.23 = f32[160,1152]{1,0:T(8,128)} fusion(bf16[160,1152]{1,0:T(8,128)(2,1)S(1)} %copy-done.1, f32[160]{0:T(256)S(1)} %get-tuple-element.2, f32[160]{0:T(256)S(1)} %add_rsqrt_fusion.4, bf16[160,1152]{1,0:T(8,128)(2,1)S(1)} %collective-permute-done.4, f32[160,1152]{1,0:T(8,128)S(1)} %get-tuple-element.3, bf16[160,1152]{1,0:T(8,128)(2,1)S(1)} %collective-permute-done.2), kind=kLoop, calls=%fused_computation.40 | loop fusion | flops 1658880 | bytes 2581760 | tf_op jit(solution)/shard_map/mul | solution.py:22
  (20 shorter events, 1.4 us)
Async XLA Ops:
  0.6 15.7 %collective-permute-start.3 = (bf16[160,1152]{1,0:T(8,128)(2,1)}, bf16[160,1152]{1,0:T(8,128)(2,1)S(1)}, u32[]{:S(2)}, u32[]{:S(2)}) collective-permute-start(bf16[160,1152]{1,0:T(8,128)(2,1)} %param.5), channel_id=1, source_target_pairs={{0,4},{2,6},{4,8},{6,10},{8,12},{10,14},{12,16},{14,18},{16,20},{1... | collective-permute-start | bytes 1105928 | tf_op jit(solution)/shard_map/ppermute | solution.py:12
  3.6 15.8 %collective-permute-start.1 = (bf16[160,1152]{1,0:T(8,128)(2,1)}, bf16[160,1152]{1,0:T(8,128)(2,1)S(1)}, u32[]{:S(2)}, u32[]{:S(2)}) collective-permute-start(bf16[160,1152]{1,0:T(8,128)(2,1)} %param.5), channel_id=1, source_target_pairs={{0,2},{2,4},{4,6},{6,8},{8,10},{10,12},{12,14},{14,16},{16,18},{18... | collective-permute-start | bytes 1105928 | tf_op jit(solution)/shard_map/ppermute | solution.py:12
  3.6 11.0 %collective-permute-start = (bf16[160,1152]{1,0:T(8,128)(2,1)}, bf16[160,1152]{1,0:T(8,128)(2,1)S(1)}, u32[]{:S(2)}, u32[]{:S(2)}) collective-permute-start(bf16[160,1152]{1,0:T(8,128)(2,1)} %param.6), channel_id=1, source_target_pairs={{0,1},{1,0},{2,3},{3,2},{4,5},{5,4},{6,7},{7,6},{8,9},{9,8},{10,11... | collective-permute-start | bytes 1105928 | tf_op jit(solution)/shard_map/ppermute | solution.py:12
  6.3 13.4 %copy-start.1 = (bf16[160,1152]{1,0:T(8,128)(2,1)S(1)}, bf16[160,1152]{1,0:T(8,128)(2,1)}, u32[]{:S(2)}) copy-start(bf16[160,1152]{1,0:T(8,128)(2,1)} %param.5) | copy-start | bytes 1105924
  22.7 7.6 %copy-start = (bf16[160,1152]{1,0:T(8,128)(2,1)S(1)}, bf16[160,1152]{1,0:T(8,128)(2,1)}, u32[]{:S(2)}) copy-start(bf16[160,1152]{1,0:T(8,128)(2,1)} %param.6) | copy-start | bytes 1105924
  22.7 7.6 %collective-permute-start.5 = (bf16[160,1152]{1,0:T(8,128)(2,1)S(1)}, bf16[160,1152]{1,0:T(8,128)(2,1)S(1)}, u32[]{:S(2)}, u32[]{:S(2)}) collective-permute-start(bf16[160,1152]{1,0:T(8,128)(2,1)S(1)} %slice.17), channel_id=1, source_target_pairs={{0,1},{1,0},{2,3},{3,2},{4,5},{5,4},{6,7},{7,6},{8,9},{9,8},{10,11... | collective-permute-start | bytes 1105928 | tf_op jit(solution)/shard_map/ppermute | solution.py:12
  24.7 7.6 %collective-permute-start.4 = (bf16[160,1152]{1,0:T(8,128)(2,1)S(1)}, bf16[160,1152]{1,0:T(8,128)(2,1)S(1)}, u32[]{:S(2)}, u32[]{:S(2)}) collective-permute-start(bf16[160,1152]{1,0:T(8,128)(2,1)S(1)} %convolution_convert_fusion), channel_id=1, source_target_pairs={{0,28},{2,30},{4,0},{6,2},{8,4},{10,6},{12,8},{14,10},{16,12},{18,... | collective-permute-start | bytes 1105928 | tf_op jit(solution)/shard_map/ppermute | solution.py:12
  26.8 9.3 %collective-permute-start.2 = (bf16[160,1152]{1,0:T(8,128)(2,1)S(1)}, bf16[160,1152]{1,0:T(8,128)(2,1)S(1)}, u32[]{:S(2)}, u32[]{:S(2)}) collective-permute-start(bf16[160,1152]{1,0:T(8,128)(2,1)S(1)} %convolution_convert_fusion.1), channel_id=1, source_target_pairs={{0,30},{2,0},{4,2},{6,4},{8,6},{10,8},{12,10},{14,12},{16,14},{18,... | collective-permute-start | bytes 1105928 | tf_op jit(solution)/shard_map/ppermute | solution.py:12

commit v2 on v1

v2 whole, which is shorter than its diff:
```python
import jax
import jax.numpy as jnp
from jax import lax
from jax.sharding import PartitionSpec as P

TURNS = 3


def unit_rows(raw_rows):
    values = raw_rows.astype(jnp.float32)
    inverse = lax.rsqrt(jnp.sum(values * values, axis=1, keepdims=True) + 1e-06)
    return (values * inverse, inverse)


def half_rows(raw_rows):
    return unit_rows(raw_rows)[0].astype(jnp.bfloat16)


def tangent_part(gradient, unit_rows_f, inverse):
    return (
        gradient - unit_rows_f * jnp.sum(unit_rows_f * gradient, axis=1, keepdims=True)
    ) * inverse


def local(image_embeds, text_embeds, pair_text, similarity_scale, logit_bias):
    rows = image_embeds.shape[0]
    cycle_count = lax.axis_size("blk")
    node_count = lax.axis_size("node")
    cycle_index = lax.axis_index("blk")
    node_index = lax.axis_index("node")
    first_core = cycle_index % 2 == 0
    scale = similarity_scale[0]
    bias = logit_bias[0]

    def send(block, parity, ahead, across=0):
        route = [
            (
                g * node_count + n,
                (g + ahead) % cycle_count * node_count + (n + across) % node_count,
            )
            for g in range(parity, cycle_count, 2)
            for n in range(node_count)
        ]
        return lax.ppermute(block, ("blk", "node"), route)

    visit_b = send(image_embeds, 1, 1)
    far_b = [send(text_embeds, 1, -1, -k) for k in range(1, node_count)]
    visit_a = send(image_embeds, 0, 2)
    far_a = [send(text_embeds, 0, 0, -k) for k in range(1, node_count)]
    mate_image = send(image_embeds, 1, -1)
    mate_text = send(text_embeds, 1, -1)

    image_unit, image_inv = unit_rows(image_embeds)
    text_unit, text_inv = unit_rows(text_embeds)

    text_a = jnp.concatenate([text_unit.astype(jnp.bfloat16)] + [half_rows(f) for f in far_a])
    text_b = jnp.concatenate([half_rows(mate_text)] + [half_rows(f) for f in far_b])
    text_ab = jnp.concatenate([text_a, text_b])
    span = text_a.shape[0]

    def weigh(images, texts, start=None, at=None):
        logits = (
            scale
            * lax.dot_general(
                images, texts, (((1,), (1,)), ((), ())), preferred_element_type=jnp.float32
            )
            + bias
        )
        if start is None:
            return (scale * jax.nn.sigmoid(logits)).astype(jnp.bfloat16)
        targets = lax.dynamic_slice_in_dim(pair_text, start, rows, 0)
        columns = jnp.concatenate(
            [
                (at * node_count + (node_index + k) % node_count) * rows
                + jnp.arange(rows, dtype=jnp.int32)
                for k in range(node_count)
            ]
        )
        paired = targets[:, None] == columns[None, :]
        return (
            jnp.where(paired, -scale, scale)
            * jax.nn.sigmoid(jnp.where(paired, -logits, logits))
        ).astype(jnp.bfloat16)

    def combine(weights, vectors):
        return jnp.dot(weights, vectors, preferred_element_type=jnp.float32)

    def gather_terms(weights, vectors):
        return lax.dot_general(
            weights, vectors, (((0,), (0,)), ((), ())), preferred_element_type=jnp.float32
        )

    group_a = cycle_index - cycle_index % 2
    va, vb = half_rows(visit_a), half_rows(visit_b)
    ia, ib = image_unit.astype(jnp.bfloat16), half_rows(mate_image)
    w_va = weigh(va, text_a)
    w_vb = weigh(vb, text_ab)
    back_a = send(combine(w_va, text_a).astype(jnp.bfloat16), 0, -2)
    back_b = send(combine(w_vb, text_ab).astype(jnp.bfloat16), 0, -1)

    start = (group_a * node_count + node_index) * rows
    w_ia = jnp.concatenate([weigh(ia, text_a, start, group_a), weigh(ia, text_b)], axis=1)
    w_ib = weigh(ib, text_b, start + node_count * rows, group_a + 1)
    terms_a = gather_terms(
        jnp.concatenate([w_ia[:, :span], w_va, w_vb[:, :span]]), jnp.concatenate([ia, va, vb])
    )
    terms_b = gather_terms(
        jnp.concatenate([w_ia[:, span:], w_ib, w_vb[:, span:]]), jnp.concatenate([ia, ib, vb])
    )

    text_back = 0.0
    for k in range(1, node_count):
        part = slice(k * rows, (k + 1) * rows)
        text_back = (
            text_back
            + send(terms_b[part].astype(jnp.bfloat16), 0, 1, k).astype(jnp.float32)
            + send(terms_a[part].astype(jnp.bfloat16), 0, 0, k).astype(jnp.float32)
        )
    image_b = send(combine(w_ib, text_b).astype(jnp.bfloat16), 0, 1)
    text_own_b = send(terms_b[:rows].astype(jnp.bfloat16), 0, 1)
    image_a = combine(w_ia, text_ab)

    image_dir = (
        jnp.where(first_core, image_a, image_b.astype(jnp.float32))
        + back_a.astype(jnp.float32)
        + back_b.astype(jnp.float32)
    )
    text_dir = jnp.where(first_core, terms_a[:rows], text_own_b.astype(jnp.float32)) + text_back
    image_grads = tangent_part(image_dir, image_unit, image_inv)
    text_grads = tangent_part(text_dir, text_unit, text_inv)
    return (image_grads, text_grads)


def solution(mesh):
    return jax.shard_map(
        local,
        mesh=mesh,
        in_specs=(P(("blk", "node"), None), P(("blk", "node"), None), P(), P(), P()),
        out_specs=(P(("blk", "node"), None), P(("blk", "node"), None)),
        check_vma=False,
    )
```

time: 38.1 us -> 51.7 us (1.36)
  starting transfers between devices: 7.95 us -> 27.9 us
  waiting for transfers between devices: 16.1 us -> 5.87 us
  matrix products: 4.13 us -> 5.76 us
  other arithmetic: 6.79 us -> 8.24 us
    ppermute x6 -> x12, starting transfers between devices: 7.95 us -> 27.9 us  [send(): return lax.ppermute(block, ('blk', 'node'), route)]
    ppermute x6 -> x12, waiting for transfers between devices: 16.1 us -> 5.87 us  [send(): return lax.ppermute(block, ('blk', 'node'), route)]
    dot_general x9 -> x11, matrix products: 4.13 us -> 5.76 us  [the longest x5 2.58 us: weigh(): lax.dot_general(images, texts, (((1,), (1,)), ((), ())), preferred_elemen...]
    convert_element_type x1 -> x7, other arithmetic: 0.13 us -> 0.93 us  [the longest x6 0.8 us: half_rows(): return unit_rows(raw_rows)[0].astype(jnp.bfloat16)]
    reduce_sum x5 -> x8, other arithmetic: 2.85 us -> 3.22 us  [unit_rows(): inverse = lax.rsqrt(jnp.sum(values * values, axis=1, keepdims=True) + 1e-06)]
  transfers between devices with their start and end apart: 6 -> 12, of which waited for: 6 -> 2; matrix products, arithmetic and copies ran while one was open for 18% -> 26% of each run, Pallas kernels for 0% -> 0%
where the time goes in v2:
time: 51.7 us; the launch traced here: 51.2 us
  starting transfers between devices  27.9 us (54%)
  other arithmetic  8.24 us (16%)
  waiting for transfers between devices  5.87 us (11%)
  matrix products  5.76 us (11%)
  between operations  2.32 us (4%)
  local copies, waits for them, and re-layouts  1.06 us (2%)
    ppermute x12, starting transfers between devices, send(): return lax.ppermute(block, ('blk', 'node'), route)  27.9 us
    ppermute x12, waiting for transfers between devices, send(): return lax.ppermute(block, ('blk', 'node'), route)  5.87 us
    reduce_sum x8, other arithmetic, unit_rows(): inverse = lax.rsqrt(jnp.sum(values * values, axis=1, keepdims=True) + 1e-06)  3.22 us
    dot_general x5, matrix products, weigh(): lax.dot_general(images, texts, (((1,), (1,)), ((), ())), preferred_elemen...  2.58 us
    mul x2, other arithmetic, tangent_part(): (gradient - unit_rows_f * jnp.sum(unit_rows_f * gradient, axis=1, keepdim...  2.39 us
    dot_general x4, matrix products, combine(): return jnp.dot(weights, vectors, preferred_element_type=jnp.float32)  1.94 us
    dot_general x2, matrix products, gather_terms(): lax.dot_general(weights, vectors, (((0,), (0,)), ((), ())), preferred_ele...  1.24 us
    convert_element_type x1, other arithmetic, local(): text_unit.astype(jnp.bfloat16)  1.12 us
  transfers between devices with their start and end apart: 12, of which 2 were waited for; matrix products, arithmetic and copies ran while one was open for 26% of the time, Pallas kernels for 0%

profile of v2, /device:TPU:0, one launch (start us, length us, event | category | flops | bytes accessed | tf_op | source)
XLA Modules:
  0.0 51.2 jit_solution(6245926983802636829)
XLA Ops:
  0.6 1.4 %collective-permute-start.2 = (bf16[160,1152]{1,0:T(8,128)(2,1)}, bf16[160,1152]{1,0:T(8,128)(2,1)S(1)}, u32[]{:S(2)}, u32[]{:S(2)}) collective-permute-start(bf16[160,1152]{1,0:T(8,128)(2,1)} %param.6), channel_id=1, source_target_pairs={{2,1},{3,0},{6,5},{7,4},{10,9},{11,8},{14,13},{15,12},{18,17},{19,... | collective-permute-start | bytes 1105928 | tf_op jit(solution)/shard_map/ppermute | solution.py:44
  2.1 1.3 %collective-permute-start.1 = (bf16[160,1152]{1,0:T(8,128)(2,1)}, bf16[160,1152]{1,0:T(8,128)(2,1)S(1)}, u32[]{:S(2)}, u32[]{:S(2)}) collective-permute-start(bf16[160,1152]{1,0:T(8,128)(2,1)} %param.6), channel_id=1, source_target_pairs={{2,0},{3,1},{6,4},{7,5},{10,8},{11,9},{14,12},{15,13},{18,16},{19,... | collective-permute-start | bytes 1105928 | tf_op jit(solution)/shard_map/ppermute | solution.py:44
  3.4 4.9 %collective-permute-start = (bf16[160,1152]{1,0:T(8,128)(2,1)}, bf16[160,1152]{1,0:T(8,128)(2,1)S(1)}, u32[]{:S(2)}, u32[]{:S(2)}) collective-permute-start(bf16[160,1152]{1,0:T(8,128)(2,1)} %param.6), channel_id=1, source_target_pairs={{0,1},{1,0},{4,5},{5,4},{8,9},{9,8},{12,13},{13,12},{16,17},{17,16... | collective-permute-start | bytes 1105928 | tf_op jit(solution)/shard_map/ppermute | solution.py:44
  8.3 1.3 %collective-permute-start.7 = (bf16[160,1152]{1,0:T(8,128)(2,1)}, bf16[160,1152]{1,0:T(8,128)(2,1)S(1)}, u32[]{:S(2)}, u32[]{:S(2)}) collective-permute-start(bf16[160,1152]{1,0:T(8,128)(2,1)} %param.5), channel_id=1, source_target_pairs={{2,4},{3,5},{6,8},{7,9},{10,12},{11,13},{14,16},{15,17},{18,20},{1... | collective-permute-start | bytes 1105928 | tf_op jit(solution)/shard_map/ppermute | solution.py:44
  9.6 3.4 %collective-permute-start.5 = (bf16[160,1152]{1,0:T(8,128)(2,1)}, bf16[160,1152]{1,0:T(8,128)(2,1)S(1)}, u32[]{:S(2)}, u32[]{:S(2)}) collective-permute-start(bf16[160,1152]{1,0:T(8,128)(2,1)} %param.5), channel_id=1, source_target_pairs={{0,4},{1,5},{4,8},{5,9},{8,12},{9,13},{12,16},{13,17},{16,20},{17,... | collective-permute-start | bytes 1105928 | tf_op jit(solution)/shard_map/ppermute | solution.py:44
  13.0 1.2 %fusion.35 = f32[160]{0:T(256)S(1)} fusion(bf16[160,1152]{1,0:T(8,128)(2,1)} %param.5), kind=kLoop, calls=%fused_computation.65 | loop fusion | flops 552800 | bytes 369280 | tf_op jit(solution)/shard_map/reduce_sum | solution.py:11
  14.1 1.1 %fusion.39 = f32[160]{0:T(256)S(1)} fusion(bf16[160,1152]{1,0:T(8,128)(2,1)} %param.6), kind=kLoop, calls=%fused_computation.69 | loop fusion | flops 552800 | bytes 369280 | tf_op jit(solution)/shard_map/reduce_sum | solution.py:11
  15.3 1.1 %fusion.28 = bf16[160,1152]{1,0:T(8,128)(2,1)S(1)} fusion(bf16[160,1152]{1,0:T(8,128)(2,1)} %param.6, f32[160]{0:T(256)S(1)} %add_rsqrt_fusion.6), kind=kLoop, calls=%fused_computation.56 | loop fusion | flops 552960 | bytes 737920 | tf_op jit(solution)/shard_map/convert_element_type | solution.py:56
  16.8 0.8 %fusion.90 = (s32[160]{0:T(256)S(1)}, s32[160]{0:T(256)S(1)}) fusion(s32[5120]{0:T(1024)} %param.7, s32[]{:T(128)S(6)} %select_n.60, s32[]{:T(128)S(6)} %select_n.55), kind=kLoop, calls=%fused_computation.143 | loop fusion | bytes 2568 | tf_op jit(solution)/shard_map/dynamic_slice | solution.py:71
  18.9 3.1 %collective-permute-done.7 = bf16[160,1152]{1,0:T(8,128)(2,1)S(1)} collective-permute-done((bf16[160,1152]{1,0:T(8,128)(2,1)}, bf16[160,1152]{1,0:T(8,128)(2,1)S(1)}, u32[]{:S(2)}, u32[]{:S(2)}) %collective-permute-start.7) | collective-permute-done | bytes 368672 | tf_op jit(solution)/shard_map/ppermute | solution.py:44
  22.0 1.3 %collective-permute-start.3 = (bf16[160,1152]{1,0:T(8,128)(2,1)S(1)}, bf16[160,1152]{1,0:T(8,128)(2,1)S(1)}, u32[]{:S(2)}, u32[]{:S(2)}) collective-permute-start(bf16[160,1152]{1,0:T(8,128)(2,1)S(1)} %copy-done.1), channel_id=1, source_target_pairs={{2,0},{3,1},{6,4},{7,5},{10,8},{11,9},{14,12},{15,13},{18,16},{19,... | collective-permute-start | bytes 1105928 | tf_op jit(solution)/shard_map/ppermute | solution.py:44
  24.5 0.7 %fusion.6 = bf16[160,640]{1,0:T(8,128)(2,1)S(1)} fusion(bf16[160,1152]{1,0:T(8,128)(2,1)S(1)} %fusion.51, f32[]{:T(128)} %bitcast.17, f32[]{:T(128)} %bitcast.12, bf16[160,1152]{1,0:T(8,128)(2,1)S(1)} %fusion.45, bf16[160,1152]{1,0:T(8,128)(2,1)S(1)} %fusion.43, bf16[160,1152]{1,0:T(8,128)(2,1)S(1)} %fusion.41, bf16[160,1152]{1,0:T(8,128)(2,1)S(1)} %fusion.28), kind=kOutput, calls=%fused_computation.16 | convolution fusion | flops 242544640 | bytes 2048008 | tf_op jit(solution)/shard_map/dot_general | solution.py:64
  25.7 4.5 %collective-permute-start.8 = (bf16[160,1152]{1,0:T(8,128)(2,1)S(1)}, bf16[160,1152]{1,0:T(8,128)(2,1)S(1)}, u32[]{:S(2)}, u32[]{:S(2)}) collective-permute-start(bf16[160,1152]{1,0:T(8,128)(2,1)S(1)} %convolution_convert_fusion.1), channel_id=1, source_target_pairs={{0,30},{1,31},{4,2},{5,3},{8,6},{9,7},{12,10},{13,11},{16,14},{17,... | collective-permute-start | bytes 1105928 | tf_op jit(solution)/shard_map/ppermute | solution.py:44
  31.8 0.6 %fusion.23 = f32[320,1152]{1,0:T(8,128)S(1)} fusion(bf16[160,1152]{1,0:T(8,128)(2,1)S(1)} %fusion.51, bf16[160,1152]{1,0:T(8,128)(2,1)S(1)} %fusion.31, bf16[160,1152]{1,0:T(8,128)(2,1)S(1)} %fusion.49, bf16[160,320]{1,0:T(8,128)(2,1)S(1)} %get-tuple-element.5, bf16[160,320]{1,0:T(8,128)(2,1)S(1)} %fusion.22, bf16[160,320]{1,0:T(8,128)(2,1)S(1)} %fusion.74), kind=kOutput, calls=%fused_computation.37 | convolution fusion | flops 358133760 | bytes 2887680 | tf_op jit(solution)/shard_map/dot_general | solution.py:89
  32.5 2.4 %collective-permute-start.11 = (bf16[160,1152]{1,0:T(8,128)(2,1)S(1)}, bf16[160,1152]{1,0:T(8,128)(2,1)S(1)}, u32[]{:S(2)}, u32[]{:S(2)}) collective-permute-start(bf16[160,1152]{1,0:T(8,128)(2,1)S(1)} %slice.41), channel_id=1, source_target_pairs={{0,1},{1,0},{4,5},{5,4},{8,9},{9,8},{12,13},{13,12},{16,17},{17,16... | collective-permute-start | bytes 1105928 | tf_op jit(solution)/shard_map/ppermute | solution.py:44
  36.0 0.6 %convolution_convert_fusion = bf16[320,1152]{1,0:T(8,128)(2,1)S(1)} fusion(bf16[160,1152]{1,0:T(8,128)(2,1)S(1)} %fusion.51, bf16[160,1152]{1,0:T(8,128)(2,1)S(1)} %fusion.31, bf16[160,1152]{1,0:T(8,128)(2,1)S(1)} %fusion.47, bf16[160,320]{1,0:T(8,128)(2,1)S(1)} %get-tuple-element.4, bf16[160,320]{1,0:T(8,128)(2,1)S(1)} %fusion.68, ...), kind=kOutput, calls=%fused_computation | convolution fusion | flops 358502400 | bytes 2150400 | tf_op jit(solution)/shard_map/dot_general | solution.py:89
  36.7 1.3 %collective-permute-start.10 = (bf16[160,1152]{1,0:T(8,128)(2,1)S(1)}, bf16[160,1152]{1,0:T(8,128)(2,1)S(1)}, u32[]{:S(2)}, u32[]{:S(2)}) collective-permute-start(bf16[160,1152]{1,0:T(8,128)(2,1)S(1)} %get-tuple-element.3), channel_id=1, source_target_pairs={{0,3},{1,2},{4,7},{5,6},{8,11},{9,10},{12,15},{13,14},{16,19},{17,... | collective-permute-start | bytes 1105928 | tf_op jit(solution)/shard_map/ppermute | solution.py:44
  38.0 1.4 %collective-permute-start.9 = (bf16[160,1152]{1,0:T(8,128)(2,1)S(1)}, bf16[160,1152]{1,0:T(8,128)(2,1)S(1)}, u32[]{:S(2)}, u32[]{:S(2)}) collective-permute-start(bf16[160,1152]{1,0:T(8,128)(2,1)S(1)} %get-tuple-element.2), channel_id=1, source_target_pairs={{0,2},{1,3},{4,6},{5,7},{8,10},{9,11},{12,14},{13,15},{16,18},{17,... | collective-permute-start | bytes 1105928 | tf_op jit(solution)/shard_map/ppermute | solution.py:44
  39.9 3.3 %collective-permute-start.6 = (bf16[160,1152]{1,0:T(8,128)(2,1)S(1)}, bf16[160,1152]{1,0:T(8,128)(2,1)S(1)}, u32[]{:S(2)}, u32[]{:S(2)}) collective-permute-start(bf16[160,1152]{1,0:T(8,128)(2,1)S(1)} %convolution_convert_fusion.2), channel_id=1, source_target_pairs={{0,28},{1,29},{4,0},{5,1},{8,4},{9,5},{12,8},{13,9},{16,12},{17,13... | collective-permute-start | bytes 1105928 | tf_op jit(solution)/shard_map/ppermute | solution.py:44
  43.6 1.3 %collective-permute-start.4 = (bf16[160,1152]{1,0:T(8,128)(2,1)S(1)}, bf16[160,1152]{1,0:T(8,128)(2,1)S(1)}, u32[]{:S(2)}, u32[]{:S(2)}) collective-permute-start(bf16[160,1152]{1,0:T(8,128)(2,1)S(1)} %convolution_convert_fusion.3), channel_id=1, source_target_pairs={{0,2},{1,3},{4,6},{5,7},{8,10},{9,11},{12,14},{13,15},{16,18},{17,... | collective-permute-start | bytes 1105928 | tf_op jit(solution)/shard_map/ppermute | solution.py:44
  45.3 1.2 %fusion.38 = f32[160,1152]{1,0:T(8,128)} fusion(bf16[160,1152]{1,0:T(8,128)(2,1)S(1)} %copy-done, f32[160]{0:T(256)S(1)} %fusion.36, f32[160]{0:T(256)S(1)} %add_rsqrt_fusion.6, bf16[160,1152]{1,0:T(8,128)(2,1)S(1)} %collective-permute-done.11, bf16[160,1152]{1,0:T(8,128)(2,1)S(1)} %collective-permute-done.10, ...), kind=kLoop, calls=%fused_computation.68 | loop fusion | flops 2027520 | bytes 2950401 | tf_op jit(solution)/shard_map/mul | solution.py:20
  46.5 2.8 %collective-permute-done.6 = bf16[160,1152]{1,0:T(8,128)(2,1)S(1)} collective-permute-done((bf16[160,1152]{1,0:T(8,128)(2,1)S(1)}, bf16[160,1152]{1,0:T(8,128)(2,1)S(1)}, u32[]{:S(2)}, u32[]{:S(2)}) %collective-permute-start.6) | collective-permute-done | bytes 368672 | tf_op jit(solution)/shard_map/ppermute | solution.py:44
  49.3 0.7 %fusion.32 = (f32[160]{0:T(256)S(1)}, f32[160,1152]{1,0:T(8,128)S(1)}) fusion(bf16[160,1152]{1,0:T(8,128)(2,1)S(1)} %copy-done.1, f32[160]{0:T(256)S(1)} %add_rsqrt_fusion.7, bf16[160,1152]{1,0:T(8,128)(2,1)S(1)} %collective-permute-done.8, bf16[160,1152]{1,0:T(8,128)(2,1)S(1)} %collective-permute-done.6, bf16[160,1152]{1,0:T(8,128)(2,1)S(1)} %collective-permute-done.4, ...), kind=kOutput, calls=%fused_computation.62 | convolution fusion | flops 244080480 | bytes 3892481 | tf_op jit(solution)/shard_map/dot_general | solution.py:86
  50.0 1.2 %fusion.34 = f32[160,1152]{1,0:T(8,128)} fusion(bf16[160,1152]{1,0:T(8,128)(2,1)S(1)} %copy-done.1, f32[160]{0:T(256)S(1)} %get-tuple-element.8, f32[160]{0:T(256)S(1)} %add_rsqrt_fusion.7, bf16[160,1152]{1,0:T(8,128)(2,1)S(1)} %collective-permute-done.8, bf16[160,1152]{1,0:T(8,128)(2,1)S(1)} %collective-permute-done.6, ...), kind=kLoop, calls=%fused_computation.64 | loop fusion | flops 2027520 | bytes 2950401 | tf_op jit(solution)/shard_map/mul | solution.py:20
  (50 shorter events, 5.9 us)
Async XLA Ops:
  0.6 15.8 %copy-start.1 = (bf16[160,1152]{1,0:T(8,128)(2,1)S(1)}, bf16[160,1152]{1,0:T(8,128)(2,1)}, u32[]{:S(2)}) copy-start(bf16[160,1152]{1,0:T(8,128)(2,1)} %param.5) | copy-start | bytes 1105924
  0.6 22.8 %collective-permute-start.2 = (bf16[160,1152]{1,0:T(8,128)(2,1)}, bf16[160,1152]{1,0:T(8,128)(2,1)S(1)}, u32[]{:S(2)}, u32[]{:S(2)}) collective-permute-start(bf16[160,1152]{1,0:T(8,128)(2,1)} %param.6), channel_id=1, source_target_pairs={{2,1},{3,0},{6,5},{7,4},{10,9},{11,8},{14,13},{15,12},{18,17},{19,... | collective-permute-start | bytes 1105928 | tf_op jit(solution)/shard_map/ppermute | solution.py:44
  2.1 21.6 %collective-permute-start.1 = (bf16[160,1152]{1,0:T(8,128)(2,1)}, bf16[160,1152]{1,0:T(8,128)(2,1)S(1)}, u32[]{:S(2)}, u32[]{:S(2)}) collective-permute-start(bf16[160,1152]{1,0:T(8,128)(2,1)} %param.6), channel_id=1, source_target_pairs={{2,0},{3,1},{6,4},{7,5},{10,8},{11,9},{14,12},{15,13},{18,16},{19,... | collective-permute-start | bytes 1105928 | tf_op jit(solution)/shard_map/ppermute | solution.py:44
  3.4 20.4 %collective-permute-start = (bf16[160,1152]{1,0:T(8,128)(2,1)}, bf16[160,1152]{1,0:T(8,128)(2,1)S(1)}, u32[]{:S(2)}, u32[]{:S(2)}) collective-permute-start(bf16[160,1152]{1,0:T(8,128)(2,1)} %param.6), channel_id=1, source_target_pairs={{0,1},{1,0},{4,5},{5,4},{8,9},{9,8},{12,13},{13,12},{16,17},{17,16... | collective-permute-start | bytes 1105928 | tf_op jit(solution)/shard_map/ppermute | solution.py:44
  8.3 13.7 %collective-permute-start.7 = (bf16[160,1152]{1,0:T(8,128)(2,1)}, bf16[160,1152]{1,0:T(8,128)(2,1)S(1)}, u32[]{:S(2)}, u32[]{:S(2)}) collective-permute-start(bf16[160,1152]{1,0:T(8,128)(2,1)} %param.5), channel_id=1, source_target_pairs={{2,4},{3,5},{6,8},{7,9},{10,12},{11,13},{14,16},{15,17},{18,20},{1... | collective-permute-start | bytes 1105928 | tf_op jit(solution)/shard_map/ppermute | solution.py:44
  9.6 20.6 %collective-permute-start.5 = (bf16[160,1152]{1,0:T(8,128)(2,1)}, bf16[160,1152]{1,0:T(8,128)(2,1)S(1)}, u32[]{:S(2)}, u32[]{:S(2)}) collective-permute-start(bf16[160,1152]{1,0:T(8,128)(2,1)} %param.5), channel_id=1, source_target_pairs={{0,4},{1,5},{4,8},{5,9},{8,12},{9,13},{12,16},{13,17},{16,20},{17,... | collective-permute-start | bytes 1105928 | tf_op jit(solution)/shard_map/ppermute | solution.py:44
  22.0 8.5 %collective-permute-start.3 = (bf16[160,1152]{1,0:T(8,128)(2,1)S(1)}, bf16[160,1152]{1,0:T(8,128)(2,1)S(1)}, u32[]{:S(2)}, u32[]{:S(2)}) collective-permute-start(bf16[160,1152]{1,0:T(8,128)(2,1)S(1)} %copy-done.1), channel_id=1, source_target_pairs={{2,0},{3,1},{6,4},{7,5},{10,8},{11,9},{14,12},{15,13},{18,16},{19,... | collective-permute-start | bytes 1105928 | tf_op jit(solution)/shard_map/ppermute | solution.py:44
  25.7 20.8 %collective-permute-start.8 = (bf16[160,1152]{1,0:T(8,128)(2,1)S(1)}, bf16[160,1152]{1,0:T(8,128)(2,1)S(1)}, u32[]{:S(2)}, u32[]{:S(2)}) collective-permute-start(bf16[160,1152]{1,0:T(8,128)(2,1)S(1)} %convolution_convert_fusion.1), channel_id=1, source_target_pairs={{0,30},{1,31},{4,2},{5,3},{8,6},{9,7},{12,10},{13,11},{16,14},{17,... | collective-permute-start | bytes 1105928 | tf_op jit(solution)/shard_map/ppermute | solution.py:44
  32.5 11.1 %collective-permute-start.11 = (bf16[160,1152]{1,0:T(8,128)(2,1)S(1)}, bf16[160,1152]{1,0:T(8,128)(2,1)S(1)}, u32[]{:S(2)}, u32[]{:S(2)}) collective-permute-start(bf16[160,1152]{1,0:T(8,128)(2,1)S(1)} %slice.41), channel_id=1, source_target_pairs={{0,1},{1,0},{4,5},{5,4},{8,9},{9,8},{12,13},{13,12},{16,17},{17,16... | collective-permute-start | bytes 1105928 | tf_op jit(solution)/shard_map/ppermute | solution.py:44
  36.7 8.2 %collective-permute-start.10 = (bf16[160,1152]{1,0:T(8,128)(2,1)S(1)}, bf16[160,1152]{1,0:T(8,128)(2,1)S(1)}, u32[]{:S(2)}, u32[]{:S(2)}) collective-permute-start(bf16[160,1152]{1,0:T(8,128)(2,1)S(1)} %get-tuple-element.3), channel_id=1, source_target_pairs={{0,3},{1,2},{4,7},{5,6},{8,11},{9,10},{12,15},{13,14},{16,19},{17,... | collective-permute-start | bytes 1105928 | tf_op jit(solution)/shard_map/ppermute | solution.py:44
  38.0 6.9 %copy-start = (bf16[160,1152]{1,0:T(8,128)(2,1)S(1)}, bf16[160,1152]{1,0:T(8,128)(2,1)}, u32[]{:S(2)}) copy-start(bf16[160,1152]{1,0:T(8,128)(2,1)} %param.6) | copy-start | bytes 1105924
  38.0 6.9 %collective-permute-start.9 = (bf16[160,1152]{1,0:T(8,128)(2,1)S(1)}, bf16[160,1152]{1,0:T(8,128)(2,1)S(1)}, u32[]{:S(2)}, u32[]{:S(2)}) collective-permute-start(bf16[160,1152]{1,0:T(8,128)(2,1)S(1)} %get-tuple-element.2), channel_id=1, source_target_pairs={{0,2},{1,3},{4,6},{5,7},{8,10},{9,11},{12,14},{13,15},{16,18},{17,... | collective-permute-start | bytes 1105928 | tf_op jit(solution)/shard_map/ppermute | solution.py:44
  39.9 9.4 %collective-permute-start.6 = (bf16[160,1152]{1,0:T(8,128)(2,1)S(1)}, bf16[160,1152]{1,0:T(8,128)(2,1)S(1)}, u32[]{:S(2)}, u32[]{:S(2)}) collective-permute-start(bf16[160,1152]{1,0:T(8,128)(2,1)S(1)} %convolution_convert_fusion.2), channel_id=1, source_target_pairs={{0,28},{1,29},{4,0},{5,1},{8,4},{9,5},{12,8},{13,9},{16,12},{17,13... | collective-permute-start | bytes 1105928 | tf_op jit(solution)/shard_map/ppermute | solution.py:44
  43.6 5.7 %collective-permute-start.4 = (bf16[160,1152]{1,0:T(8,128)(2,1)S(1)}, bf16[160,1152]{1,0:T(8,128)(2,1)S(1)}, u32[]{:S(2)}, u32[]{:S(2)}) collective-permute-start(bf16[160,1152]{1,0:T(8,128)(2,1)S(1)} %convolution_convert_fusion.3), channel_id=1, source_target_pairs={{0,2},{1,3},{4,6},{5,7},{8,10},{9,11},{12,14},{13,15},{16,18},{17,... | collective-permute-start | bytes 1105928 | tf_op jit(solution)/shard_map/ppermute | solution.py:44

commit v3 on v1

v3 whole, which is shorter than its diff:
```python
import functools

import jax
import jax.numpy as jnp
from jax import lax
from jax.experimental import pallas as pl
from jax.experimental.pallas import tpu as pltpu
from jax.sharding import PartitionSpec as P

HALF = jnp.bfloat16
FULL = jnp.float32
VMEM_LIMIT = 40 * 1024 * 1024


def half_rows(raw_ref):
    values = raw_ref[...].astype(FULL)
    inverse = lax.rsqrt(jnp.sum(values * values, axis=1, keepdims=True) + 1e-06)
    return (values * inverse).astype(HALF)


def logits_of(images, texts, params):
    dots = lax.dot_general(images, texts, (((1,), (1,)), ((), ())), preferred_element_type=FULL)
    return params[0:1, 0:1] * dots + params[1:2, 0:1]


def weigh(images, texts, params):
    return (params[0:1, 0:1] * jax.nn.sigmoid(logits_of(images, texts, params))).astype(HALF)


def weigh_own(images, texts, params, targets, node):
    rows = texts.shape[0]
    logits = logits_of(images, texts, params)
    columns = lax.broadcasted_iota(jnp.int32, logits.shape, 1) + node * rows
    paired = targets == columns
    scale = params[0:1, 0:1]
    return (
        jnp.where(paired, -scale, scale) * jax.nn.sigmoid(jnp.where(paired, -logits, logits))
    ).astype(HALF)


def mix(weights, vectors):
    return jnp.dot(weights, vectors, preferred_element_type=FULL)


def mix_back(weights, vectors):
    return lax.dot_general(weights, vectors, (((0,), (0,)), ((), ())), preferred_element_type=FULL)


def roles():
    return lax.rem(lax.axis_index("blk"), 2) == 0, lax.axis_index("node")


def early_kernel(
    scale, bias, image, text, mate_image, mate_text, targets,
    params, image_h, text_h, mate_image_h, mate_text_h, image_dir, text_dir,
):
    first, node = roles()
    row = lax.broadcasted_iota(jnp.int32, params.shape, 0)
    params[...] = jnp.where(row == 0, scale[0], bias[0])
    image_h[...] = half_rows(image)
    text_h[...] = half_rows(text)
    mate_image_h[...] = half_rows(mate_image)
    mate_text_h[...] = half_rows(mate_text)
    own = weigh_own(image_h[...], text_h[...], params, targets[...], node)
    image_dir[...] = mix(own, text_h[...])
    text_dir[...] = mix_back(own, image_h[...])

    @pl.when(first)
    def _():
        cross = weigh(image_h[...], mate_text_h[...], params)
        image_dir[...] += mix(cross, mate_text_h[...])

    @pl.when(jnp.logical_not(first))
    def _():
        cross = weigh(mate_image_h[...], text_h[...], params)
        text_dir[...] += mix_back(cross, mate_image_h[...])


def first_kernel(
    far, params, targets, image_h, text_h, mate_image_h, visit_a, visit_b, *refs
):
    far_a, far_b = refs[:far], refs[far : 2 * far]
    visit_h, far_h, weights, back = refs[2 * far :]
    first, node = roles()
    nodes = far + 1

    @pl.when(first)
    def _():
        visit_h[...] = half_rows(visit_a)
        own = weigh(visit_h[...], text_h[...], params)
        weights[1, 0] = own
        total = mix(own, text_h[...])
        for k in range(far):
            far_h[k] = half_rows(far_a[k])
            outer = weigh(visit_h[...], far_h[k], params)
            weights[1, k + 1] = outer
            total += mix(outer, far_h[k])
        back[0] = total.astype(HALF)

    @pl.when(jnp.logical_not(first))
    def _():
        visit_h[...] = half_rows(visit_b)
        for k in range(far):
            far_h[k] = half_rows(far_b[k])
            one = weigh_own(
                image_h[...], far_h[k], params, targets[...], lax.rem(node + k + 1, nodes)
            )
            two = weigh(visit_h[...], far_h[k], params)
            three = weigh(mate_image_h[...], far_h[k], params)
            weights[0, k + 1] = one
            weights[1, k + 1] = two
            total = mix_back(one, image_h[...])
            total += mix_back(two, visit_h[...])
            total += mix_back(three, mate_image_h[...])
            back[k] = total.astype(HALF)


def second_kernel(
    far, params, targets, image_h, text_h, mate_text_h, visit_h, far_h, weights, relay_visit, *refs
):
    relay_far = refs[:far]
    third_h, more, back = refs[far:]
    first, node = roles()
    nodes = far + 1

    @pl.when(first)
    def _():
        third_h[...] = half_rows(relay_visit)
        more[2, 0] = weigh(third_h[...], text_h[...], params)
        for k in range(far):
            one = weigh_own(
                image_h[...], far_h[k], params, targets[...], lax.rem(node + k + 1, nodes)
            )
            three = weigh(third_h[...], far_h[k], params)
            more[0, k + 1] = one
            total = mix_back(one, image_h[...])
            total += mix_back(weights[1, k + 1], visit_h[...])
            total += mix_back(three, third_h[...])
            back[k] = total.astype(HALF)

    @pl.when(jnp.logical_not(first))
    def _():
        own = weigh(visit_h[...], text_h[...], params)
        more[1, 0] = own
        total = mix(own, text_h[...])
        total += mix(weigh(visit_h[...], mate_text_h[...], params), mate_text_h[...])
        for k in range(far):
            total += mix(weights[1, k + 1], far_h[k])
            beyond = half_rows(relay_far[k])
            total += mix(weigh(visit_h[...], beyond, params), beyond)
        back[0] = total.astype(HALF)


def third_kernel(
    far, params, image_h, visit_h, third_h, far_h, weights, more, image_part, text_part, *refs
):
    mate_far = refs[:far]
    image_dir, text_dir = refs[far:]
    first, _ = roles()

    @pl.when(first)
    def _():
        total = text_part[...] + mix_back(weights[1, 0], visit_h[...])
        text_dir[...] = total + mix_back(more[2, 0], third_h[...])
        total = image_part[...]
        for k in range(far):
            total += mix(more[0, k + 1], far_h[k])
            beyond = half_rows(mate_far[k])
            total += mix(weigh(image_h[...], beyond, params), beyond)
        image_dir[...] = total

    @pl.when(jnp.logical_not(first))
    def _():
        text_dir[...] = text_part[...] + mix_back(more[1, 0], visit_h[...])
        total = image_part[...]
        for k in range(far):
            total += mix(weights[0, k + 1], far_h[k])
        image_dir[...] = total


def last_kernel(far, image, text, image_dir, text_dir, *refs):
    one, two = refs[:far], refs[far : 2 * far]
    image_grads, text_grads = refs[2 * far :]
    first, _ = roles()

    def summed(parts):
        total = parts[0][...].astype(FULL)
        for part in parts[1:]:
            total += part[...].astype(FULL)
        return total

    def tangent(raw, gradient):
        values = raw[...].astype(FULL)
        inverse = lax.rsqrt(jnp.sum(values * values, axis=1, keepdims=True) + 1e-06)
        unit = values * inverse
        return (gradient - unit * jnp.sum(unit * gradient, axis=1, keepdims=True)) * inverse

    @pl.when(first)
    def _():
        image_grads[...] = tangent(image, image_dir[...] + one[0][...].astype(FULL))
        text_grads[...] = tangent(text, text_dir[...] + summed(two))

    @pl.when(jnp.logical_not(first))
    def _():
        image_grads[...] = tangent(image, image_dir[...] + two[0][...].astype(FULL))
        text_grads[...] = tangent(text, text_dir[...] + summed(one))


def call(kernel, name, operands, shapes, smem=0, flops=0, result_in_vmem=True):
    place = pltpu.VMEM if result_in_vmem else (lambda s, d: jax.ShapeDtypeStruct(s, d))
    operands = list(operands)
    size = sum(x.size * x.dtype.itemsize for x in operands)
    return pl.pallas_call(
        kernel,
        name=name,
        out_shape=[place(s, d) for s, d in shapes],
        in_specs=[pl.BlockSpec(memory_space=pltpu.SMEM)] * smem
        + [pl.BlockSpec(memory_space=pltpu.VMEM)] * (len(operands) - smem),
        out_specs=[pl.BlockSpec(memory_space=pltpu.VMEM)] * len(shapes),
        compiler_params=pltpu.CompilerParams(vmem_limit_bytes=VMEM_LIMIT),
        cost_estimate=pl.CostEstimate(flops=flops, bytes_accessed=size, transcendentals=0),
    )(*operands)


def local(image_embeds, text_embeds, pair_text, similarity_scale, logit_bias):
    rows, width = image_embeds.shape
    cycle_count = lax.axis_size("blk")
    node_count = lax.axis_size("node")
    far = node_count - 1
    cycle_index = lax.axis_index("blk")
    node_index = lax.axis_index("node")

    def send(block, even, odd):
        route = []
        for g in range(cycle_count):
            ahead, across = odd if g % 2 else even
            for n in range(node_count):
                to = (g + ahead) % cycle_count * node_count + (n + across) % node_count
                route.append((g * node_count + n, to))
        return lax.ppermute(block, ("blk", "node"), route)

    stay = (0, 0)

    def swap(block):
        return send(block, (1, 0), (-1, 0))

    mate_text = swap(text_embeds)
    mate_image = swap(image_embeds)
    visit_b = send(image_embeds, stay, (2, 0))
    far_a = [send(text_embeds, (0, -k), stay) for k in range(1, node_count)]
    visit_a = send(image_embeds, (2, 0), stay)
    far_b = [send(text_embeds, stay, (0, -k)) for k in range(1, node_count)]

    start = (cycle_index * node_count + node_index) * rows
    targets = lax.dynamic_slice_in_dim(pair_text, start, rows, 0)
    targets = (targets - cycle_index * node_count * rows)[:, None]

    block_h = ((rows, width), HALF)
    block_f = ((rows, width), FULL)
    params, image_h, text_h, mate_image_h, mate_text_h, image_part, text_part = call(
        early_kernel,
        "early",
        [similarity_scale, logit_bias, image_embeds, text_embeds, mate_image, mate_text, targets],
        [((8, 128), FULL), block_h, block_h, block_h, block_h, block_f, block_f],
        smem=2,
    )
    relay_visit = swap(visit_b)
    relay_far = [swap(block) for block in far_a]
    tiles = ((3, node_count, rows, rows), HALF)
    returns = ((far, rows, width), HALF)
    visit_h, far_h, weights, back = call(
        functools.partial(first_kernel, far),
        "first",
        [params, targets, image_h, text_h, mate_image_h, visit_a, visit_b, *far_a, *far_b],
        [block_h, ((far, rows, width), HALF), tiles, returns],
    )
    one = [send(back[0], (-2, 0), (0, 1))] + [
        send(back[k], stay, (0, k + 1)) for k in range(1, far)
    ]
    mate_far = [swap(block) for block in far_b]
    third_h, more, back = call(
        functools.partial(second_kernel, far),
        "second",
        [params, targets, image_h, text_h, mate_text_h, visit_h, far_h, weights, relay_visit]
        + relay_far,
        [block_h, tiles, returns],
    )
    two = [send(back[0], (0, 1), (-2, 0))] + [
        send(back[k], (0, k + 1), stay) for k in range(1, far)
    ]
    image_dir, text_dir = call(
        functools.partial(third_kernel, far),
        "third",
        [params, image_h, visit_h, third_h, far_h, weights, more, image_part, text_part]
        + mate_far,
        [block_f, block_f],
    )
    return tuple(
        call(
            functools.partial(last_kernel, far),
            "last",
            [image_embeds, text_embeds, image_dir, text_dir, *one, *two],
            [block_f, block_f],
            result_in_vmem=False,
        )
    )


def solution(mesh):
    return jax.shard_map(
        local,
        mesh=mesh,
        in_specs=(P(("blk", "node"), None), P(("blk", "node"), None), P(), P(), P()),
        out_specs=(P(("blk", "node"), None), P(("blk", "node"), None)),
        check_vma=False,
    )
```

time: 38.1 us -> 37.3 us (0.979)
  starting transfers between devices: 7.95 us -> 19.2 us
  waiting for transfers between devices: 16.1 us -> 6.19 us
  Pallas kernels: 0 us -> 6.58 us
  other arithmetic: 6.79 us -> 0.77 us
  matrix products: 4.13 us -> 0 us
  local copies, waits for them, and re-layouts: 0.83 us -> 2.09 us
    ppermute x6 -> x11, starting transfers between devices: 7.95 us -> 19.2 us  [send(): return lax.ppermute(block, ('blk', 'node'), route)]
    ppermute x6 -> x11, waiting for transfers between devices: 16.1 us -> 6.19 us  [send(): return lax.ppermute(block, ('blk', 'node'), route)]
    pallas_call x0 -> x5, Pallas kernels: none -> 6.58 us  [call(): pl.pallas_call(kernel, name=name, out_shape=[place(s, d) for s, d in shap...]
    dot_general x9 -> x0, matrix products: 4.13 us -> none  [the longest x3 1.46 us: local(): lax.dot_general(image_halves[t], text_all, (((1,), (1,)), ((), ())), pref...]
    reduce_sum x6 -> x0, other arithmetic: 3.11 us -> none  [the longest x5 2.85 us: unit_rows(): inverse = lax.rsqrt(jnp.sum(values * values, axis=1, keepdims=True) + 1e-06)]
    mul x2 -> x0, other arithmetic: 2.31 us -> none  [tangent_part(): (gradient - unit_rows_f * jnp.sum(unit_rows_f * gradient, axis=1, keepdim...]
    unnamed x4 -> x8, local copies, waits for them, and re-layouts: 0.01 us -> 1.98 us
    convert_element_type x2 -> x0, other arithmetic: 1.25 us -> none  [the longest x1 1.12 us: local(): text_unit.astype(jnp.bfloat16)]
  transfers between devices with their start and end apart: 6 -> 11, of which waited for: 6 -> 3; matrix products, arithmetic and copies ran while one was open for 18% -> 2% of each run, Pallas kernels for 0% -> 13%
where the time goes in v3:
time: 37.3 us; the launch traced here: 36.9 us
  starting transfers between devices  19.2 us (51%)
  Pallas kernels  6.58 us (18%)
  waiting for transfers between devices  6.19 us (17%)
  local copies, waits for them, and re-layouts  2.09 us (6%)
  between operations  2.04 us (5%)
  other arithmetic  0.77 us (2%)
    ppermute x11, starting transfers between devices, send(): return lax.ppermute(block, ('blk', 'node'), route)  19.2 us
    pallas_call x5, Pallas kernels, call(): pl.pallas_call(kernel, name=name, out_shape=[place(s, d) for s, d in shap...  6.58 us
    ppermute x11, waiting for transfers between devices, send(): return lax.ppermute(block, ('blk', 'node'), route)  6.19 us
    unnamed x8, local copies, waits for them, and re-layouts  1.98 us
    sub x1, other arithmetic, local(): targets = (targets - cycle_index * node_count * rows)[:, None]  0.77 us
  transfers between devices with their start and end apart: 11, of which 3 were waited for; matrix products, arithmetic and copies ran while one was open for 2% of the time, Pallas kernels for 13%

profile of v3, /device:TPU:0, one launch (start us, length us, event | category | flops | bytes accessed | tf_op | source)
XLA Modules:
  0.0 36.9 jit_solution(16210862783854039020)
XLA Ops:
  0.6 0.5 %collective-permute-start = (bf16[160,1152]{1,0:T(8,128)(2,1)}, bf16[160,1152]{1,0:T(8,128)(2,1)S(1)}, u32[]{:S(2)}, u32[]{:S(2)}) collective-permute-start(bf16[160,1152]{1,0:T(8,128)(2,1)} %image.3), channel_id=1, source_target_pairs={{0,2},{1,3},{2,0},{3,1},{4,6},{5,7},{6,4},{7,5},{8,10},{9,11},{10,... | collective-permute-start | bytes 1105928 | tf_op jit(solution)/shard_map/ppermute | solution.py:240
  1.1 1.6 %collective-permute-start.3 = (bf16[160,1152]{1,0:T(8,128)(2,1)}, bf16[160,1152]{1,0:T(8,128)(2,1)S(1)}, u32[]{:S(2)}, u32[]{:S(2)}) collective-permute-start(bf16[160,1152]{1,0:T(8,128)(2,1)} %image.3), channel_id=1, source_target_pairs={{0,0},{1,1},{2,6},{3,7},{4,4},{5,5},{6,10},{7,11},{8,8},{9,9},{10,... | collective-permute-start | bytes 1105928 | tf_op jit(solution)/shard_map/ppermute | solution.py:240
  2.8 4.4 %collective-permute-start.4 = (bf16[160,1152]{1,0:T(8,128)(2,1)}, bf16[160,1152]{1,0:T(8,128)(2,1)S(1)}, u32[]{:S(2)}, u32[]{:S(2)}) collective-permute-start(bf16[160,1152]{1,0:T(8,128)(2,1)} %text.3), channel_id=1, source_target_pairs={{0,1},{1,0},{2,2},{3,3},{4,5},{5,4},{6,6},{7,7},{8,9},{9,8},{10,10... | collective-permute-start | bytes 1105928 | tf_op jit(solution)/shard_map/ppermute | solution.py:240
  7.2 0.2 collective-permute-start.1
  7.4 1.6 %collective-permute-start.5 = (bf16[160,1152]{1,0:T(8,128)(2,1)}, bf16[160,1152]{1,0:T(8,128)(2,1)S(1)}, u32[]{:S(2)}, u32[]{:S(2)}) collective-permute-start(bf16[160,1152]{1,0:T(8,128)(2,1)} %text.3), channel_id=1, source_target_pairs={{0,0},{1,1},{2,3},{3,2},{4,4},{5,5},{6,7},{7,6},{8,8},{9,9},{10,11... | collective-permute-start | bytes 1105928 | tf_op jit(solution)/shard_map/ppermute | solution.py:240
  9.1 0.0 collective-permute-done.mate_image
  9.1 3.4 %collective-permute-start.2 = (bf16[160,1152]{1,0:T(8,128)(2,1)}, bf16[160,1152]{1,0:T(8,128)(2,1)S(1)}, u32[]{:S(2)}, u32[]{:S(2)}) collective-permute-start(bf16[160,1152]{1,0:T(8,128)(2,1)} %image.3), channel_id=1, source_target_pairs={{0,4},{1,5},{2,2},{3,3},{4,8},{5,9},{6,6},{7,7},{8,12},{9,13},{10,... | collective-permute-start | bytes 1105928 | tf_op jit(solution)/shard_map/ppermute | solution.py:240
  12.5 1.4 %collective-permute-start.6 = (bf16[160,1152]{1,0:T(8,128)(2,1)S(1)}, bf16[160,1152]{1,0:T(8,128)(2,1)S(1)}, u32[]{:S(2)}, u32[]{:S(2)}) collective-permute-start(bf16[160,1152]{1,0:T(8,128)(2,1)S(1)} %collective-permute-done.3.visit_b), channel_id=1, source_target_pairs={{0,2},{1,3},{2,0},{3,1},{4,6},{5,7},{6,4},{7,5},{8,10},{9,11},{10,... | collective-permute-start | bytes 1105928 | tf_op jit(solution)/shard_map/ppermute | solution.py:240
  13.9 0.0 collective-permute-start.7
  13.9 0.8 %dynamic-slice_subtract_fusion = s32[160]{0:T(256)S(1)} fusion(s32[5120]{0:T(1024)} %param.7, s32[]{:T(128)S(6)} %select_n.3, s32[]{:T(128)S(6)} %mul.12), kind=kLoop, calls=%fused_computation | loop fusion | flops 160 | bytes 1288 | tf_op jit(solution)/shard_map/sub | solution.py:256
  14.7 0.1 copy.7.targets
  16.1 0.0 copy-start
  16.1 1.0 %copy-done = bf16[160,1152]{1,0:T(8,128)(2,1)S(1)} copy-done((bf16[160,1152]{1,0:T(8,128)(2,1)S(1)}, bf16[160,1152]{1,0:T(8,128)(2,1)}, u32[]{:S(2)}) %copy-start) | copy-done | bytes 368664
  17.1 1.0 %copy-done.2 = bf16[160,1152]{1,0:T(8,128)(2,1)S(1)} copy-done((bf16[160,1152]{1,0:T(8,128)(2,1)S(1)}, bf16[160,1152]{1,0:T(8,128)(2,1)}, u32[]{:S(2)}) %copy-start.2) | copy-done | bytes 368664
  18.1 1.7 %early.1 = (f32[8,128]{1,0:T(8,128)S(1)}, bf16[160,1152]{1,0:T(8,128)(2,1)S(1)}, bf16[160,1152]{1,0:T(8,128)(2,1)S(1)}, bf16[160,1152]{1,0:T(8,128)(2,1)S(1)}, b...) custom-call(f32[1]{0:T(128)S(6)} %copy.10.scale, f32[1]{0:T(128)S(6)} %copy.11.bias, ...), custom_call_target="tpu_custom_call" | custom-call | bytes 1475208 | tf_op jit(solution)/shard_map/early/pallas_call | solution.py:213
  19.8 1.6 %collective-permute-done.2.visit_a = bf16[160,1152]{1,0:T(8,128)(2,1)S(1)} collective-permute-done((bf16[160,1152]{1,0:T(8,128)(2,1)}, bf16[160,1152]{1,0:T(8,128)(2,1)S(1)}, u32[]{:S(2)}, u32[]{:S(2)}) %collective-permute-start.2) | collective-permute-done | bytes 368672 | tf_op jit(solution)/shard_map/ppermute | solution.py:240
  21.4 1.0 %first.1 = (bf16[160,1152]{1,0:T(8,128)(2,1)S(1)}, bf16[1,160,1152]{2,1,0:T(8,128)(2,1)S(1)}, bf16[3,2,160,160]{3,2,1,0:T(8,128)(2,1)S(1)}, bf16[1,160,1152]{2,1,0:T(8,128)(2,1)S(1)}) custom-call(f32[8,128]{1,0:T(8,128)S(1)} %get-tuple-element.18.params, s32[160,1]{1,0:T(8,128)S(1)} %copy.7.targets, bf16[160,1152]{1,0:T(8,128)(2,1)S(1)} %get-tuple-element.19.image_h, ...), custom_call_target="tpu_custom_call" | custom-call | bytes 2585216 | tf_op jit(solution)/shard_map/first/pallas_call | solution.py:213
  22.4 3.5 %collective-permute-start.9 = (bf16[160,1152]{1,0:T(8,128)(2,1)S(1)}, bf16[160,1152]{1,0:T(8,128)(2,1)S(1)}, u32[]{:S(2)}, u32[]{:S(2)}) collective-permute-start(bf16[160,1152]{1,0:T(8,128)(2,1)S(1)} %bitcast.3), channel_id=1, source_target_pairs={{0,28},{1,29},{2,3},{3,2},{4,0},{5,1},{6,7},{7,6},{8,4},{9,5},{10,... | collective-permute-start | bytes 1105928 | tf_op jit(solution)/shard_map/ppermute | solution.py:240
  25.9 1.3 %second.1 = (bf16[160,1152]{1,0:T(8,128)(2,1)S(1)}, bf16[3,2,160,160]{3,2,1,0:T(8,128)(2,1)S(1)}, bf16[1,160,1152]{2,1,0:T(8,128)(2,1)S(1)}) custom-call(f32[8,128]{1,0:T(8,128)S(1)} %get-tuple-element.18.params, s32[160,1]{1,0:T(8,128)S(1)} %copy.7.targets, bf16[160,1152]{1,0:T(8,128)(2,1)S(1)} %get-tuple-element.19.image_h, ...), custom_call_target="tpu_custom_call" | custom-call | bytes 2892416 | tf_op jit(solution)/shard_map/second/pallas_call | solution.py:213
  27.3 2.4 %collective-permute-start.10 = (bf16[160,1152]{1,0:T(8,128)(2,1)S(1)}, bf16[160,1152]{1,0:T(8,128)(2,1)S(1)}, u32[]{:S(2)}, u32[]{:S(2)}) collective-permute-start(bf16[160,1152]{1,0:T(8,128)(2,1)S(1)} %bitcast.4), channel_id=1, source_target_pairs={{0,1},{1,0},{2,30},{3,31},{4,5},{5,4},{6,2},{7,3},{8,9},{9,8},{10,... | collective-permute-start | bytes 1105928 | tf_op jit(solution)/shard_map/ppermute | solution.py:240
  29.7 0.9 %third.1 = (f32[160,1152]{1,0:T(8,128)S(1)}, f32[160,1152]{1,0:T(8,128)S(1)}) custom-call(f32[8,128]{1,0:T(8,128)S(1)} %get-tuple-element.18.params, bf16[160,1152]{1,0:T(8,128)(2,1)S(1)} %get-tuple-element.19.image_h, bf16[160,1152]{1,0:T(8,128)(2,1)S(1)} %get-tuple-element.22.visit_h, bf16[160,1152]{1,0:T(8,128)(2,1)S(1)} %get-tuple-element.26.third_h, ...), custom_call_target="tpu_custom_call" | custom-call | bytes 3936256 | tf_op jit(solution)/shard_map/third/pallas_call | solution.py:213
  30.6 0.6 %collective-permute-done.9.refs_0_ = bf16[160,1152]{1,0:T(8,128)(2,1)S(1)} collective-permute-done((bf16[160,1152]{1,0:T(8,128)(2,1)S(1)}, bf16[160,1152]{1,0:T(8,128)(2,1)S(1)}, u32[]{:S(2)}, u32[]{:S(2)}) %collective-permute-start.9) | collective-permute-done | bytes 368672 | tf_op jit(solution)/shard_map/ppermute | solution.py:240
  31.2 4.0 %collective-permute-done.10.refs_1_ = bf16[160,1152]{1,0:T(8,128)(2,1)S(1)} collective-permute-done((bf16[160,1152]{1,0:T(8,128)(2,1)S(1)}, bf16[160,1152]{1,0:T(8,128)(2,1)S(1)}, u32[]{:S(2)}, u32[]{:S(2)}) %collective-permute-start.10) | collective-permute-done | bytes 368672 | tf_op jit(solution)/shard_map/ppermute | solution.py:240
  35.2 1.7 %last.1 = (f32[160,1152]{1,0:T(8,128)}, f32[160,1152]{1,0:T(8,128)}) custom-call(bf16[160,1152]{1,0:T(8,128)(2,1)S(1)} %copy-done.1, bf16[160,1152]{1,0:T(8,128)(2,1)S(1)} %copy-done.3, f32[160,1152]{1,0:T(8,128)S(1)} %get-tuple-element.30.image_dir, f32[160,1152]{1,0:T(8,128)S(1)} %get-tuple-element.31.text_dir, ...), custom_call_target="tpu_custom_call" | custom-call | bytes 2949120 | tf_op jit(solution)/shard_map/last/pallas_call | solution.py:213
  (13 shorter events, 0.0 us)
Async XLA Ops:
  0.6 8.4 %collective-permute-start = (bf16[160,1152]{1,0:T(8,128)(2,1)}, bf16[160,1152]{1,0:T(8,128)(2,1)S(1)}, u32[]{:S(2)}, u32[]{:S(2)}) collective-permute-start(bf16[160,1152]{1,0:T(8,128)(2,1)} %image.3), channel_id=1, source_target_pairs={{0,2},{1,3},{2,0},{3,1},{4,6},{5,7},{6,4},{7,5},{8,10},{9,11},{10,... | collective-permute-start | bytes 1105928 | tf_op jit(solution)/shard_map/ppermute | solution.py:240
  1.1 11.4 %collective-permute-start.3 = (bf16[160,1152]{1,0:T(8,128)(2,1)}, bf16[160,1152]{1,0:T(8,128)(2,1)S(1)}, u32[]{:S(2)}, u32[]{:S(2)}) collective-permute-start(bf16[160,1152]{1,0:T(8,128)(2,1)} %image.3), channel_id=1, source_target_pairs={{0,0},{1,1},{2,6},{3,7},{4,4},{5,5},{6,10},{7,11},{8,8},{9,9},{10,... | collective-permute-start | bytes 1105928 | tf_op jit(solution)/shard_map/ppermute | solution.py:240
  2.8 11.1 %collective-permute-start.4 = (bf16[160,1152]{1,0:T(8,128)(2,1)}, bf16[160,1152]{1,0:T(8,128)(2,1)S(1)}, u32[]{:S(2)}, u32[]{:S(2)}) collective-permute-start(bf16[160,1152]{1,0:T(8,128)(2,1)} %text.3), channel_id=1, source_target_pairs={{0,1},{1,0},{2,2},{3,3},{4,5},{5,4},{6,6},{7,7},{8,9},{9,8},{10,10... | collective-permute-start | bytes 1105928 | tf_op jit(solution)/shard_map/ppermute | solution.py:240
  7.2 8.9 %collective-permute-start.1 = (bf16[160,1152]{1,0:T(8,128)(2,1)}, bf16[160,1152]{1,0:T(8,128)(2,1)S(1)}, u32[]{:S(2)}, u32[]{:S(2)}) collective-permute-start(bf16[160,1152]{1,0:T(8,128)(2,1)} %text.3), channel_id=1, source_target_pairs={{0,2},{1,3},{2,0},{3,1},{4,6},{5,7},{6,4},{7,5},{8,10},{9,11},{10,... | collective-permute-start | bytes 1105928 | tf_op jit(solution)/shard_map/ppermute | solution.py:240
  7.4 12.4 %collective-permute-start.5 = (bf16[160,1152]{1,0:T(8,128)(2,1)}, bf16[160,1152]{1,0:T(8,128)(2,1)S(1)}, u32[]{:S(2)}, u32[]{:S(2)}) collective-permute-start(bf16[160,1152]{1,0:T(8,128)(2,1)} %text.3), channel_id=1, source_target_pairs={{0,0},{1,1},{2,3},{3,2},{4,4},{5,5},{6,7},{7,6},{8,8},{9,9},{10,11... | collective-permute-start | bytes 1105928 | tf_op jit(solution)/shard_map/ppermute | solution.py:240
  9.1 12.3 %collective-permute-start.2 = (bf16[160,1152]{1,0:T(8,128)(2,1)}, bf16[160,1152]{1,0:T(8,128)(2,1)S(1)}, u32[]{:S(2)}, u32[]{:S(2)}) collective-permute-start(bf16[160,1152]{1,0:T(8,128)(2,1)} %image.3), channel_id=1, source_target_pairs={{0,4},{1,5},{2,2},{3,3},{4,8},{5,9},{6,6},{7,7},{8,12},{9,13},{10,... | collective-permute-start | bytes 1105928 | tf_op jit(solution)/shard_map/ppermute | solution.py:240
  12.5 13.4 %collective-permute-start.6 = (bf16[160,1152]{1,0:T(8,128)(2,1)S(1)}, bf16[160,1152]{1,0:T(8,128)(2,1)S(1)}, u32[]{:S(2)}, u32[]{:S(2)}) collective-permute-start(bf16[160,1152]{1,0:T(8,128)(2,1)S(1)} %collective-permute-done.3.visit_b), channel_id=1, source_target_pairs={{0,2},{1,3},{2,0},{3,1},{4,6},{5,7},{6,4},{7,5},{8,10},{9,11},{10,... | collective-permute-start | bytes 1105928 | tf_op jit(solution)/shard_map/ppermute | solution.py:240
  13.9 12.0 %collective-permute-start.7 = (bf16[160,1152]{1,0:T(8,128)(2,1)S(1)}, bf16[160,1152]{1,0:T(8,128)(2,1)S(1)}, u32[]{:S(2)}, u32[]{:S(2)}) collective-permute-start(bf16[160,1152]{1,0:T(8,128)(2,1)S(1)} %collective-permute-done.4.refs_0_), channel_id=1, source_target_pairs={{0,2},{1,3},{2,0},{3,1},{4,6},{5,7},{6,4},{7,5},{8,10},{9,11},{10,... | collective-permute-start | bytes 1105928 | tf_op jit(solution)/shard_map/ppermute | solution.py:240
  16.1 1.0 %copy-start = (bf16[160,1152]{1,0:T(8,128)(2,1)S(1)}, bf16[160,1152]{1,0:T(8,128)(2,1)}, u32[]{:S(2)}) copy-start(bf16[160,1152]{1,0:T(8,128)(2,1)} %image.3) | copy-start | bytes 1105924
  17.1 1.0 %copy-start.2 = (bf16[160,1152]{1,0:T(8,128)(2,1)S(1)}, bf16[160,1152]{1,0:T(8,128)(2,1)}, u32[]{:S(2)}) copy-start(bf16[160,1152]{1,0:T(8,128)(2,1)} %text.3) | copy-start | bytes 1105924
  22.4 8.8 %collective-permute-start.9 = (bf16[160,1152]{1,0:T(8,128)(2,1)S(1)}, bf16[160,1152]{1,0:T(8,128)(2,1)S(1)}, u32[]{:S(2)}, u32[]{:S(2)}) collective-permute-start(bf16[160,1152]{1,0:T(8,128)(2,1)S(1)} %bitcast.3), channel_id=1, source_target_pairs={{0,28},{1,29},{2,3},{3,2},{4,0},{5,1},{6,7},{7,6},{8,4},{9,5},{10,... | collective-permute-start | bytes 1105928 | tf_op jit(solution)/shard_map/ppermute | solution.py:240
  25.9 3.8 %collective-permute-start.8 = (bf16[160,1152]{1,0:T(8,128)(2,1)S(1)}, bf16[160,1152]{1,0:T(8,128)(2,1)S(1)}, u32[]{:S(2)}, u32[]{:S(2)}) collective-permute-start(bf16[160,1152]{1,0:T(8,128)(2,1)S(1)} %collective-permute-done.5.refs_1_), channel_id=1, source_target_pairs={{0,2},{1,3},{2,0},{3,1},{4,6},{5,7},{6,4},{7,5},{8,10},{9,11},{10,... | collective-permute-start | bytes 1105928 | tf_op jit(solution)/shard_map/ppermute | solution.py:240
  27.3 7.9 %collective-permute-start.10 = (bf16[160,1152]{1,0:T(8,128)(2,1)S(1)}, bf16[160,1152]{1,0:T(8,128)(2,1)S(1)}, u32[]{:S(2)}, u32[]{:S(2)}) collective-permute-start(bf16[160,1152]{1,0:T(8,128)(2,1)S(1)} %bitcast.4), channel_id=1, source_target_pairs={{0,1},{1,0},{2,30},{3,31},{4,5},{5,4},{6,2},{7,3},{8,9},{9,8},{10,... | collective-permute-start | bytes 1105928 | tf_op jit(solution)/shard_map/ppermute | solution.py:240
  29.7 5.5 %copy-start.1 = (bf16[160,1152]{1,0:T(8,128)(2,1)S(1)}, bf16[160,1152]{1,0:T(8,128)(2,1)}, u32[]{:S(2)}) copy-start(bf16[160,1152]{1,0:T(8,128)(2,1)} %image.3) | copy-start | bytes 1105924
  29.7 5.5 %copy-start.3 = (bf16[160,1152]{1,0:T(8,128)(2,1)S(1)}, bf16[160,1152]{1,0:T(8,128)(2,1)}, u32[]{:S(2)}) copy-start(bf16[160,1152]{1,0:T(8,128)(2,1)} %text.3) | copy-start | bytes 1105924

commit v4 on v1

v4 whole, which is shorter than its diff:
```python
import functools

import jax
import jax.numpy as jnp
from jax import lax
from jax.experimental import pallas as pl
from jax.experimental.pallas import tpu as pltpu
from jax.sharding import PartitionSpec as P

HALF = jnp.bfloat16
FULL = jnp.float32
VMEM_LIMIT = 40 * 1024 * 1024


def roles():
    return lax.rem(lax.axis_index("blk"), 2) == 0, lax.axis_index("node")


def by_role(on_first, on_second):
    first, node = roles()
    pl.when(first)(functools.partial(on_first, node))
    pl.when(jnp.logical_not(first))(functools.partial(on_second, node))


def logits_of(images, texts, params):
    dots = lax.dot_general(images, texts, (((1,), (1,)), ((), ())), preferred_element_type=FULL)
    return params[0:1, 0:1] * dots + params[1:2, 0:1]


def weigh(images, texts, params):
    return (params[0:1, 0:1] * jax.nn.sigmoid(logits_of(images, texts, params))).astype(HALF)


def weigh_own(images, texts, params, targets, node):
    rows = texts.shape[0]
    logits = logits_of(images, texts, params)
    columns = lax.broadcasted_iota(jnp.int32, logits.shape, 1) + node * rows
    paired = targets == columns
    scale = params[0:1, 0:1]
    return (
        jnp.where(paired, -scale, scale) * jax.nn.sigmoid(jnp.where(paired, -logits, logits))
    ).astype(HALF)


def mix(weights, vectors):
    return jnp.dot(weights, vectors, preferred_element_type=FULL)


def mix_back(weights, vectors):
    return lax.dot_general(weights, vectors, (((0,), (0,)), ((), ())), preferred_element_type=FULL)


def unit_kernel(image, text, lead_raw, rest_raw, lead, rest, lead_inv, rest_inv, sems):
    rows = lead.shape[0]
    part = rows // 2 if rows % 32 == 0 else rows
    pieces = [pl.ds(at, part) for at in range(0, rows, part)]

    def copies(source, target, base):
        return [
            pltpu.make_async_copy(source.at[piece], target.at[piece], sems.at[base + i])
            for i, piece in enumerate(pieces)
        ]

    def fetch(lead_source, rest_source, node):
        for copy in copies(lead_source, lead_raw, 0) + copies(rest_source, rest_raw, 2):
            copy.start()

    by_role(functools.partial(fetch, text, image), functools.partial(fetch, image, text))
    for base, raw, half, inv in ((0, lead_raw, lead, lead_inv), (2, rest_raw, rest, rest_inv)):
        for piece, copy in zip(pieces, copies(image, raw, base)):
            copy.wait()
            values = raw[piece, :].astype(FULL)
            inverse = lax.rsqrt(jnp.sum(values * values, axis=1, keepdims=True) + 1e-06)
            half[piece, :] = (values * inverse).astype(HALF)
            inv[piece, :] = inverse


def half_rows(raw):
    values = raw[...].astype(FULL)
    inverse = lax.rsqrt(jnp.sum(values * values, axis=1, keepdims=True) + 1e-06)
    return (values * inverse).astype(HALF)


def early_kernel(
    scale, bias, targets, lead, rest, mate_image, mate_text,
    params, mate_lead, mate_rest, lead_part, rest_part,
):
    row = lax.broadcasted_iota(jnp.int32, params.shape, 0)
    params[...] = jnp.where(row == 0, scale[0], bias[0])

    def on_first(node):
        mate_rest[...] = half_rows(mate_text)
        own = weigh_own(rest[...], lead[...], params, targets[...], node)
        cross = weigh(rest[...], mate_rest[...], params)
        rest_part[...] = mix(own, lead[...]) + mix(cross, mate_rest[...])
        lead_part[...] = mix_back(own, rest[...])

    def on_second(node):
        mate_rest[...] = half_rows(mate_image)
        mate_lead[...] = half_rows(mate_text)
        own = weigh_own(lead[...], rest[...], params, targets[...], node)
        cross = weigh(mate_rest[...], rest[...], params)
        lead_part[...] = mix(own, rest[...])
        rest_part[...] = mix_back(own, lead[...]) + mix_back(cross, mate_rest[...])

    by_role(on_first, on_second)


def first_kernel(far, params, targets, lead, rest, mate_rest, *refs):
    got1, got2 = refs[:far], refs[far : 2 * far]
    weights, back = refs[2 * far :]

    def on_first(node):
        visit = got2[0][...]
        own = weigh(visit, lead[...], params)
        weights[1, 0] = own
        total = mix(own, lead[...])
        for k in range(far):
            outer = weigh(visit, got1[k][...], params)
            weights[1, k + 1] = outer
            total += mix(outer, got1[k][...])
        back[0] = total.astype(HALF)

    def on_second(node):
        visit = got1[0][...]
        for k in range(far):
            texts = got2[k][...]
            one = weigh_own(
                lead[...], texts, params, targets[...], lax.rem(node + k + 1, far + 1)
            )
            two = weigh(visit, texts, params)
            three = weigh(mate_rest[...], texts, params)
            weights[0, k + 1] = one
            weights[1, k + 1] = two
            total = mix_back(one, lead[...]) + mix_back(two, visit)
            back[k] = (total + mix_back(three, mate_rest[...])).astype(HALF)

    by_role(on_first, on_second)


def second_kernel(far, params, targets, lead, rest, mate_lead, weights, *refs):
    got1, got2, relay1 = refs[:far], refs[far : 2 * far], refs[2 * far : 3 * far]
    more, back = refs[3 * far :]

    def on_first(node):
        third = relay1[0][...]
        for k in range(far):
            texts = got1[k][...]
            one = weigh_own(
                rest[...], texts, params, targets[...], lax.rem(node + k + 1, far + 1)
            )
            three = weigh(third, texts, params)
            more[0, k + 1] = one
            total = mix_back(one, rest[...]) + mix_back(weights[1, k + 1], got2[0][...])
            back[k] = (total + mix_back(three, third)).astype(HALF)

    def on_second(node):
        visit = got1[0][...]
        own = weigh(visit, rest[...], params)
        more[1, 0] = own
        total = mix(own, rest[...]) + mix(weigh(visit, mate_lead[...], params), mate_lead[...])
        for k in range(far):
            total += mix(weights[1, k + 1], got2[k][...])
            beyond = relay1[k][...]
            total += mix(weigh(visit, beyond, params), beyond)
        back[0] = total.astype(HALF)

    by_role(on_first, on_second)


def third_kernel(far, params, lead, rest, weights, more, lead_part, rest_part, *refs):
    got1, got2 = refs[:far], refs[far : 2 * far]
    relay1, relay2 = refs[2 * far : 3 * far], refs[3 * far : 4 * far]
    lead_dir, rest_dir = refs[4 * far :]

    def on_first(node):
        total = rest_part[...]
        for k in range(far):
            total += mix(more[0, k + 1], got1[k][...])
            beyond = relay2[k][...]
            total += mix(weigh(rest[...], beyond, params), beyond)
        rest_dir[...] = total
        third = relay1[0][...]
        total = lead_part[...] + mix_back(weights[1, 0], got2[0][...])
        lead_dir[...] = total + mix_back(weigh(third, lead[...], params), third)

    def on_second(node):
        rest_dir[...] = rest_part[...] + mix_back(more[1, 0], got1[0][...])
        total = lead_part[...]
        for k in range(far):
            total += mix(weights[0, k + 1], got2[k][...])
        lead_dir[...] = total

    by_role(on_first, on_second)


def tangent_kernel(far, sums_on_first, raw, inverse, direction, *refs):
    parts = refs[:far]
    image_grads, text_grads, held, sems = refs[-4:]
    rows = raw.shape[0]
    part = rows // 5 if rows % 80 == 0 else rows
    pieces = [pl.ds(at, part) for at in range(0, rows, part)]

    def run(out, count, node):
        copies = []
        for i, piece in enumerate(pieces):
            gradient = direction[piece, :]
            for k in range(count):
                gradient += parts[k][piece, :].astype(FULL)
            inv = inverse[piece, :]
            unit = raw[piece, :].astype(FULL) * inv
            along = jnp.sum(unit * gradient, axis=1, keepdims=True)
            held[piece, :] = (gradient - unit * along) * inv
            copy = pltpu.make_async_copy(held.at[piece], out.at[piece], sems.at[i])
            copy.start()
            copies.append(copy)
        for copy in copies:
            copy.wait()

    if sums_on_first:
        by_role(
            functools.partial(run, text_grads, far), functools.partial(run, image_grads, 1)
        )
    else:
        by_role(
            functools.partial(run, image_grads, 1), functools.partial(run, text_grads, far)
        )


def call(kernel, name, operands, shapes, smem=0, anywhere=0, scratch=(), flops=0, **more):
    operands = list(operands)
    size = sum(x.size * x.dtype.itemsize for x in operands)
    held = pl.BlockSpec(memory_space=pltpu.VMEM)
    for i in range(smem, smem + anywhere):
        operands[i] = pltpu.with_memory_space_constraint(operands[i], pltpu.HBM)
    return pl.pallas_call(
        kernel,
        name=name,
        out_shape=[pltpu.VMEM(s, d) for s, d in shapes],
        in_specs=[pl.BlockSpec(memory_space=pltpu.SMEM)] * smem
        + [pl.BlockSpec(memory_space=pltpu.HBM)] * anywhere
        + [held] * (len(operands) - smem - anywhere),
        out_specs=[held] * len(shapes),
        scratch_shapes=scratch,
        compiler_params=pltpu.CompilerParams(vmem_limit_bytes=VMEM_LIMIT),
        cost_estimate=pl.CostEstimate(flops=flops, bytes_accessed=size, transcendentals=0),
        **more,
    )(*operands)


def tangent(far, sums_on_first, operands, grads, block):
    rows = block[0][0]
    anywhere = pl.BlockSpec(memory_space=pl.ANY)
    count = len(operands)
    return pl.pallas_call(
        functools.partial(tangent_kernel, far, sums_on_first),
        name="tangent",
        out_shape=[jax.ShapeDtypeStruct(*block)] * 2,
        in_specs=[pl.BlockSpec(memory_space=pltpu.VMEM)] * count + [anywhere] * len(grads),
        out_specs=[anywhere] * 2,
        scratch_shapes=[pltpu.VMEM(*block), pltpu.SemaphoreType.DMA((5,))],
        input_output_aliases={count + i: i for i in range(len(grads))},
        compiler_params=pltpu.CompilerParams(vmem_limit_bytes=VMEM_LIMIT),
    )(*operands, *grads)


def local(image_embeds, text_embeds, pair_text, similarity_scale, logit_bias):
    rows, width = image_embeds.shape
    cycle_count = lax.axis_size("blk")
    node_count = lax.axis_size("node")
    far = node_count - 1
    cycle_index = lax.axis_index("blk")
    node_index = lax.axis_index("node")

    def send(block, even, odd):
        route = []
        for g in range(cycle_count):
            ahead, across = odd if g % 2 else even
            for n in range(node_count):
                to = (g + ahead) % cycle_count * node_count + (n + across) % node_count
                route.append((g * node_count + n, to))
        return lax.ppermute(block, ("blk", "node"), route)

    def swap(block):
        return send(block, (1, 0), (-1, 0))

    stay = (0, 0)
    ahead, behind = (2, 0), (-2, 0)
    block_h = ((rows, width), HALF)
    block_f = ((rows, width), FULL)
    column = ((rows, 1), FULL)
    tiles = ((3, node_count, rows, rows), HALF)
    returns = ((far, rows, width), HALF)

    mate_image = swap(image_embeds)
    mate_text = swap(text_embeds)
    lead_raw, rest_raw, lead, rest, lead_inv, rest_inv = call(
        unit_kernel,
        "unit",
        [image_embeds, text_embeds],
        [block_h, block_h, block_h, block_h, column, column],
        anywhere=2,
        scratch=[pltpu.SemaphoreType.DMA((4,))],
    )
    got1 = [send(lead, (0, -k), ahead if k == 1 else stay) for k in range(1, node_count)]
    got2 = [send(rest, ahead if k == 1 else stay, (0, -k)) for k in range(1, node_count)]

    start = (cycle_index * node_count + node_index) * rows
    targets = lax.dynamic_slice_in_dim(pair_text, start, rows, 0)
    targets = (targets - cycle_index * node_count * rows)[:, None]

    params, mate_lead, mate_rest, lead_part, rest_part = call(
        early_kernel,
        "early",
        [similarity_scale, logit_bias, targets, lead, rest, mate_image, mate_text],
        [((8, 128), FULL), block_h, block_h, block_f, block_f],
        smem=2,
    )
    *got2, params = lax.optimization_barrier((*got2, params))
    relay1 = [swap(block) for block in got1]
    relay2 = [swap(block) for block in got2]
    weights, back = call(
        functools.partial(first_kernel, far),
        "first",
        [params, targets, lead, rest, mate_rest, *got1, *got2],
        [tiles, returns],
    )
    one = [
        send(back[k], behind if k == 0 else stay, (0, k + 1)) for k in range(far)
    ]
    more, back = call(
        functools.partial(second_kernel, far),
        "second",
        [params, targets, lead, rest, mate_lead, weights, *got1, *got2, *relay1],
        [tiles, returns],
    )
    two = [
        send(back[k], (0, k + 1), behind if k == 0 else stay) for k in range(far)
    ]
    lead_dir, rest_dir = call(
        functools.partial(third_kernel, far),
        "third",
        [params, lead, rest, weights, more, lead_part, rest_part, *got1, *got2, *relay1, *relay2],
        [block_f, block_f],
    )
    grads = tangent(far, False, [rest_raw, rest_inv, rest_dir, *one], [], block_f)
    return tuple(tangent(far, True, [lead_raw, lead_inv, lead_dir, *two], grads, block_f))


def solution(mesh):
    return jax.shard_map(
        local,
        mesh=mesh,
        in_specs=(P(("blk", "node"), None), P(("blk", "node"), None), P(), P(), P()),
        out_specs=(P(("blk", "node"), None), P(("blk", "node"), None)),
        check_vma=False,
    )
```

time: 38.1 us -> 34.4 us (0.903); the launches traced: 37.8 us -> 33.7 us
  Pallas kernels: 0 us -> 7.83 us
  waiting for transfers between devices: 16.1 us -> 9.27 us
  other arithmetic: 6.79 us -> 0.78 us
  starting transfers between devices: 7.95 us -> 13.1 us
  matrix products: 4.13 us -> 0 us
    pallas_call x0 -> x7, Pallas kernels: none -> 7.83 us  [the longest x5 5.61 us: call(): pl.pallas_call(kernel, name=name, out_shape=[pltpu.VMEM(s, d) for s, d in...]
    ppermute x6 -> x8, waiting for transfers between devices: 16.1 us -> 9.27 us  [send(): return lax.ppermute(block, ('blk', 'node'), route)]
    ppermute x6 -> x8, starting transfers between devices: 7.95 us -> 13.1 us  [send(): return lax.ppermute(block, ('blk', 'node'), route)]
    dot_general x9 -> x0, matrix products: 4.13 us -> none  [the longest x3 1.46 us: local(): lax.dot_general(image_halves[t], text_all, (((1,), (1,)), ((), ())), pref...]
    reduce_sum x6 -> x0, other arithmetic: 3.11 us -> none  [the longest x5 2.85 us: unit_rows(): inverse = lax.rsqrt(jnp.sum(values * values, axis=1, keepdims=True) + 1e-06)]
    mul x2 -> x0, other arithmetic: 2.31 us -> none  [tangent_part(): (gradient - unit_rows_f * jnp.sum(unit_rows_f * gradient, axis=1, keepdim...]
    convert_element_type x2 -> x0, other arithmetic: 1.25 us -> none  [the longest x1 1.12 us: local(): text_unit.astype(jnp.bfloat16)]
    sub x0 -> x1, other arithmetic: none -> 0.78 us  [local(): targets = (targets - cycle_index * node_count * rows)[:, None]]
  transfers between devices with their start and end apart: 6 -> 8, of which waited for: 6 -> 3; matrix products, arithmetic and copies ran while one was open for 18% -> 3% of each run, Pallas kernels for 0% -> 16%
where the time goes in v4:
time: 34.4 us; the launch traced here: 33.7 us
  starting transfers between devices  13.1 us (38%)
  waiting for transfers between devices  9.27 us (27%)
  Pallas kernels  7.83 us (23%)
  between operations  2.02 us (6%)
  other arithmetic  0.78 us (2%)
  local copies, waits for them, and re-layouts  0.74 us (2%)
    ppermute x8, starting transfers between devices, send(): return lax.ppermute(block, ('blk', 'node'), route)  13.1 us
    ppermute x8, waiting for transfers between devices, send(): return lax.ppermute(block, ('blk', 'node'), route)  9.27 us
    pallas_call x5, Pallas kernels, call(): pl.pallas_call(kernel, name=name, out_shape=[pltpu.VMEM(s, d) for s, d in...  5.61 us
    pallas_call x2, Pallas kernels, tangent(): pl.pallas_call(functools.partial(tangent_kernel, far, sums_on_first), nam...  2.22 us
    sub x1, other arithmetic, local(): targets = (targets - cycle_index * node_count * rows)[:, None]  0.78 us
  transfers between devices with their start and end apart: 8, of which 3 were waited for; matrix products, arithmetic and copies ran while one was open for 3% of the time, Pallas kernels for 16%

profile of v4, /device:TPU:0, one launch (start us, length us, event | category | flops | bytes accessed | tf_op | source)
XLA Modules:
  0.0 33.7 jit_solution(17353911758106886003)
XLA Ops:
  0.6 1.5 %unit.1 = (bf16[160,1152]{1,0:T(8,128)(2,1)S(1)}, bf16[160,1152]{1,0:T(8,128)(2,1)S(1)}, bf16[160,1152]{1,0:T(8,128)(2,1)S(1)}, bf16[160,1152]{1,0:T(8,128)(2,1)...) custom-call(bf16[160,1152]{1,0:T(8,128)(2,1)} %image.1, bf16[160,1152]{1,0:T(8,128)(2,1)} %text.1), custom_call_target="tpu_custom_call" | custom-call | bytes 737280 | tf_op jit(solution)/shard_map/unit/pallas_call | solution.py:236
  2.1 0.0 copy-start
  2.1 0.6 %copy-done = f32[160,1]{1,0:T(8,128)} copy-done((f32[160,1]{1,0:T(8,128)}, f32[160,1]{1,0:T(8,128)S(1)}, u32[]{:S(2)}) %copy-start) | copy-done | bytes 664
  2.8 3.0 %collective-permute-start.3 = (bf16[160,1152]{1,0:T(8,128)(2,1)S(1)}, bf16[160,1152]{1,0:T(8,128)(2,1)S(1)}, u32[]{:S(2)}, u32[]{:S(2)}) collective-permute-start(bf16[160,1152]{1,0:T(8,128)(2,1)S(1)} %get-tuple-element.26.lead), channel_id=1, source_target_pairs={{0,1},{1,0},{2,6},{3,7},{4,5},{5,4},{6,10},{7,11},{8,9},{9,8},{10,... | collective-permute-start | bytes 1105928 | tf_op jit(solution)/shard_map/ppermute | solution.py:282
  5.7 0.0 collective-permute-start.1
  5.7 0.5 %collective-permute-start.2 = (bf16[160,1152]{1,0:T(8,128)(2,1)}, bf16[160,1152]{1,0:T(8,128)(2,1)S(1)}, u32[]{:S(2)}, u32[]{:S(2)}) collective-permute-start(bf16[160,1152]{1,0:T(8,128)(2,1)} %text.1), channel_id=1, source_target_pairs={{0,2},{1,3},{2,0},{3,1},{4,6},{5,7},{6,4},{7,5},{8,10},{9,11},{10,... | collective-permute-start | bytes 1105928 | tf_op jit(solution)/shard_map/ppermute | solution.py:282
  6.2 1.5 %collective-permute-start = (bf16[160,1152]{1,0:T(8,128)(2,1)S(1)}, bf16[160,1152]{1,0:T(8,128)(2,1)S(1)}, u32[]{:S(2)}, u32[]{:S(2)}) collective-permute-start(bf16[160,1152]{1,0:T(8,128)(2,1)S(1)} %get-tuple-element.25.rest), channel_id=1, source_target_pairs={{0,4},{1,5},{2,3},{3,2},{4,8},{5,9},{6,7},{7,6},{8,12},{9,13},{10,... | collective-permute-start | bytes 1105928 | tf_op jit(solution)/shard_map/ppermute | solution.py:282
  7.7 6.4 %collective-permute-done.3.refs_0_ = bf16[160,1152]{1,0:T(8,128)(2,1)S(1)} collective-permute-done((bf16[160,1152]{1,0:T(8,128)(2,1)S(1)}, bf16[160,1152]{1,0:T(8,128)(2,1)S(1)}, u32[]{:S(2)}, u32[]{:S(2)}) %collective-permute-start.3) | collective-permute-done | bytes 368672 | tf_op jit(solution)/shard_map/ppermute | solution.py:282
  14.2 0.1 collective-permute-start.4
  15.6 0.8 %dynamic-slice_subtract_fusion = s32[160]{0:T(256)S(1)} fusion(s32[5120]{0:T(1024)} %param.7, s32[]{:T(128)S(6)} %select_n.3, s32[]{:T(128)S(6)} %mul.12), kind=kLoop, calls=%fused_computation | loop fusion | flops 160 | bytes 1288 | tf_op jit(solution)/shard_map/sub | solution.py:310
  16.4 0.1 copy.9.targets
  16.5 0.0 collective-permute-done.1.mate_image
  16.5 0.0 collective-permute-done.2.mate_text
  16.5 1.0 %early.1 = (f32[8,128]{1,0:T(8,128)S(1)}, bf16[160,1152]{1,0:T(8,128)(2,1)S(1)}, bf16[160,1152]{1,0:T(8,128)(2,1)S(1)}, f32[160,1152]{1,0:T(8,128)S(1)}, f32[160,1152]{1,0:T(8,128)S(1)}) custom-call(f32[1]{0:T(128)S(6)} %copy.14.scale, f32[1]{0:T(128)S(6)} %copy.15.bias, s32[160,1]{1,0:T(8,128)S(1)} %copy.9.targets, ...), custom_call_target="tpu_custom_call" | custom-call | bytes 1475208 | tf_op jit(solution)/shard_map/early/pallas_call | solution.py:236
  17.5 0.4 %collective-permute-start.5 = (bf16[160,1152]{1,0:T(8,128)(2,1)S(1)}, bf16[160,1152]{1,0:T(8,128)(2,1)S(1)}, u32[]{:S(2)}, u32[]{:S(2)}) collective-permute-start(bf16[160,1152]{1,0:T(8,128)(2,1)S(1)} %collective-permute-done.refs_1_), channel_id=1, source_target_pairs={{0,2},{1,3},{2,0},{3,1},{4,6},{5,7},{6,4},{7,5},{8,10},{9,11},{10,... | collective-permute-start | bytes 1105928 | tf_op jit(solution)/shard_map/ppermute | solution.py:282
  17.9 0.8 %first.1 = (bf16[3,2,160,160]{3,2,1,0:T(8,128)(2,1)S(1)}, bf16[1,160,1152]{2,1,0:T(8,128)(2,1)S(1)}) custom-call(f32[8,128]{1,0:T(8,128)S(1)} %get-tuple-element.28.params, s32[160,1]{1,0:T(8,128)S(1)} %copy.9.targets, bf16[160,1152]{1,0:T(8,128)(2,1)S(1)} %get-tuple-element.26.lead, bf16[160,1152]{1,0:T(8,128)(2,1)S(1)} %get-tuple-element.25.rest, ...), custom_call_target="tpu_custom_call" | custom-call | bytes 1847936 | tf_op jit(solution)/shard_map/first/pallas_call | solution.py:236
  18.7 5.0 %collective-permute-start.7 = (bf16[160,1152]{1,0:T(8,128)(2,1)S(1)}, bf16[160,1152]{1,0:T(8,128)(2,1)S(1)}, u32[]{:S(2)}, u32[]{:S(2)}) collective-permute-start(bf16[160,1152]{1,0:T(8,128)(2,1)S(1)} %bitcast.3), channel_id=1, source_target_pairs={{0,28},{1,29},{2,3},{3,2},{4,0},{5,1},{6,7},{7,6},{8,4},{9,5},{10,... | collective-permute-start | bytes 1105928 | tf_op jit(solution)/shard_map/ppermute | solution.py:282
  23.8 0.8 %second.1 = (bf16[3,2,160,160]{3,2,1,0:T(8,128)(2,1)S(1)}, bf16[1,160,1152]{2,1,0:T(8,128)(2,1)S(1)}) custom-call(f32[8,128]{1,0:T(8,128)S(1)} %get-tuple-element.28.params, s32[160,1]{1,0:T(8,128)S(1)} %copy.9.targets, bf16[160,1152]{1,0:T(8,128)(2,1)S(1)} %get-tuple-element.26.lead, bf16[160,1152]{1,0:T(8,128)(2,1)S(1)} %get-tuple-element.25.rest, ...), custom_call_target="tpu_custom_call" | custom-call | bytes 2523776 | tf_op jit(solution)/shard_map/second/pallas_call | solution.py:236
  24.6 2.5 %collective-permute-start.6 = (bf16[160,1152]{1,0:T(8,128)(2,1)S(1)}, bf16[160,1152]{1,0:T(8,128)(2,1)S(1)}, u32[]{:S(2)}, u32[]{:S(2)}) collective-permute-start(bf16[160,1152]{1,0:T(8,128)(2,1)S(1)} %bitcast.4), channel_id=1, source_target_pairs={{0,1},{1,0},{2,30},{3,31},{4,5},{5,4},{6,2},{7,3},{8,9},{9,8},{10,... | collective-permute-start | bytes 1105928 | tf_op jit(solution)/shard_map/ppermute | solution.py:282
  27.1 1.6 %third.1 = (f32[160,1152]{1,0:T(8,128)S(1)}, f32[160,1152]{1,0:T(8,128)S(1)}) custom-call(f32[8,128]{1,0:T(8,128)S(1)} %get-tuple-element.28.params, bf16[160,1152]{1,0:T(8,128)(2,1)S(1)} %get-tuple-element.26.lead, bf16[160,1152]{1,0:T(8,128)(2,1)S(1)} %get-tuple-element.25.rest, bf16[3,2,160,160]{3,2,1,0:T(8,128)(2,1)S(1)} %get-tuple-element.31.weights, ...), custom_call_target="tpu_custom_call" | custom-call | bytes 4304896 | tf_op jit(solution)/shard_map/third/pallas_call | solution.py:236
  28.7 0.8 %collective-permute-done.7.refs_0_ = bf16[160,1152]{1,0:T(8,128)(2,1)S(1)} collective-permute-done((bf16[160,1152]{1,0:T(8,128)(2,1)S(1)}, bf16[160,1152]{1,0:T(8,128)(2,1)S(1)}, u32[]{:S(2)}, u32[]{:S(2)}) %collective-permute-start.7) | collective-permute-done | bytes 368672 | tf_op jit(solution)/shard_map/ppermute | solution.py:282
  29.5 1.1 %tangent.2 = (f32[160,1152]{1,0:T(8,128)}, f32[160,1152]{1,0:T(8,128)}) custom-call(bf16[160,1152]{1,0:T(8,128)(2,1)S(1)} %get-tuple-element.38.raw, f32[160,1]{1,0:T(8,128)S(1)} %copy-done.1, f32[160,1152]{1,0:T(8,128)S(1)} %get-tuple-element.40.direction, bf16[160,1152]{1,0:T(8,128)(2,1)S(1)} %collective-permute-done.7.refs_0_), custom_call_target="tpu_custom_call" | custom-call | tf_op jit(solution)/shard_map/tangent/pallas_call | solution.py:255
  30.6 2.0 %collective-permute-done.6.refs_0_ = bf16[160,1152]{1,0:T(8,128)(2,1)S(1)} collective-permute-done((bf16[160,1152]{1,0:T(8,128)(2,1)S(1)}, bf16[160,1152]{1,0:T(8,128)(2,1)S(1)}, u32[]{:S(2)}, u32[]{:S(2)}) %collective-permute-start.6) | collective-permute-done | bytes 368672 | tf_op jit(solution)/shard_map/ppermute | solution.py:282
  32.6 1.1 %tangent.3 = (f32[160,1152]{1,0:T(8,128)}, f32[160,1152]{1,0:T(8,128)}) custom-call(bf16[160,1152]{1,0:T(8,128)(2,1)S(1)} %get-tuple-element.23.raw, f32[160,1]{1,0:T(8,128)S(1)} %get-tuple-element.24.inverse, f32[160,1152]{1,0:T(8,128)S(1)} %get-tuple-element.36.direction, ...), custom_call_target="tpu_custom_call", output_to_operand_aliasing={{0}: (4, {}), {1}: (5, {})} | custom-call | tf_op jit(solution)/shard_map/tangent/pallas_call | solution.py:255
  (5 shorter events, 0.0 us)
Async XLA Ops:
  2.1 0.6 %copy-start = (f32[160,1]{1,0:T(8,128)}, f32[160,1]{1,0:T(8,128)S(1)}, u32[]{:S(2)}) copy-start(f32[160,1]{1,0:T(8,128)S(1)} %get-tuple-element.39.inverse) | copy-start | bytes 1924
  2.8 11.4 %collective-permute-start.3 = (bf16[160,1152]{1,0:T(8,128)(2,1)S(1)}, bf16[160,1152]{1,0:T(8,128)(2,1)S(1)}, u32[]{:S(2)}, u32[]{:S(2)}) collective-permute-start(bf16[160,1152]{1,0:T(8,128)(2,1)S(1)} %get-tuple-element.26.lead), channel_id=1, source_target_pairs={{0,1},{1,0},{2,6},{3,7},{4,5},{5,4},{6,10},{7,11},{8,9},{9,8},{10,... | collective-permute-start | bytes 1105928 | tf_op jit(solution)/shard_map/ppermute | solution.py:282
  5.7 10.8 %collective-permute-start.1 = (bf16[160,1152]{1,0:T(8,128)(2,1)}, bf16[160,1152]{1,0:T(8,128)(2,1)S(1)}, u32[]{:S(2)}, u32[]{:S(2)}) collective-permute-start(bf16[160,1152]{1,0:T(8,128)(2,1)} %image.1), channel_id=1, source_target_pairs={{0,2},{1,3},{2,0},{3,1},{4,6},{5,7},{6,4},{7,5},{8,10},{9,11},{10,... | collective-permute-start | bytes 1105928 | tf_op jit(solution)/shard_map/ppermute | solution.py:282
  5.7 10.8 %collective-permute-start.2 = (bf16[160,1152]{1,0:T(8,128)(2,1)}, bf16[160,1152]{1,0:T(8,128)(2,1)S(1)}, u32[]{:S(2)}, u32[]{:S(2)}) collective-permute-start(bf16[160,1152]{1,0:T(8,128)(2,1)} %text.1), channel_id=1, source_target_pairs={{0,2},{1,3},{2,0},{3,1},{4,6},{5,7},{6,4},{7,5},{8,10},{9,11},{10,... | collective-permute-start | bytes 1105928 | tf_op jit(solution)/shard_map/ppermute | solution.py:282
  6.2 11.2 %collective-permute-start = (bf16[160,1152]{1,0:T(8,128)(2,1)S(1)}, bf16[160,1152]{1,0:T(8,128)(2,1)S(1)}, u32[]{:S(2)}, u32[]{:S(2)}) collective-permute-start(bf16[160,1152]{1,0:T(8,128)(2,1)S(1)} %get-tuple-element.25.rest), channel_id=1, source_target_pairs={{0,4},{1,5},{2,3},{3,2},{4,8},{5,9},{6,7},{7,6},{8,12},{9,13},{10,... | collective-permute-start | bytes 1105928 | tf_op jit(solution)/shard_map/ppermute | solution.py:282
  14.2 9.6 %collective-permute-start.4 = (bf16[160,1152]{1,0:T(8,128)(2,1)S(1)}, bf16[160,1152]{1,0:T(8,128)(2,1)S(1)}, u32[]{:S(2)}, u32[]{:S(2)}) collective-permute-start(bf16[160,1152]{1,0:T(8,128)(2,1)S(1)} %collective-permute-done.3.refs_0_), channel_id=1, source_target_pairs={{0,2},{1,3},{2,0},{3,1},{4,6},{5,7},{6,4},{7,5},{8,10},{9,11},{10,... | collective-permute-start | bytes 1105928 | tf_op jit(solution)/shard_map/ppermute | solution.py:282
  17.5 9.6 %collective-permute-start.5 = (bf16[160,1152]{1,0:T(8,128)(2,1)S(1)}, bf16[160,1152]{1,0:T(8,128)(2,1)S(1)}, u32[]{:S(2)}, u32[]{:S(2)}) collective-permute-start(bf16[160,1152]{1,0:T(8,128)(2,1)S(1)} %collective-permute-done.refs_1_), channel_id=1, source_target_pairs={{0,2},{1,3},{2,0},{3,1},{4,6},{5,7},{6,4},{7,5},{8,10},{9,11},{10,... | collective-permute-start | bytes 1105928 | tf_op jit(solution)/shard_map/ppermute | solution.py:282
  18.7 10.8 %collective-permute-start.7 = (bf16[160,1152]{1,0:T(8,128)(2,1)S(1)}, bf16[160,1152]{1,0:T(8,128)(2,1)S(1)}, u32[]{:S(2)}, u32[]{:S(2)}) collective-permute-start(bf16[160,1152]{1,0:T(8,128)(2,1)S(1)} %bitcast.3), channel_id=1, source_target_pairs={{0,28},{1,29},{2,3},{3,2},{4,0},{5,1},{6,7},{7,6},{8,4},{9,5},{10,... | collective-permute-start | bytes 1105928 | tf_op jit(solution)/shard_map/ppermute | solution.py:282
  24.6 8.0 %collective-permute-start.6 = (bf16[160,1152]{1,0:T(8,128)(2,1)S(1)}, bf16[160,1152]{1,0:T(8,128)(2,1)S(1)}, u32[]{:S(2)}, u32[]{:S(2)}) collective-permute-start(bf16[160,1152]{1,0:T(8,128)(2,1)S(1)} %bitcast.4), channel_id=1, source_target_pairs={{0,1},{1,0},{2,30},{3,31},{4,5},{5,4},{6,2},{7,3},{8,9},{9,8},{10,... | collective-permute-start | bytes 1105928 | tf_op jit(solution)/shard_map/ppermute | solution.py:282
  27.1 2.4 %copy-start.1 = (f32[160,1]{1,0:T(8,128)S(1)}, f32[160,1]{1,0:T(8,128)}, u32[]{:S(2)}) copy-start(f32[160,1]{1,0:T(8,128)} %copy-done) | copy-start | bytes 1924

commit v5 on v4

--- a/solution.py
+++ b/solution.py
@@ -75,29 +75,19 @@
             inv[piece, :] = inverse
 
 
-def half_rows(raw):
-    values = raw[...].astype(FULL)
-    inverse = lax.rsqrt(jnp.sum(values * values, axis=1, keepdims=True) + 1e-06)
-    return (values * inverse).astype(HALF)
-
-
 def early_kernel(
-    scale, bias, targets, lead, rest, mate_image, mate_text,
-    params, mate_lead, mate_rest, lead_part, rest_part,
+    scale, bias, targets, lead, rest, mate_rest, params, lead_part, rest_part
 ):
     row = lax.broadcasted_iota(jnp.int32, params.shape, 0)
     params[...] = jnp.where(row == 0, scale[0], bias[0])
 
     def on_first(node):
-        mate_rest[...] = half_rows(mate_text)
         own = weigh_own(rest[...], lead[...], params, targets[...], node)
         cross = weigh(rest[...], mate_rest[...], params)
         rest_part[...] = mix(own, lead[...]) + mix(cross, mate_rest[...])
         lead_part[...] = mix_back(own, rest[...])
 
     def on_second(node):
-        mate_rest[...] = half_rows(mate_image)
-        mate_lead[...] = half_rows(mate_text)
         own = weigh_own(lead[...], rest[...], params, targets[...], node)
         cross = weigh(mate_rest[...], rest[...], params)
         lead_part[...] = mix(own, rest[...])
@@ -292,8 +282,6 @@
     tiles = ((3, node_count, rows, rows), HALF)
     returns = ((far, rows, width), HALF)
 
-    mate_image = swap(image_embeds)
-    mate_text = swap(text_embeds)
     lead_raw, rest_raw, lead, rest, lead_inv, rest_inv = call(
         unit_kernel,
         "unit",
@@ -304,20 +292,23 @@
     )
     got1 = [send(lead, (0, -k), ahead if k == 1 else stay) for k in range(1, node_count)]
     got2 = [send(rest, ahead if k == 1 else stay, (0, -k)) for k in range(1, node_count)]
+    mate_rest = swap(rest)
+    mate_lead = swap(lead)
 
     start = (cycle_index * node_count + node_index) * rows
     targets = lax.dynamic_slice_in_dim(pair_text, start, rows, 0)
     targets = (targets - cycle_index * node_count * rows)[:, None]
 
-    params, mate_lead, mate_rest, lead_part, rest_part = call(
+    params, lead_part, rest_part = call(
         early_kernel,
         "early",
-        [similarity_scale, logit_bias, targets, lead, rest, mate_image, mate_text],
-        [((8, 128), FULL), block_h, block_h, block_f, block_f],
+        [similarity_scale, logit_bias, targets, lead, rest, mate_rest],
+        [((8, 128), FULL), block_f, block_f],
         smem=2,
     )
+    *got1, params = lax.optimization_barrier((*got1, params))
+    relay1 = [swap(block) for block in got1]
     *got2, params = lax.optimization_barrier((*got2, params))
-    relay1 = [swap(block) for block in got1]
     relay2 = [swap(block) for block in got2]
     weights, back = call(
         functools.partial(first_kernel, far),

time: 34.4 us -> 31.2 us (0.907); the launches traced: 33.7 us -> 31 us
  starting transfers between devices: 13.1 us -> 10.4 us
  waiting for transfers between devices: 9.27 us -> 9.96 us
  local copies, waits for them, and re-layouts: 0.74 us -> 0.11 us
    ppermute x8, starting transfers between devices: 13.1 us -> 10.4 us  [send(): return lax.ppermute(block, ('blk', 'node'), route)]
    ppermute x8, waiting for transfers between devices: 9.27 us -> 9.96 us  [send(): return lax.ppermute(block, ('blk', 'node'), route)]
    unnamed x4 -> x0, local copies, waits for them, and re-layouts: 0.63 us -> none
  transfers between devices with their start and end apart: 8 -> 8, of which waited for: 3 -> 4; matrix products, arithmetic and copies ran while one was open for 3% -> 3% of each run, Pallas kernels for 16% -> 17%
where the time goes in v5:
time: 31.2 us; the launch traced here: 31 us
  starting transfers between devices  10.4 us (33%)
  waiting for transfers between devices  9.96 us (32%)
  Pallas kernels  7.74 us (25%)
  between operations  2 us (6%)
  other arithmetic  0.77 us (2%)
    ppermute x8, starting transfers between devices, send(): return lax.ppermute(block, ('blk', 'node'), route)  10.4 us
    ppermute x8, waiting for transfers between devices, send(): return lax.ppermute(block, ('blk', 'node'), route)  9.96 us
    pallas_call x5, Pallas kernels, call(): pl.pallas_call(kernel, name=name, out_shape=[pltpu.VMEM(s, d) for s, d in...  5.52 us
    pallas_call x2, Pallas kernels, tangent(): pl.pallas_call(functools.partial(tangent_kernel, far, sums_on_first), nam...  2.22 us
    sub x1, other arithmetic, local(): targets = (targets - cycle_index * node_count * rows)[:, None]  0.77 us
  transfers between devices with their start and end apart: 8, of which 4 were waited for; matrix products, arithmetic and copies ran while one was open for 3% of the time, Pallas kernels for 17%

profile of v5, /device:TPU:0, one launch (start us, length us, event | category | flops | bytes accessed | tf_op | source)
XLA Modules:
  0.0 31.0 jit_solution(9949238886624240006)
XLA Ops:
  0.6 1.5 %unit.1 = (bf16[160,1152]{1,0:T(8,128)(2,1)S(1)}, bf16[160,1152]{1,0:T(8,128)(2,1)S(1)}, bf16[160,1152]{1,0:T(8,128)(2,1)S(1)}, bf16[160,1152]{1,0:T(8,128)(2,1)...) custom-call(bf16[160,1152]{1,0:T(8,128)(2,1)} %image.1, bf16[160,1152]{1,0:T(8,128)(2,1)} %text.1), custom_call_target="tpu_custom_call" | custom-call | bytes 737280 | tf_op jit(solution)/shard_map/unit/pallas_call | solution.py:226
  2.1 0.5 %collective-permute-start.2 = (bf16[160,1152]{1,0:T(8,128)(2,1)S(1)}, bf16[160,1152]{1,0:T(8,128)(2,1)S(1)}, u32[]{:S(2)}, u32[]{:S(2)}) collective-permute-start(bf16[160,1152]{1,0:T(8,128)(2,1)S(1)} %get-tuple-element.25.rest), channel_id=1, source_target_pairs={{0,2},{1,3},{2,0},{3,1},{4,6},{5,7},{6,4},{7,5},{8,10},{9,11},{10,... | collective-permute-start | bytes 1105928 | tf_op jit(solution)/shard_map/ppermute | solution.py:272
  2.6 2.6 %collective-permute-start.1 = (bf16[160,1152]{1,0:T(8,128)(2,1)S(1)}, bf16[160,1152]{1,0:T(8,128)(2,1)S(1)}, u32[]{:S(2)}, u32[]{:S(2)}) collective-permute-start(bf16[160,1152]{1,0:T(8,128)(2,1)S(1)} %get-tuple-element.26.lead), channel_id=1, source_target_pairs={{0,1},{1,0},{2,6},{3,7},{4,5},{5,4},{6,10},{7,11},{8,9},{9,8},{10,... | collective-permute-start | bytes 1105928 | tf_op jit(solution)/shard_map/ppermute | solution.py:272
  5.2 1.5 %collective-permute-start = (bf16[160,1152]{1,0:T(8,128)(2,1)S(1)}, bf16[160,1152]{1,0:T(8,128)(2,1)S(1)}, u32[]{:S(2)}, u32[]{:S(2)}) collective-permute-start(bf16[160,1152]{1,0:T(8,128)(2,1)S(1)} %get-tuple-element.25.rest), channel_id=1, source_target_pairs={{0,4},{1,5},{2,3},{3,2},{4,8},{5,9},{6,7},{7,6},{8,12},{9,13},{10,... | collective-permute-start | bytes 1105928 | tf_op jit(solution)/shard_map/ppermute | solution.py:272
  6.7 0.0 collective-permute-start.3
  6.7 0.8 %dynamic-slice_subtract_fusion = s32[160]{0:T(256)S(1)} fusion(s32[5120]{0:T(1024)} %param.7, s32[]{:T(128)S(6)} %select_n.3, s32[]{:T(128)S(6)} %mul.12), kind=kLoop, calls=%fused_computation | loop fusion | flops 160 | bytes 1288 | tf_op jit(solution)/shard_map/sub | solution.py:300
  8.8 0.1 copy.9.targets
  8.9 0.0 collective-permute-done.2.mate_rest
  8.9 0.9 %early.1 = (f32[8,128]{1,0:T(8,128)S(1)}, f32[160,1152]{1,0:T(8,128)S(1)}, f32[160,1152]{1,0:T(8,128)S(1)}) custom-call(f32[1]{0:T(128)S(6)} %copy.14.scale, f32[1]{0:T(128)S(6)} %copy.15.bias, s32[160,1]{1,0:T(8,128)S(1)} %copy.9.targets, bf16[160,1152]{1,0:T(8,128)(2,1)S(1)} %get-tuple-element.26.lead, bf16[160,1152]{1,0:T(8,128)(2,1)S(1)} %get-tuple-element.25.rest, ...), custom_call_target="tpu_custom_call" | custom-call | bytes 1106568 | tf_op jit(solution)/shard_map/early/pallas_call | solution.py:226
  9.8 3.8 %collective-permute-done.1.refs_0_ = bf16[160,1152]{1,0:T(8,128)(2,1)S(1)} collective-permute-done((bf16[160,1152]{1,0:T(8,128)(2,1)S(1)}, bf16[160,1152]{1,0:T(8,128)(2,1)S(1)}, u32[]{:S(2)}, u32[]{:S(2)}) %collective-permute-start.1) | collective-permute-done | bytes 368672 | tf_op jit(solution)/shard_map/ppermute | solution.py:272
  13.5 2.0 %collective-permute-start.4 = (bf16[160,1152]{1,0:T(8,128)(2,1)S(1)}, bf16[160,1152]{1,0:T(8,128)(2,1)S(1)}, u32[]{:S(2)}, u32[]{:S(2)}) collective-permute-start(bf16[160,1152]{1,0:T(8,128)(2,1)S(1)} %collective-permute-done.1.refs_0_), channel_id=1, source_target_pairs={{0,2},{1,3},{2,0},{3,1},{4,6},{5,7},{6,4},{7,5},{8,10},{9,11},{10,... | collective-permute-start | bytes 1105928 | tf_op jit(solution)/shard_map/ppermute | solution.py:272
  15.5 1.9 %collective-permute-done.refs_1_ = bf16[160,1152]{1,0:T(8,128)(2,1)S(1)} collective-permute-done((bf16[160,1152]{1,0:T(8,128)(2,1)S(1)}, bf16[160,1152]{1,0:T(8,128)(2,1)S(1)}, u32[]{:S(2)}, u32[]{:S(2)}) %collective-permute-start) | collective-permute-done | bytes 368672 | tf_op jit(solution)/shard_map/ppermute | solution.py:272
  17.4 0.0 collective-permute-start.5
  17.4 0.8 %first.1 = (bf16[3,2,160,160]{3,2,1,0:T(8,128)(2,1)S(1)}, bf16[1,160,1152]{2,1,0:T(8,128)(2,1)S(1)}) custom-call(f32[8,128]{1,0:T(8,128)S(1)} %get-tuple-element.29.params, s32[160,1]{1,0:T(8,128)S(1)} %copy.9.targets, bf16[160,1152]{1,0:T(8,128)(2,1)S(1)} %get-tuple-element.26.lead, bf16[160,1152]{1,0:T(8,128)(2,1)S(1)} %get-tuple-element.25.rest, ...), custom_call_target="tpu_custom_call" | custom-call | bytes 1847936 | tf_op jit(solution)/shard_map/first/pallas_call | solution.py:226
  18.2 2.3 %collective-permute-start.7 = (bf16[160,1152]{1,0:T(8,128)(2,1)S(1)}, bf16[160,1152]{1,0:T(8,128)(2,1)S(1)}, u32[]{:S(2)}, u32[]{:S(2)}) collective-permute-start(bf16[160,1152]{1,0:T(8,128)(2,1)S(1)} %bitcast.3), channel_id=1, source_target_pairs={{0,28},{1,29},{2,3},{3,2},{4,0},{5,1},{6,7},{7,6},{8,4},{9,5},{10,... | collective-permute-start | bytes 1105928 | tf_op jit(solution)/shard_map/ppermute | solution.py:272
  20.5 0.0 collective-permute-done.3.mate_lead
  20.5 0.0 collective-permute-done.4.refs_2_
  20.5 0.8 %second.1 = (bf16[3,2,160,160]{3,2,1,0:T(8,128)(2,1)S(1)}, bf16[1,160,1152]{2,1,0:T(8,128)(2,1)S(1)}) custom-call(f32[8,128]{1,0:T(8,128)S(1)} %get-tuple-element.29.params, s32[160,1]{1,0:T(8,128)S(1)} %copy.9.targets, bf16[160,1152]{1,0:T(8,128)(2,1)S(1)} %get-tuple-element.26.lead, bf16[160,1152]{1,0:T(8,128)(2,1)S(1)} %get-tuple-element.25.rest, ...), custom_call_target="tpu_custom_call" | custom-call | bytes 2523776 | tf_op jit(solution)/shard_map/second/pallas_call | solution.py:226
  21.4 1.6 %collective-permute-start.6 = (bf16[160,1152]{1,0:T(8,128)(2,1)S(1)}, bf16[160,1152]{1,0:T(8,128)(2,1)S(1)}, u32[]{:S(2)}, u32[]{:S(2)}) collective-permute-start(bf16[160,1152]{1,0:T(8,128)(2,1)S(1)} %bitcast.4), channel_id=1, source_target_pairs={{0,1},{1,0},{2,30},{3,31},{4,5},{5,4},{6,2},{7,3},{8,9},{9,8},{10,... | collective-permute-start | bytes 1105928 | tf_op jit(solution)/shard_map/ppermute | solution.py:272
  22.9 1.6 %third.1 = (f32[160,1152]{1,0:T(8,128)S(1)}, f32[160,1152]{1,0:T(8,128)S(1)}) custom-call(f32[8,128]{1,0:T(8,128)S(1)} %get-tuple-element.29.params, bf16[160,1152]{1,0:T(8,128)(2,1)S(1)} %get-tuple-element.26.lead, bf16[160,1152]{1,0:T(8,128)(2,1)S(1)} %get-tuple-element.25.rest, bf16[3,2,160,160]{3,2,1,0:T(8,128)(2,1)S(1)} %get-tuple-element.32.weights, ...), custom_call_target="tpu_custom_call" | custom-call | bytes 4304896 | tf_op jit(solution)/shard_map/third/pallas_call | solution.py:226
  24.5 2.8 %collective-permute-done.7.refs_0_ = bf16[160,1152]{1,0:T(8,128)(2,1)S(1)} collective-permute-done((bf16[160,1152]{1,0:T(8,128)(2,1)S(1)}, bf16[160,1152]{1,0:T(8,128)(2,1)S(1)}, u32[]{:S(2)}, u32[]{:S(2)}) %collective-permute-start.7) | collective-permute-done | bytes 368672 | tf_op jit(solution)/shard_map/ppermute | solution.py:272
  27.3 1.1 %tangent.2 = (f32[160,1152]{1,0:T(8,128)}, f32[160,1152]{1,0:T(8,128)}) custom-call(bf16[160,1152]{1,0:T(8,128)(2,1)S(1)} %get-tuple-element.38.raw, f32[160,1]{1,0:T(8,128)S(1)} %get-tuple-element.39.inverse, f32[160,1152]{1,0:T(8,128)S(1)} %get-tuple-element.40.direction, bf16[160,1152]{1,0:T(8,128)(2,1)S(1)} %collective-permute-done.7.refs_0_), custom_call_target="tpu_custom_call" | custom-call | tf_op jit(solution)/shard_map/tangent/pallas_call | solution.py:245
  28.4 1.5 %collective-permute-done.6.refs_0_ = bf16[160,1152]{1,0:T(8,128)(2,1)S(1)} collective-permute-done((bf16[160,1152]{1,0:T(8,128)(2,1)S(1)}, bf16[160,1152]{1,0:T(8,128)(2,1)S(1)}, u32[]{:S(2)}, u32[]{:S(2)}) %collective-permute-start.6) | collective-permute-done | bytes 368672 | tf_op jit(solution)/shard_map/ppermute | solution.py:272
  29.9 1.1 %tangent.3 = (f32[160,1152]{1,0:T(8,128)}, f32[160,1152]{1,0:T(8,128)}) custom-call(bf16[160,1152]{1,0:T(8,128)(2,1)S(1)} %get-tuple-element.23.raw, f32[160,1]{1,0:T(8,128)S(1)} %get-tuple-element.24.inverse, f32[160,1152]{1,0:T(8,128)S(1)} %get-tuple-element.36.direction, ...), custom_call_target="tpu_custom_call", output_to_operand_aliasing={{0}: (4, {}), {1}: (5, {})} | custom-call | tf_op jit(solution)/shard_map/tangent/pallas_call | solution.py:245
  (1 shorter events, 0.0 us)
Async XLA Ops:
  2.1 6.8 %collective-permute-start.2 = (bf16[160,1152]{1,0:T(8,128)(2,1)S(1)}, bf16[160,1152]{1,0:T(8,128)(2,1)S(1)}, u32[]{:S(2)}, u32[]{:S(2)}) collective-permute-start(bf16[160,1152]{1,0:T(8,128)(2,1)S(1)} %get-tuple-element.25.rest), channel_id=1, source_target_pairs={{0,2},{1,3},{2,0},{3,1},{4,6},{5,7},{6,4},{7,5},{8,10},{9,11},{10,... | collective-permute-start | bytes 1105928 | tf_op jit(solution)/shard_map/ppermute | solution.py:272
  2.6 10.9 %collective-permute-start.1 = (bf16[160,1152]{1,0:T(8,128)(2,1)S(1)}, bf16[160,1152]{1,0:T(8,128)(2,1)S(1)}, u32[]{:S(2)}, u32[]{:S(2)}) collective-permute-start(bf16[160,1152]{1,0:T(8,128)(2,1)S(1)} %get-tuple-element.26.lead), channel_id=1, source_target_pairs={{0,1},{1,0},{2,6},{3,7},{4,5},{5,4},{6,10},{7,11},{8,9},{9,8},{10,... | collective-permute-start | bytes 1105928 | tf_op jit(solution)/shard_map/ppermute | solution.py:272
  5.2 12.2 %collective-permute-start = (bf16[160,1152]{1,0:T(8,128)(2,1)S(1)}, bf16[160,1152]{1,0:T(8,128)(2,1)S(1)}, u32[]{:S(2)}, u32[]{:S(2)}) collective-permute-start(bf16[160,1152]{1,0:T(8,128)(2,1)S(1)} %get-tuple-element.25.rest), channel_id=1, source_target_pairs={{0,4},{1,5},{2,3},{3,2},{4,8},{5,9},{6,7},{7,6},{8,12},{9,13},{10,... | collective-permute-start | bytes 1105928 | tf_op jit(solution)/shard_map/ppermute | solution.py:272
  6.7 13.8 %collective-permute-start.3 = (bf16[160,1152]{1,0:T(8,128)(2,1)S(1)}, bf16[160,1152]{1,0:T(8,128)(2,1)S(1)}, u32[]{:S(2)}, u32[]{:S(2)}) collective-permute-start(bf16[160,1152]{1,0:T(8,128)(2,1)S(1)} %get-tuple-element.26.lead), channel_id=1, source_target_pairs={{0,2},{1,3},{2,0},{3,1},{4,6},{5,7},{6,4},{7,5},{8,10},{9,11},{10,... | collective-permute-start | bytes 1105928 | tf_op jit(solution)/shard_map/ppermute | solution.py:272
  13.5 7.0 %collective-permute-start.4 = (bf16[160,1152]{1,0:T(8,128)(2,1)S(1)}, bf16[160,1152]{1,0:T(8,128)(2,1)S(1)}, u32[]{:S(2)}, u32[]{:S(2)}) collective-permute-start(bf16[160,1152]{1,0:T(8,128)(2,1)S(1)} %collective-permute-done.1.refs_0_), channel_id=1, source_target_pairs={{0,2},{1,3},{2,0},{3,1},{4,6},{5,7},{6,4},{7,5},{8,10},{9,11},{10,... | collective-permute-start | bytes 1105928 | tf_op jit(solution)/shard_map/ppermute | solution.py:272
  17.4 5.5 %collective-permute-start.5 = (bf16[160,1152]{1,0:T(8,128)(2,1)S(1)}, bf16[160,1152]{1,0:T(8,128)(2,1)S(1)}, u32[]{:S(2)}, u32[]{:S(2)}) collective-permute-start(bf16[160,1152]{1,0:T(8,128)(2,1)S(1)} %collective-permute-done.refs_1_), channel_id=1, source_target_pairs={{0,2},{1,3},{2,0},{3,1},{4,6},{5,7},{6,4},{7,5},{8,10},{9,11},{10,... | collective-permute-start | bytes 1105928 | tf_op jit(solution)/shard_map/ppermute | solution.py:272
  18.2 9.0 %collective-permute-start.7 = (bf16[160,1152]{1,0:T(8,128)(2,1)S(1)}, bf16[160,1152]{1,0:T(8,128)(2,1)S(1)}, u32[]{:S(2)}, u32[]{:S(2)}) collective-permute-start(bf16[160,1152]{1,0:T(8,128)(2,1)S(1)} %bitcast.3), channel_id=1, source_target_pairs={{0,28},{1,29},{2,3},{3,2},{4,0},{5,1},{6,7},{7,6},{8,4},{9,5},{10,... | collective-permute-start | bytes 1105928 | tf_op jit(solution)/shard_map/ppermute | solution.py:272
  21.4 8.5 %collective-permute-start.6 = (bf16[160,1152]{1,0:T(8,128)(2,1)S(1)}, bf16[160,1152]{1,0:T(8,128)(2,1)S(1)}, u32[]{:S(2)}, u32[]{:S(2)}) collective-permute-start(bf16[160,1152]{1,0:T(8,128)(2,1)S(1)} %bitcast.4), channel_id=1, source_target_pairs={{0,1},{1,0},{2,30},{3,31},{4,5},{5,4},{6,2},{7,3},{8,9},{9,8},{10,... | collective-permute-start | bytes 1105928 | tf_op jit(solution)/shard_map/ppermute | solution.py:272

commit v6 on v5

v6 whole, which is shorter than its diff:
```python
import functools

import jax
import jax.numpy as jnp
from jax import lax
from jax.experimental import pallas as pl
from jax.experimental.pallas import tpu as pltpu
from jax.sharding import PartitionSpec as P

HALF = jnp.bfloat16
FULL = jnp.float32
VMEM_LIMIT = 40 * 1024 * 1024


def roles():
    return lax.rem(lax.axis_index("blk"), 2) == 0, lax.axis_index("node")


def by_role(on_first, on_second):
    first, node = roles()
    pl.when(first)(functools.partial(on_first, node))
    pl.when(jnp.logical_not(first))(functools.partial(on_second, node))


def drawn(params, rows, partners, paired=None):
    vectors = jnp.concatenate([partner[...] for partner in partners], axis=0)
    dots = lax.dot_general(
        rows[...], vectors, (((1,), (1,)), ((), ())), preferred_element_type=FULL
    )
    scale, bias = params[0:1, 0:1], params[1:2, 0:1]
    logits = scale * dots + bias
    if paired is None:
        weights = scale * jax.nn.sigmoid(logits)
    else:
        pairs = paired(logits.shape)
        weights = jnp.where(pairs, -scale, scale) * jax.nn.sigmoid(
            jnp.where(pairs, -logits, logits)
        )
    return jnp.dot(weights.astype(HALF), vectors, preferred_element_type=FULL)


def text_pairs(targets, node):
    def paired(shape):
        rows = shape[0]
        return lax.broadcasted_iota(jnp.int32, shape, 0) + node * rows == targets[...]

    return paired


def image_pairs(targets, node, nodes):
    def paired(shape):
        rows = shape[0]
        columns = lax.broadcasted_iota(jnp.int32, shape, 1)
        names = jnp.where(columns < nodes * rows, columns, -1 - nodes * rows)
        for k in range(nodes):
            here = jnp.logical_and(columns >= k * rows, columns < (k + 1) * rows)
            shift = (lax.rem(node + k, nodes) - k) * rows
            names = jnp.where(here, columns + shift, names)
        return names == targets[...]

    return paired


def unit_kernel(lead, image, text, raw, half, inv, sems):
    rows = half.shape[0]
    part = rows // 2 if rows % 32 == 0 else rows
    pieces = [pl.ds(at, part) for at in range(0, rows, part)]

    def copies(source):
        return [
            pltpu.make_async_copy(source.at[piece], raw.at[piece], sems.at[i])
            for i, piece in enumerate(pieces)
        ]

    def fetch(source, node):
        for copy in copies(source):
            copy.start()

    sources = (text, image) if lead else (image, text)
    by_role(*[functools.partial(fetch, source) for source in sources])
    for piece, copy in zip(pieces, copies(image)):
        copy.wait()
        values = raw[piece, :].astype(FULL)
        inverse = lax.rsqrt(jnp.sum(values * values, axis=1, keepdims=True) + 1e-06)
        half[piece, :] = (values * inverse).astype(HALF)
        inv[piece, :] = inverse


def first_kernel(far, params, row_targets, lead, mate_rest, *refs):
    got1, got2, back = refs[:far], refs[far : 2 * far], refs[2 * far]

    def on_first(node):
        back[0] = drawn(params, got2[0], [lead, *got1]).astype(HALF)

    def on_second(node):
        for k in range(far):
            pairs = text_pairs(row_targets, lax.rem(node + k + 1, far + 1))
            images = [lead, mate_rest, got1[0]]
            back[k] = drawn(params, got2[k], images, pairs).astype(HALF)

    by_role(on_first, on_second)


def second_kernel(far, params, row_targets, rest, mate_lead, *refs):
    got1, got2, relay1 = refs[:far], refs[far : 2 * far], refs[2 * far : 3 * far]
    back = refs[3 * far]

    def on_first(node):
        for k in range(far):
            pairs = text_pairs(row_targets, lax.rem(node + k + 1, far + 1))
            images = [rest, got2[0], relay1[0]]
            back[k] = drawn(params, got1[k], images, pairs).astype(HALF)

    def on_second(node):
        back[0] = drawn(params, got1[0], [rest, *got2, mate_lead, *relay1]).astype(HALF)

    by_role(on_first, on_second)


def third_kernel(far, params, row_targets, targets, lead, rest, mate_rest, *refs):
    got1, got2 = refs[:far], refs[far : 2 * far]
    relay1, relay2 = refs[2 * far : 3 * far], refs[3 * far : 4 * far]
    lead_dir, rest_dir = refs[4 * far :]
    nodes = far + 1

    def on_first(node):
        pairs = image_pairs(targets, node, nodes)
        rest_dir[...] = drawn(params, rest, [lead, *got1, mate_rest, *relay2], pairs)
        pairs = text_pairs(row_targets, node)
        lead_dir[...] = drawn(params, lead, [rest, got2[0], relay1[0]], pairs)

    def on_second(node):
        pairs = text_pairs(row_targets, node)
        rest_dir[...] = drawn(params, rest, [lead, mate_rest, got1[0]], pairs)
        pairs = image_pairs(targets, node, nodes)
        lead_dir[...] = drawn(params, lead, [rest, *got2], pairs)

    by_role(on_first, on_second)


def tangent_kernel(far, sums_on_first, raw, inverse, direction, *refs):
    parts = refs[:far]
    image_grads, text_grads, held, sems = refs[-4:]
    rows = raw.shape[0]
    part = rows // 5 if rows % 80 == 0 else rows
    pieces = [pl.ds(at, part) for at in range(0, rows, part)]

    def run(out, count, node):
        copies = []
        for i, piece in enumerate(pieces):
            gradient = direction[piece, :]
            for k in range(count):
                gradient += parts[k][piece, :].astype(FULL)
            inv = inverse[piece, :]
            unit = raw[piece, :].astype(FULL) * inv
            along = jnp.sum(unit * gradient, axis=1, keepdims=True)
            held[piece, :] = (gradient - unit * along) * inv
            copy = pltpu.make_async_copy(held.at[piece], out.at[piece], sems.at[i])
            copy.start()
            copies.append(copy)
        for copy in copies:
            copy.wait()

    if sums_on_first:
        by_role(
            functools.partial(run, text_grads, far), functools.partial(run, image_grads, 1)
        )
    else:
        by_role(
            functools.partial(run, image_grads, 1), functools.partial(run, text_grads, far)
        )


def call(kernel, name, operands, shapes, anywhere=0, scratch=()):
    operands = list(operands)
    held = pl.BlockSpec(memory_space=pltpu.VMEM)
    for i in range(anywhere):
        operands[i] = pltpu.with_memory_space_constraint(operands[i], pltpu.HBM)
    return pl.pallas_call(
        kernel,
        name=name,
        out_shape=[pltpu.VMEM(s, d) for s, d in shapes],
        in_specs=[pl.BlockSpec(memory_space=pltpu.HBM)] * anywhere
        + [held] * (len(operands) - anywhere),
        out_specs=[held] * len(shapes),
        scratch_shapes=scratch,
        compiler_params=pltpu.CompilerParams(vmem_limit_bytes=VMEM_LIMIT),
    )(*operands)


def tangent(far, sums_on_first, operands, grads, block):
    rows = block[0][0]
    anywhere = pl.BlockSpec(memory_space=pl.ANY)
    count = len(operands)
    return pl.pallas_call(
        functools.partial(tangent_kernel, far, sums_on_first),
        name="tangent",
        out_shape=[jax.ShapeDtypeStruct(*block)] * 2,
        in_specs=[pl.BlockSpec(memory_space=pltpu.VMEM)] * count + [anywhere] * len(grads),
        out_specs=[anywhere] * 2,
        scratch_shapes=[pltpu.VMEM(*block), pltpu.SemaphoreType.DMA((5,))],
        input_output_aliases={count + i: i for i in range(len(grads))},
        compiler_params=pltpu.CompilerParams(vmem_limit_bytes=VMEM_LIMIT),
    )(*operands, *grads)


def local(image_embeds, text_embeds, pair_text, similarity_scale, logit_bias):
    rows, width = image_embeds.shape
    cycle_count = lax.axis_size("blk")
    node_count = lax.axis_size("node")
    far = node_count - 1
    cycle_index = lax.axis_index("blk")
    node_index = lax.axis_index("node")

    def send(block, even, odd):
        route = []
        for g in range(cycle_count):
            ahead, across = odd if g % 2 else even
            for n in range(node_count):
                to = (g + ahead) % cycle_count * node_count + (n + across) % node_count
                route.append((g * node_count + n, to))
        return lax.ppermute(block, ("blk", "node"), route)

    def swap(block):
        return send(block, (1, 0), (-1, 0))

    stay = (0, 0)
    ahead, behind = (2, 0), (-2, 0)
    block_h = ((rows, width), HALF)
    block_f = ((rows, width), FULL)
    column = ((rows, 1), FULL)
    returns = ((far, rows, width), HALF)

    def unit(lead, operands):
        return call(
            functools.partial(unit_kernel, lead),
            "unit",
            operands,
            [block_h, block_h, column],
            anywhere=2,
            scratch=[pltpu.SemaphoreType.DMA((2,))],
        )

    lead_raw, lead, lead_inv = unit(True, [image_embeds, text_embeds])
    got1 = [send(lead, (0, -k), ahead if k == 1 else stay) for k in range(1, node_count)]
    image, text, _ = lax.optimization_barrier((image_embeds, text_embeds, lead_inv))
    rest_raw, rest, rest_inv = unit(False, [image, text])
    got2 = [send(rest, ahead if k == 1 else stay, (0, -k)) for k in range(1, node_count)]
    mate_rest = swap(rest)
    mate_lead = swap(lead)

    start = (cycle_index * node_count + node_index) * rows
    targets = lax.dynamic_slice_in_dim(pair_text, start, rows, 0)
    targets = targets - cycle_index * node_count * rows
    row_targets = jnp.pad(targets, (0, 2 * rows), constant_values=-1)[None, :]
    targets = targets[:, None]

    params = jnp.concatenate([similarity_scale, logit_bias])[:, None]
    params = jnp.broadcast_to(params, (2, 128))
    *got1, row_targets, params = lax.optimization_barrier((*got1, row_targets, params))
    relay1 = [swap(block) for block in got1]
    relay2 = [swap(block) for block in got2]
    (back,) = call(
        functools.partial(first_kernel, far),
        "first",
        [params, row_targets, lead, mate_rest, *got1, *got2],
        [returns],
    )
    one = [send(back[k], behind if k == 0 else stay, (0, k + 1)) for k in range(far)]
    (back,) = call(
        functools.partial(second_kernel, far),
        "second",
        [params, row_targets, rest, mate_lead, *got1, *got2, *relay1],
        [returns],
    )
    two = [send(back[k], (0, k + 1), behind if k == 0 else stay) for k in range(far)]
    lead_dir, rest_dir = call(
        functools.partial(third_kernel, far),
        "third",
        [params, row_targets, targets, lead, rest, mate_rest]
        + [*got1, *got2, *relay1, *relay2],
        [block_f, block_f],
    )
    grads = tangent(far, False, [rest_raw, rest_inv, rest_dir, *one], [], block_f)
    return tuple(tangent(far, True, [lead_raw, lead_inv, lead_dir, *two], grads, block_f))


def solution(mesh):
    return jax.shard_map(
        local,
        mesh=mesh,
        in_specs=(P(("blk", "node"), None), P(("blk", "node"), None), P(), P(), P()),
        out_specs=(P(("blk", "node"), None), P(("blk", "node"), None)),
        check_vma=False,
    )
```

time: 31.2 us -> 33.3 us (1.067)
  Pallas kernels: 7.74 us -> 10.9 us
  starting transfers between devices: 10.4 us -> 8.8 us
  local copies, waits for them, and re-layouts: 0.11 us -> 1.55 us
  waiting for transfers between devices: 9.96 us -> 8.83 us
    pallas_call x5, Pallas kernels: 5.52 us -> 7.73 us  [call(): pl.pallas_call(kernel, name=name, out_shape=[pltpu.VMEM(s, d) for s, d in...]
    ppermute x8, starting transfers between devices: 10.4 us -> 8.8 us  [send(): return lax.ppermute(block, ('blk', 'node'), route)]
    unnamed x0 -> x8, local copies, waits for them, and re-layouts: none -> 1.37 us
    ppermute x8, waiting for transfers between devices: 9.96 us -> 8.83 us  [send(): return lax.ppermute(block, ('blk', 'node'), route)]
    pallas_call x2, Pallas kernels: 2.22 us -> 3.21 us  [tangent(): pl.pallas_call(functools.partial(tangent_kernel, far, sums_on_first), nam...]
  transfers between devices with their start and end apart: 8 -> 8, of which waited for: 4 -> 2; matrix products, arithmetic and copies ran while one was open for 3% -> 3% of each run, Pallas kernels for 17% -> 26%
where the time goes in v6:
time: 33.3 us; the launch traced here: 33 us
  Pallas kernels  10.9 us (33%)
  waiting for transfers between devices  8.83 us (27%)
  starting transfers between devices  8.8 us (26%)
  between operations  2.03 us (6%)
  local copies, waits for them, and re-layouts  1.55 us (5%)
  other arithmetic  0.85 us (3%)
    ppermute x8, waiting for transfers between devices, send(): return lax.ppermute(block, ('blk', 'node'), route)  8.83 us
    ppermute x8, starting transfers between devices, send(): return lax.ppermute(block, ('blk', 'node'), route)  8.8 us
    pallas_call x5, Pallas kernels, call(): pl.pallas_call(kernel, name=name, out_shape=[pltpu.VMEM(s, d) for s, d in...  7.73 us
    pallas_call x2, Pallas kernels, tangent(): pl.pallas_call(functools.partial(tangent_kernel, far, sums_on_first), nam...  3.21 us
    unnamed x8, local copies, waits for them, and re-layouts  1.37 us
    sub x1, other arithmetic, local(): targets = targets - cycle_index * node_count * rows  0.78 us
  transfers between devices with their start and end apart: 8, of which 2 were waited for; matrix products, arithmetic and copies ran while one was open for 3% of the time, Pallas kernels for 26%

profile of v6, /device:TPU:0, one launch (start us, length us, event | category | flops | bytes accessed | tf_op | source)
XLA Modules:
  0.0 33.0 jit_solution(3780764466064499920)
XLA Ops:
  0.6 1.2 %unit.2 = (bf16[160,1152]{1,0:T(8,128)(2,1)S(1)}, bf16[160,1152]{1,0:T(8,128)(2,1)S(1)}, f32[160,1]{1,0:T(8,128)S(1)}) custom-call(bf16[160,1152]{1,0:T(8,128)(2,1)} %image.2, bf16[160,1152]{1,0:T(8,128)(2,1)} %text.2), custom_call_target="tpu_custom_call" | custom-call | tf_op jit(solution)/shard_map/unit/pallas_call | solution.py:179
  1.8 3.0 %collective-permute-start = (bf16[160,1152]{1,0:T(8,128)(2,1)S(1)}, bf16[160,1152]{1,0:T(8,128)(2,1)S(1)}, u32[]{:S(2)}, u32[]{:S(2)}) collective-permute-start(bf16[160,1152]{1,0:T(8,128)(2,1)S(1)} %get-tuple-element.19.lead), channel_id=1, source_target_pairs={{0,1},{1,0},{2,6},{3,7},{4,5},{5,4},{6,10},{7,11},{8,9},{9,8},{10,... | collective-permute-start | bytes 1105928 | tf_op jit(solution)/shard_map/ppermute | solution.py:222
  4.9 1.2 %unit.3 = (bf16[160,1152]{1,0:T(8,128)(2,1)S(1)}, bf16[160,1152]{1,0:T(8,128)(2,1)S(1)}, f32[160,1]{1,0:T(8,128)S(1)}) custom-call(bf16[160,1152]{1,0:T(8,128)(2,1)} %image.2, bf16[160,1152]{1,0:T(8,128)(2,1)} %text.2), custom_call_target="tpu_custom_call" | custom-call | tf_op jit(solution)/shard_map/unit/pallas_call | solution.py:179
  6.1 0.0 copy-start
  6.1 0.7 %copy-done = bf16[160,1152]{1,0:T(8,128)(2,1)} copy-done((bf16[160,1152]{1,0:T(8,128)(2,1)}, bf16[160,1152]{1,0:T(8,128)(2,1)S(1)}, u32[]{:S(2)}) %copy-start) | copy-done | bytes 368664
  6.8 0.6 %copy-done.2 = f32[160,1]{1,0:T(8,128)} copy-done((f32[160,1]{1,0:T(8,128)}, f32[160,1]{1,0:T(8,128)S(1)}, u32[]{:S(2)}) %copy-start.2) | copy-done | bytes 664
  7.4 0.0 collective-permute-start.1
  7.4 1.5 %collective-permute-start.2 = (bf16[160,1152]{1,0:T(8,128)(2,1)S(1)}, bf16[160,1152]{1,0:T(8,128)(2,1)S(1)}, u32[]{:S(2)}, u32[]{:S(2)}) collective-permute-start(bf16[160,1152]{1,0:T(8,128)(2,1)S(1)} %get-tuple-element.24.rest), channel_id=1, source_target_pairs={{0,4},{1,5},{2,3},{3,2},{4,8},{5,9},{6,7},{7,6},{8,12},{9,13},{10,... | collective-permute-start | bytes 1105928 | tf_op jit(solution)/shard_map/ppermute | solution.py:222
  10.2 0.8 %dynamic-slice_subtract_fusion = s32[160]{0:T(256)S(1)} fusion(s32[5120]{0:T(1024)} %param.7, s32[]{:T(128)S(6)} %select_n.3, s32[]{:T(128)S(6)} %mul.12), kind=kLoop, calls=%fused_computation | loop fusion | flops 160 | bytes 1288 | tf_op jit(solution)/shard_map/sub | solution.py:254
  11.0 0.1 pad_maximum_fusion
  11.1 0.0 collective-permute-done.refs_0_
  11.1 0.1 broadcast_in_dim.13.params
  11.2 1.2 %collective-permute-start.3 = (bf16[160,1152]{1,0:T(8,128)(2,1)S(1)}, bf16[160,1152]{1,0:T(8,128)(2,1)S(1)}, u32[]{:S(2)}, u32[]{:S(2)}) collective-permute-start(bf16[160,1152]{1,0:T(8,128)(2,1)S(1)} %collective-permute-done.refs_0_), channel_id=1, source_target_pairs={{0,2},{1,3},{2,0},{3,1},{4,6},{5,7},{6,4},{7,5},{8,10},{9,11},{10,... | collective-permute-start | bytes 1105928 | tf_op jit(solution)/shard_map/ppermute | solution.py:222
  12.4 5.2 %collective-permute-done.2.refs_1_ = bf16[160,1152]{1,0:T(8,128)(2,1)S(1)} collective-permute-done((bf16[160,1152]{1,0:T(8,128)(2,1)S(1)}, bf16[160,1152]{1,0:T(8,128)(2,1)S(1)}, u32[]{:S(2)}, u32[]{:S(2)}) %collective-permute-start.2) | collective-permute-done | bytes 368672 | tf_op jit(solution)/shard_map/ppermute | solution.py:222
  17.6 1.6 %first.1 = bf16[1,160,1152]{2,1,0:T(8,128)(2,1)} custom-call(f32[2,128]{1,0:T(2,128)S(1)} %broadcast_in_dim.13.params, s32[1,480]{1,0:T(1,128)S(1)} %bitcast.5, bf16[160,1152]{1,0:T(8,128)(2,1)S(1)} %get-tuple-element.19.lead, bf16[160,1152]{1,0:T(8,128)(2,1)S(1)} %collective-permute-done.1.mate_rest, bf16[160,1152]{1,0:T(8,128)(2,1)S(1)} %collective-permute-done.refs_0_, ...), custom_call_target="tpu_custom_call" | custom-call | tf_op jit(solution)/shard_map/first/pallas_call | solution.py:179
  19.3 1.8 %collective-permute-start.7 = (bf16[160,1152]{1,0:T(8,128)(2,1)}, bf16[160,1152]{1,0:T(8,128)(2,1)}, u32[]{:S(2)}, u32[]{:S(2)}) collective-permute-start(bf16[160,1152]{1,0:T(8,128)(2,1)} %bitcast.3), channel_id=1, source_target_pairs={{0,28},{1,29},{2,3},{3,2},{4,0},{5,1},{6,7},{7,6},{8,4},{9,5},{10,... | collective-permute-start | bytes 1105928 | tf_op jit(solution)/shard_map/ppermute | solution.py:222
  21.1 0.9 %second.1 = bf16[1,160,1152]{2,1,0:T(8,128)(2,1)S(1)} custom-call(f32[2,128]{1,0:T(2,128)S(1)} %broadcast_in_dim.13.params, s32[1,480]{1,0:T(1,128)S(1)} %bitcast.6, bf16[160,1152]{1,0:T(8,128)(2,1)S(1)} %get-tuple-element.24.rest, bf16[160,1152]{1,0:T(8,128)(2,1)S(1)} %collective-permute-done.5.mate_lead, ...), custom_call_target="tpu_custom_call" | custom-call | tf_op jit(solution)/shard_map/second/pallas_call | solution.py:179
  22.0 1.2 %collective-permute-start.6 = (bf16[160,1152]{1,0:T(8,128)(2,1)S(1)}, bf16[160,1152]{1,0:T(8,128)(2,1)S(1)}, u32[]{:S(2)}, u32[]{:S(2)}) collective-permute-start(bf16[160,1152]{1,0:T(8,128)(2,1)S(1)} %bitcast.4), channel_id=1, source_target_pairs={{0,1},{1,0},{2,30},{3,31},{4,5},{5,4},{6,2},{7,3},{8,9},{9,8},{10,... | collective-permute-start | bytes 1105928 | tf_op jit(solution)/shard_map/ppermute | solution.py:222
  23.3 0.1 copy.9.targets
  23.4 0.0 copy-start.1
  23.4 2.8 %third.1 = (f32[160,1152]{1,0:T(8,128)S(1)}, f32[160,1152]{1,0:T(8,128)S(1)}) custom-call(f32[2,128]{1,0:T(2,128)S(1)} %broadcast_in_dim.13.params, s32[1,480]{1,0:T(1,128)S(1)} %bitcast.7, s32[160,1]{1,0:T(8,128)S(1)} %copy.9.targets, bf16[160,1152]{1,0:T(8,128)(2,1)S(1)} %get-tuple-element.19.lead, bf16[160,1152]{1,0:T(8,128)(2,1)S(1)} %get-tuple-element.24.rest, ...), custom_call_target="tpu_custom_call" | custom-call | tf_op jit(solution)/shard_map/third/pallas_call | solution.py:179
  26.2 3.5 %collective-permute-done.7.refs_0_ = bf16[160,1152]{1,0:T(8,128)(2,1)} collective-permute-done((bf16[160,1152]{1,0:T(8,128)(2,1)}, bf16[160,1152]{1,0:T(8,128)(2,1)}, u32[]{:S(2)}, u32[]{:S(2)}) %collective-permute-start.7) | collective-permute-done | bytes 368672 | tf_op jit(solution)/shard_map/ppermute | solution.py:222
  29.8 2.1 %tangent.2 = (f32[160,1152]{1,0:T(8,128)}, f32[160,1152]{1,0:T(8,128)}) custom-call(bf16[160,1152]{1,0:T(8,128)(2,1)S(1)} %copy-done.1, f32[160,1]{1,0:T(8,128)S(1)} %copy-done.3, f32[160,1152]{1,0:T(8,128)S(1)} %get-tuple-element.29.direction, bf16[160,1152]{1,0:T(8,128)(2,1)} %collective-permute-done.7.refs_0_), custom_call_target="tpu_custom_call" | custom-call | tf_op jit(solution)/shard_map/tangent/pallas_call | solution.py:195
  31.9 1.1 %tangent.3 = (f32[160,1152]{1,0:T(8,128)}, f32[160,1152]{1,0:T(8,128)}) custom-call(bf16[160,1152]{1,0:T(8,128)(2,1)S(1)} %get-tuple-element.17.raw, f32[160,1]{1,0:T(8,128)S(1)} %get-tuple-element.18.inverse, f32[160,1152]{1,0:T(8,128)S(1)} %get-tuple-element.26.direction, ...), custom_call_target="tpu_custom_call", output_to_operand_aliasing={{0}: (4, {}), {1}: (5, {})} | custom-call | tf_op jit(solution)/shard_map/tangent/pallas_call | solution.py:195
  (12 shorter events, 0.0 us)
Async XLA Ops:
  1.8 9.3 %collective-permute-start = (bf16[160,1152]{1,0:T(8,128)(2,1)S(1)}, bf16[160,1152]{1,0:T(8,128)(2,1)S(1)}, u32[]{:S(2)}, u32[]{:S(2)}) collective-permute-start(bf16[160,1152]{1,0:T(8,128)(2,1)S(1)} %get-tuple-element.19.lead), channel_id=1, source_target_pairs={{0,1},{1,0},{2,6},{3,7},{4,5},{5,4},{6,10},{7,11},{8,9},{9,8},{10,... | collective-permute-start | bytes 1105928 | tf_op jit(solution)/shard_map/ppermute | solution.py:222
  6.1 0.7 %copy-start = (bf16[160,1152]{1,0:T(8,128)(2,1)}, bf16[160,1152]{1,0:T(8,128)(2,1)S(1)}, u32[]{:S(2)}) copy-start(bf16[160,1152]{1,0:T(8,128)(2,1)S(1)} %get-tuple-element.27.raw) | copy-start | bytes 1105924
  6.8 0.6 %copy-start.2 = (f32[160,1]{1,0:T(8,128)}, f32[160,1]{1,0:T(8,128)S(1)}, u32[]{:S(2)}) copy-start(f32[160,1]{1,0:T(8,128)S(1)} %get-tuple-element.28.inverse) | copy-start | bytes 1924
  7.4 10.2 %collective-permute-start.1 = (bf16[160,1152]{1,0:T(8,128)(2,1)S(1)}, bf16[160,1152]{1,0:T(8,128)(2,1)S(1)}, u32[]{:S(2)}, u32[]{:S(2)}) collective-permute-start(bf16[160,1152]{1,0:T(8,128)(2,1)S(1)} %get-tuple-element.24.rest), channel_id=1, source_target_pairs={{0,2},{1,3},{2,0},{3,1},{4,6},{5,7},{6,4},{7,5},{8,10},{9,11},{10,... | collective-permute-start | bytes 1105928 | tf_op jit(solution)/shard_map/ppermute | solution.py:222
  7.4 10.2 %collective-permute-start.2 = (bf16[160,1152]{1,0:T(8,128)(2,1)S(1)}, bf16[160,1152]{1,0:T(8,128)(2,1)S(1)}, u32[]{:S(2)}, u32[]{:S(2)}) collective-permute-start(bf16[160,1152]{1,0:T(8,128)(2,1)S(1)} %get-tuple-element.24.rest), channel_id=1, source_target_pairs={{0,4},{1,5},{2,3},{3,2},{4,8},{5,9},{6,7},{7,6},{8,12},{9,13},{10,... | collective-permute-start | bytes 1105928 | tf_op jit(solution)/shard_map/ppermute | solution.py:222
  8.9 12.2 %collective-permute-start.5 = (bf16[160,1152]{1,0:T(8,128)(2,1)S(1)}, bf16[160,1152]{1,0:T(8,128)(2,1)S(1)}, u32[]{:S(2)}, u32[]{:S(2)}) collective-permute-start(bf16[160,1152]{1,0:T(8,128)(2,1)S(1)} %get-tuple-element.19.lead), channel_id=1, source_target_pairs={{0,2},{1,3},{2,0},{3,1},{4,6},{5,7},{6,4},{7,5},{8,10},{9,11},{10,... | collective-permute-start | bytes 1105928 | tf_op jit(solution)/shard_map/ppermute | solution.py:222
  11.2 9.9 %collective-permute-start.3 = (bf16[160,1152]{1,0:T(8,128)(2,1)S(1)}, bf16[160,1152]{1,0:T(8,128)(2,1)S(1)}, u32[]{:S(2)}, u32[]{:S(2)}) collective-permute-start(bf16[160,1152]{1,0:T(8,128)(2,1)S(1)} %collective-permute-done.refs_0_), channel_id=1, source_target_pairs={{0,2},{1,3},{2,0},{3,1},{4,6},{5,7},{6,4},{7,5},{8,10},{9,11},{10,... | collective-permute-start | bytes 1105928 | tf_op jit(solution)/shard_map/ppermute | solution.py:222
  17.6 5.7 %collective-permute-start.4 = (bf16[160,1152]{1,0:T(8,128)(2,1)S(1)}, bf16[160,1152]{1,0:T(8,128)(2,1)}, u32[]{:S(2)}, u32[]{:S(2)}) collective-permute-start(bf16[160,1152]{1,0:T(8,128)(2,1)S(1)} %collective-permute-done.2.refs_1_), channel_id=1, source_target_pairs={{0,2},{1,3},{2,0},{3,1},{4,6},{5,7},{6,4},{7,5},{8,10},{9,11},{10,... | collective-permute-start | bytes 1105928 | tf_op jit(solution)/shard_map/ppermute | solution.py:222
  19.3 10.5 %collective-permute-start.7 = (bf16[160,1152]{1,0:T(8,128)(2,1)}, bf16[160,1152]{1,0:T(8,128)(2,1)}, u32[]{:S(2)}, u32[]{:S(2)}) collective-permute-start(bf16[160,1152]{1,0:T(8,128)(2,1)} %bitcast.3), channel_id=1, source_target_pairs={{0,28},{1,29},{2,3},{3,2},{4,0},{5,1},{6,7},{7,6},{8,4},{9,5},{10,... | collective-permute-start | bytes 1105928 | tf_op jit(solution)/shard_map/ppermute | solution.py:222
  22.0 9.9 %collective-permute-start.6 = (bf16[160,1152]{1,0:T(8,128)(2,1)S(1)}, bf16[160,1152]{1,0:T(8,128)(2,1)S(1)}, u32[]{:S(2)}, u32[]{:S(2)}) collective-permute-start(bf16[160,1152]{1,0:T(8,128)(2,1)S(1)} %bitcast.4), channel_id=1, source_target_pairs={{0,1},{1,0},{2,30},{3,31},{4,5},{5,4},{6,2},{7,3},{8,9},{9,8},{10,... | collective-permute-start | bytes 1105928 | tf_op jit(solution)/shard_map/ppermute | solution.py:222
  23.4 6.4 %copy-start.1 = (bf16[160,1152]{1,0:T(8,128)(2,1)S(1)}, bf16[160,1152]{1,0:T(8,128)(2,1)}, u32[]{:S(2)}) copy-start(bf16[160,1152]{1,0:T(8,128)(2,1)} %copy-done) | copy-start | bytes 1105924
  23.4 6.4 %copy-start.3 = (f32[160,1]{1,0:T(8,128)S(1)}, f32[160,1]{1,0:T(8,128)}, u32[]{:S(2)}) copy-start(f32[160,1]{1,0:T(8,128)} %copy-done.2) | copy-start | bytes 1924

commit v7 on v6

--- a/solution.py
+++ b/solution.py
@@ -9,7 +9,7 @@
 
 HALF = jnp.bfloat16
 FULL = jnp.float32
-VMEM_LIMIT = 40 * 1024 * 1024
+VMEM_LIMIT = 8 * 1024 * 1024
 
 
 def roles():

time: 33.3 us -> 33.3 us (level)
  no operation moved by 1% of the time
where the time goes in v7:
time: 33.3 us; the launch traced here: 33 us
  Pallas kernels  10.9 us (33%)
  waiting for transfers between devices  8.83 us (27%)
  starting transfers between devices  8.8 us (26%)
  between operations  2.03 us (6%)
  local copies, waits for them, and re-layouts  1.55 us (5%)
  other arithmetic  0.85 us (3%)
    ppermute x8, waiting for transfers between devices, send(): return lax.ppermute(block, ('blk', 'node'), route)  8.83 us
    ppermute x8, starting transfers between devices, send(): return lax.ppermute(block, ('blk', 'node'), route)  8.8 us
    pallas_call x5, Pallas kernels, call(): pl.pallas_call(kernel, name=name, out_shape=[pltpu.VMEM(s, d) for s, d in...  7.73 us
    pallas_call x2, Pallas kernels, tangent(): pl.pallas_call(functools.partial(tangent_kernel, far, sums_on_first), nam...  3.21 us
    unnamed x8, local copies, waits for them, and re-layouts  1.37 us
    sub x1, other arithmetic, local(): targets = targets - cycle_index * node_count * rows  0.78 us
  transfers between devices with their start and end apart: 8, of which 2 were waited for; matrix products, arithmetic and copies ran while one was open for 3% of the time, Pallas kernels for 26%

profile of v7, /device:TPU:0, one launch (start us, length us, event | category | flops | bytes accessed | tf_op | source)
XLA Modules:
  0.0 33.0 jit_solution(8847781416097507274)
XLA Ops:
  0.6 1.2 %unit.2 = (bf16[160,1152]{1,0:T(8,128)(2,1)S(1)}, bf16[160,1152]{1,0:T(8,128)(2,1)S(1)}, f32[160,1]{1,0:T(8,128)S(1)}) custom-call(bf16[160,1152]{1,0:T(8,128)(2,1)} %image.2, bf16[160,1152]{1,0:T(8,128)(2,1)} %text.2), custom_call_target="tpu_custom_call" | custom-call | tf_op jit(solution)/shard_map/unit/pallas_call | solution.py:179
  1.8 3.0 %collective-permute-start = (bf16[160,1152]{1,0:T(8,128)(2,1)S(1)}, bf16[160,1152]{1,0:T(8,128)(2,1)S(1)}, u32[]{:S(2)}, u32[]{:S(2)}) collective-permute-start(bf16[160,1152]{1,0:T(8,128)(2,1)S(1)} %get-tuple-element.19.lead), channel_id=1, source_target_pairs={{0,1},{1,0},{2,6},{3,7},{4,5},{5,4},{6,10},{7,11},{8,9},{9,8},{10,... | collective-permute-start | bytes 1105928 | tf_op jit(solution)/shard_map/ppermute | solution.py:222
  4.9 1.2 %unit.3 = (bf16[160,1152]{1,0:T(8,128)(2,1)S(1)}, bf16[160,1152]{1,0:T(8,128)(2,1)S(1)}, f32[160,1]{1,0:T(8,128)S(1)}) custom-call(bf16[160,1152]{1,0:T(8,128)(2,1)} %image.2, bf16[160,1152]{1,0:T(8,128)(2,1)} %text.2), custom_call_target="tpu_custom_call" | custom-call | tf_op jit(solution)/shard_map/unit/pallas_call | solution.py:179
  6.1 0.0 copy-start
  6.1 0.7 %copy-done = bf16[160,1152]{1,0:T(8,128)(2,1)} copy-done((bf16[160,1152]{1,0:T(8,128)(2,1)}, bf16[160,1152]{1,0:T(8,128)(2,1)S(1)}, u32[]{:S(2)}) %copy-start) | copy-done | bytes 368664
  6.8 0.6 %copy-done.2 = f32[160,1]{1,0:T(8,128)} copy-done((f32[160,1]{1,0:T(8,128)}, f32[160,1]{1,0:T(8,128)S(1)}, u32[]{:S(2)}) %copy-start.2) | copy-done | bytes 664
  7.4 0.0 collective-permute-start.1
  7.4 1.5 %collective-permute-start.2 = (bf16[160,1152]{1,0:T(8,128)(2,1)S(1)}, bf16[160,1152]{1,0:T(8,128)(2,1)S(1)}, u32[]{:S(2)}, u32[]{:S(2)}) collective-permute-start(bf16[160,1152]{1,0:T(8,128)(2,1)S(1)} %get-tuple-element.24.rest), channel_id=1, source_target_pairs={{0,4},{1,5},{2,3},{3,2},{4,8},{5,9},{6,7},{7,6},{8,12},{9,13},{10,... | collective-permute-start | bytes 1105928 | tf_op jit(solution)/shard_map/ppermute | solution.py:222
  10.2 0.8 %dynamic-slice_subtract_fusion = s32[160]{0:T(256)S(1)} fusion(s32[5120]{0:T(1024)} %param.7, s32[]{:T(128)S(6)} %select_n.3, s32[]{:T(128)S(6)} %mul.12), kind=kLoop, calls=%fused_computation | loop fusion | flops 160 | bytes 1288 | tf_op jit(solution)/shard_map/sub | solution.py:254
  11.0 0.1 pad_maximum_fusion
  11.1 0.0 collective-permute-done.refs_0_
  11.1 0.1 broadcast_in_dim.13.params
  11.2 1.2 %collective-permute-start.3 = (bf16[160,1152]{1,0:T(8,128)(2,1)S(1)}, bf16[160,1152]{1,0:T(8,128)(2,1)S(1)}, u32[]{:S(2)}, u32[]{:S(2)}) collective-permute-start(bf16[160,1152]{1,0:T(8,128)(2,1)S(1)} %collective-permute-done.refs_0_), channel_id=1, source_target_pairs={{0,2},{1,3},{2,0},{3,1},{4,6},{5,7},{6,4},{7,5},{8,10},{9,11},{10,... | collective-permute-start | bytes 1105928 | tf_op jit(solution)/shard_map/ppermute | solution.py:222
  12.4 5.2 %collective-permute-done.2.refs_1_ = bf16[160,1152]{1,0:T(8,128)(2,1)S(1)} collective-permute-done((bf16[160,1152]{1,0:T(8,128)(2,1)S(1)}, bf16[160,1152]{1,0:T(8,128)(2,1)S(1)}, u32[]{:S(2)}, u32[]{:S(2)}) %collective-permute-start.2) | collective-permute-done | bytes 368672 | tf_op jit(solution)/shard_map/ppermute | solution.py:222
  17.6 1.6 %first.1 = bf16[1,160,1152]{2,1,0:T(8,128)(2,1)} custom-call(f32[2,128]{1,0:T(2,128)S(1)} %broadcast_in_dim.13.params, s32[1,480]{1,0:T(1,128)S(1)} %bitcast.5, bf16[160,1152]{1,0:T(8,128)(2,1)S(1)} %get-tuple-element.19.lead, bf16[160,1152]{1,0:T(8,128)(2,1)S(1)} %collective-permute-done.1.mate_rest, bf16[160,1152]{1,0:T(8,128)(2,1)S(1)} %collective-permute-done.refs_0_, ...), custom_call_target="tpu_custom_call" | custom-call | tf_op jit(solution)/shard_map/first/pallas_call | solution.py:179
  19.3 1.8 %collective-permute-start.7 = (bf16[160,1152]{1,0:T(8,128)(2,1)}, bf16[160,1152]{1,0:T(8,128)(2,1)}, u32[]{:S(2)}, u32[]{:S(2)}) collective-permute-start(bf16[160,1152]{1,0:T(8,128)(2,1)} %bitcast.3), channel_id=1, source_target_pairs={{0,28},{1,29},{2,3},{3,2},{4,0},{5,1},{6,7},{7,6},{8,4},{9,5},{10,... | collective-permute-start | bytes 1105928 | tf_op jit(solution)/shard_map/ppermute | solution.py:222
  21.1 0.9 %second.1 = bf16[1,160,1152]{2,1,0:T(8,128)(2,1)S(1)} custom-call(f32[2,128]{1,0:T(2,128)S(1)} %broadcast_in_dim.13.params, s32[1,480]{1,0:T(1,128)S(1)} %bitcast.6, bf16[160,1152]{1,0:T(8,128)(2,1)S(1)} %get-tuple-element.24.rest, bf16[160,1152]{1,0:T(8,128)(2,1)S(1)} %collective-permute-done.5.mate_lead, ...), custom_call_target="tpu_custom_call" | custom-call | tf_op jit(solution)/shard_map/second/pallas_call | solution.py:179
  22.0 1.2 %collective-permute-start.6 = (bf16[160,1152]{1,0:T(8,128)(2,1)S(1)}, bf16[160,1152]{1,0:T(8,128)(2,1)S(1)}, u32[]{:S(2)}, u32[]{:S(2)}) collective-permute-start(bf16[160,1152]{1,0:T(8,128)(2,1)S(1)} %bitcast.4), channel_id=1, source_target_pairs={{0,1},{1,0},{2,30},{3,31},{4,5},{5,4},{6,2},{7,3},{8,9},{9,8},{10,... | collective-permute-start | bytes 1105928 | tf_op jit(solution)/shard_map/ppermute | solution.py:222
  23.3 0.1 copy.9.targets
  23.4 0.0 copy-start.1
  23.4 2.8 %third.1 = (f32[160,1152]{1,0:T(8,128)S(1)}, f32[160,1152]{1,0:T(8,128)S(1)}) custom-call(f32[2,128]{1,0:T(2,128)S(1)} %broadcast_in_dim.13.params, s32[1,480]{1,0:T(1,128)S(1)} %bitcast.7, s32[160,1]{1,0:T(8,128)S(1)} %copy.9.targets, bf16[160,1152]{1,0:T(8,128)(2,1)S(1)} %get-tuple-element.19.lead, bf16[160,1152]{1,0:T(8,128)(2,1)S(1)} %get-tuple-element.24.rest, ...), custom_call_target="tpu_custom_call" | custom-call | tf_op jit(solution)/shard_map/third/pallas_call | solution.py:179
  26.2 3.5 %collective-permute-done.7.refs_0_ = bf16[160,1152]{1,0:T(8,128)(2,1)} collective-permute-done((bf16[160,1152]{1,0:T(8,128)(2,1)}, bf16[160,1152]{1,0:T(8,128)(2,1)}, u32[]{:S(2)}, u32[]{:S(2)}) %collective-permute-start.7) | collective-permute-done | bytes 368672 | tf_op jit(solution)/shard_map/ppermute | solution.py:222
  29.8 2.1 %tangent.2 = (f32[160,1152]{1,0:T(8,128)}, f32[160,1152]{1,0:T(8,128)}) custom-call(bf16[160,1152]{1,0:T(8,128)(2,1)S(1)} %copy-done.1, f32[160,1]{1,0:T(8,128)S(1)} %copy-done.3, f32[160,1152]{1,0:T(8,128)S(1)} %get-tuple-element.29.direction, bf16[160,1152]{1,0:T(8,128)(2,1)} %collective-permute-done.7.refs_0_), custom_call_target="tpu_custom_call" | custom-call | tf_op jit(solution)/shard_map/tangent/pallas_call | solution.py:195
  31.9 1.1 %tangent.3 = (f32[160,1152]{1,0:T(8,128)}, f32[160,1152]{1,0:T(8,128)}) custom-call(bf16[160,1152]{1,0:T(8,128)(2,1)S(1)} %get-tuple-element.17.raw, f32[160,1]{1,0:T(8,128)S(1)} %get-tuple-element.18.inverse, f32[160,1152]{1,0:T(8,128)S(1)} %get-tuple-element.26.direction, ...), custom_call_target="tpu_custom_call", output_to_operand_aliasing={{0}: (4, {}), {1}: (5, {})} | custom-call | tf_op jit(solution)/shard_map/tangent/pallas_call | solution.py:195
  (12 shorter events, 0.0 us)
Async XLA Ops:
  1.8 9.3 %collective-permute-start = (bf16[160,1152]{1,0:T(8,128)(2,1)S(1)}, bf16[160,1152]{1,0:T(8,128)(2,1)S(1)}, u32[]{:S(2)}, u32[]{:S(2)}) collective-permute-start(bf16[160,1152]{1,0:T(8,128)(2,1)S(1)} %get-tuple-element.19.lead), channel_id=1, source_target_pairs={{0,1},{1,0},{2,6},{3,7},{4,5},{5,4},{6,10},{7,11},{8,9},{9,8},{10,... | collective-permute-start | bytes 1105928 | tf_op jit(solution)/shard_map/ppermute | solution.py:222
  6.1 0.7 %copy-start = (bf16[160,1152]{1,0:T(8,128)(2,1)}, bf16[160,1152]{1,0:T(8,128)(2,1)S(1)}, u32[]{:S(2)}) copy-start(bf16[160,1152]{1,0:T(8,128)(2,1)S(1)} %get-tuple-element.27.raw) | copy-start | bytes 1105924
  6.8 0.6 %copy-start.2 = (f32[160,1]{1,0:T(8,128)}, f32[160,1]{1,0:T(8,128)S(1)}, u32[]{:S(2)}) copy-start(f32[160,1]{1,0:T(8,128)S(1)} %get-tuple-element.28.inverse) | copy-start | bytes 1924
  7.4 10.2 %collective-permute-start.1 = (bf16[160,1152]{1,0:T(8,128)(2,1)S(1)}, bf16[160,1152]{1,0:T(8,128)(2,1)S(1)}, u32[]{:S(2)}, u32[]{:S(2)}) collective-permute-start(bf16[160,1152]{1,0:T(8,128)(2,1)S(1)} %get-tuple-element.24.rest), channel_id=1, source_target_pairs={{0,2},{1,3},{2,0},{3,1},{4,6},{5,7},{6,4},{7,5},{8,10},{9,11},{10,... | collective-permute-start | bytes 1105928 | tf_op jit(solution)/shard_map/ppermute | solution.py:222
  7.4 10.2 %collective-permute-start.2 = (bf16[160,1152]{1,0:T(8,128)(2,1)S(1)}, bf16[160,1152]{1,0:T(8,128)(2,1)S(1)}, u32[]{:S(2)}, u32[]{:S(2)}) collective-permute-start(bf16[160,1152]{1,0:T(8,128)(2,1)S(1)} %get-tuple-element.24.rest), channel_id=1, source_target_pairs={{0,4},{1,5},{2,3},{3,2},{4,8},{5,9},{6,7},{7,6},{8,12},{9,13},{10,... | collective-permute-start | bytes 1105928 | tf_op jit(solution)/shard_map/ppermute | solution.py:222
  8.9 12.2 %collective-permute-start.5 = (bf16[160,1152]{1,0:T(8,128)(2,1)S(1)}, bf16[160,1152]{1,0:T(8,128)(2,1)S(1)}, u32[]{:S(2)}, u32[]{:S(2)}) collective-permute-start(bf16[160,1152]{1,0:T(8,128)(2,1)S(1)} %get-tuple-element.19.lead), channel_id=1, source_target_pairs={{0,2},{1,3},{2,0},{3,1},{4,6},{5,7},{6,4},{7,5},{8,10},{9,11},{10,... | collective-permute-start | bytes 1105928 | tf_op jit(solution)/shard_map/ppermute | solution.py:222
  11.2 9.9 %collective-permute-start.3 = (bf16[160,1152]{1,0:T(8,128)(2,1)S(1)}, bf16[160,1152]{1,0:T(8,128)(2,1)S(1)}, u32[]{:S(2)}, u32[]{:S(2)}) collective-permute-start(bf16[160,1152]{1,0:T(8,128)(2,1)S(1)} %collective-permute-done.refs_0_), channel_id=1, source_target_pairs={{0,2},{1,3},{2,0},{3,1},{4,6},{5,7},{6,4},{7,5},{8,10},{9,11},{10,... | collective-permute-start | bytes 1105928 | tf_op jit(solution)/shard_map/ppermute | solution.py:222
  17.6 5.7 %collective-permute-start.4 = (bf16[160,1152]{1,0:T(8,128)(2,1)S(1)}, bf16[160,1152]{1,0:T(8,128)(2,1)}, u32[]{:S(2)}, u32[]{:S(2)}) collective-permute-start(bf16[160,1152]{1,0:T(8,128)(2,1)S(1)} %collective-permute-done.2.refs_1_), channel_id=1, source_target_pairs={{0,2},{1,3},{2,0},{3,1},{4,6},{5,7},{6,4},{7,5},{8,10},{9,11},{10,... | collective-permute-start | bytes 1105928 | tf_op jit(solution)/shard_map/ppermute | solution.py:222
  19.3 10.5 %collective-permute-start.7 = (bf16[160,1152]{1,0:T(8,128)(2,1)}, bf16[160,1152]{1,0:T(8,128)(2,1)}, u32[]{:S(2)}, u32[]{:S(2)}) collective-permute-start(bf16[160,1152]{1,0:T(8,128)(2,1)} %bitcast.3), channel_id=1, source_target_pairs={{0,28},{1,29},{2,3},{3,2},{4,0},{5,1},{6,7},{7,6},{8,4},{9,5},{10,... | collective-permute-start | bytes 1105928 | tf_op jit(solution)/shard_map/ppermute | solution.py:222
  22.0 9.9 %collective-permute-start.6 = (bf16[160,1152]{1,0:T(8,128)(2,1)S(1)}, bf16[160,1152]{1,0:T(8,128)(2,1)S(1)}, u32[]{:S(2)}, u32[]{:S(2)}) collective-permute-start(bf16[160,1152]{1,0:T(8,128)(2,1)S(1)} %bitcast.4), channel_id=1, source_target_pairs={{0,1},{1,0},{2,30},{3,31},{4,5},{5,4},{6,2},{7,3},{8,9},{9,8},{10,... | collective-permute-start | bytes 1105928 | tf_op jit(solution)/shard_map/ppermute | solution.py:222
  23.4 6.4 %copy-start.1 = (bf16[160,1152]{1,0:T(8,128)(2,1)S(1)}, bf16[160,1152]{1,0:T(8,128)(2,1)}, u32[]{:S(2)}) copy-start(bf16[160,1152]{1,0:T(8,128)(2,1)} %copy-done) | copy-start | bytes 1105924
  23.4 6.4 %copy-start.3 = (f32[160,1]{1,0:T(8,128)S(1)}, f32[160,1]{1,0:T(8,128)}, u32[]{:S(2)}) copy-start(f32[160,1]{1,0:T(8,128)} %copy-done.2) | copy-start | bytes 1924

commit v8 on v7

--- a/solution.py
+++ b/solution.py
@@ -61,33 +61,34 @@
     return paired
 
 
-def unit_kernel(lead, image, text, raw, half, inv, sems):
-    rows = half.shape[0]
+def unit_kernel(image, text, lead_raw, rest_raw, lead, rest, lead_inv, rest_inv, sems):
+    rows = lead.shape[0]
     part = rows // 2 if rows % 32 == 0 else rows
     pieces = [pl.ds(at, part) for at in range(0, rows, part)]
 
-    def copies(source):
+    def copies(source, target, base):
         return [
-            pltpu.make_async_copy(source.at[piece], raw.at[piece], sems.at[i])
+            pltpu.make_async_copy(source.at[piece], target.at[piece], sems.at[base + i])
             for i, piece in enumerate(pieces)
         ]
 
-    def fetch(source, node):
-        for copy in copies(source):
+    def fetch(lead_source, rest_source, node):
+        for copy in copies(lead_source, lead_raw, 0) + copies(rest_source, rest_raw, 2):
             copy.start()
 
-    sources = (text, image) if lead else (image, text)
-    by_role(*[functools.partial(fetch, source) for source in sources])
-    for piece, copy in zip(pieces, copies(image)):
-        copy.wait()
-        values = raw[piece, :].astype(FULL)
-        inverse = lax.rsqrt(jnp.sum(values * values, axis=1, keepdims=True) + 1e-06)
-        half[piece, :] = (values * inverse).astype(HALF)
-        inv[piece, :] = inverse
+    by_role(functools.partial(fetch, text, image), functools.partial(fetch, image, text))
+    for base, raw, half, inv in ((0, lead_raw, lead, lead_inv), (2, rest_raw, rest, rest_inv)):
+        for piece, copy in zip(pieces, copies(image, raw, base)):
+            copy.wait()
+            values = raw[piece, :].astype(FULL)
+            inverse = lax.rsqrt(jnp.sum(values * values, axis=1, keepdims=True) + 1e-06)
+            half[piece, :] = (values * inverse).astype(HALF)
+            inv[piece, :] = inverse
 
 
 def first_kernel(far, params, row_targets, lead, mate_rest, *refs):
     got1, got2, back = refs[:far], refs[far : 2 * far], refs[2 * far]
+    refs[-1][...] = jnp.zeros(refs[-1].shape, FULL)
 
     def on_first(node):
         back[0] = drawn(params, got2[0], [lead, *got1]).astype(HALF)
@@ -104,6 +105,7 @@
 def second_kernel(far, params, row_targets, rest, mate_lead, *refs):
     got1, got2, relay1 = refs[:far], refs[far : 2 * far], refs[2 * far : 3 * far]
     back = refs[3 * far]
+    refs[-1][...] = jnp.zeros(refs[-1].shape, FULL)
 
     def on_first(node):
         for k in range(far):
@@ -231,20 +233,15 @@
     column = ((rows, 1), FULL)
     returns = ((far, rows, width), HALF)
 
-    def unit(lead, operands):
-        return call(
-            functools.partial(unit_kernel, lead),
-            "unit",
-            operands,
-            [block_h, block_h, column],
-            anywhere=2,
-            scratch=[pltpu.SemaphoreType.DMA((2,))],
-        )
-
-    lead_raw, lead, lead_inv = unit(True, [image_embeds, text_embeds])
+    lead_raw, rest_raw, lead, rest, lead_inv, rest_inv = call(
+        unit_kernel,
+        "unit",
+        [image_embeds, text_embeds],
+        [block_h, block_h, block_h, block_h, column, column],
+        anywhere=2,
+        scratch=[pltpu.SemaphoreType.DMA((4,))],
+    )
     got1 = [send(lead, (0, -k), ahead if k == 1 else stay) for k in range(1, node_count)]
-    image, text, _ = lax.optimization_barrier((image_embeds, text_embeds, lead_inv))
-    rest_raw, rest, rest_inv = unit(False, [image, text])
     got2 = [send(rest, ahead if k == 1 else stay, (0, -k)) for k in range(1, node_count)]
     mate_rest = swap(rest)
     mate_lead = swap(lead)
@@ -260,18 +257,18 @@
     *got1, row_targets, params = lax.optimization_barrier((*got1, row_targets, params))
     relay1 = [swap(block) for block in got1]
     relay2 = [swap(block) for block in got2]
-    (back,) = call(
+    back, _ = call(
         functools.partial(first_kernel, far),
         "first",
         [params, row_targets, lead, mate_rest, *got1, *got2],
-        [returns],
+        [returns, ((8, 128), FULL)],
     )
     one = [send(back[k], behind if k == 0 else stay, (0, k + 1)) for k in range(far)]
-    (back,) = call(
+    back, _ = call(
         functools.partial(second_kernel, far),
         "second",
         [params, row_targets, rest, mate_lead, *got1, *got2, *relay1],
-        [returns],
+        [returns, ((8, 128), FULL)],
     )
     two = [send(back[k], (0, k + 1), behind if k == 0 else stay) for k in range(far)]
     lead_dir, rest_dir = call(

time: 33.3 us -> 32.8 us (0.985)
  the two profiles are of different devices: /device:TPU:0 before, /device:TPU:30 now
where the time goes in v8:
time: 32.8 us; the launch traced here: 32.5 us
  waiting for transfers between devices  15.4 us (47%)
  Pallas kernels  10.8 us (33%)
  starting transfers between devices  3.32 us (10%)
  between operations  2 us (6%)
  other arithmetic  0.84 us (3%)
    ppermute x8, waiting for transfers between devices, send(): return lax.ppermute(block, ('blk', 'node'), route)  15.4 us
    pallas_call x4, Pallas kernels, call(): pl.pallas_call(kernel, name=name, out_shape=[pltpu.VMEM(s, d) for s, d in...  7.56 us
    ppermute x8, starting transfers between devices, send(): return lax.ppermute(block, ('blk', 'node'), route)  3.32 us
    pallas_call x2, Pallas kernels, tangent(): pl.pallas_call(functools.partial(tangent_kernel, far, sums_on_first), nam...  3.21 us
    sub x1, other arithmetic, local(): targets = targets - cycle_index * node_count * rows  0.77 us
  transfers between devices with their start and end apart: 8, of which 2 were waited for; matrix products, arithmetic and copies ran while one was open for 3% of the time, Pallas kernels for 25%

profile of v8, /device:TPU:30, one launch (start us, length us, event | category | flops | bytes accessed | tf_op | source)
XLA Modules:
  0.0 32.5 jit_solution(18234055371884130341)
XLA Ops:
  0.6 1.5 %unit.1 = (bf16[160,1152]{1,0:T(8,128)(2,1)S(1)}, bf16[160,1152]{1,0:T(8,128)(2,1)S(1)}, bf16[160,1152]{1,0:T(8,128)(2,1)S(1)}, bf16[160,1152]{1,0:T(8,128)(2,1)...) custom-call(bf16[160,1152]{1,0:T(8,128)(2,1)} %image.1, bf16[160,1152]{1,0:T(8,128)(2,1)} %text.1), custom_call_target="tpu_custom_call" | custom-call | tf_op jit(solution)/shard_map/unit/pallas_call | solution.py:181
  2.1 0.0 copy-start
  2.1 0.6 %collective-permute-start = (bf16[160,1152]{1,0:T(8,128)(2,1)S(1)}, bf16[160,1152]{1,0:T(8,128)(2,1)S(1)}, u32[]{:S(2)}, u32[]{:S(2)}) collective-permute-start(bf16[160,1152]{1,0:T(8,128)(2,1)S(1)} %get-tuple-element.19.lead), channel_id=1, source_target_pairs={{0,1},{1,0},{2,6},{3,7},{4,5},{5,4},{6,10},{7,11},{8,9},{9,8},{10,... | collective-permute-start | bytes 1105928 | tf_op jit(solution)/shard_map/ppermute | solution.py:224
  2.7 0.0 collective-permute-start.1
  2.7 0.7 %collective-permute-start.2 = (bf16[160,1152]{1,0:T(8,128)(2,1)S(1)}, bf16[160,1152]{1,0:T(8,128)(2,1)S(1)}, u32[]{:S(2)}, u32[]{:S(2)}) collective-permute-start(bf16[160,1152]{1,0:T(8,128)(2,1)S(1)} %get-tuple-element.22.rest), channel_id=1, source_target_pairs={{0,4},{1,5},{2,3},{3,2},{4,8},{5,9},{6,7},{7,6},{8,12},{9,13},{10,... | collective-permute-start | bytes 1105928 | tf_op jit(solution)/shard_map/ppermute | solution.py:224
  3.4 1.0 %collective-permute-start.5 = (bf16[160,1152]{1,0:T(8,128)(2,1)S(1)}, bf16[160,1152]{1,0:T(8,128)(2,1)S(1)}, u32[]{:S(2)}, u32[]{:S(2)}) collective-permute-start(bf16[160,1152]{1,0:T(8,128)(2,1)S(1)} %get-tuple-element.19.lead), channel_id=1, source_target_pairs={{0,2},{1,3},{2,0},{3,1},{4,6},{5,7},{6,4},{7,5},{8,10},{9,11},{10,... | collective-permute-start | bytes 1105928 | tf_op jit(solution)/shard_map/ppermute | solution.py:224
  5.7 0.8 %dynamic-slice_subtract_fusion = s32[160]{0:T(256)S(1)} fusion(s32[5120]{0:T(1024)} %param.7, s32[]{:T(128)S(6)} %select_n.3, s32[]{:T(128)S(6)} %mul.12), kind=kLoop, calls=%fused_computation | loop fusion | flops 160 | bytes 1288 | tf_op jit(solution)/shard_map/sub | solution.py:251
  6.5 0.1 pad_maximum_fusion
  6.6 7.0 %collective-permute-done.refs_0_ = bf16[160,1152]{1,0:T(8,128)(2,1)S(1)} collective-permute-done((bf16[160,1152]{1,0:T(8,128)(2,1)S(1)}, bf16[160,1152]{1,0:T(8,128)(2,1)S(1)}, u32[]{:S(2)}, u32[]{:S(2)}) %collective-permute-start) | collective-permute-done | bytes 368672 | tf_op jit(solution)/shard_map/ppermute | solution.py:224
  13.6 0.1 broadcast_in_dim.13.params
  13.7 0.0 collective-permute-start.3
  13.7 0.0 collective-permute-done.2.refs_1_
  13.7 0.5 %collective-permute-start.4 = (bf16[160,1152]{1,0:T(8,128)(2,1)S(1)}, bf16[160,1152]{1,0:T(8,128)(2,1)}, u32[]{:S(2)}, u32[]{:S(2)}) collective-permute-start(bf16[160,1152]{1,0:T(8,128)(2,1)S(1)} %collective-permute-done.2.refs_1_), channel_id=1, source_target_pairs={{0,2},{1,3},{2,0},{3,1},{4,6},{5,7},{6,4},{7,5},{8,10},{9,11},{10,... | collective-permute-start | bytes 1105928 | tf_op jit(solution)/shard_map/ppermute | solution.py:224
  14.2 0.0 collective-permute-done.1.mate_rest
  14.2 1.6 %first.1 = (bf16[1,160,1152]{2,1,0:T(8,128)(2,1)}, f32[8,128]{1,0:T(8,128)}) custom-call(f32[2,128]{1,0:T(2,128)S(1)} %broadcast_in_dim.13.params, s32[1,480]{1,0:T(1,128)S(1)} %bitcast.4, bf16[160,1152]{1,0:T(8,128)(2,1)S(1)} %get-tuple-element.19.lead, bf16[160,1152]{1,0:T(8,128)(2,1)S(1)} %collective-permute-done.1.mate_rest, ...), custom_call_target="tpu_custom_call" | custom-call | tf_op jit(solution)/shard_map/first/pallas_call | solution.py:181
  15.8 0.5 %collective-permute-start.7 = (bf16[160,1152]{1,0:T(8,128)(2,1)}, bf16[160,1152]{1,0:T(8,128)(2,1)}, u32[]{:S(2)}, u32[]{:S(2)}) collective-permute-start(bf16[160,1152]{1,0:T(8,128)(2,1)} %bitcast.3), channel_id=1, source_target_pairs={{0,28},{1,29},{2,3},{3,2},{4,0},{5,1},{6,7},{7,6},{8,4},{9,5},{10,... | collective-permute-start | bytes 1105928 | tf_op jit(solution)/shard_map/ppermute | solution.py:224
  16.3 0.0 collective-permute-done.5.mate_lead
  16.3 1.6 %second.1 = (bf16[1,160,1152]{2,1,0:T(8,128)(2,1)}, f32[8,128]{1,0:T(8,128)}) custom-call(f32[2,128]{1,0:T(2,128)S(1)} %broadcast_in_dim.13.params, s32[1,480]{1,0:T(1,128)S(1)} %bitcast.5, bf16[160,1152]{1,0:T(8,128)(2,1)S(1)} %get-tuple-element.22.rest, bf16[160,1152]{1,0:T(8,128)(2,1)S(1)} %collective-permute-done.5.mate_lead, ...), custom_call_target="tpu_custom_call" | custom-call | tf_op jit(solution)/shard_map/second/pallas_call | solution.py:181
  18.0 0.1 copy.9.targets
  18.1 0.0 copy-start.1
  18.1 2.8 %third.1 = (f32[160,1152]{1,0:T(8,128)S(1)}, f32[160,1152]{1,0:T(8,128)S(1)}) custom-call(f32[2,128]{1,0:T(2,128)S(1)} %broadcast_in_dim.13.params, s32[1,480]{1,0:T(1,128)S(1)} %bitcast.6, s32[160,1]{1,0:T(8,128)S(1)} %copy.9.targets, bf16[160,1152]{1,0:T(8,128)(2,1)S(1)} %get-tuple-element.19.lead, bf16[160,1152]{1,0:T(8,128)(2,1)S(1)} %get-tuple-element.22.rest, ...), custom_call_target="tpu_custom_call" | custom-call | tf_op jit(solution)/shard_map/third/pallas_call | solution.py:181
  20.9 8.3 %collective-permute-done.7.refs_0_ = bf16[160,1152]{1,0:T(8,128)(2,1)} collective-permute-done((bf16[160,1152]{1,0:T(8,128)(2,1)}, bf16[160,1152]{1,0:T(8,128)(2,1)}, u32[]{:S(2)}, u32[]{:S(2)}) %collective-permute-start.7) | collective-permute-done | bytes 368672 | tf_op jit(solution)/shard_map/ppermute | solution.py:224
  29.3 2.1 %tangent.2 = (f32[160,1152]{1,0:T(8,128)}, f32[160,1152]{1,0:T(8,128)}) custom-call(bf16[160,1152]{1,0:T(8,128)(2,1)S(1)} %get-tuple-element.26.raw, f32[160,1]{1,0:T(8,128)S(1)} %copy-done.1, f32[160,1152]{1,0:T(8,128)S(1)} %get-tuple-element.28.direction, bf16[160,1152]{1,0:T(8,128)(2,1)} %collective-permute-done.7.refs_0_), custom_call_target="tpu_custom_call" | custom-call | tf_op jit(solution)/shard_map/tangent/pallas_call | solution.py:197
  31.4 1.1 %tangent.3 = (f32[160,1152]{1,0:T(8,128)}, f32[160,1152]{1,0:T(8,128)}) custom-call(bf16[160,1152]{1,0:T(8,128)(2,1)S(1)} %get-tuple-element.17.raw, f32[160,1]{1,0:T(8,128)S(1)} %get-tuple-element.18.inverse, f32[160,1152]{1,0:T(8,128)S(1)} %get-tuple-element.24.direction, ...), custom_call_target="tpu_custom_call", output_to_operand_aliasing={{0}: (4, {}), {1}: (5, {})} | custom-call | tf_op jit(solution)/shard_map/tangent/pallas_call | solution.py:197
  (7 shorter events, 0.0 us)
Async XLA Ops:
  2.1 13.7 %copy-start = (f32[160,1]{1,0:T(8,128)}, f32[160,1]{1,0:T(8,128)S(1)}, u32[]{:S(2)}) copy-start(f32[160,1]{1,0:T(8,128)S(1)} %get-tuple-element.27.inverse) | copy-start | bytes 1924
  2.1 11.5 %collective-permute-start = (bf16[160,1152]{1,0:T(8,128)(2,1)S(1)}, bf16[160,1152]{1,0:T(8,128)(2,1)S(1)}, u32[]{:S(2)}, u32[]{:S(2)}) collective-permute-start(bf16[160,1152]{1,0:T(8,128)(2,1)S(1)} %get-tuple-element.19.lead), channel_id=1, source_target_pairs={{0,1},{1,0},{2,6},{3,7},{4,5},{5,4},{6,10},{7,11},{8,9},{9,8},{10,... | collective-permute-start | bytes 1105928 | tf_op jit(solution)/shard_map/ppermute | solution.py:224
  2.7 11.5 %collective-permute-start.1 = (bf16[160,1152]{1,0:T(8,128)(2,1)S(1)}, bf16[160,1152]{1,0:T(8,128)(2,1)S(1)}, u32[]{:S(2)}, u32[]{:S(2)}) collective-permute-start(bf16[160,1152]{1,0:T(8,128)(2,1)S(1)} %get-tuple-element.22.rest), channel_id=1, source_target_pairs={{0,2},{1,3},{2,0},{3,1},{4,6},{5,7},{6,4},{7,5},{8,10},{9,11},{10,... | collective-permute-start | bytes 1105928 | tf_op jit(solution)/shard_map/ppermute | solution.py:224
  2.7 11.0 %collective-permute-start.2 = (bf16[160,1152]{1,0:T(8,128)(2,1)S(1)}, bf16[160,1152]{1,0:T(8,128)(2,1)S(1)}, u32[]{:S(2)}, u32[]{:S(2)}) collective-permute-start(bf16[160,1152]{1,0:T(8,128)(2,1)S(1)} %get-tuple-element.22.rest), channel_id=1, source_target_pairs={{0,4},{1,5},{2,3},{3,2},{4,8},{5,9},{6,7},{7,6},{8,12},{9,13},{10,... | collective-permute-start | bytes 1105928 | tf_op jit(solution)/shard_map/ppermute | solution.py:224
  3.4 12.9 %collective-permute-start.5 = (bf16[160,1152]{1,0:T(8,128)(2,1)S(1)}, bf16[160,1152]{1,0:T(8,128)(2,1)S(1)}, u32[]{:S(2)}, u32[]{:S(2)}) collective-permute-start(bf16[160,1152]{1,0:T(8,128)(2,1)S(1)} %get-tuple-element.19.lead), channel_id=1, source_target_pairs={{0,2},{1,3},{2,0},{3,1},{4,6},{5,7},{6,4},{7,5},{8,10},{9,11},{10,... | collective-permute-start | bytes 1105928 | tf_op jit(solution)/shard_map/ppermute | solution.py:224
  13.7 2.7 %collective-permute-start.3 = (bf16[160,1152]{1,0:T(8,128)(2,1)S(1)}, bf16[160,1152]{1,0:T(8,128)(2,1)S(1)}, u32[]{:S(2)}, u32[]{:S(2)}) collective-permute-start(bf16[160,1152]{1,0:T(8,128)(2,1)S(1)} %collective-permute-done.refs_0_), channel_id=1, source_target_pairs={{0,2},{1,3},{2,0},{3,1},{4,6},{5,7},{6,4},{7,5},{8,10},{9,11},{10,... | collective-permute-start | bytes 1105928 | tf_op jit(solution)/shard_map/ppermute | solution.py:224
  13.7 4.4 %collective-permute-start.4 = (bf16[160,1152]{1,0:T(8,128)(2,1)S(1)}, bf16[160,1152]{1,0:T(8,128)(2,1)}, u32[]{:S(2)}, u32[]{:S(2)}) collective-permute-start(bf16[160,1152]{1,0:T(8,128)(2,1)S(1)} %collective-permute-done.2.refs_1_), channel_id=1, source_target_pairs={{0,2},{1,3},{2,0},{3,1},{4,6},{5,7},{6,4},{7,5},{8,10},{9,11},{10,... | collective-permute-start | bytes 1105928 | tf_op jit(solution)/shard_map/ppermute | solution.py:224
  15.8 13.5 %collective-permute-start.7 = (bf16[160,1152]{1,0:T(8,128)(2,1)}, bf16[160,1152]{1,0:T(8,128)(2,1)}, u32[]{:S(2)}, u32[]{:S(2)}) collective-permute-start(bf16[160,1152]{1,0:T(8,128)(2,1)} %bitcast.3), channel_id=1, source_target_pairs={{0,28},{1,29},{2,3},{3,2},{4,0},{5,1},{6,7},{7,6},{8,4},{9,5},{10,... | collective-permute-start | bytes 1105928 | tf_op jit(solution)/shard_map/ppermute | solution.py:224
  18.0 13.4 %collective-permute-start.6 = (bf16[160,1152]{1,0:T(8,128)(2,1)}, bf16[160,1152]{1,0:T(8,128)(2,1)S(1)}, u32[]{:S(2)}, u32[]{:S(2)}) collective-permute-start(bf16[160,1152]{1,0:T(8,128)(2,1)} %bitcast.2), channel_id=1, source_target_pairs={{0,1},{1,0},{2,30},{3,31},{4,5},{5,4},{6,2},{7,3},{8,9},{9,8},{10,... | collective-permute-start | bytes 1105928 | tf_op jit(solution)/shard_map/ppermute | solution.py:224
  18.1 11.2 %copy-start.1 = (f32[160,1]{1,0:T(8,128)S(1)}, f32[160,1]{1,0:T(8,128)}, u32[]{:S(2)}) copy-start(f32[160,1]{1,0:T(8,128)} %copy-done) | copy-start | bytes 1924

commit v9 on v8

--- a/solution.py
+++ b/solution.py
@@ -1,4 +1,5 @@
 import functools
+import math
 
 import jax
 import jax.numpy as jnp
@@ -86,9 +87,39 @@
             inv[piece, :] = inverse
 
 
+def prep_kernel(
+    names, scale, bias, after, params, row_targets, targets, held, sems
+):
+    copy = pltpu.make_async_copy(names, held, sems.at[0])
+    copy.start()
+    row = lax.broadcasted_iota(jnp.int32, params.shape, 0)
+    params[...] = jnp.where(row == 0, scale[...], bias[...])
+    copy.wait()
+
+    rows = targets.shape[0]
+    group, node = lax.axis_index("blk"), lax.axis_index("node")
+    nodes = lax.axis_size("node")
+    start = (group * nodes + node) * rows
+    step = math.gcd(rows, 128)
+    lines = -(-(128 - step + rows) // 128)
+    window = held[pl.ds(start // 128, lines), :]
+    window = jnp.concatenate([window[i : i + 1] for i in range(lines)], axis=1)
+    mine = window[:, :rows]
+    for at in range(step, 128, step):
+        mine = jnp.where(lax.rem(start, 128) == at, window[:, at : at + rows], mine)
+    mine = mine - group * nodes * rows
+    row_targets[...] = jnp.full(row_targets.shape, -1, jnp.int32)
+    row_targets[:, :rows] = mine
+    square = (rows, rows)
+    same = lax.broadcasted_iota(jnp.int32, square, 0) == lax.broadcasted_iota(
+        jnp.int32, square, 1
+    )
+    turned = jnp.sum(jnp.where(same, mine.astype(FULL), 0.0), axis=1, keepdims=True)
+    targets[...] = turned.astype(jnp.int32)
+
+
 def first_kernel(far, params, row_targets, lead, mate_rest, *refs):
     got1, got2, back = refs[:far], refs[far : 2 * far], refs[2 * far]
-    refs[-1][...] = jnp.zeros(refs[-1].shape, FULL)
 
     def on_first(node):
         back[0] = drawn(params, got2[0], [lead, *got1]).astype(HALF)
@@ -105,7 +136,6 @@
 def second_kernel(far, params, row_targets, rest, mate_lead, *refs):
     got1, got2, relay1 = refs[:far], refs[far : 2 * far], refs[2 * far : 3 * far]
     back = refs[3 * far]
-    refs[-1][...] = jnp.zeros(refs[-1].shape, FULL)
 
     def on_first(node):
         for k in range(far):
@@ -211,8 +241,6 @@
     cycle_count = lax.axis_size("blk")
     node_count = lax.axis_size("node")
     far = node_count - 1
-    cycle_index = lax.axis_index("blk")
-    node_index = lax.axis_index("node")
 
     def send(block, even, odd):
         route = []
@@ -246,29 +274,30 @@
     mate_rest = swap(rest)
     mate_lead = swap(lead)
 
-    start = (cycle_index * node_count + node_index) * rows
-    targets = lax.dynamic_slice_in_dim(pair_text, start, rows, 0)
-    targets = targets - cycle_index * node_count * rows
-    row_targets = jnp.pad(targets, (0, 2 * rows), constant_values=-1)[None, :]
-    targets = targets[:, None]
-
-    params = jnp.concatenate([similarity_scale, logit_bias])[:, None]
-    params = jnp.broadcast_to(params, (2, 128))
+    names = pair_text.reshape(-1, 128)
+    params, row_targets, targets = call(
+        prep_kernel,
+        "prep",
+        [names, similarity_scale[:, None], logit_bias[:, None], rest_inv],
+        [((8, 128), FULL), ((1, 3 * rows), jnp.int32), ((rows, 1), jnp.int32)],
+        anywhere=1,
+        scratch=[pltpu.VMEM(names.shape, jnp.int32), pltpu.SemaphoreType.DMA((1,))],
+    )
     *got1, row_targets, params = lax.optimization_barrier((*got1, row_targets, params))
     relay1 = [swap(block) for block in got1]
     relay2 = [swap(block) for block in got2]
-    back, _ = call(
+    (back,) = call(
         functools.partial(first_kernel, far),
         "first",
         [params, row_targets, lead, mate_rest, *got1, *got2],
-        [returns, ((8, 128), FULL)],
+        [returns],
     )
     one = [send(back[k], behind if k == 0 else stay, (0, k + 1)) for k in range(far)]
-    back, _ = call(
+    (back,) = call(
         functools.partial(second_kernel, far),
         "second",
         [params, row_targets, rest, mate_lead, *got1, *got2, *relay1],
-        [returns, ((8, 128), FULL)],
+        [returns],
     )
     two = [send(back[k], (0, k + 1), behind if k == 0 else stay) for k in range(far)]
     lead_dir, rest_dir = call(

time: 32.8 us -> 31.2 us (0.951)
  Pallas kernels: 10.8 us -> 8.41 us
  waiting for transfers between devices: 15.4 us -> 17.1 us
  other arithmetic: 0.84 us -> 0 us
    ppermute x8, waiting for transfers between devices: 15.4 us -> 17.1 us  [send(): return lax.ppermute(block, ('blk', 'node'), route)]
    pallas_call x4 -> x5, Pallas kernels: 7.56 us -> 6.18 us  [call(): pl.pallas_call(kernel, name=name, out_shape=[pltpu.VMEM(s, d) for s, d in...]
    pallas_call x2, Pallas kernels: 3.21 us -> 2.22 us  [tangent(): pl.pallas_call(functools.partial(tangent_kernel, far, sums_on_first), nam...]
    sub x1 -> x0, other arithmetic: 0.77 us -> none  [local(): targets = targets - cycle_index * node_count * rows]
  transfers between devices with their start and end apart: 8 -> 8, of which waited for: 2 -> 2; matrix products, arithmetic and copies ran while one was open for 3% -> 0% of each run, Pallas kernels for 25% -> 19%
where the time goes in v9:
time: 31.2 us; the launch traced here: 31 us
  waiting for transfers between devices  17.1 us (55%)
  Pallas kernels  8.41 us (27%)
  starting transfers between devices  3.43 us (11%)
  between operations  2.01 us (6%)
    ppermute x8, waiting for transfers between devices, send(): return lax.ppermute(block, ('blk', 'node'), route)  17.1 us
    pallas_call x5, Pallas kernels, call(): pl.pallas_call(kernel, name=name, out_shape=[pltpu.VMEM(s, d) for s, d in...  6.18 us
    ppermute x8, starting transfers between devices, send(): return lax.ppermute(block, ('blk', 'node'), route)  3.43 us
    pallas_call x2, Pallas kernels, tangent(): pl.pallas_call(functools.partial(tangent_kernel, far, sums_on_first), nam...  2.22 us
  transfers between devices with their start and end apart: 8, of which 2 were waited for; matrix products, arithmetic and copies ran while one was open for 0% of the time, Pallas kernels for 19%

profile of v9, /device:TPU:30, one launch (start us, length us, event | category | flops | bytes accessed | tf_op | source)
XLA Modules:
  0.0 31.0 jit_solution(231507375797922855)
XLA Ops:
  0.6 1.5 %unit.1 = (bf16[160,1152]{1,0:T(8,128)(2,1)S(1)}, bf16[160,1152]{1,0:T(8,128)(2,1)S(1)}, bf16[160,1152]{1,0:T(8,128)(2,1)S(1)}, bf16[160,1152]{1,0:T(8,128)(2,1)...) custom-call(bf16[160,1152]{1,0:T(8,128)(2,1)} %image.1, bf16[160,1152]{1,0:T(8,128)(2,1)} %text.1), custom_call_target="tpu_custom_call" | custom-call | tf_op jit(solution)/shard_map/unit/pallas_call | solution.py:211
  2.1 0.6 %collective-permute-start = (bf16[160,1152]{1,0:T(8,128)(2,1)S(1)}, bf16[160,1152]{1,0:T(8,128)(2,1)S(1)}, u32[]{:S(2)}, u32[]{:S(2)}) collective-permute-start(bf16[160,1152]{1,0:T(8,128)(2,1)S(1)} %get-tuple-element.20.lead), channel_id=1, source_target_pairs={{0,1},{1,0},{2,6},{3,7},{4,5},{5,4},{6,10},{7,11},{8,9},{9,8},{10,... | collective-permute-start | bytes 1105928 | tf_op jit(solution)/shard_map/ppermute | solution.py:252
  2.7 0.0 collective-permute-start.1
  2.7 0.7 %collective-permute-start.2 = (bf16[160,1152]{1,0:T(8,128)(2,1)S(1)}, bf16[160,1152]{1,0:T(8,128)(2,1)S(1)}, u32[]{:S(2)}, u32[]{:S(2)}) collective-permute-start(bf16[160,1152]{1,0:T(8,128)(2,1)S(1)} %get-tuple-element.27.rest), channel_id=1, source_target_pairs={{0,4},{1,5},{2,3},{3,2},{4,8},{5,9},{6,7},{7,6},{8,12},{9,13},{10,... | collective-permute-start | bytes 1105928 | tf_op jit(solution)/shard_map/ppermute | solution.py:252
  3.4 1.0 %collective-permute-start.5 = (bf16[160,1152]{1,0:T(8,128)(2,1)S(1)}, bf16[160,1152]{1,0:T(8,128)(2,1)S(1)}, u32[]{:S(2)}, u32[]{:S(2)}) collective-permute-start(bf16[160,1152]{1,0:T(8,128)(2,1)S(1)} %get-tuple-element.20.lead), channel_id=1, source_target_pairs={{0,2},{1,3},{2,0},{3,1},{4,6},{5,7},{6,4},{7,5},{8,10},{9,11},{10,... | collective-permute-start | bytes 1105928 | tf_op jit(solution)/shard_map/ppermute | solution.py:252
  5.7 1.1 %prep.1 = (f32[8,128]{1,0:T(8,128)S(1)}, s32[1,480]{1,0:T(1,128)S(1)}, s32[160,1]{1,0:T(8,128)S(1)}) custom-call(s32[40,128]{1,0:T(8,128)} %bitcast.9, f32[1,1]{1,0:T(1,128)} %bitcast.5.scale, f32[1,1]{1,0:T(1,128)} %bitcast.6.bias, f32[160,1]{1,0:T(8,128)S(1)} %get-tuple-element.21.after.inverse), custom_call_target="tpu_custom_call" | custom-call | tf_op jit(solution)/shard_map/prep/pallas_call | solution.py:211
  6.9 6.7 %collective-permute-done.refs_0_ = bf16[160,1152]{1,0:T(8,128)(2,1)S(1)} collective-permute-done((bf16[160,1152]{1,0:T(8,128)(2,1)S(1)}, bf16[160,1152]{1,0:T(8,128)(2,1)S(1)}, u32[]{:S(2)}, u32[]{:S(2)}) %collective-permute-start) | collective-permute-done | bytes 368672 | tf_op jit(solution)/shard_map/ppermute | solution.py:252
  13.6 0.0 collective-permute-start.3
  13.6 0.0 collective-permute-done.2.refs_1_
  13.6 0.5 %collective-permute-start.4 = (bf16[160,1152]{1,0:T(8,128)(2,1)S(1)}, bf16[160,1152]{1,0:T(8,128)(2,1)S(1)}, u32[]{:S(2)}, u32[]{:S(2)}) collective-permute-start(bf16[160,1152]{1,0:T(8,128)(2,1)S(1)} %collective-permute-done.2.refs_1_), channel_id=1, source_target_pairs={{0,2},{1,3},{2,0},{3,1},{4,6},{5,7},{6,4},{7,5},{8,10},{9,11},{10,... | collective-permute-start | bytes 1105928 | tf_op jit(solution)/shard_map/ppermute | solution.py:252
  14.1 0.0 collective-permute-done.1.mate_rest
  14.1 0.9 %first.1 = bf16[1,160,1152]{2,1,0:T(8,128)(2,1)S(1)} custom-call(f32[8,128]{1,0:T(8,128)S(1)} %get-tuple-element.24.params, s32[1,480]{1,0:T(1,128)S(1)} %get-tuple-element.25.row_targets, bf16[160,1152]{1,0:T(8,128)(2,1)S(1)} %get-tuple-element.20.lead, bf16[160,1152]{1,0:T(8,128)(2,1)S(1)} %collective-permute-done.1.mate_rest, ...), custom_call_target="tpu_custom_call" | custom-call | tf_op jit(solution)/shard_map/first/pallas_call | solution.py:211
  15.0 0.6 %collective-permute-start.7 = (bf16[160,1152]{1,0:T(8,128)(2,1)S(1)}, bf16[160,1152]{1,0:T(8,128)(2,1)S(1)}, u32[]{:S(2)}, u32[]{:S(2)}) collective-permute-start(bf16[160,1152]{1,0:T(8,128)(2,1)S(1)} %bitcast.8), channel_id=1, source_target_pairs={{0,28},{1,29},{2,3},{3,2},{4,0},{5,1},{6,7},{7,6},{8,4},{9,5},{10,... | collective-permute-start | bytes 1105928 | tf_op jit(solution)/shard_map/ppermute | solution.py:252
  15.5 0.0 collective-permute-done.5.mate_lead
  15.5 0.0 collective-permute-done.3.refs_2_
  15.6 0.9 %second.1 = bf16[1,160,1152]{2,1,0:T(8,128)(2,1)S(1)} custom-call(f32[8,128]{1,0:T(8,128)S(1)} %get-tuple-element.24.params, s32[1,480]{1,0:T(1,128)S(1)} %get-tuple-element.25.row_targets, bf16[160,1152]{1,0:T(8,128)(2,1)S(1)} %get-tuple-element.27.rest, bf16[160,1152]{1,0:T(8,128)(2,1)S(1)} %collective-permute-done.5.mate_lead, ...), custom_call_target="tpu_custom_call" | custom-call | tf_op jit(solution)/shard_map/second/pallas_call | solution.py:211
  16.4 0.1 collective-permute-start.6
  16.5 0.0 collective-permute-done.4.refs_3_
  16.5 1.8 %third.1 = (f32[160,1152]{1,0:T(8,128)S(1)}, f32[160,1152]{1,0:T(8,128)S(1)}) custom-call(f32[8,128]{1,0:T(8,128)S(1)} %get-tuple-element.24.params, s32[1,480]{1,0:T(1,128)S(1)} %get-tuple-element.25.row_targets, s32[160,1]{1,0:T(8,128)S(1)} %get-tuple-element.26.targets, bf16[160,1152]{1,0:T(8,128)(2,1)S(1)} %get-tuple-element.20.lead, ...), custom_call_target="tpu_custom_call" | custom-call | tf_op jit(solution)/shard_map/third/pallas_call | solution.py:211
  18.3 10.4 %collective-permute-done.7.refs_0_ = bf16[160,1152]{1,0:T(8,128)(2,1)S(1)} collective-permute-done((bf16[160,1152]{1,0:T(8,128)(2,1)S(1)}, bf16[160,1152]{1,0:T(8,128)(2,1)S(1)}, u32[]{:S(2)}, u32[]{:S(2)}) %collective-permute-start.7) | collective-permute-done | bytes 368672 | tf_op jit(solution)/shard_map/ppermute | solution.py:252
  28.7 1.1 %tangent.2 = (f32[160,1152]{1,0:T(8,128)}, f32[160,1152]{1,0:T(8,128)}) custom-call(bf16[160,1152]{1,0:T(8,128)(2,1)S(1)} %get-tuple-element.30.raw, f32[160,1]{1,0:T(8,128)S(1)} %get-tuple-element.21.after.inverse, f32[160,1152]{1,0:T(8,128)S(1)} %get-tuple-element.31.direction, bf16[160,1152]{1,0:T(8,128)(2,1)S(1)} %collective-permute-done.7.refs_0_), custom_call_target="tpu_custom_call" | custom-call | tf_op jit(solution)/shard_map/tangent/pallas_call | solution.py:227
  29.8 0.0 collective-permute-done.6.refs_0_
  29.8 1.1 %tangent.3 = (f32[160,1152]{1,0:T(8,128)}, f32[160,1152]{1,0:T(8,128)}) custom-call(bf16[160,1152]{1,0:T(8,128)(2,1)S(1)} %get-tuple-element.18.raw, f32[160,1]{1,0:T(8,128)S(1)} %get-tuple-element.19.inverse, f32[160,1152]{1,0:T(8,128)S(1)} %get-tuple-element.29.direction, ...), custom_call_target="tpu_custom_call", output_to_operand_aliasing={{0}: (4, {}), {1}: (5, {})} | custom-call | tf_op jit(solution)/shard_map/tangent/pallas_call | solution.py:227
Async XLA Ops:
  2.1 11.5 %collective-permute-start = (bf16[160,1152]{1,0:T(8,128)(2,1)S(1)}, bf16[160,1152]{1,0:T(8,128)(2,1)S(1)}, u32[]{:S(2)}, u32[]{:S(2)}) collective-permute-start(bf16[160,1152]{1,0:T(8,128)(2,1)S(1)} %get-tuple-element.20.lead), channel_id=1, source_target_pairs={{0,1},{1,0},{2,6},{3,7},{4,5},{5,4},{6,10},{7,11},{8,9},{9,8},{10,... | collective-permute-start | bytes 1105928 | tf_op jit(solution)/shard_map/ppermute | solution.py:252
  2.7 11.4 %collective-permute-start.1 = (bf16[160,1152]{1,0:T(8,128)(2,1)S(1)}, bf16[160,1152]{1,0:T(8,128)(2,1)S(1)}, u32[]{:S(2)}, u32[]{:S(2)}) collective-permute-start(bf16[160,1152]{1,0:T(8,128)(2,1)S(1)} %get-tuple-element.27.rest), channel_id=1, source_target_pairs={{0,2},{1,3},{2,0},{3,1},{4,6},{5,7},{6,4},{7,5},{8,10},{9,11},{10,... | collective-permute-start | bytes 1105928 | tf_op jit(solution)/shard_map/ppermute | solution.py:252
  2.7 10.9 %collective-permute-start.2 = (bf16[160,1152]{1,0:T(8,128)(2,1)S(1)}, bf16[160,1152]{1,0:T(8,128)(2,1)S(1)}, u32[]{:S(2)}, u32[]{:S(2)}) collective-permute-start(bf16[160,1152]{1,0:T(8,128)(2,1)S(1)} %get-tuple-element.27.rest), channel_id=1, source_target_pairs={{0,4},{1,5},{2,3},{3,2},{4,8},{5,9},{6,7},{7,6},{8,12},{9,13},{10,... | collective-permute-start | bytes 1105928 | tf_op jit(solution)/shard_map/ppermute | solution.py:252
  3.4 12.1 %collective-permute-start.5 = (bf16[160,1152]{1,0:T(8,128)(2,1)S(1)}, bf16[160,1152]{1,0:T(8,128)(2,1)S(1)}, u32[]{:S(2)}, u32[]{:S(2)}) collective-permute-start(bf16[160,1152]{1,0:T(8,128)(2,1)S(1)} %get-tuple-element.20.lead), channel_id=1, source_target_pairs={{0,2},{1,3},{2,0},{3,1},{4,6},{5,7},{6,4},{7,5},{8,10},{9,11},{10,... | collective-permute-start | bytes 1105928 | tf_op jit(solution)/shard_map/ppermute | solution.py:252
  13.6 2.0 %collective-permute-start.3 = (bf16[160,1152]{1,0:T(8,128)(2,1)S(1)}, bf16[160,1152]{1,0:T(8,128)(2,1)S(1)}, u32[]{:S(2)}, u32[]{:S(2)}) collective-permute-start(bf16[160,1152]{1,0:T(8,128)(2,1)S(1)} %collective-permute-done.refs_0_), channel_id=1, source_target_pairs={{0,2},{1,3},{2,0},{3,1},{4,6},{5,7},{6,4},{7,5},{8,10},{9,11},{10,... | collective-permute-start | bytes 1105928 | tf_op jit(solution)/shard_map/ppermute | solution.py:252
  13.6 2.9 %collective-permute-start.4 = (bf16[160,1152]{1,0:T(8,128)(2,1)S(1)}, bf16[160,1152]{1,0:T(8,128)(2,1)S(1)}, u32[]{:S(2)}, u32[]{:S(2)}) collective-permute-start(bf16[160,1152]{1,0:T(8,128)(2,1)S(1)} %collective-permute-done.2.refs_1_), channel_id=1, source_target_pairs={{0,2},{1,3},{2,0},{3,1},{4,6},{5,7},{6,4},{7,5},{8,10},{9,11},{10,... | collective-permute-start | bytes 1105928 | tf_op jit(solution)/shard_map/ppermute | solution.py:252
  15.0 13.7 %collective-permute-start.7 = (bf16[160,1152]{1,0:T(8,128)(2,1)S(1)}, bf16[160,1152]{1,0:T(8,128)(2,1)S(1)}, u32[]{:S(2)}, u32[]{:S(2)}) collective-permute-start(bf16[160,1152]{1,0:T(8,128)(2,1)S(1)} %bitcast.8), channel_id=1, source_target_pairs={{0,28},{1,29},{2,3},{3,2},{4,0},{5,1},{6,7},{7,6},{8,4},{9,5},{10,... | collective-permute-start | bytes 1105928 | tf_op jit(solution)/shard_map/ppermute | solution.py:252
  16.4 13.4 %collective-permute-start.6 = (bf16[160,1152]{1,0:T(8,128)(2,1)S(1)}, bf16[160,1152]{1,0:T(8,128)(2,1)S(1)}, u32[]{:S(2)}, u32[]{:S(2)}) collective-permute-start(bf16[160,1152]{1,0:T(8,128)(2,1)S(1)} %bitcast.7), channel_id=1, source_target_pairs={{0,1},{1,0},{2,30},{3,31},{4,5},{5,4},{6,2},{7,3},{8,9},{9,8},{10,... | collective-permute-start | bytes 1105928 | tf_op jit(solution)/shard_map/ppermute | solution.py:252

commit v10 on v9

--- a/solution.py
+++ b/solution.py
@@ -174,7 +174,7 @@
     parts = refs[:far]
     image_grads, text_grads, held, sems = refs[-4:]
     rows = raw.shape[0]
-    part = rows // 5 if rows % 80 == 0 else rows
+    part = rows // 2 if rows % 32 == 0 else rows
     pieces = [pl.ds(at, part) for at in range(0, rows, part)]
 
     def run(out, count, node):
@@ -230,7 +230,7 @@
         out_shape=[jax.ShapeDtypeStruct(*block)] * 2,
         in_specs=[pl.BlockSpec(memory_space=pltpu.VMEM)] * count + [anywhere] * len(grads),
         out_specs=[anywhere] * 2,
-        scratch_shapes=[pltpu.VMEM(*block), pltpu.SemaphoreType.DMA((5,))],
+        scratch_shapes=[pltpu.VMEM(*block), pltpu.SemaphoreType.DMA((2,))],
         input_output_aliases={count + i: i for i in range(len(grads))},
         compiler_params=pltpu.CompilerParams(vmem_limit_bytes=VMEM_LIMIT),
     )(*operands, *grads)
@@ -272,8 +272,6 @@
     got1 = [send(lead, (0, -k), ahead if k == 1 else stay) for k in range(1, node_count)]
     got2 = [send(rest, ahead if k == 1 else stay, (0, -k)) for k in range(1, node_count)]
     mate_rest = swap(rest)
-    mate_lead = swap(lead)
-
     names = pair_text.reshape(-1, 128)
     params, row_targets, targets = call(
         prep_kernel,
@@ -283,7 +281,10 @@
         anywhere=1,
         scratch=[pltpu.VMEM(names.shape, jnp.int32), pltpu.SemaphoreType.DMA((1,))],
     )
-    *got1, row_targets, params = lax.optimization_barrier((*got1, row_targets, params))
+    *got1, late, row_targets, params = lax.optimization_barrier(
+        (*got1, lead, row_targets, params)
+    )
+    mate_lead = swap(late)
     relay1 = [swap(block) for block in got1]
     relay2 = [swap(block) for block in got2]
     (back,) = call(

time: 31.2 us -> 30.6 us (0.981)
  the two profiles are of different devices: /device:TPU:30 before, /device:TPU:0 now
where the time goes in v10:
time: 30.6 us; the launch traced here: 30.1 us
  starting transfers between devices  10 us (33%)
  waiting for transfers between devices  9.75 us (32%)
  Pallas kernels  8.36 us (27%)
  between operations  1.98 us (6%)
    ppermute x8, starting transfers between devices, send(): return lax.ppermute(block, ('blk', 'node'), route)  10 us
    ppermute x8, waiting for transfers between devices, send(): return lax.ppermute(block, ('blk', 'node'), route)  9.75 us
    pallas_call x5, Pallas kernels, call(): pl.pallas_call(kernel, name=name, out_shape=[pltpu.VMEM(s, d) for s, d in...  6.15 us
    pallas_call x2, Pallas kernels, tangent(): pl.pallas_call(functools.partial(tangent_kernel, far, sums_on_first), nam...  2.21 us
  transfers between devices with their start and end apart: 8, of which 4 were waited for; matrix products, arithmetic and copies ran while one was open for 0% of the time, Pallas kernels for 19%

profile of v10, /device:TPU:0, one launch (start us, length us, event | category | flops | bytes accessed | tf_op | source)
XLA Modules:
  0.0 30.1 jit_solution(10434148703671356591)
XLA Ops:
  0.6 1.5 %unit.1 = (bf16[160,1152]{1,0:T(8,128)(2,1)S(1)}, bf16[160,1152]{1,0:T(8,128)(2,1)S(1)}, bf16[160,1152]{1,0:T(8,128)(2,1)S(1)}, bf16[160,1152]{1,0:T(8,128)(2,1)...) custom-call(bf16[160,1152]{1,0:T(8,128)(2,1)} %image.1, bf16[160,1152]{1,0:T(8,128)(2,1)} %text.1), custom_call_target="tpu_custom_call" | custom-call | tf_op jit(solution)/shard_map/unit/pallas_call | solution.py:211
  2.1 3.0 %collective-permute-start = (bf16[160,1152]{1,0:T(8,128)(2,1)S(1)}, bf16[160,1152]{1,0:T(8,128)(2,1)S(1)}, u32[]{:S(2)}, u32[]{:S(2)}) collective-permute-start(bf16[160,1152]{1,0:T(8,128)(2,1)S(1)} %get-tuple-element.31.lead), channel_id=1, source_target_pairs={{0,1},{1,0},{2,6},{3,7},{4,5},{5,4},{6,10},{7,11},{8,9},{9,8},{10,... | collective-permute-start | bytes 1105928 | tf_op jit(solution)/shard_map/ppermute | solution.py:252
  5.1 0.0 collective-permute-start.1
  5.1 1.5 %collective-permute-start.2 = (bf16[160,1152]{1,0:T(8,128)(2,1)S(1)}, bf16[160,1152]{1,0:T(8,128)(2,1)S(1)}, u32[]{:S(2)}, u32[]{:S(2)}) collective-permute-start(bf16[160,1152]{1,0:T(8,128)(2,1)S(1)} %get-tuple-element.28.rest), channel_id=1, source_target_pairs={{0,4},{1,5},{2,3},{3,2},{4,8},{5,9},{6,7},{7,6},{8,12},{9,13},{10,... | collective-permute-start | bytes 1105928 | tf_op jit(solution)/shard_map/ppermute | solution.py:252
  7.9 1.1 %prep.1 = (f32[8,128]{1,0:T(8,128)S(1)}, s32[1,480]{1,0:T(1,128)S(1)}, s32[160,1]{1,0:T(8,128)S(1)}) custom-call(s32[40,128]{1,0:T(8,128)} %bitcast.9, f32[1,1]{1,0:T(1,128)} %bitcast.5.scale, f32[1,1]{1,0:T(1,128)} %bitcast.6.bias, f32[160,1]{1,0:T(8,128)S(1)} %get-tuple-element.22.after.inverse), custom_call_target="tpu_custom_call" | custom-call | tf_op jit(solution)/shard_map/prep/pallas_call | solution.py:211
  9.1 5.0 %collective-permute-done.refs_0_ = bf16[160,1152]{1,0:T(8,128)(2,1)S(1)} collective-permute-done((bf16[160,1152]{1,0:T(8,128)(2,1)S(1)}, bf16[160,1152]{1,0:T(8,128)(2,1)S(1)}, u32[]{:S(2)}, u32[]{:S(2)}) %collective-permute-start) | collective-permute-done | bytes 368672 | tf_op jit(solution)/shard_map/ppermute | solution.py:252
  14.0 0.2 collective-permute-start.3
  14.2 0.3 %collective-permute-start.5 = (bf16[160,1152]{1,0:T(8,128)(2,1)S(1)}, bf16[160,1152]{1,0:T(8,128)(2,1)S(1)}, u32[]{:S(2)}, u32[]{:S(2)}) collective-permute-start(bf16[160,1152]{1,0:T(8,128)(2,1)S(1)} %get-tuple-element.31.lead), channel_id=1, source_target_pairs={{0,2},{1,3},{2,0},{3,1},{4,6},{5,7},{6,4},{7,5},{8,10},{9,11},{10,... | collective-permute-start | bytes 1105928 | tf_op jit(solution)/shard_map/ppermute | solution.py:252
  14.5 2.2 %collective-permute-done.2.refs_1_ = bf16[160,1152]{1,0:T(8,128)(2,1)S(1)} collective-permute-done((bf16[160,1152]{1,0:T(8,128)(2,1)S(1)}, bf16[160,1152]{1,0:T(8,128)(2,1)S(1)}, u32[]{:S(2)}, u32[]{:S(2)}) %collective-permute-start.2) | collective-permute-done | bytes 368672 | tf_op jit(solution)/shard_map/ppermute | solution.py:252
  16.7 0.0 collective-permute-start.4
  16.7 0.0 collective-permute-done.1.mate_rest
  16.7 0.9 %first.1 = bf16[1,160,1152]{2,1,0:T(8,128)(2,1)S(1)} custom-call(f32[8,128]{1,0:T(8,128)S(1)} %get-tuple-element.25.params, s32[1,480]{1,0:T(1,128)S(1)} %get-tuple-element.26.row_targets, bf16[160,1152]{1,0:T(8,128)(2,1)S(1)} %get-tuple-element.31.lead, bf16[160,1152]{1,0:T(8,128)(2,1)S(1)} %collective-permute-done.1.mate_rest, ...), custom_call_target="tpu_custom_call" | custom-call | tf_op jit(solution)/shard_map/first/pallas_call | solution.py:211
  17.6 2.7 %collective-permute-start.7 = (bf16[160,1152]{1,0:T(8,128)(2,1)S(1)}, bf16[160,1152]{1,0:T(8,128)(2,1)S(1)}, u32[]{:S(2)}, u32[]{:S(2)}) collective-permute-start(bf16[160,1152]{1,0:T(8,128)(2,1)S(1)} %bitcast.8), channel_id=1, source_target_pairs={{0,28},{1,29},{2,3},{3,2},{4,0},{5,1},{6,7},{7,6},{8,4},{9,5},{10,... | collective-permute-start | bytes 1105928 | tf_op jit(solution)/shard_map/ppermute | solution.py:252
  20.4 0.0 collective-permute-done.3.refs_2_
  20.4 0.0 collective-permute-done.5.mate_lead
  20.4 0.9 %second.1 = bf16[1,160,1152]{2,1,0:T(8,128)(2,1)S(1)} custom-call(f32[8,128]{1,0:T(8,128)S(1)} %get-tuple-element.25.params, s32[1,480]{1,0:T(1,128)S(1)} %get-tuple-element.26.row_targets, bf16[160,1152]{1,0:T(8,128)(2,1)S(1)} %get-tuple-element.28.rest, bf16[160,1152]{1,0:T(8,128)(2,1)S(1)} %collective-permute-done.5.mate_lead, ...), custom_call_target="tpu_custom_call" | custom-call | tf_op jit(solution)/shard_map/second/pallas_call | solution.py:211
  21.3 2.2 %collective-permute-start.6 = (bf16[160,1152]{1,0:T(8,128)(2,1)S(1)}, bf16[160,1152]{1,0:T(8,128)(2,1)S(1)}, u32[]{:S(2)}, u32[]{:S(2)}) collective-permute-start(bf16[160,1152]{1,0:T(8,128)(2,1)S(1)} %bitcast.7), channel_id=1, source_target_pairs={{0,1},{1,0},{2,30},{3,31},{4,5},{5,4},{6,2},{7,3},{8,9},{9,8},{10,... | collective-permute-start | bytes 1105928 | tf_op jit(solution)/shard_map/ppermute | solution.py:252
  23.5 0.0 collective-permute-done.4.refs_3_
  23.5 1.8 %third.1 = (f32[160,1152]{1,0:T(8,128)S(1)}, f32[160,1152]{1,0:T(8,128)S(1)}) custom-call(f32[8,128]{1,0:T(8,128)S(1)} %get-tuple-element.25.params, s32[1,480]{1,0:T(1,128)S(1)} %get-tuple-element.26.row_targets, s32[160,1]{1,0:T(8,128)S(1)} %get-tuple-element.27.targets, bf16[160,1152]{1,0:T(8,128)(2,1)S(1)} %get-tuple-element.31.lead, ...), custom_call_target="tpu_custom_call" | custom-call | tf_op jit(solution)/shard_map/third/pallas_call | solution.py:211
  25.3 1.8 %collective-permute-done.7.refs_0_ = bf16[160,1152]{1,0:T(8,128)(2,1)S(1)} collective-permute-done((bf16[160,1152]{1,0:T(8,128)(2,1)S(1)}, bf16[160,1152]{1,0:T(8,128)(2,1)S(1)}, u32[]{:S(2)}, u32[]{:S(2)}) %collective-permute-start.7) | collective-permute-done | bytes 368672 | tf_op jit(solution)/shard_map/ppermute | solution.py:252
  27.2 1.1 %tangent.2 = (f32[160,1152]{1,0:T(8,128)}, f32[160,1152]{1,0:T(8,128)}) custom-call(bf16[160,1152]{1,0:T(8,128)(2,1)S(1)} %get-tuple-element.32.raw, f32[160,1]{1,0:T(8,128)S(1)} %get-tuple-element.22.after.inverse, f32[160,1152]{1,0:T(8,128)S(1)} %get-tuple-element.33.direction, bf16[160,1152]{1,0:T(8,128)(2,1)S(1)} %collective-permute-done.7.refs_0_), custom_call_target="tpu_custom_call" | custom-call | tf_op jit(solution)/shard_map/tangent/pallas_call | solution.py:227
  28.3 0.7 %collective-permute-done.6.refs_0_ = bf16[160,1152]{1,0:T(8,128)(2,1)S(1)} collective-permute-done((bf16[160,1152]{1,0:T(8,128)(2,1)S(1)}, bf16[160,1152]{1,0:T(8,128)(2,1)S(1)}, u32[]{:S(2)}, u32[]{:S(2)}) %collective-permute-start.6) | collective-permute-done | bytes 368672 | tf_op jit(solution)/shard_map/ppermute | solution.py:252
  29.0 1.1 %tangent.3 = (f32[160,1152]{1,0:T(8,128)}, f32[160,1152]{1,0:T(8,128)}) custom-call(bf16[160,1152]{1,0:T(8,128)(2,1)S(1)} %get-tuple-element.19.raw, f32[160,1]{1,0:T(8,128)S(1)} %get-tuple-element.20.inverse, f32[160,1152]{1,0:T(8,128)S(1)} %get-tuple-element.30.direction, ...), custom_call_target="tpu_custom_call", output_to_operand_aliasing={{0}: (4, {}), {1}: (5, {})} | custom-call | tf_op jit(solution)/shard_map/tangent/pallas_call | solution.py:227
Async XLA Ops:
  2.1 11.9 %collective-permute-start = (bf16[160,1152]{1,0:T(8,128)(2,1)S(1)}, bf16[160,1152]{1,0:T(8,128)(2,1)S(1)}, u32[]{:S(2)}, u32[]{:S(2)}) collective-permute-start(bf16[160,1152]{1,0:T(8,128)(2,1)S(1)} %get-tuple-element.31.lead), channel_id=1, source_target_pairs={{0,1},{1,0},{2,6},{3,7},{4,5},{5,4},{6,10},{7,11},{8,9},{9,8},{10,... | collective-permute-start | bytes 1105928 | tf_op jit(solution)/shard_map/ppermute | solution.py:252
  5.1 11.6 %collective-permute-start.1 = (bf16[160,1152]{1,0:T(8,128)(2,1)S(1)}, bf16[160,1152]{1,0:T(8,128)(2,1)S(1)}, u32[]{:S(2)}, u32[]{:S(2)}) collective-permute-start(bf16[160,1152]{1,0:T(8,128)(2,1)S(1)} %get-tuple-element.28.rest), channel_id=1, source_target_pairs={{0,2},{1,3},{2,0},{3,1},{4,6},{5,7},{6,4},{7,5},{8,10},{9,11},{10,... | collective-permute-start | bytes 1105928 | tf_op jit(solution)/shard_map/ppermute | solution.py:252
  5.1 11.6 %collective-permute-start.2 = (bf16[160,1152]{1,0:T(8,128)(2,1)S(1)}, bf16[160,1152]{1,0:T(8,128)(2,1)S(1)}, u32[]{:S(2)}, u32[]{:S(2)}) collective-permute-start(bf16[160,1152]{1,0:T(8,128)(2,1)S(1)} %get-tuple-element.28.rest), channel_id=1, source_target_pairs={{0,4},{1,5},{2,3},{3,2},{4,8},{5,9},{6,7},{7,6},{8,12},{9,13},{10,... | collective-permute-start | bytes 1105928 | tf_op jit(solution)/shard_map/ppermute | solution.py:252
  14.0 6.3 %collective-permute-start.3 = (bf16[160,1152]{1,0:T(8,128)(2,1)S(1)}, bf16[160,1152]{1,0:T(8,128)(2,1)S(1)}, u32[]{:S(2)}, u32[]{:S(2)}) collective-permute-start(bf16[160,1152]{1,0:T(8,128)(2,1)S(1)} %collective-permute-done.refs_0_), channel_id=1, source_target_pairs={{0,2},{1,3},{2,0},{3,1},{4,6},{5,7},{6,4},{7,5},{8,10},{9,11},{10,... | collective-permute-start | bytes 1105928 | tf_op jit(solution)/shard_map/ppermute | solution.py:252
  14.2 6.2 %collective-permute-start.5 = (bf16[160,1152]{1,0:T(8,128)(2,1)S(1)}, bf16[160,1152]{1,0:T(8,128)(2,1)S(1)}, u32[]{:S(2)}, u32[]{:S(2)}) collective-permute-start(bf16[160,1152]{1,0:T(8,128)(2,1)S(1)} %get-tuple-element.31.lead), channel_id=1, source_target_pairs={{0,2},{1,3},{2,0},{3,1},{4,6},{5,7},{6,4},{7,5},{8,10},{9,11},{10,... | collective-permute-start | bytes 1105928 | tf_op jit(solution)/shard_map/ppermute | solution.py:252
  16.7 6.8 %collective-permute-start.4 = (bf16[160,1152]{1,0:T(8,128)(2,1)S(1)}, bf16[160,1152]{1,0:T(8,128)(2,1)S(1)}, u32[]{:S(2)}, u32[]{:S(2)}) collective-permute-start(bf16[160,1152]{1,0:T(8,128)(2,1)S(1)} %collective-permute-done.2.refs_1_), channel_id=1, source_target_pairs={{0,2},{1,3},{2,0},{3,1},{4,6},{5,7},{6,4},{7,5},{8,10},{9,11},{10,... | collective-permute-start | bytes 1105928 | tf_op jit(solution)/shard_map/ppermute | solution.py:252
  17.6 9.5 %collective-permute-start.7 = (bf16[160,1152]{1,0:T(8,128)(2,1)S(1)}, bf16[160,1152]{1,0:T(8,128)(2,1)S(1)}, u32[]{:S(2)}, u32[]{:S(2)}) collective-permute-start(bf16[160,1152]{1,0:T(8,128)(2,1)S(1)} %bitcast.8), channel_id=1, source_target_pairs={{0,28},{1,29},{2,3},{3,2},{4,0},{5,1},{6,7},{7,6},{8,4},{9,5},{10,... | collective-permute-start | bytes 1105928 | tf_op jit(solution)/shard_map/ppermute | solution.py:252
  21.3 7.7 %collective-permute-start.6 = (bf16[160,1152]{1,0:T(8,128)(2,1)S(1)}, bf16[160,1152]{1,0:T(8,128)(2,1)S(1)}, u32[]{:S(2)}, u32[]{:S(2)}) collective-permute-start(bf16[160,1152]{1,0:T(8,128)(2,1)S(1)} %bitcast.7), channel_id=1, source_target_pairs={{0,1},{1,0},{2,30},{3,31},{4,5},{5,4},{6,2},{7,3},{8,9},{9,8},{10,... | collective-permute-start | bytes 1105928 | tf_op jit(solution)/shard_map/ppermute | solution.py:252

commit v11 on v9

--- a/solution.py
+++ b/solution.py
@@ -43,7 +43,8 @@
 def text_pairs(targets, node):
     def paired(shape):
         rows = shape[0]
-        return lax.broadcasted_iota(jnp.int32, shape, 0) + node * rows == targets[...]
+        names = lax.broadcasted_iota(jnp.int32, shape, 0) + node * rows
+        return names == targets[:, : shape[1]]
 
     return paired
 
@@ -77,7 +78,7 @@
         for copy in copies(lead_source, lead_raw, 0) + copies(rest_source, rest_raw, 2):
             copy.start()
 
-    by_role(functools.partial(fetch, text, image), functools.partial(fetch, image, text))
+    by_role(functools.partial(fetch, image, text), functools.partial(fetch, text, image))
     for base, raw, half, inv in ((0, lead_raw, lead, lead_inv), (2, rest_raw, rest, rest_inv)):
         for piece, copy in zip(pieces, copies(image, raw, base)):
             copy.wait()
@@ -118,38 +119,50 @@
     targets[...] = turned.astype(jnp.int32)
 
 
-def first_kernel(far, params, row_targets, lead, mate_rest, *refs):
-    got1, got2, back = refs[:far], refs[far : 2 * far], refs[2 * far]
+def before_kernel(far, params, row_targets, rest, mate_lead, *refs):
+    got1, sums = refs[:far], refs[far]
 
     def on_first(node):
-        back[0] = drawn(params, got2[0], [lead, *got1]).astype(HALF)
+        sums[0] = drawn(params, got1[0], [rest])
 
     def on_second(node):
         for k in range(far):
             pairs = text_pairs(row_targets, lax.rem(node + k + 1, far + 1))
-            images = [lead, mate_rest, got1[0]]
-            back[k] = drawn(params, got2[k], images, pairs).astype(HALF)
+            sums[k] = drawn(params, got1[k], [rest, mate_lead], pairs)
 
     by_role(on_first, on_second)
 
 
-def second_kernel(far, params, row_targets, rest, mate_lead, *refs):
-    got1, got2, relay1 = refs[:far], refs[far : 2 * far], refs[2 * far : 3 * far]
+def first_kernel(far, params, sums, *refs):
+    got1, got2, back = refs[:far], refs[far : 2 * far], refs[2 * far]
+
+    def on_first(node):
+        back[0] = (sums[0] + drawn(params, got1[0], got2)).astype(HALF)
+
+    def on_second(node):
+        for k in range(far):
+            back[k] = (sums[k] + drawn(params, got1[k], [got2[0]])).astype(HALF)
+
+    by_role(on_first, on_second)
+
+
+def second_kernel(far, params, row_targets, lead, mate_rest, *refs):
+    got1, got2, relay2 = refs[:far], refs[far : 2 * far], refs[2 * far : 3 * far]
     back = refs[3 * far]
 
     def on_first(node):
         for k in range(far):
             pairs = text_pairs(row_targets, lax.rem(node + k + 1, far + 1))
-            images = [rest, got2[0], relay1[0]]
-            back[k] = drawn(params, got1[k], images, pairs).astype(HALF)
+            images = [lead, got1[0], relay2[0]]
+            back[k] = drawn(params, got2[k], images, pairs).astype(HALF)
 
     def on_second(node):
-        back[0] = drawn(params, got1[0], [rest, *got2, mate_lead, *relay1]).astype(HALF)
+        back[0] = drawn(params, got2[0], [lead, *got1, mate_rest, *relay2]).astype(HALF)
 
     by_role(on_first, on_second)
 
 
-def third_kernel(far, params, row_targets, targets, lead, rest, mate_rest, *refs):
+def third_kernel(far, params, row_targets, targets, lead, rest, mate_lead, *refs):
     got1, got2 = refs[:far], refs[far : 2 * far]
     relay1, relay2 = refs[2 * far : 3 * far], refs[3 * far : 4 * far]
     lead_dir, rest_dir = refs[4 * far :]
@@ -157,15 +170,15 @@
 
     def on_first(node):
         pairs = image_pairs(targets, node, nodes)
-        rest_dir[...] = drawn(params, rest, [lead, *got1, mate_rest, *relay2], pairs)
+        lead_dir[...] = drawn(params, lead, [rest, *got2, mate_lead, *relay1], pairs)
         pairs = text_pairs(row_targets, node)
-        lead_dir[...] = drawn(params, lead, [rest, got2[0], relay1[0]], pairs)
+        rest_dir[...] = drawn(params, rest, [lead, got1[0], relay2[0]], pairs)
 
     def on_second(node):
         pairs = text_pairs(row_targets, node)
-        rest_dir[...] = drawn(params, rest, [lead, mate_rest, got1[0]], pairs)
+        lead_dir[...] = drawn(params, lead, [rest, mate_lead, got2[0]], pairs)
         pairs = image_pairs(targets, node, nodes)
-        lead_dir[...] = drawn(params, lead, [rest, *got2], pairs)
+        rest_dir[...] = drawn(params, rest, [lead, *got1], pairs)
 
     by_role(on_first, on_second)
 
@@ -175,18 +188,18 @@
     image_grads, text_grads, held, sems = refs[-4:]
     rows = raw.shape[0]
     part = rows // 5 if rows % 80 == 0 else rows
-    pieces = [pl.ds(at, part) for at in range(0, rows, part)]
 
     def run(out, count, node):
+        gradient = direction[...]
+        for k in range(count):
+            gradient += parts[k][...].astype(FULL)
+        inv = inverse[...]
+        unit = raw[...].astype(FULL) * inv
+        along = jnp.sum(unit * gradient, axis=1, keepdims=True)
         copies = []
-        for i, piece in enumerate(pieces):
-            gradient = direction[piece, :]
-            for k in range(count):
-                gradient += parts[k][piece, :].astype(FULL)
-            inv = inverse[piece, :]
-            unit = raw[piece, :].astype(FULL) * inv
-            along = jnp.sum(unit * gradient, axis=1, keepdims=True)
-            held[piece, :] = (gradient - unit * along) * inv
+        for i, at in enumerate(range(0, rows, part)):
+            piece = slice(at, at + part)
+            held[piece, :] = (gradient[piece] - unit[piece] * along[piece]) * inv[piece]
             copy = pltpu.make_async_copy(held.at[piece], out.at[piece], sems.at[i])
             copy.start()
             copies.append(copy)
@@ -269,11 +282,8 @@
         anywhere=2,
         scratch=[pltpu.SemaphoreType.DMA((4,))],
     )
-    got1 = [send(lead, (0, -k), ahead if k == 1 else stay) for k in range(1, node_count)]
-    got2 = [send(rest, ahead if k == 1 else stay, (0, -k)) for k in range(1, node_count)]
-    mate_rest = swap(rest)
+    got1 = [send(lead, ahead if k == 1 else stay, (0, -k)) for k in range(1, node_count)]
     mate_lead = swap(lead)
-
     names = pair_text.reshape(-1, 128)
     params, row_targets, targets = call(
         prep_kernel,
@@ -283,32 +293,42 @@
         anywhere=1,
         scratch=[pltpu.VMEM(names.shape, jnp.int32), pltpu.SemaphoreType.DMA((1,))],
     )
-    *got1, row_targets, params = lax.optimization_barrier((*got1, row_targets, params))
+    later, params = lax.optimization_barrier((rest, params))
+    got2 = [send(later, (0, -k), ahead if k == 1 else stay) for k in range(1, node_count)]
+    mate_rest = swap(later)
+
+    (sums,) = call(
+        functools.partial(before_kernel, far),
+        "before",
+        [params, row_targets, rest, mate_lead, *got1],
+        [((far, rows, width), FULL)],
+    )
+    *got2, sums = lax.optimization_barrier((*got2, sums))
     relay1 = [swap(block) for block in got1]
     relay2 = [swap(block) for block in got2]
     (back,) = call(
         functools.partial(first_kernel, far),
         "first",
-        [params, row_targets, lead, mate_rest, *got1, *got2],
+        [params, sums, *got1, *got2],
         [returns],
     )
     one = [send(back[k], behind if k == 0 else stay, (0, k + 1)) for k in range(far)]
     (back,) = call(
         functools.partial(second_kernel, far),
         "second",
-        [params, row_targets, rest, mate_lead, *got1, *got2, *relay1],
+        [params, row_targets, lead, mate_rest, *got1, *got2, *relay2],
         [returns],
     )
     two = [send(back[k], (0, k + 1), behind if k == 0 else stay) for k in range(far)]
     lead_dir, rest_dir = call(
         functools.partial(third_kernel, far),
         "third",
-        [params, row_targets, targets, lead, rest, mate_rest]
+        [params, row_targets, targets, lead, rest, mate_lead]
         + [*got1, *got2, *relay1, *relay2],
         [block_f, block_f],
     )
-    grads = tangent(far, False, [rest_raw, rest_inv, rest_dir, *one], [], block_f)
-    return tuple(tangent(far, True, [lead_raw, lead_inv, lead_dir, *two], grads, block_f))
+    grads = tangent(far, False, [lead_raw, lead_inv, lead_dir, *one], [], block_f)
+    return tuple(tangent(far, True, [rest_raw, rest_inv, rest_dir, *two], grads, block_f))
 
 
 def solution(mesh):

time: 31.2 us -> 30.5 us (0.978)
  the two profiles are of different devices: /device:TPU:30 before, /device:TPU:0 now
where the time goes in v11:
time: 30.5 us; the launch traced here: 30.3 us
  starting transfers between devices  10.8 us (35%)
  Pallas kernels  8.86 us (29%)
  waiting for transfers between devices  8.65 us (28%)
  between operations  1.99 us (7%)
    ppermute x8, starting transfers between devices, send(): return lax.ppermute(block, ('blk', 'node'), route)  10.8 us
    ppermute x8, waiting for transfers between devices, send(): return lax.ppermute(block, ('blk', 'node'), route)  8.65 us
    pallas_call x6, Pallas kernels, call(): pl.pallas_call(kernel, name=name, out_shape=[pltpu.VMEM(s, d) for s, d in...  6.63 us
    pallas_call x2, Pallas kernels, tangent(): pl.pallas_call(functools.partial(tangent_kernel, far, sums_on_first), nam...  2.22 us
  transfers between devices with their start and end apart: 8, of which 4 were waited for; matrix products, arithmetic and copies ran while one was open for 0% of the time, Pallas kernels for 21%

profile of v11, /device:TPU:0, one launch (start us, length us, event | category | flops | bytes accessed | tf_op | source)
XLA Modules:
  0.0 30.3 jit_solution(11124871680164558563)
XLA Ops:
  0.6 1.5 %unit.1 = (bf16[160,1152]{1,0:T(8,128)(2,1)S(1)}, bf16[160,1152]{1,0:T(8,128)(2,1)S(1)}, bf16[160,1152]{1,0:T(8,128)(2,1)S(1)}, bf16[160,1152]{1,0:T(8,128)(2,1)...) custom-call(bf16[160,1152]{1,0:T(8,128)(2,1)} %image.1, bf16[160,1152]{1,0:T(8,128)(2,1)} %text.1), custom_call_target="tpu_custom_call" | custom-call | tf_op jit(solution)/shard_map/unit/pallas_call | solution.py:224
  2.1 3.0 %collective-permute-start.1 = (bf16[160,1152]{1,0:T(8,128)(2,1)S(1)}, bf16[160,1152]{1,0:T(8,128)(2,1)S(1)}, u32[]{:S(2)}, u32[]{:S(2)}) collective-permute-start(bf16[160,1152]{1,0:T(8,128)(2,1)S(1)} %get-tuple-element.26.lead), channel_id=1, source_target_pairs={{0,4},{1,5},{2,3},{3,2},{4,8},{5,9},{6,7},{7,6},{8,12},{9,13},{10,... | collective-permute-start | bytes 1105928 | tf_op jit(solution)/shard_map/ppermute | solution.py:265
  5.1 0.0 collective-permute-start
  6.4 1.1 %prep.1 = (f32[8,128]{1,0:T(8,128)S(1)}, s32[1,480]{1,0:T(1,128)S(1)}, s32[160,1]{1,0:T(8,128)S(1)}) custom-call(s32[40,128]{1,0:T(8,128)} %bitcast.9, f32[1,1]{1,0:T(1,128)} %bitcast.5.scale, f32[1,1]{1,0:T(1,128)} %bitcast.6.bias, f32[160,1]{1,0:T(8,128)S(1)} %get-tuple-element.20.after.inverse), custom_call_target="tpu_custom_call" | custom-call | tf_op jit(solution)/shard_map/prep/pallas_call | solution.py:224
  7.5 1.6 %collective-permute-start.2 = (bf16[160,1152]{1,0:T(8,128)(2,1)S(1)}, bf16[160,1152]{1,0:T(8,128)(2,1)S(1)}, u32[]{:S(2)}, u32[]{:S(2)}) collective-permute-start(bf16[160,1152]{1,0:T(8,128)(2,1)S(1)} %get-tuple-element.27.rest), channel_id=1, source_target_pairs={{0,1},{1,0},{2,6},{3,7},{4,5},{5,4},{6,10},{7,11},{8,9},{9,8},{10,... | collective-permute-start | bytes 1105928 | tf_op jit(solution)/shard_map/ppermute | solution.py:265
  9.1 0.3 collective-permute-start.5
  9.4 4.5 %collective-permute-done.1.refs_0_ = bf16[160,1152]{1,0:T(8,128)(2,1)S(1)} collective-permute-done((bf16[160,1152]{1,0:T(8,128)(2,1)S(1)}, bf16[160,1152]{1,0:T(8,128)(2,1)S(1)}, u32[]{:S(2)}, u32[]{:S(2)}) %collective-permute-start.1) | collective-permute-done | bytes 368672 | tf_op jit(solution)/shard_map/ppermute | solution.py:265
  13.8 0.0 collective-permute-done.mate_lead
  13.8 0.7 %before.1.sums = f32[1,160,1152]{2,1,0:T(8,128)S(1)} custom-call(f32[8,128]{1,0:T(8,128)S(1)} %get-tuple-element.23.params, s32[1,480]{1,0:T(1,128)S(1)} %get-tuple-element.24.row_targets, bf16[160,1152]{1,0:T(8,128)(2,1)S(1)} %get-tuple-element.27.rest, bf16[160,1152]{1,0:T(8,128)(2,1)S(1)} %collective-permute-done.mate_lead, ...), custom_call_target="tpu_custom_call" | custom-call | tf_op jit(solution)/shard_map/before/pallas_call | solution.py:224
  14.5 0.6 %collective-permute-done.2.refs_1_ = bf16[160,1152]{1,0:T(8,128)(2,1)S(1)} collective-permute-done((bf16[160,1152]{1,0:T(8,128)(2,1)S(1)}, bf16[160,1152]{1,0:T(8,128)(2,1)S(1)}, u32[]{:S(2)}, u32[]{:S(2)}) %collective-permute-start.2) | collective-permute-done | bytes 368672 | tf_op jit(solution)/shard_map/ppermute | solution.py:265
  15.1 2.3 %collective-permute-start.4 = (bf16[160,1152]{1,0:T(8,128)(2,1)S(1)}, bf16[160,1152]{1,0:T(8,128)(2,1)S(1)}, u32[]{:S(2)}, u32[]{:S(2)}) collective-permute-start(bf16[160,1152]{1,0:T(8,128)(2,1)S(1)} %collective-permute-done.2.refs_1_), channel_id=1, source_target_pairs={{0,2},{1,3},{2,0},{3,1},{4,6},{5,7},{6,4},{7,5},{8,10},{9,11},{10,... | collective-permute-start | bytes 1105928 | tf_op jit(solution)/shard_map/ppermute | solution.py:265
  17.4 0.0 collective-permute-start.3
  17.4 0.7 %first.1 = bf16[1,160,1152]{2,1,0:T(8,128)(2,1)S(1)} custom-call(f32[8,128]{1,0:T(8,128)S(1)} %get-tuple-element.23.params, f32[1,160,1152]{2,1,0:T(8,128)S(1)} %before.1.sums, bf16[160,1152]{1,0:T(8,128)(2,1)S(1)} %collective-permute-done.1.refs_0_, bf16[160,1152]{1,0:T(8,128)(2,1)S(1)} %collective-permute-done.2.refs_1_), custom_call_target="tpu_custom_call" | custom-call | tf_op jit(solution)/shard_map/first/pallas_call | solution.py:224
  18.1 2.4 %collective-permute-start.7 = (bf16[160,1152]{1,0:T(8,128)(2,1)S(1)}, bf16[160,1152]{1,0:T(8,128)(2,1)S(1)}, u32[]{:S(2)}, u32[]{:S(2)}) collective-permute-start(bf16[160,1152]{1,0:T(8,128)(2,1)S(1)} %bitcast.8), channel_id=1, source_target_pairs={{0,28},{1,29},{2,3},{3,2},{4,0},{5,1},{6,7},{7,6},{8,4},{9,5},{10,... | collective-permute-start | bytes 1105928 | tf_op jit(solution)/shard_map/ppermute | solution.py:265
  20.5 0.0 collective-permute-done.5.mate_rest
  20.5 0.0 collective-permute-done.4.refs_3_.refs_2_
  20.5 0.9 %second.1 = bf16[1,160,1152]{2,1,0:T(8,128)(2,1)S(1)} custom-call(f32[8,128]{1,0:T(8,128)S(1)} %get-tuple-element.23.params, s32[1,480]{1,0:T(1,128)S(1)} %get-tuple-element.24.row_targets, bf16[160,1152]{1,0:T(8,128)(2,1)S(1)} %get-tuple-element.26.lead, bf16[160,1152]{1,0:T(8,128)(2,1)S(1)} %collective-permute-done.5.mate_rest, ...), custom_call_target="tpu_custom_call" | custom-call | tf_op jit(solution)/shard_map/second/pallas_call | solution.py:224
  21.4 1.3 %collective-permute-start.6 = (bf16[160,1152]{1,0:T(8,128)(2,1)S(1)}, bf16[160,1152]{1,0:T(8,128)(2,1)S(1)}, u32[]{:S(2)}, u32[]{:S(2)}) collective-permute-start(bf16[160,1152]{1,0:T(8,128)(2,1)S(1)} %bitcast.7), channel_id=1, source_target_pairs={{0,1},{1,0},{2,30},{3,31},{4,5},{5,4},{6,2},{7,3},{8,9},{9,8},{10,... | collective-permute-start | bytes 1105928 | tf_op jit(solution)/shard_map/ppermute | solution.py:265
  22.6 0.0 collective-permute-done.3.refs_2_
  22.6 1.8 %third.1 = (f32[160,1152]{1,0:T(8,128)S(1)}, f32[160,1152]{1,0:T(8,128)S(1)}) custom-call(f32[8,128]{1,0:T(8,128)S(1)} %get-tuple-element.23.params, s32[1,480]{1,0:T(1,128)S(1)} %get-tuple-element.24.row_targets, s32[160,1]{1,0:T(8,128)S(1)} %get-tuple-element.25.targets, bf16[160,1152]{1,0:T(8,128)(2,1)S(1)} %get-tuple-element.26.lead, ...), custom_call_target="tpu_custom_call" | custom-call | tf_op jit(solution)/shard_map/third/pallas_call | solution.py:224
  24.5 3.3 %collective-permute-done.7.refs_0_ = bf16[160,1152]{1,0:T(8,128)(2,1)S(1)} collective-permute-done((bf16[160,1152]{1,0:T(8,128)(2,1)S(1)}, bf16[160,1152]{1,0:T(8,128)(2,1)S(1)}, u32[]{:S(2)}, u32[]{:S(2)}) %collective-permute-start.7) | collective-permute-done | bytes 368672 | tf_op jit(solution)/shard_map/ppermute | solution.py:265
  27.7 1.1 %tangent.2 = (f32[160,1152]{1,0:T(8,128)}, f32[160,1152]{1,0:T(8,128)}) custom-call(bf16[160,1152]{1,0:T(8,128)(2,1)S(1)} %get-tuple-element.30.raw, f32[160,1]{1,0:T(8,128)S(1)} %get-tuple-element.31.inverse, f32[160,1152]{1,0:T(8,128)S(1)} %get-tuple-element.32.direction, bf16[160,1152]{1,0:T(8,128)(2,1)S(1)} %collective-permute-done.7.refs_0_), custom_call_target="tpu_custom_call" | custom-call | tf_op jit(solution)/shard_map/tangent/pallas_call | solution.py:240
  28.9 0.3 collective-permute-done.6.refs_0_
  29.1 1.1 %tangent.3 = (f32[160,1152]{1,0:T(8,128)}, f32[160,1152]{1,0:T(8,128)}) custom-call(bf16[160,1152]{1,0:T(8,128)(2,1)S(1)} %get-tuple-element.19.raw, f32[160,1]{1,0:T(8,128)S(1)} %get-tuple-element.20.after.inverse, f32[160,1152]{1,0:T(8,128)S(1)} %get-tuple-element.29.direction, ...), custom_call_target="tpu_custom_call", output_to_operand_aliasing={{0}: (4, {}), {1}: (5, {})} | custom-call | tf_op jit(solution)/shard_map/tangent/pallas_call | solution.py:240
Async XLA Ops:
  2.1 11.7 %collective-permute-start.1 = (bf16[160,1152]{1,0:T(8,128)(2,1)S(1)}, bf16[160,1152]{1,0:T(8,128)(2,1)S(1)}, u32[]{:S(2)}, u32[]{:S(2)}) collective-permute-start(bf16[160,1152]{1,0:T(8,128)(2,1)S(1)} %get-tuple-element.26.lead), channel_id=1, source_target_pairs={{0,4},{1,5},{2,3},{3,2},{4,8},{5,9},{6,7},{7,6},{8,12},{9,13},{10,... | collective-permute-start | bytes 1105928 | tf_op jit(solution)/shard_map/ppermute | solution.py:265
  5.1 8.7 %collective-permute-start = (bf16[160,1152]{1,0:T(8,128)(2,1)S(1)}, bf16[160,1152]{1,0:T(8,128)(2,1)S(1)}, u32[]{:S(2)}, u32[]{:S(2)}) collective-permute-start(bf16[160,1152]{1,0:T(8,128)(2,1)S(1)} %get-tuple-element.26.lead), channel_id=1, source_target_pairs={{0,2},{1,3},{2,0},{3,1},{4,6},{5,7},{6,4},{7,5},{8,10},{9,11},{10,... | collective-permute-start | bytes 1105928 | tf_op jit(solution)/shard_map/ppermute | solution.py:265
  7.5 7.6 %collective-permute-start.2 = (bf16[160,1152]{1,0:T(8,128)(2,1)S(1)}, bf16[160,1152]{1,0:T(8,128)(2,1)S(1)}, u32[]{:S(2)}, u32[]{:S(2)}) collective-permute-start(bf16[160,1152]{1,0:T(8,128)(2,1)S(1)} %get-tuple-element.27.rest), channel_id=1, source_target_pairs={{0,1},{1,0},{2,6},{3,7},{4,5},{5,4},{6,10},{7,11},{8,9},{9,8},{10,... | collective-permute-start | bytes 1105928 | tf_op jit(solution)/shard_map/ppermute | solution.py:265
  9.1 11.4 %collective-permute-start.5 = (bf16[160,1152]{1,0:T(8,128)(2,1)S(1)}, bf16[160,1152]{1,0:T(8,128)(2,1)S(1)}, u32[]{:S(2)}, u32[]{:S(2)}) collective-permute-start(bf16[160,1152]{1,0:T(8,128)(2,1)S(1)} %get-tuple-element.27.rest), channel_id=1, source_target_pairs={{0,2},{1,3},{2,0},{3,1},{4,6},{5,7},{6,4},{7,5},{8,10},{9,11},{10,... | collective-permute-start | bytes 1105928 | tf_op jit(solution)/shard_map/ppermute | solution.py:265
  15.1 5.4 %collective-permute-start.4 = (bf16[160,1152]{1,0:T(8,128)(2,1)S(1)}, bf16[160,1152]{1,0:T(8,128)(2,1)S(1)}, u32[]{:S(2)}, u32[]{:S(2)}) collective-permute-start(bf16[160,1152]{1,0:T(8,128)(2,1)S(1)} %collective-permute-done.2.refs_1_), channel_id=1, source_target_pairs={{0,2},{1,3},{2,0},{3,1},{4,6},{5,7},{6,4},{7,5},{8,10},{9,11},{10,... | collective-permute-start | bytes 1105928 | tf_op jit(solution)/shard_map/ppermute | solution.py:265
  17.4 5.2 %collective-permute-start.3 = (bf16[160,1152]{1,0:T(8,128)(2,1)S(1)}, bf16[160,1152]{1,0:T(8,128)(2,1)S(1)}, u32[]{:S(2)}, u32[]{:S(2)}) collective-permute-start(bf16[160,1152]{1,0:T(8,128)(2,1)S(1)} %collective-permute-done.1.refs_0_), channel_id=1, source_target_pairs={{0,2},{1,3},{2,0},{3,1},{4,6},{5,7},{6,4},{7,5},{8,10},{9,11},{10,... | collective-permute-start | bytes 1105928 | tf_op jit(solution)/shard_map/ppermute | solution.py:265
  18.1 9.6 %collective-permute-start.7 = (bf16[160,1152]{1,0:T(8,128)(2,1)S(1)}, bf16[160,1152]{1,0:T(8,128)(2,1)S(1)}, u32[]{:S(2)}, u32[]{:S(2)}) collective-permute-start(bf16[160,1152]{1,0:T(8,128)(2,1)S(1)} %bitcast.8), channel_id=1, source_target_pairs={{0,28},{1,29},{2,3},{3,2},{4,0},{5,1},{6,7},{7,6},{8,4},{9,5},{10,... | collective-permute-start | bytes 1105928 | tf_op jit(solution)/shard_map/ppermute | solution.py:265
  21.4 7.8 %collective-permute-start.6 = (bf16[160,1152]{1,0:T(8,128)(2,1)S(1)}, bf16[160,1152]{1,0:T(8,128)(2,1)S(1)}, u32[]{:S(2)}, u32[]{:S(2)}) collective-permute-start(bf16[160,1152]{1,0:T(8,128)(2,1)S(1)} %bitcast.7), channel_id=1, source_target_pairs={{0,1},{1,0},{2,30},{3,31},{4,5},{5,4},{6,2},{7,3},{8,9},{9,8},{10,... | collective-permute-start | bytes 1105928 | tf_op jit(solution)/shard_map/ppermute | solution.py:265

commit v12 on v9

v12 whole, which is shorter than its diff:
```python
import functools
import math

import jax
import jax.numpy as jnp
from jax import lax
from jax.experimental import pallas as pl
from jax.experimental.pallas import tpu as pltpu
from jax.sharding import PartitionSpec as P

HALF = jnp.bfloat16
FULL = jnp.float32
VMEM_LIMIT = 8 * 1024 * 1024


def roles():
    return lax.rem(lax.axis_index("blk"), 2) == 0, lax.axis_index("node")


def by_role(on_first, on_second):
    first, node = roles()
    pl.when(first)(functools.partial(on_first, node))
    pl.when(jnp.logical_not(first))(functools.partial(on_second, node))


def drawn(params, rows, partners, paired=None):
    vectors = jnp.concatenate([partner[...] for partner in partners], axis=0)
    dots = lax.dot_general(
        rows[...], vectors, (((1,), (1,)), ((), ())), preferred_element_type=FULL
    )
    scale, bias = params[0:1, 0:1], params[1:2, 0:1]
    logits = scale * dots + bias
    if paired is None:
        weights = scale * jax.nn.sigmoid(logits)
    else:
        pairs = paired(logits.shape)
        weights = jnp.where(pairs, -scale, scale) * jax.nn.sigmoid(
            jnp.where(pairs, -logits, logits)
        )
    return jnp.dot(weights.astype(HALF), vectors, preferred_element_type=FULL)


def text_pairs(targets, node):
    def paired(shape):
        rows = shape[0]
        names = lax.broadcasted_iota(jnp.int32, shape, 0) + node * rows
        return names == targets[:, : shape[1]]

    return paired


def image_pairs(targets, node, nodes):
    def paired(shape):
        rows = shape[0]
        columns = lax.broadcasted_iota(jnp.int32, shape, 1)
        names = jnp.where(columns < nodes * rows, columns, -1 - nodes * rows)
        for k in range(nodes):
            here = jnp.logical_and(columns >= k * rows, columns < (k + 1) * rows)
            shift = (lax.rem(node + k, nodes) - k) * rows
            names = jnp.where(here, columns + shift, names)
        return names == targets[...]

    return paired


def inverse_of(values):
    return lax.rsqrt(jnp.sum(values * values, axis=1, keepdims=True) + 1e-06)


def half_rows(raw):
    values = raw[...].astype(FULL)
    return (values * inverse_of(values)).astype(HALF)


def unit_kernel(
    image, text, image_raw, text_raw, image_half, text_half, image_inv, text_inv, sems
):
    blocks = ((image, image_raw, image_half, image_inv), (text, text_raw, text_half, text_inv))
    copies = [
        pltpu.make_async_copy(source, raw, sems.at[i])
        for i, (source, raw, _, _) in enumerate(blocks)
    ]
    for copy in copies:
        copy.start()
    for copy, (_, raw, half, inv) in zip(copies, blocks):
        copy.wait()
        values = raw[...].astype(FULL)
        inverse = inverse_of(values)
        half[...] = (values * inverse).astype(HALF)
        inv[...] = inverse


def visit_kernel(raw, after, half):
    half[...] = half_rows(raw)


def prep_kernel(
    names, scale, bias, after, params, row_targets, targets, held, sems
):
    copy = pltpu.make_async_copy(names, held, sems.at[0])
    copy.start()
    row = lax.broadcasted_iota(jnp.int32, params.shape, 0)
    params[...] = jnp.where(row == 0, scale[...], bias[...])
    copy.wait()

    rows = targets.shape[0]
    group, node = lax.axis_index("blk"), lax.axis_index("node")
    nodes = lax.axis_size("node")
    start = (group * nodes + node) * rows
    step = math.gcd(rows, 128)
    lines = -(-(128 - step + rows) // 128)
    window = held[pl.ds(start // 128, lines), :]
    window = jnp.concatenate([window[i : i + 1] for i in range(lines)], axis=1)
    mine = window[:, :rows]
    for at in range(step, 128, step):
        mine = jnp.where(lax.rem(start, 128) == at, window[:, at : at + rows], mine)
    mine = mine - group * nodes * rows
    row_targets[...] = jnp.full(row_targets.shape, -1, jnp.int32)
    row_targets[:, :rows] = mine
    square = (rows, rows)
    same = lax.broadcasted_iota(jnp.int32, square, 0) == lax.broadcasted_iota(
        jnp.int32, square, 1
    )
    turned = jnp.sum(jnp.where(same, mine.astype(FULL), 0.0), axis=1, keepdims=True)
    targets[...] = turned.astype(jnp.int32)


def first_kernel(far, params, row_targets, image, text, mate_image, visit, *refs):
    far_raw, far_text, back = refs[:far], refs[far : 2 * far], refs[2 * far]
    for k in range(far):
        far_text[k][...] = half_rows(far_raw[k])

    def on_first(node):
        back[0] = drawn(params, visit, [text, *far_text]).astype(HALF)

    def on_second(node):
        for k in range(far):
            pairs = text_pairs(row_targets, lax.rem(node + k + 1, far + 1))
            images = [image, mate_image, visit]
            back[k] = drawn(params, far_text[k], images, pairs).astype(HALF)

    by_role(on_first, on_second)


def second_kernel(
    far, params, row_targets, image, text, mate_text, visit, mate_visit, *refs
):
    far_text, relay = refs[:far], refs[far : 2 * far]
    mate_far, back = refs[2 * far : 3 * far], refs[3 * far]

    def on_first(node):
        for k in range(far):
            mate_far[k][...] = half_rows(relay[k])
            pairs = text_pairs(row_targets, lax.rem(node + k + 1, far + 1))
            images = [image, visit, mate_visit]
            back[k] = drawn(params, far_text[k], images, pairs).astype(HALF)

    def on_second(node):
        for k in range(far):
            mate_far[k][...] = half_rows(relay[k])
        texts = [text, *far_text, mate_text, *mate_far]
        back[0] = drawn(params, visit, texts).astype(HALF)

    by_role(on_first, on_second)


def third_kernel(
    far, params, row_targets, targets, image, text, mate_image, mate_text, visit, mate_visit, *refs
):
    far_text, mate_far = refs[:far], refs[far : 2 * far]
    image_dir, text_dir = refs[2 * far :]
    nodes = far + 1

    def on_first(node):
        pairs = image_pairs(targets, node, nodes)
        texts = [text, *far_text, mate_text, *mate_far]
        image_dir[...] = drawn(params, image, texts, pairs)
        pairs = text_pairs(row_targets, node)
        text_dir[...] = drawn(params, text, [image, visit, mate_visit], pairs)

    def on_second(node):
        pairs = text_pairs(row_targets, node)
        text_dir[...] = drawn(params, text, [image, mate_image, visit], pairs)
        pairs = image_pairs(targets, node, nodes)
        image_dir[...] = drawn(params, image, [text, *far_text], pairs)

    by_role(on_first, on_second)


def tangent_kernel(far, image_on_first, *refs):
    image, text, parts = refs[0:3], refs[3:6], refs[6 : 6 + far]
    image_grads, text_grads, held, sems = refs[-4:]
    rows = held.shape[0]
    part = rows // 5 if rows % 80 == 0 else rows

    def run(own, out, count, node):
        raw, inverse, direction = own
        gradient = direction[...]
        for k in range(count):
            gradient += parts[k][...].astype(FULL)
        inv = inverse[...]
        unit = raw[...].astype(FULL) * inv
        along = jnp.sum(unit * gradient, axis=1, keepdims=True)
        copies = []
        for i, at in enumerate(range(0, rows, part)):
            piece = slice(at, at + part)
            held[piece, :] = (gradient[piece] - unit[piece] * along[piece]) * inv[piece]
            copy = pltpu.make_async_copy(held.at[piece], out.at[piece], sems.at[i])
            copy.start()
            copies.append(copy)
        for copy in copies:
            copy.wait()

    on_images = functools.partial(run, image, image_grads, 1)
    on_texts = functools.partial(run, text, text_grads, far)
    if image_on_first:
        by_role(on_images, on_texts)
    else:
        by_role(on_texts, on_images)


def call(kernel, name, operands, shapes, anywhere=0, scratch=()):
    operands = list(operands)
    held = pl.BlockSpec(memory_space=pltpu.VMEM)
    for i in range(anywhere):
        operands[i] = pltpu.with_memory_space_constraint(operands[i], pltpu.HBM)
    return pl.pallas_call(
        kernel,
        name=name,
        out_shape=[pltpu.VMEM(s, d) for s, d in shapes],
        in_specs=[pl.BlockSpec(memory_space=pltpu.HBM)] * anywhere
        + [held] * (len(operands) - anywhere),
        out_specs=[held] * len(shapes),
        scratch_shapes=scratch,
        compiler_params=pltpu.CompilerParams(vmem_limit_bytes=VMEM_LIMIT),
    )(*operands)


def tangent(far, image_on_first, operands, grads, block):
    anywhere = pl.BlockSpec(memory_space=pl.ANY)
    count = len(operands)
    return pl.pallas_call(
        functools.partial(tangent_kernel, far, image_on_first),
        name="tangent",
        out_shape=[jax.ShapeDtypeStruct(*block)] * 2,
        in_specs=[pl.BlockSpec(memory_space=pltpu.VMEM)] * count + [anywhere] * len(grads),
        out_specs=[anywhere] * 2,
        scratch_shapes=[pltpu.VMEM(*block), pltpu.SemaphoreType.DMA((5,))],
        input_output_aliases={count + i: i for i in range(len(grads))},
        compiler_params=pltpu.CompilerParams(vmem_limit_bytes=VMEM_LIMIT),
    )(*operands, *grads)


def local(image_embeds, text_embeds, pair_text, similarity_scale, logit_bias):
    rows, width = image_embeds.shape
    cycle_count = lax.axis_size("blk")
    node_count = lax.axis_size("node")
    far = node_count - 1

    def send(block, even, odd):
        route = []
        for g in range(cycle_count):
            ahead, across = odd if g % 2 else even
            for n in range(node_count):
                to = (g + ahead) % cycle_count * node_count + (n + across) % node_count
                route.append((g * node_count + n, to))
        return lax.ppermute(block, ("blk", "node"), route)

    def swap(block):
        return send(block, (1, 0), (-1, 0))

    stay = (0, 0)
    ahead, behind = (2, 0), (-2, 0)
    block_h = ((rows, width), HALF)
    block_f = ((rows, width), FULL)
    column = ((rows, 1), FULL)
    returns = ((far, rows, width), HALF)

    visit_raw = send(image_embeds, ahead, ahead)
    far_raw = [send(text_embeds, (0, -k), (0, -k)) for k in range(1, node_count)]

    image_raw, text_raw, image, text, image_inv, text_inv = call(
        unit_kernel,
        "unit",
        [image_embeds, text_embeds],
        [block_h, block_h, block_h, block_h, column, column],
        anywhere=2,
        scratch=[pltpu.SemaphoreType.DMA((2,))],
    )
    mate_image = swap(image)
    mate_text = swap(text)
    names = pair_text.reshape(-1, 128)
    params, row_targets, targets = call(
        prep_kernel,
        "prep",
        [names, similarity_scale[:, None], logit_bias[:, None], image_inv],
        [((8, 128), FULL), ((1, 3 * rows), jnp.int32), ((rows, 1), jnp.int32)],
        anywhere=1,
        scratch=[pltpu.VMEM(names.shape, jnp.int32), pltpu.SemaphoreType.DMA((1,))],
    )
    (visit,) = call(visit_kernel, "visit", [visit_raw, params], [block_h])
    mate_visit = swap(visit)
    *far_raw, visit = lax.optimization_barrier((*far_raw, visit))
    relay = [swap(block) for block in far_raw]
    *far_text, back = call(
        functools.partial(first_kernel, far),
        "first",
        [params, row_targets, image, text, mate_image, visit, *far_raw],
        [block_h] * far + [returns],
    )
    one = [send(back[k], behind if k == 0 else stay, (0, k + 1)) for k in range(far)]
    *mate_far, back = call(
        functools.partial(second_kernel, far),
        "second",
        [params, row_targets, image, text, mate_text, visit, mate_visit, *far_text, *relay],
        [block_h] * far + [returns],
    )
    two = [send(back[k], (0, k + 1), behind if k == 0 else stay) for k in range(far)]
    image_dir, text_dir = call(
        functools.partial(third_kernel, far),
        "third",
        [params, row_targets, targets, image, text, mate_image, mate_text, visit, mate_visit]
        + [*far_text, *mate_far],
        [block_f, block_f],
    )
    own = [image_raw, image_inv, image_dir, text_raw, text_inv, text_dir]
    grads = tangent(far, True, [*own, *one], [], block_f)
    return tuple(tangent(far, False, [*own, *two], grads, block_f))


def solution(mesh):
    return jax.shard_map(
        local,
        mesh=mesh,
        in_specs=(P(("blk", "node"), None), P(("blk", "node"), None), P(), P(), P()),
        out_specs=(P(("blk", "node"), None), P(("blk", "node"), None)),
        check_vma=False,
    )
```

time: 31.2 us -> 29.7 us (0.952)
  the two profiles are of different devices: /device:TPU:30 before, /device:TPU:0 now
where the time goes in v12:
time: 29.7 us; the launch traced here: 29.5 us
  waiting for transfers between devices  9.86 us (33%)
  starting transfers between devices  9.02 us (30%)
  Pallas kernels  8.55 us (29%)
  between operations  2.02 us (7%)
    ppermute x8, waiting for transfers between devices, send(): return lax.ppermute(block, ('blk', 'node'), route)  9.86 us
    ppermute x8, starting transfers between devices, send(): return lax.ppermute(block, ('blk', 'node'), route)  9.02 us
    pallas_call x6, Pallas kernels, call(): pl.pallas_call(kernel, name=name, out_shape=[pltpu.VMEM(s, d) for s, d in...  6.33 us
    pallas_call x2, Pallas kernels, tangent(): pl.pallas_call(functools.partial(tangent_kernel, far, image_on_first), na...  2.22 us
  transfers between devices with their start and end apart: 8, of which 2 were waited for; matrix products, arithmetic and copies ran while one was open for 0% of the time, Pallas kernels for 25%

profile of v12, /device:TPU:0, one launch (start us, length us, event | category | flops | bytes accessed | tf_op | source)
XLA Modules:
  0.0 29.5 jit_solution(2192342576792632722)
XLA Ops:
  0.6 3.0 %collective-permute-start.3 = (bf16[160,1152]{1,0:T(8,128)(2,1)}, bf16[160,1152]{1,0:T(8,128)(2,1)S(1)}, u32[]{:S(2)}, u32[]{:S(2)}) collective-permute-start(bf16[160,1152]{1,0:T(8,128)(2,1)} %image.1), channel_id=1, source_target_pairs={{0,4},{1,5},{2,6},{3,7},{4,8},{5,9},{6,10},{7,11},{8,12},{9,13},{1... | collective-permute-start | bytes 1105928 | tf_op jit(solution)/shard_map/ppermute | solution.py:267
  3.6 1.5 %collective-permute-start.2 = (bf16[160,1152]{1,0:T(8,128)(2,1)}, bf16[160,1152]{1,0:T(8,128)(2,1)S(1)}, u32[]{:S(2)}, u32[]{:S(2)}) collective-permute-start(bf16[160,1152]{1,0:T(8,128)(2,1)} %text.1), channel_id=1, source_target_pairs={{0,1},{1,0},{2,3},{3,2},{4,5},{5,4},{6,7},{7,6},{8,9},{9,8},{10,11... | collective-permute-start | bytes 1105928 | tf_op jit(solution)/shard_map/ppermute | solution.py:267
  5.1 1.3 %unit.1 = (bf16[160,1152]{1,0:T(8,128)(2,1)S(1)}, bf16[160,1152]{1,0:T(8,128)(2,1)S(1)}, bf16[160,1152]{1,0:T(8,128)(2,1)S(1)}, bf16[160,1152]{1,0:T(8,128)(2,1)...) custom-call(bf16[160,1152]{1,0:T(8,128)(2,1)} %image.1, bf16[160,1152]{1,0:T(8,128)(2,1)} %text.1), custom_call_target="tpu_custom_call" | custom-call | tf_op jit(solution)/shard_map/unit/pallas_call | solution.py:227
  6.5 0.1 collective-permute-start
  6.6 0.5 %collective-permute-start.1 = (bf16[160,1152]{1,0:T(8,128)(2,1)S(1)}, bf16[160,1152]{1,0:T(8,128)(2,1)S(1)}, u32[]{:S(2)}, u32[]{:S(2)}) collective-permute-start(bf16[160,1152]{1,0:T(8,128)(2,1)S(1)} %get-tuple-element.27.text), channel_id=1, source_target_pairs={{0,2},{1,3},{2,0},{3,1},{4,6},{5,7},{6,4},{7,5},{8,10},{9,11},{10,... | collective-permute-start | bytes 1105928 | tf_op jit(solution)/shard_map/ppermute | solution.py:267
  8.3 1.1 %prep.1 = (f32[8,128]{1,0:T(8,128)S(1)}, s32[1,480]{1,0:T(1,128)S(1)}, s32[160,1]{1,0:T(8,128)S(1)}) custom-call(s32[40,128]{1,0:T(8,128)} %bitcast.9, f32[1,1]{1,0:T(1,128)} %bitcast.5.scale, f32[1,1]{1,0:T(1,128)} %bitcast.6.bias, f32[160,1]{1,0:T(8,128)S(1)} %get-tuple-element.22.after.refs_1_), custom_call_target="tpu_custom_call" | custom-call | tf_op jit(solution)/shard_map/prep/pallas_call | solution.py:227
  9.5 6.0 %collective-permute-done.3.raw = bf16[160,1152]{1,0:T(8,128)(2,1)S(1)} collective-permute-done((bf16[160,1152]{1,0:T(8,128)(2,1)}, bf16[160,1152]{1,0:T(8,128)(2,1)S(1)}, u32[]{:S(2)}, u32[]{:S(2)}) %collective-permute-start.3) | collective-permute-done | bytes 368672 | tf_op jit(solution)/shard_map/ppermute | solution.py:267
  15.5 0.2 visit.1
  15.6 0.0 collective-permute-done.2.refs_0_
  15.6 0.1 collective-permute-start.5
  15.7 0.5 %collective-permute-start.4 = (bf16[160,1152]{1,0:T(8,128)(2,1)S(1)}, bf16[160,1152]{1,0:T(8,128)(2,1)S(1)}, u32[]{:S(2)}, u32[]{:S(2)}) collective-permute-start(bf16[160,1152]{1,0:T(8,128)(2,1)S(1)} %visit.1), channel_id=1, source_target_pairs={{0,2},{1,3},{2,0},{3,1},{4,6},{5,7},{6,4},{7,5},{8,10},{9,11},{10,... | collective-permute-start | bytes 1105928 | tf_op jit(solution)/shard_map/ppermute | solution.py:267
  16.2 0.0 collective-permute-done.mate_image
  16.2 1.0 %first.1 = (bf16[160,1152]{1,0:T(8,128)(2,1)S(1)}, bf16[1,160,1152]{2,1,0:T(8,128)(2,1)S(1)}) custom-call(f32[8,128]{1,0:T(8,128)S(1)} %get-tuple-element.23.after.params, s32[1,480]{1,0:T(1,128)S(1)} %get-tuple-element.24.row_targets, bf16[160,1152]{1,0:T(8,128)(2,1)S(1)} %get-tuple-element.26.image, bf16[160,1152]{1,0:T(8,128)(2,1)S(1)} %get-tuple-element.27.text, ...), custom_call_target="tpu_custom_call" | custom-call | tf_op jit(solution)/shard_map/first/pallas_call | solution.py:227
  17.3 1.8 %collective-permute-start.7 = (bf16[160,1152]{1,0:T(8,128)(2,1)S(1)}, bf16[160,1152]{1,0:T(8,128)(2,1)S(1)}, u32[]{:S(2)}, u32[]{:S(2)}) collective-permute-start(bf16[160,1152]{1,0:T(8,128)(2,1)S(1)} %bitcast.7), channel_id=1, source_target_pairs={{0,28},{1,29},{2,3},{3,2},{4,0},{5,1},{6,7},{7,6},{8,4},{9,5},{10,... | collective-permute-start | bytes 1105928 | tf_op jit(solution)/shard_map/ppermute | solution.py:267
  19.0 0.0 collective-permute-done.1.mate_text
  19.1 0.0 collective-permute-done.5.refs_1_
  19.1 0.0 collective-permute-done.4.mate_visit
  19.1 0.9 %second.1 = (bf16[160,1152]{1,0:T(8,128)(2,1)S(1)}, bf16[1,160,1152]{2,1,0:T(8,128)(2,1)S(1)}) custom-call(f32[8,128]{1,0:T(8,128)S(1)} %get-tuple-element.23.after.params, s32[1,480]{1,0:T(1,128)S(1)} %get-tuple-element.24.row_targets, bf16[160,1152]{1,0:T(8,128)(2,1)S(1)} %get-tuple-element.26.image, bf16[160,1152]{1,0:T(8,128)(2,1)S(1)} %get-tuple-element.27.text, ...), custom_call_target="tpu_custom_call" | custom-call | tf_op jit(solution)/shard_map/second/pallas_call | solution.py:227
  20.0 1.6 %collective-permute-start.6 = (bf16[160,1152]{1,0:T(8,128)(2,1)S(1)}, bf16[160,1152]{1,0:T(8,128)(2,1)S(1)}, u32[]{:S(2)}, u32[]{:S(2)}) collective-permute-start(bf16[160,1152]{1,0:T(8,128)(2,1)S(1)} %bitcast.8), channel_id=1, source_target_pairs={{0,1},{1,0},{2,30},{3,31},{4,5},{5,4},{6,2},{7,3},{8,9},{9,8},{10,... | collective-permute-start | bytes 1105928 | tf_op jit(solution)/shard_map/ppermute | solution.py:267
  21.5 1.8 %third.1 = (f32[160,1152]{1,0:T(8,128)S(1)}, f32[160,1152]{1,0:T(8,128)S(1)}) custom-call(f32[8,128]{1,0:T(8,128)S(1)} %get-tuple-element.23.after.params, s32[1,480]{1,0:T(1,128)S(1)} %get-tuple-element.24.row_targets, s32[160,1]{1,0:T(8,128)S(1)} %get-tuple-element.25.targets, bf16[160,1152]{1,0:T(8,128)(2,1)S(1)} %get-tuple-element.26.image, ...), custom_call_target="tpu_custom_call" | custom-call | tf_op jit(solution)/shard_map/third/pallas_call | solution.py:227
  23.3 3.9 %collective-permute-done.7.refs_6_ = bf16[160,1152]{1,0:T(8,128)(2,1)S(1)} collective-permute-done((bf16[160,1152]{1,0:T(8,128)(2,1)S(1)}, bf16[160,1152]{1,0:T(8,128)(2,1)S(1)}, u32[]{:S(2)}, u32[]{:S(2)}) %collective-permute-start.7) | collective-permute-done | bytes 368672 | tf_op jit(solution)/shard_map/ppermute | solution.py:267
  27.2 1.1 %tangent.2 = (f32[160,1152]{1,0:T(8,128)}, f32[160,1152]{1,0:T(8,128)}) custom-call(bf16[160,1152]{1,0:T(8,128)(2,1)S(1)} %get-tuple-element.21.refs_0_, f32[160,1]{1,0:T(8,128)S(1)} %get-tuple-element.22.after.refs_1_, f32[160,1152]{1,0:T(8,128)S(1)} %get-tuple-element.32.refs_2_, bf16[160,1152]{1,0:T(8,128)(2,1)S(1)} %get-tuple-element.33.refs_3_, ...), custom_call_target="tpu_custom_call" | custom-call | tf_op jit(solution)/shard_map/tangent/pallas_call | solution.py:242
  28.3 0.0 collective-permute-done.6.refs_6_
  28.3 1.1 %tangent.3 = (f32[160,1152]{1,0:T(8,128)}, f32[160,1152]{1,0:T(8,128)}) custom-call(bf16[160,1152]{1,0:T(8,128)(2,1)S(1)} %get-tuple-element.21.refs_0_, f32[160,1]{1,0:T(8,128)S(1)} %get-tuple-element.22.after.refs_1_, f32[160,1152]{1,0:T(8,128)S(1)} %get-tuple-element.32.refs_2_, ...), custom_call_target="tpu_custom_call", output_to_operand_aliasing={{0}: (7, {}), {1}: (8, {})} | custom-call | tf_op jit(solution)/shard_map/tangent/pallas_call | solution.py:242
Async XLA Ops:
  0.6 14.8 %collective-permute-start.3 = (bf16[160,1152]{1,0:T(8,128)(2,1)}, bf16[160,1152]{1,0:T(8,128)(2,1)S(1)}, u32[]{:S(2)}, u32[]{:S(2)}) collective-permute-start(bf16[160,1152]{1,0:T(8,128)(2,1)} %image.1), channel_id=1, source_target_pairs={{0,4},{1,5},{2,6},{3,7},{4,8},{5,9},{6,10},{7,11},{8,12},{9,13},{1... | collective-permute-start | bytes 1105928 | tf_op jit(solution)/shard_map/ppermute | solution.py:267
  3.6 12.0 %collective-permute-start.2 = (bf16[160,1152]{1,0:T(8,128)(2,1)}, bf16[160,1152]{1,0:T(8,128)(2,1)S(1)}, u32[]{:S(2)}, u32[]{:S(2)}) collective-permute-start(bf16[160,1152]{1,0:T(8,128)(2,1)} %text.1), channel_id=1, source_target_pairs={{0,1},{1,0},{2,3},{3,2},{4,5},{5,4},{6,7},{7,6},{8,9},{9,8},{10,11... | collective-permute-start | bytes 1105928 | tf_op jit(solution)/shard_map/ppermute | solution.py:267
  6.5 9.7 %collective-permute-start = (bf16[160,1152]{1,0:T(8,128)(2,1)S(1)}, bf16[160,1152]{1,0:T(8,128)(2,1)S(1)}, u32[]{:S(2)}, u32[]{:S(2)}) collective-permute-start(bf16[160,1152]{1,0:T(8,128)(2,1)S(1)} %get-tuple-element.26.image), channel_id=1, source_target_pairs={{0,2},{1,3},{2,0},{3,1},{4,6},{5,7},{6,4},{7,5},{8,10},{9,11},{10,... | collective-permute-start | bytes 1105928 | tf_op jit(solution)/shard_map/ppermute | solution.py:267
  6.6 12.5 %collective-permute-start.1 = (bf16[160,1152]{1,0:T(8,128)(2,1)S(1)}, bf16[160,1152]{1,0:T(8,128)(2,1)S(1)}, u32[]{:S(2)}, u32[]{:S(2)}) collective-permute-start(bf16[160,1152]{1,0:T(8,128)(2,1)S(1)} %get-tuple-element.27.text), channel_id=1, source_target_pairs={{0,2},{1,3},{2,0},{3,1},{4,6},{5,7},{6,4},{7,5},{8,10},{9,11},{10,... | collective-permute-start | bytes 1105928 | tf_op jit(solution)/shard_map/ppermute | solution.py:267
  15.6 3.4 %collective-permute-start.5 = (bf16[160,1152]{1,0:T(8,128)(2,1)S(1)}, bf16[160,1152]{1,0:T(8,128)(2,1)S(1)}, u32[]{:S(2)}, u32[]{:S(2)}) collective-permute-start(bf16[160,1152]{1,0:T(8,128)(2,1)S(1)} %collective-permute-done.2.refs_0_), channel_id=1, source_target_pairs={{0,2},{1,3},{2,0},{3,1},{4,6},{5,7},{6,4},{7,5},{8,10},{9,11},{10,... | collective-permute-start | bytes 1105928 | tf_op jit(solution)/shard_map/ppermute | solution.py:267
  15.7 3.3 %collective-permute-start.4 = (bf16[160,1152]{1,0:T(8,128)(2,1)S(1)}, bf16[160,1152]{1,0:T(8,128)(2,1)S(1)}, u32[]{:S(2)}, u32[]{:S(2)}) collective-permute-start(bf16[160,1152]{1,0:T(8,128)(2,1)S(1)} %visit.1), channel_id=1, source_target_pairs={{0,2},{1,3},{2,0},{3,1},{4,6},{5,7},{6,4},{7,5},{8,10},{9,11},{10,... | collective-permute-start | bytes 1105928 | tf_op jit(solution)/shard_map/ppermute | solution.py:267
  17.3 10.0 %collective-permute-start.7 = (bf16[160,1152]{1,0:T(8,128)(2,1)S(1)}, bf16[160,1152]{1,0:T(8,128)(2,1)S(1)}, u32[]{:S(2)}, u32[]{:S(2)}) collective-permute-start(bf16[160,1152]{1,0:T(8,128)(2,1)S(1)} %bitcast.7), channel_id=1, source_target_pairs={{0,28},{1,29},{2,3},{3,2},{4,0},{5,1},{6,7},{7,6},{8,4},{9,5},{10,... | collective-permute-start | bytes 1105928 | tf_op jit(solution)/shard_map/ppermute | solution.py:267
  20.0 8.4 %collective-permute-start.6 = (bf16[160,1152]{1,0:T(8,128)(2,1)S(1)}, bf16[160,1152]{1,0:T(8,128)(2,1)S(1)}, u32[]{:S(2)}, u32[]{:S(2)}) collective-permute-start(bf16[160,1152]{1,0:T(8,128)(2,1)S(1)} %bitcast.8), channel_id=1, source_target_pairs={{0,1},{1,0},{2,30},{3,31},{4,5},{5,4},{6,2},{7,3},{8,9},{9,8},{10,... | collective-permute-start | bytes 1105928 | tf_op jit(solution)/shard_map/ppermute | solution.py:267

commit v13 on v12

--- a/solution.py
+++ b/solution.py
@@ -88,10 +88,6 @@
         inverse = inverse_of(values)
         half[...] = (values * inverse).astype(HALF)
         inv[...] = inverse
-
-
-def visit_kernel(raw, after, half):
-    half[...] = half_rows(raw)
 
 
 def prep_kernel(
@@ -125,6 +121,10 @@
     targets[...] = turned.astype(jnp.int32)
 
 
+def visit_kernel(raw, after, half):
+    half[...] = half_rows(raw)
+
+
 def first_kernel(far, params, row_targets, image, text, mate_image, visit, *refs):
     far_raw, far_text, back = refs[:far], refs[far : 2 * far], refs[2 * far]
     for k in range(far):
@@ -142,69 +142,75 @@
     by_role(on_first, on_second)
 
 
-def second_kernel(
-    far, params, row_targets, image, text, mate_text, visit, mate_visit, *refs
-):
-    far_text, relay = refs[:far], refs[far : 2 * far]
-    mate_far, back = refs[2 * far : 3 * far], refs[3 * far]
+def second_kernel(far, params, row_targets, image, text, mate_text, visit, mate_visit, *refs):
+    far_text, mate_far, back = refs[:far], refs[far : 2 * far], refs[2 * far]
 
     def on_first(node):
         for k in range(far):
-            mate_far[k][...] = half_rows(relay[k])
             pairs = text_pairs(row_targets, lax.rem(node + k + 1, far + 1))
             images = [image, visit, mate_visit]
             back[k] = drawn(params, far_text[k], images, pairs).astype(HALF)
 
     def on_second(node):
-        for k in range(far):
-            mate_far[k][...] = half_rows(relay[k])
         texts = [text, *far_text, mate_text, *mate_far]
         back[0] = drawn(params, visit, texts).astype(HALF)
 
     by_role(on_first, on_second)
+
+
+def local_part(raw, inverse, direction):
+    inv = inverse[...]
+    unit = raw[...].astype(FULL) * inv
+    along = jnp.sum(unit * direction, axis=1, keepdims=True)
+    return (direction - unit * along) * inv
 
 
 def third_kernel(
     far, params, row_targets, targets, image, text, mate_image, mate_text, visit, mate_visit, *refs
 ):
     far_text, mate_far = refs[:far], refs[far : 2 * far]
-    image_dir, text_dir = refs[2 * far :]
+    image_raw, image_inv, text_raw, text_inv, image_part, text_part = refs[2 * far :]
     nodes = far + 1
 
     def on_first(node):
         pairs = image_pairs(targets, node, nodes)
         texts = [text, *far_text, mate_text, *mate_far]
-        image_dir[...] = drawn(params, image, texts, pairs)
+        direction = drawn(params, image, texts, pairs)
+        image_part[...] = local_part(image_raw, image_inv, direction)
         pairs = text_pairs(row_targets, node)
-        text_dir[...] = drawn(params, text, [image, visit, mate_visit], pairs)
+        direction = drawn(params, text, [image, visit, mate_visit], pairs)
+        text_part[...] = local_part(text_raw, text_inv, direction)
 
     def on_second(node):
         pairs = text_pairs(row_targets, node)
-        text_dir[...] = drawn(params, text, [image, mate_image, visit], pairs)
+        direction = drawn(params, text, [image, mate_image, visit], pairs)
+        text_part[...] = local_part(text_raw, text_inv, direction)
         pairs = image_pairs(targets, node, nodes)
-        image_dir[...] = drawn(params, image, [text, *far_text], pairs)
+        direction = drawn(params, image, [text, *far_text], pairs)
+        image_part[...] = local_part(image_raw, image_inv, direction)
 
     by_role(on_first, on_second)
 
 
 def tangent_kernel(far, image_on_first, *refs):
-    image, text, parts = refs[0:3], refs[3:6], refs[6 : 6 + far]
+    image, text, received = refs[0:3], refs[3:6], refs[6 : 6 + far]
     image_grads, text_grads, held, sems = refs[-4:]
     rows = held.shape[0]
     part = rows // 5 if rows % 80 == 0 else rows
 
     def run(own, out, count, node):
-        raw, inverse, direction = own
-        gradient = direction[...]
-        for k in range(count):
-            gradient += parts[k][...].astype(FULL)
+        raw, inverse, base = own
+        gradient = received[0][...].astype(FULL)
+        for k in range(1, count):
+            gradient += received[k][...].astype(FULL)
         inv = inverse[...]
-        unit = raw[...].astype(FULL) * inv
-        along = jnp.sum(unit * gradient, axis=1, keepdims=True)
+        values = raw[...].astype(FULL)
+        along = jnp.sum(values * gradient, axis=1, keepdims=True) * (inv * inv * inv)
         copies = []
         for i, at in enumerate(range(0, rows, part)):
             piece = slice(at, at + part)
-            held[piece, :] = (gradient[piece] - unit[piece] * along[piece]) * inv[piece]
+            turned = gradient[piece] * inv[piece] - values[piece] * along[piece]
+            held[piece, :] = base[piece, :] + turned
             copy = pltpu.make_async_copy(held.at[piece], out.at[piece], sems.at[i])
             copy.start()
             copies.append(copy)
@@ -299,9 +305,7 @@
         scratch=[pltpu.VMEM(names.shape, jnp.int32), pltpu.SemaphoreType.DMA((1,))],
     )
     (visit,) = call(visit_kernel, "visit", [visit_raw, params], [block_h])
-    mate_visit = swap(visit)
     *far_raw, visit = lax.optimization_barrier((*far_raw, visit))
-    relay = [swap(block) for block in far_raw]
     *far_text, back = call(
         functools.partial(first_kernel, far),
         "first",
@@ -309,21 +313,24 @@
         [block_h] * far + [returns],
     )
     one = [send(back[k], behind if k == 0 else stay, (0, k + 1)) for k in range(far)]
-    *mate_far, back = call(
+    visit, *far_text = lax.optimization_barrier((visit, *far_text))
+    mate_visit = swap(visit)
+    mate_far = [swap(block) for block in far_text]
+    (back,) = call(
         functools.partial(second_kernel, far),
         "second",
-        [params, row_targets, image, text, mate_text, visit, mate_visit, *far_text, *relay],
-        [block_h] * far + [returns],
+        [params, row_targets, image, text, mate_text, visit, mate_visit, *far_text, *mate_far],
+        [returns],
     )
     two = [send(back[k], (0, k + 1), behind if k == 0 else stay) for k in range(far)]
-    image_dir, text_dir = call(
+    image_part, text_part = call(
         functools.partial(third_kernel, far),
         "third",
         [params, row_targets, targets, image, text, mate_image, mate_text, visit, mate_visit]
-        + [*far_text, *mate_far],
+        + [*far_text, *mate_far, image_raw, image_inv, text_raw, text_inv],
         [block_f, block_f],
     )
-    own = [image_raw, image_inv, image_dir, text_raw, text_inv, text_dir]
+    own = [image_raw, image_inv, image_part, text_raw, text_inv, text_part]
     grads = tangent(far, True, [*own, *one], [], block_f)
     return tuple(tangent(far, False, [*own, *two], grads, block_f))
 

time: 29.7 us -> 29.5 us (level)
  waiting for transfers between devices: 9.86 us -> 9.19 us
  Pallas kernels: 8.55 us -> 8.86 us
    ppermute x8, waiting for transfers between devices: 9.86 us -> 9.19 us  [send(): return lax.ppermute(block, ('blk', 'node'), route)]
  transfers between devices with their start and end apart: 8 -> 8, of which waited for: 2 -> 2; matrix products, arithmetic and copies ran while one was open for 0% -> 0% of each run, Pallas kernels for 25% -> 26%
where the time goes in v13:
time: 29.5 us; the launch traced here: 29 us
  waiting for transfers between devices  9.19 us (31%)
  starting transfers between devices  8.95 us (30%)
  Pallas kernels  8.86 us (30%)
  between operations  2.02 us (7%)
    ppermute x8, waiting for transfers between devices, send(): return lax.ppermute(block, ('blk', 'node'), route)  9.19 us
    ppermute x8, starting transfers between devices, send(): return lax.ppermute(block, ('blk', 'node'), route)  8.95 us
    pallas_call x6, Pallas kernels, call(): pl.pallas_call(kernel, name=name, out_shape=[pltpu.VMEM(s, d) for s, d in...  6.5 us
    pallas_call x2, Pallas kernels, tangent(): pl.pallas_call(functools.partial(tangent_kernel, far, image_on_first), na...  2.36 us
  transfers between devices with their start and end apart: 8, of which 2 were waited for; matrix products, arithmetic and copies ran while one was open for 0% of the time, Pallas kernels for 26%

profile of v13, /device:TPU:0, one launch (start us, length us, event | category | flops | bytes accessed | tf_op | source)
XLA Modules:
  0.0 29.0 jit_solution(828253206333041974)
XLA Ops:
  0.6 3.0 %collective-permute-start.3 = (bf16[160,1152]{1,0:T(8,128)(2,1)}, bf16[160,1152]{1,0:T(8,128)(2,1)S(1)}, u32[]{:S(2)}, u32[]{:S(2)}) collective-permute-start(bf16[160,1152]{1,0:T(8,128)(2,1)} %image.1), channel_id=1, source_target_pairs={{0,4},{1,5},{2,6},{3,7},{4,8},{5,9},{6,10},{7,11},{8,12},{9,13},{1... | collective-permute-start | bytes 1105928 | tf_op jit(solution)/shard_map/ppermute | solution.py:273
  3.6 1.5 %collective-permute-start.2 = (bf16[160,1152]{1,0:T(8,128)(2,1)}, bf16[160,1152]{1,0:T(8,128)(2,1)S(1)}, u32[]{:S(2)}, u32[]{:S(2)}) collective-permute-start(bf16[160,1152]{1,0:T(8,128)(2,1)} %text.1), channel_id=1, source_target_pairs={{0,1},{1,0},{2,3},{3,2},{4,5},{5,4},{6,7},{7,6},{8,9},{9,8},{10,11... | collective-permute-start | bytes 1105928 | tf_op jit(solution)/shard_map/ppermute | solution.py:273
  5.1 1.3 %unit.1 = (bf16[160,1152]{1,0:T(8,128)(2,1)S(1)}, bf16[160,1152]{1,0:T(8,128)(2,1)S(1)}, bf16[160,1152]{1,0:T(8,128)(2,1)S(1)}, bf16[160,1152]{1,0:T(8,128)(2,1)...) custom-call(bf16[160,1152]{1,0:T(8,128)(2,1)} %image.1, bf16[160,1152]{1,0:T(8,128)(2,1)} %text.1), custom_call_target="tpu_custom_call" | custom-call | tf_op jit(solution)/shard_map/unit/pallas_call | solution.py:233
  6.5 0.1 collective-permute-start
  6.6 0.5 %collective-permute-start.1 = (bf16[160,1152]{1,0:T(8,128)(2,1)S(1)}, bf16[160,1152]{1,0:T(8,128)(2,1)S(1)}, u32[]{:S(2)}, u32[]{:S(2)}) collective-permute-start(bf16[160,1152]{1,0:T(8,128)(2,1)S(1)} %get-tuple-element.27.text), channel_id=1, source_target_pairs={{0,2},{1,3},{2,0},{3,1},{4,6},{5,7},{6,4},{7,5},{8,10},{9,11},{10,... | collective-permute-start | bytes 1105928 | tf_op jit(solution)/shard_map/ppermute | solution.py:273
  8.3 1.1 %prep.1 = (f32[8,128]{1,0:T(8,128)S(1)}, s32[1,480]{1,0:T(1,128)S(1)}, s32[160,1]{1,0:T(8,128)S(1)}) custom-call(s32[40,128]{1,0:T(8,128)} %bitcast.9, f32[1,1]{1,0:T(1,128)} %bitcast.5.scale, f32[1,1]{1,0:T(1,128)} %bitcast.6.bias, f32[160,1]{1,0:T(8,128)S(1)} %get-tuple-element.22.after.refs_3_.refs_1_), custom_call_target="tpu_custom_call" | custom-call | tf_op jit(solution)/shard_map/prep/pallas_call | solution.py:233
  9.5 6.0 %collective-permute-done.3.raw = bf16[160,1152]{1,0:T(8,128)(2,1)S(1)} collective-permute-done((bf16[160,1152]{1,0:T(8,128)(2,1)}, bf16[160,1152]{1,0:T(8,128)(2,1)S(1)}, u32[]{:S(2)}, u32[]{:S(2)}) %collective-permute-start.3) | collective-permute-done | bytes 368672 | tf_op jit(solution)/shard_map/ppermute | solution.py:273
  15.5 0.2 visit.1
  15.6 0.0 collective-permute-done.2.refs_0_
  15.6 0.0 collective-permute-done.mate_image
  15.6 1.0 %first.1 = (bf16[160,1152]{1,0:T(8,128)(2,1)S(1)}, bf16[1,160,1152]{2,1,0:T(8,128)(2,1)S(1)}) custom-call(f32[8,128]{1,0:T(8,128)S(1)} %get-tuple-element.23.after.params, s32[1,480]{1,0:T(1,128)S(1)} %get-tuple-element.24.row_targets, bf16[160,1152]{1,0:T(8,128)(2,1)S(1)} %get-tuple-element.26.image, bf16[160,1152]{1,0:T(8,128)(2,1)S(1)} %get-tuple-element.27.text, ...), custom_call_target="tpu_custom_call" | custom-call | tf_op jit(solution)/shard_map/first/pallas_call | solution.py:233
  16.7 0.1 collective-permute-start.4
  16.8 0.5 %collective-permute-start.5 = (bf16[160,1152]{1,0:T(8,128)(2,1)S(1)}, bf16[160,1152]{1,0:T(8,128)(2,1)S(1)}, u32[]{:S(2)}, u32[]{:S(2)}) collective-permute-start(bf16[160,1152]{1,0:T(8,128)(2,1)S(1)} %get-tuple-element.32.refs_0_), channel_id=1, source_target_pairs={{0,2},{1,3},{2,0},{3,1},{4,6},{5,7},{6,4},{7,5},{8,10},{9,11},{10,... | collective-permute-start | bytes 1105928 | tf_op jit(solution)/shard_map/ppermute | solution.py:273
  17.3 1.7 %collective-permute-start.7 = (bf16[160,1152]{1,0:T(8,128)(2,1)S(1)}, bf16[160,1152]{1,0:T(8,128)(2,1)S(1)}, u32[]{:S(2)}, u32[]{:S(2)}) collective-permute-start(bf16[160,1152]{1,0:T(8,128)(2,1)S(1)} %bitcast.8), channel_id=1, source_target_pairs={{0,28},{1,29},{2,3},{3,2},{4,0},{5,1},{6,7},{7,6},{8,4},{9,5},{10,... | collective-permute-start | bytes 1105928 | tf_op jit(solution)/shard_map/ppermute | solution.py:273
  19.0 0.0 collective-permute-done.1.mate_text
  19.0 0.0 collective-permute-done.4.mate_visit
  19.0 0.0 collective-permute-done.5.refs_1_
  19.0 0.9 %second.1 = bf16[1,160,1152]{2,1,0:T(8,128)(2,1)S(1)} custom-call(f32[8,128]{1,0:T(8,128)S(1)} %get-tuple-element.23.after.params, s32[1,480]{1,0:T(1,128)S(1)} %get-tuple-element.24.row_targets, bf16[160,1152]{1,0:T(8,128)(2,1)S(1)} %get-tuple-element.26.image, bf16[160,1152]{1,0:T(8,128)(2,1)S(1)} %get-tuple-element.27.text, ...), custom_call_target="tpu_custom_call" | custom-call | tf_op jit(solution)/shard_map/second/pallas_call | solution.py:233
  19.9 1.6 %collective-permute-start.6 = (bf16[160,1152]{1,0:T(8,128)(2,1)S(1)}, bf16[160,1152]{1,0:T(8,128)(2,1)S(1)}, u32[]{:S(2)}, u32[]{:S(2)}) collective-permute-start(bf16[160,1152]{1,0:T(8,128)(2,1)S(1)} %bitcast.7), channel_id=1, source_target_pairs={{0,1},{1,0},{2,30},{3,31},{4,5},{5,4},{6,2},{7,3},{8,9},{9,8},{10,... | collective-permute-start | bytes 1105928 | tf_op jit(solution)/shard_map/ppermute | solution.py:273
  21.5 2.0 %third.1 = (f32[160,1152]{1,0:T(8,128)S(1)}, f32[160,1152]{1,0:T(8,128)S(1)}) custom-call(f32[8,128]{1,0:T(8,128)S(1)} %get-tuple-element.23.after.params, s32[1,480]{1,0:T(1,128)S(1)} %get-tuple-element.24.row_targets, s32[160,1]{1,0:T(8,128)S(1)} %get-tuple-element.25.targets, bf16[160,1152]{1,0:T(8,128)(2,1)S(1)} %get-tuple-element.26.image, ...), custom_call_target="tpu_custom_call" | custom-call | tf_op jit(solution)/shard_map/third/pallas_call | solution.py:233
  23.5 3.2 %collective-permute-done.7.refs_6_ = bf16[160,1152]{1,0:T(8,128)(2,1)S(1)} collective-permute-done((bf16[160,1152]{1,0:T(8,128)(2,1)S(1)}, bf16[160,1152]{1,0:T(8,128)(2,1)S(1)}, u32[]{:S(2)}, u32[]{:S(2)}) %collective-permute-start.7) | collective-permute-done | bytes 368672 | tf_op jit(solution)/shard_map/ppermute | solution.py:273
  26.6 1.2 %tangent.2 = (f32[160,1152]{1,0:T(8,128)}, f32[160,1152]{1,0:T(8,128)}) custom-call(bf16[160,1152]{1,0:T(8,128)(2,1)S(1)} %get-tuple-element.21.refs_2_.refs_0_, f32[160,1]{1,0:T(8,128)S(1)} %get-tuple-element.22.after.refs_3_.refs_1_, f32[160,1152]{1,0:T(8,128)S(1)} %get-tuple-element.35.refs_2_, bf16[160,1152]{1,0:T(8,128)(2,1)S(1)} %get-tuple-element.33.refs_4_.refs_3_, ...), custom_call_target="tpu_custom_call" | custom-call | tf_op jit(solution)/shard_map/tangent/pallas_call | solution.py:248
  27.8 0.0 collective-permute-done.6.refs_6_
  27.8 1.2 %tangent.3 = (f32[160,1152]{1,0:T(8,128)}, f32[160,1152]{1,0:T(8,128)}) custom-call(bf16[160,1152]{1,0:T(8,128)(2,1)S(1)} %get-tuple-element.21.refs_2_.refs_0_, f32[160,1]{1,0:T(8,128)S(1)} %get-tuple-element.22.after.refs_3_.refs_1_, f32[160,1152]{1,0:T(8,128)S(1)} %get-tuple-element.35.refs_2_, ...), custom_call_target="tpu_custom_call", output_to_operand_aliasing={{0}: (7, {}), {1}: (8, {})} | custom-call | tf_op jit(solution)/shard_map/tangent/pallas_call | solution.py:248
Async XLA Ops:
  0.6 14.8 %collective-permute-start.3 = (bf16[160,1152]{1,0:T(8,128)(2,1)}, bf16[160,1152]{1,0:T(8,128)(2,1)S(1)}, u32[]{:S(2)}, u32[]{:S(2)}) collective-permute-start(bf16[160,1152]{1,0:T(8,128)(2,1)} %image.1), channel_id=1, source_target_pairs={{0,4},{1,5},{2,6},{3,7},{4,8},{5,9},{6,10},{7,11},{8,12},{9,13},{1... | collective-permute-start | bytes 1105928 | tf_op jit(solution)/shard_map/ppermute | solution.py:273
  3.6 12.0 %collective-permute-start.2 = (bf16[160,1152]{1,0:T(8,128)(2,1)}, bf16[160,1152]{1,0:T(8,128)(2,1)S(1)}, u32[]{:S(2)}, u32[]{:S(2)}) collective-permute-start(bf16[160,1152]{1,0:T(8,128)(2,1)} %text.1), channel_id=1, source_target_pairs={{0,1},{1,0},{2,3},{3,2},{4,5},{5,4},{6,7},{7,6},{8,9},{9,8},{10,11... | collective-permute-start | bytes 1105928 | tf_op jit(solution)/shard_map/ppermute | solution.py:273
  6.5 9.2 %collective-permute-start = (bf16[160,1152]{1,0:T(8,128)(2,1)S(1)}, bf16[160,1152]{1,0:T(8,128)(2,1)S(1)}, u32[]{:S(2)}, u32[]{:S(2)}) collective-permute-start(bf16[160,1152]{1,0:T(8,128)(2,1)S(1)} %get-tuple-element.26.image), channel_id=1, source_target_pairs={{0,2},{1,3},{2,0},{3,1},{4,6},{5,7},{6,4},{7,5},{8,10},{9,11},{10,... | collective-permute-start | bytes 1105928 | tf_op jit(solution)/shard_map/ppermute | solution.py:273
  6.6 12.5 %collective-permute-start.1 = (bf16[160,1152]{1,0:T(8,128)(2,1)S(1)}, bf16[160,1152]{1,0:T(8,128)(2,1)S(1)}, u32[]{:S(2)}, u32[]{:S(2)}) collective-permute-start(bf16[160,1152]{1,0:T(8,128)(2,1)S(1)} %get-tuple-element.27.text), channel_id=1, source_target_pairs={{0,2},{1,3},{2,0},{3,1},{4,6},{5,7},{6,4},{7,5},{8,10},{9,11},{10,... | collective-permute-start | bytes 1105928 | tf_op jit(solution)/shard_map/ppermute | solution.py:273
  16.7 2.3 %collective-permute-start.4 = (bf16[160,1152]{1,0:T(8,128)(2,1)S(1)}, bf16[160,1152]{1,0:T(8,128)(2,1)S(1)}, u32[]{:S(2)}, u32[]{:S(2)}) collective-permute-start(bf16[160,1152]{1,0:T(8,128)(2,1)S(1)} %visit.1), channel_id=1, source_target_pairs={{0,2},{1,3},{2,0},{3,1},{4,6},{5,7},{6,4},{7,5},{8,10},{9,11},{10,... | collective-permute-start | bytes 1105928 | tf_op jit(solution)/shard_map/ppermute | solution.py:273
  16.8 2.2 %collective-permute-start.5 = (bf16[160,1152]{1,0:T(8,128)(2,1)S(1)}, bf16[160,1152]{1,0:T(8,128)(2,1)S(1)}, u32[]{:S(2)}, u32[]{:S(2)}) collective-permute-start(bf16[160,1152]{1,0:T(8,128)(2,1)S(1)} %get-tuple-element.32.refs_0_), channel_id=1, source_target_pairs={{0,2},{1,3},{2,0},{3,1},{4,6},{5,7},{6,4},{7,5},{8,10},{9,11},{10,... | collective-permute-start | bytes 1105928 | tf_op jit(solution)/shard_map/ppermute | solution.py:273
  17.3 9.4 %collective-permute-start.7 = (bf16[160,1152]{1,0:T(8,128)(2,1)S(1)}, bf16[160,1152]{1,0:T(8,128)(2,1)S(1)}, u32[]{:S(2)}, u32[]{:S(2)}) collective-permute-start(bf16[160,1152]{1,0:T(8,128)(2,1)S(1)} %bitcast.8), channel_id=1, source_target_pairs={{0,28},{1,29},{2,3},{3,2},{4,0},{5,1},{6,7},{7,6},{8,4},{9,5},{10,... | collective-permute-start | bytes 1105928 | tf_op jit(solution)/shard_map/ppermute | solution.py:273
  19.9 7.9 %collective-permute-start.6 = (bf16[160,1152]{1,0:T(8,128)(2,1)S(1)}, bf16[160,1152]{1,0:T(8,128)(2,1)S(1)}, u32[]{:S(2)}, u32[]{:S(2)}) collective-permute-start(bf16[160,1152]{1,0:T(8,128)(2,1)S(1)} %bitcast.7), channel_id=1, source_target_pairs={{0,1},{1,0},{2,30},{3,31},{4,5},{5,4},{6,2},{7,3},{8,9},{9,8},{10,... | collective-permute-start | bytes 1105928 | tf_op jit(solution)/shard_map/ppermute | solution.py:273

commit v14 on v13

--- a/solution.py
+++ b/solution.py
@@ -125,8 +125,10 @@
     half[...] = half_rows(raw)
 
 
-def first_kernel(far, params, row_targets, image, text, mate_image, visit, *refs):
-    far_raw, far_text, back = refs[:far], refs[far : 2 * far], refs[2 * far]
+def first_kernel(far, params, row_targets, image, text, mate_image, mate_text, visit, *refs):
+    far_raw, got, back = refs[:far], refs[far], refs[far + 1]
+    far_text = [got.at[k + 1] for k in range(far)]
+    got[0] = visit[...]
     for k in range(far):
         far_text[k][...] = half_rows(far_raw[k])
 
@@ -142,8 +144,13 @@
     by_role(on_first, on_second)
 
 
-def second_kernel(far, params, row_targets, image, text, mate_text, visit, mate_visit, *refs):
-    far_text, mate_far, back = refs[:far], refs[far : 2 * far], refs[2 * far]
+def parted(far, got):
+    return got.at[0], [got.at[k + 1] for k in range(far)]
+
+
+def second_kernel(far, params, row_targets, image, text, mate_text, got, mate_got, back):
+    visit, far_text = parted(far, got)
+    mate_visit, mate_far = parted(far, mate_got)
 
     def on_first(node):
         for k in range(far):
@@ -166,10 +173,11 @@
 
 
 def third_kernel(
-    far, params, row_targets, targets, image, text, mate_image, mate_text, visit, mate_visit, *refs
+    far, params, row_targets, targets, image, text, mate_image, mate_text, got, mate_got,
+    image_raw, image_inv, text_raw, text_inv, image_part, text_part,
 ):
-    far_text, mate_far = refs[:far], refs[far : 2 * far]
-    image_raw, image_inv, text_raw, text_inv, image_part, text_part = refs[2 * far :]
+    visit, far_text = parted(far, got)
+    mate_visit, mate_far = parted(far, mate_got)
     nodes = far + 1
 
     def on_first(node):
@@ -192,37 +200,46 @@
     by_role(on_first, on_second)
 
 
-def tangent_kernel(far, image_on_first, *refs):
+def finished(far, received, own, count):
+    raw, inverse, part = own
+    gradient = received[0][...].astype(FULL)
+    for k in range(1, count):
+        gradient += received[k][...].astype(FULL)
+    inv = inverse[...]
+    values = raw[...].astype(FULL)
+    along = jnp.sum(values * gradient, axis=1, keepdims=True) * (inv * inv * inv)
+    return gradient * inv - values * along + part[...]
+
+
+def fourth_kernel(far, *refs):
+    image, text, received, ready = refs[0:3], refs[3:6], refs[6 : 6 + far], refs[6 + far]
+
+    def on_first(node):
+        ready[...] = finished(far, received, image, 1)
+
+    def on_second(node):
+        ready[...] = finished(far, received, text, far)
+
+    by_role(on_first, on_second)
+
+
+def last_kernel(far, ready, *refs):
     image, text, received = refs[0:3], refs[3:6], refs[6 : 6 + far]
-    image_grads, text_grads, held, sems = refs[-4:]
-    rows = held.shape[0]
-    part = rows // 5 if rows % 80 == 0 else rows
-
-    def run(own, out, count, node):
-        raw, inverse, base = own
-        gradient = received[0][...].astype(FULL)
-        for k in range(1, count):
-            gradient += received[k][...].astype(FULL)
-        inv = inverse[...]
-        values = raw[...].astype(FULL)
-        along = jnp.sum(values * gradient, axis=1, keepdims=True) * (inv * inv * inv)
-        copies = []
-        for i, at in enumerate(range(0, rows, part)):
-            piece = slice(at, at + part)
-            turned = gradient[piece] * inv[piece] - values[piece] * along[piece]
-            held[piece, :] = base[piece, :] + turned
-            copy = pltpu.make_async_copy(held.at[piece], out.at[piece], sems.at[i])
-            copy.start()
-            copies.append(copy)
-        for copy in copies:
-            copy.wait()
-
-    on_images = functools.partial(run, image, image_grads, 1)
-    on_texts = functools.partial(run, text, text_grads, far)
-    if image_on_first:
-        by_role(on_images, on_texts)
-    else:
-        by_role(on_texts, on_images)
+    image_grads, text_grads, held, sems = refs[6 + far :]
+
+    def run(own, count, ready_out, out, node):
+        early = pltpu.make_async_copy(ready, ready_out, sems.at[0])
+        early.start()
+        held[...] = finished(far, received, own, count)
+        late = pltpu.make_async_copy(held, out, sems.at[1])
+        late.start()
+        early.wait()
+        late.wait()
+
+    by_role(
+        functools.partial(run, text, far, image_grads, text_grads),
+        functools.partial(run, image, 1, text_grads, image_grads),
+    )
 
 
 def call(kernel, name, operands, shapes, anywhere=0, scratch=()):
@@ -242,19 +259,17 @@
     )(*operands)
 
 
-def tangent(far, image_on_first, operands, grads, block):
+def last(far, operands, block):
     anywhere = pl.BlockSpec(memory_space=pl.ANY)
-    count = len(operands)
     return pl.pallas_call(
-        functools.partial(tangent_kernel, far, image_on_first),
-        name="tangent",
+        functools.partial(last_kernel, far),
+        name="last",
         out_shape=[jax.ShapeDtypeStruct(*block)] * 2,
-        in_specs=[pl.BlockSpec(memory_space=pltpu.VMEM)] * count + [anywhere] * len(grads),
+        in_specs=[pl.BlockSpec(memory_space=pltpu.VMEM)] * len(operands),
         out_specs=[anywhere] * 2,
-        scratch_shapes=[pltpu.VMEM(*block), pltpu.SemaphoreType.DMA((5,))],
-        input_output_aliases={count + i: i for i in range(len(grads))},
+        scratch_shapes=[pltpu.VMEM(*block), pltpu.SemaphoreType.DMA((2,))],
         compiler_params=pltpu.CompilerParams(vmem_limit_bytes=VMEM_LIMIT),
-    )(*operands, *grads)
+    )(*operands)
 
 
 def local(image_embeds, text_embeds, pair_text, similarity_scale, logit_bias):
@@ -306,33 +321,33 @@
     )
     (visit,) = call(visit_kernel, "visit", [visit_raw, params], [block_h])
     *far_raw, visit = lax.optimization_barrier((*far_raw, visit))
-    *far_text, back = call(
+    got, back = call(
         functools.partial(first_kernel, far),
         "first",
-        [params, row_targets, image, text, mate_image, visit, *far_raw],
-        [block_h] * far + [returns],
+        [params, row_targets, image, text, mate_image, mate_text, visit, *far_raw],
+        [((node_count, rows, width), HALF), returns],
     )
     one = [send(back[k], behind if k == 0 else stay, (0, k + 1)) for k in range(far)]
-    visit, *far_text = lax.optimization_barrier((visit, *far_text))
-    mate_visit = swap(visit)
-    mate_far = [swap(block) for block in far_text]
+    mate_got = swap(got)
     (back,) = call(
         functools.partial(second_kernel, far),
         "second",
-        [params, row_targets, image, text, mate_text, visit, mate_visit, *far_text, *mate_far],
+        [params, row_targets, image, text, mate_text, got, mate_got],
         [returns],
     )
     two = [send(back[k], (0, k + 1), behind if k == 0 else stay) for k in range(far)]
     image_part, text_part = call(
         functools.partial(third_kernel, far),
         "third",
-        [params, row_targets, targets, image, text, mate_image, mate_text, visit, mate_visit]
-        + [*far_text, *mate_far, image_raw, image_inv, text_raw, text_inv],
+        [params, row_targets, targets, image, text, mate_image, mate_text, got, mate_got]
+        + [image_raw, image_inv, text_raw, text_inv],
         [block_f, block_f],
     )
     own = [image_raw, image_inv, image_part, text_raw, text_inv, text_part]
-    grads = tangent(far, True, [*own, *one], [], block_f)
-    return tuple(tangent(far, False, [*own, *two], grads, block_f))
+    (ready,) = call(
+        functools.partial(fourth_kernel, far), "fourth", [*own, *one], [block_f]
+    )
+    return tuple(last(far, [ready, *own, *two], block_f))
 
 
 def solution(mesh):

time: 29.5 us -> 29.2 us (0.990)
  waiting for transfers between devices: 9.19 us -> 10.4 us
  Pallas kernels: 8.86 us -> 8.11 us
  starting transfers between devices: 8.95 us -> 8.52 us
    ppermute x8 -> x7, waiting for transfers between devices: 9.19 us -> 10.4 us  [send(): return lax.ppermute(block, ('blk', 'node'), route)]
    pallas_call x2 -> x1, Pallas kernels: 2.36 us -> 1.24 us  [last(): pl.pallas_call(functools.partial(last_kernel, far), name='last', out_shap...]
    ppermute x8 -> x7, starting transfers between devices: 8.95 us -> 8.52 us  [send(): return lax.ppermute(block, ('blk', 'node'), route)]
    pallas_call x6 -> x7, Pallas kernels: 6.5 us -> 6.86 us  [call(): pl.pallas_call(kernel, name=name, out_shape=[pltpu.VMEM(s, d) for s, d in...]
  transfers between devices with their start and end apart: 8 -> 7, of which waited for: 2 -> 4; matrix products, arithmetic and copies ran while one was open for 0% -> 0% of each run, Pallas kernels for 26% -> 20%
where the time goes in v14:
time: 29.2 us; the launch traced here: 29 us
  waiting for transfers between devices  10.4 us (36%)
  starting transfers between devices  8.52 us (29%)
  Pallas kernels  8.11 us (28%)
  between operations  2.02 us (7%)
    ppermute x7, waiting for transfers between devices, send(): return lax.ppermute(block, ('blk', 'node'), route)  10.4 us
    ppermute x7, starting transfers between devices, send(): return lax.ppermute(block, ('blk', 'node'), route)  8.52 us
    pallas_call x7, Pallas kernels, call(): pl.pallas_call(kernel, name=name, out_shape=[pltpu.VMEM(s, d) for s, d in...  6.86 us
    pallas_call x1, Pallas kernels, last(): pl.pallas_call(functools.partial(last_kernel, far), name='last', out_shap...  1.24 us
  transfers between devices with their start and end apart: 7, of which 4 were waited for; matrix products, arithmetic and copies ran while one was open for 0% of the time, Pallas kernels for 20%

profile of v14, /device:TPU:0, one launch (start us, length us, event | category | flops | bytes accessed | tf_op | source)
XLA Modules:
  0.0 29.0 jit_solution(8192943170294327294)
XLA Ops:
  0.6 3.0 %collective-permute-start.3 = (bf16[160,1152]{1,0:T(8,128)(2,1)}, bf16[160,1152]{1,0:T(8,128)(2,1)S(1)}, u32[]{:S(2)}, u32[]{:S(2)}) collective-permute-start(bf16[160,1152]{1,0:T(8,128)(2,1)} %image.1), channel_id=1, source_target_pairs={{0,4},{1,5},{2,6},{3,7},{4,8},{5,9},{6,10},{7,11},{8,12},{9,13},{1... | collective-permute-start | bytes 1105928 | tf_op jit(solution)/shard_map/ppermute | solution.py:288
  3.6 1.5 %collective-permute-start.2 = (bf16[160,1152]{1,0:T(8,128)(2,1)}, bf16[160,1152]{1,0:T(8,128)(2,1)S(1)}, u32[]{:S(2)}, u32[]{:S(2)}) collective-permute-start(bf16[160,1152]{1,0:T(8,128)(2,1)} %text.1), channel_id=1, source_target_pairs={{0,1},{1,0},{2,3},{3,2},{4,5},{5,4},{6,7},{7,6},{8,9},{9,8},{10,11... | collective-permute-start | bytes 1105928 | tf_op jit(solution)/shard_map/ppermute | solution.py:288
  5.1 1.3 %unit.1 = (bf16[160,1152]{1,0:T(8,128)(2,1)S(1)}, bf16[160,1152]{1,0:T(8,128)(2,1)S(1)}, bf16[160,1152]{1,0:T(8,128)(2,1)S(1)}, bf16[160,1152]{1,0:T(8,128)(2,1)...) custom-call(bf16[160,1152]{1,0:T(8,128)(2,1)} %image.1, bf16[160,1152]{1,0:T(8,128)(2,1)} %text.1), custom_call_target="tpu_custom_call" | custom-call | tf_op jit(solution)/shard_map/unit/pallas_call | solution.py:250
  6.5 0.1 collective-permute-start
  6.6 0.5 %collective-permute-start.1 = (bf16[160,1152]{1,0:T(8,128)(2,1)S(1)}, bf16[160,1152]{1,0:T(8,128)(2,1)S(1)}, u32[]{:S(2)}, u32[]{:S(2)}) collective-permute-start(bf16[160,1152]{1,0:T(8,128)(2,1)S(1)} %get-tuple-element.23.text), channel_id=1, source_target_pairs={{0,2},{1,3},{2,0},{3,1},{4,6},{5,7},{6,4},{7,5},{8,10},{9,11},{10,... | collective-permute-start | bytes 1105928 | tf_op jit(solution)/shard_map/ppermute | solution.py:288
  8.3 1.1 %prep.1 = (f32[8,128]{1,0:T(8,128)S(1)}, s32[1,480]{1,0:T(1,128)S(1)}, s32[160,1]{1,0:T(8,128)S(1)}) custom-call(s32[40,128]{1,0:T(8,128)} %bitcast.9, f32[1,1]{1,0:T(1,128)} %bitcast.5.scale, f32[1,1]{1,0:T(1,128)} %bitcast.6.bias, f32[160,1]{1,0:T(8,128)S(1)} %get-tuple-element.18.after.image_inv.refs_1_), custom_call_target="tpu_custom_call" | custom-call | tf_op jit(solution)/shard_map/prep/pallas_call | solution.py:250
  9.5 6.0 %collective-permute-done.3.raw = bf16[160,1152]{1,0:T(8,128)(2,1)S(1)} collective-permute-done((bf16[160,1152]{1,0:T(8,128)(2,1)}, bf16[160,1152]{1,0:T(8,128)(2,1)S(1)}, u32[]{:S(2)}, u32[]{:S(2)}) %collective-permute-start.3) | collective-permute-done | bytes 368672 | tf_op jit(solution)/shard_map/ppermute | solution.py:288
  15.5 0.2 visit.1
  15.6 0.0 collective-permute-done.2.refs_0_
  15.6 0.0 collective-permute-done.mate_image
  15.6 0.0 collective-permute-done.1.mate_text
  15.7 1.0 %first.1 = (bf16[2,160,1152]{2,1,0:T(8,128)(2,1)S(1)}, bf16[1,160,1152]{2,1,0:T(8,128)(2,1)S(1)}) custom-call(f32[8,128]{1,0:T(8,128)S(1)} %get-tuple-element.19.after.params, s32[1,480]{1,0:T(1,128)S(1)} %get-tuple-element.20.row_targets, bf16[160,1152]{1,0:T(8,128)(2,1)S(1)} %get-tuple-element.22.image, bf16[160,1152]{1,0:T(8,128)(2,1)S(1)} %get-tuple-element.23.text, ...), custom_call_target="tpu_custom_call" | custom-call | tf_op jit(solution)/shard_map/first/pallas_call | solution.py:250
  16.7 0.1 collective-permute-start.4
  16.8 1.8 %collective-permute-start.5 = (bf16[160,1152]{1,0:T(8,128)(2,1)S(1)}, bf16[160,1152]{1,0:T(8,128)(2,1)S(1)}, u32[]{:S(2)}, u32[]{:S(2)}) collective-permute-start(bf16[160,1152]{1,0:T(8,128)(2,1)S(1)} %bitcast.8), channel_id=1, source_target_pairs={{0,28},{1,29},{2,3},{3,2},{4,0},{5,1},{6,7},{7,6},{8,4},{9,5},{10,... | collective-permute-start | bytes 1105928 | tf_op jit(solution)/shard_map/ppermute | solution.py:288
  18.6 0.4 %collective-permute-done.4.mate_got = bf16[2,160,1152]{2,1,0:T(8,128)(2,1)S(1)} collective-permute-done((bf16[2,160,1152]{2,1,0:T(8,128)(2,1)S(1)}, bf16[2,160,1152]{2,1,0:T(8,128)(2,1)S(1)}, u32[]{:S(2)}, u32[]{:S(2)}) %collective-permute-start.4) | collective-permute-done | bytes 737312 | tf_op jit(solution)/shard_map/ppermute | solution.py:288
  19.0 0.9 %second.1 = bf16[1,160,1152]{2,1,0:T(8,128)(2,1)S(1)} custom-call(f32[8,128]{1,0:T(8,128)S(1)} %get-tuple-element.19.after.params, s32[1,480]{1,0:T(1,128)S(1)} %get-tuple-element.20.row_targets, bf16[160,1152]{1,0:T(8,128)(2,1)S(1)} %get-tuple-element.22.image, bf16[160,1152]{1,0:T(8,128)(2,1)S(1)} %get-tuple-element.23.text, ...), custom_call_target="tpu_custom_call" | custom-call | tf_op jit(solution)/shard_map/second/pallas_call | solution.py:250
  19.9 1.6 %collective-permute-start.6 = (bf16[160,1152]{1,0:T(8,128)(2,1)S(1)}, bf16[160,1152]{1,0:T(8,128)(2,1)S(1)}, u32[]{:S(2)}, u32[]{:S(2)}) collective-permute-start(bf16[160,1152]{1,0:T(8,128)(2,1)S(1)} %bitcast.7), channel_id=1, source_target_pairs={{0,1},{1,0},{2,30},{3,31},{4,5},{5,4},{6,2},{7,3},{8,9},{9,8},{10,... | collective-permute-start | bytes 1105928 | tf_op jit(solution)/shard_map/ppermute | solution.py:288
  21.4 2.0 %third.1 = (f32[160,1152]{1,0:T(8,128)S(1)}, f32[160,1152]{1,0:T(8,128)S(1)}) custom-call(f32[8,128]{1,0:T(8,128)S(1)} %get-tuple-element.19.after.params, s32[1,480]{1,0:T(1,128)S(1)} %get-tuple-element.20.row_targets, s32[160,1]{1,0:T(8,128)S(1)} %get-tuple-element.21.targets, bf16[160,1152]{1,0:T(8,128)(2,1)S(1)} %get-tuple-element.22.image, ...), custom_call_target="tpu_custom_call" | custom-call | tf_op jit(solution)/shard_map/third/pallas_call | solution.py:250
  23.4 2.3 %collective-permute-done.5.refs_6_ = bf16[160,1152]{1,0:T(8,128)(2,1)S(1)} collective-permute-done((bf16[160,1152]{1,0:T(8,128)(2,1)S(1)}, bf16[160,1152]{1,0:T(8,128)(2,1)S(1)}, u32[]{:S(2)}, u32[]{:S(2)}) %collective-permute-start.5) | collective-permute-done | bytes 368672 | tf_op jit(solution)/shard_map/ppermute | solution.py:288
  25.8 0.4 %fourth.1.ready = f32[160,1152]{1,0:T(8,128)S(1)} custom-call(bf16[160,1152]{1,0:T(8,128)(2,1)S(1)} %get-tuple-element.17.image_raw.refs_0_, f32[160,1]{1,0:T(8,128)S(1)} %get-tuple-element.18.after.image_inv.refs_1_, f32[160,1152]{1,0:T(8,128)S(1)} %get-tuple-element.29.refs_2_, bf16[160,1152]{1,0:T(8,128)(2,1)S(1)} %get-tuple-element.27.text_raw.refs_3_, ...), custom_call_target="tpu_custom_call" | custom-call | tf_op jit(solution)/shard_map/fourth/pallas_call | solution.py:250
  26.1 1.6 %collective-permute-done.6.refs_6_ = bf16[160,1152]{1,0:T(8,128)(2,1)S(1)} collective-permute-done((bf16[160,1152]{1,0:T(8,128)(2,1)S(1)}, bf16[160,1152]{1,0:T(8,128)(2,1)S(1)}, u32[]{:S(2)}, u32[]{:S(2)}) %collective-permute-start.6) | collective-permute-done | bytes 368672 | tf_op jit(solution)/shard_map/ppermute | solution.py:288
  27.8 1.2 %last.1 = (f32[160,1152]{1,0:T(8,128)}, f32[160,1152]{1,0:T(8,128)}) custom-call(f32[160,1152]{1,0:T(8,128)S(1)} %fourth.1.ready, bf16[160,1152]{1,0:T(8,128)(2,1)S(1)} %get-tuple-element.17.image_raw.refs_0_, f32[160,1]{1,0:T(8,128)S(1)} %get-tuple-element.18.after.image_inv.refs_1_, f32[160,1152]{1,0:T(8,128)S(1)} %get-tuple-element.29.refs_2_, ...), custom_call_target="tpu_custom_call" | custom-call | tf_op jit(solution)/shard_map/last/pallas_call | solution.py:264
Async XLA Ops:
  0.6 14.8 %collective-permute-start.3 = (bf16[160,1152]{1,0:T(8,128)(2,1)}, bf16[160,1152]{1,0:T(8,128)(2,1)S(1)}, u32[]{:S(2)}, u32[]{:S(2)}) collective-permute-start(bf16[160,1152]{1,0:T(8,128)(2,1)} %image.1), channel_id=1, source_target_pairs={{0,4},{1,5},{2,6},{3,7},{4,8},{5,9},{6,10},{7,11},{8,12},{9,13},{1... | collective-permute-start | bytes 1105928 | tf_op jit(solution)/shard_map/ppermute | solution.py:288
  3.6 12.0 %collective-permute-start.2 = (bf16[160,1152]{1,0:T(8,128)(2,1)}, bf16[160,1152]{1,0:T(8,128)(2,1)S(1)}, u32[]{:S(2)}, u32[]{:S(2)}) collective-permute-start(bf16[160,1152]{1,0:T(8,128)(2,1)} %text.1), channel_id=1, source_target_pairs={{0,1},{1,0},{2,3},{3,2},{4,5},{5,4},{6,7},{7,6},{8,9},{9,8},{10,11... | collective-permute-start | bytes 1105928 | tf_op jit(solution)/shard_map/ppermute | solution.py:288
  6.5 9.2 %collective-permute-start = (bf16[160,1152]{1,0:T(8,128)(2,1)S(1)}, bf16[160,1152]{1,0:T(8,128)(2,1)S(1)}, u32[]{:S(2)}, u32[]{:S(2)}) collective-permute-start(bf16[160,1152]{1,0:T(8,128)(2,1)S(1)} %get-tuple-element.22.image), channel_id=1, source_target_pairs={{0,2},{1,3},{2,0},{3,1},{4,6},{5,7},{6,4},{7,5},{8,10},{9,11},{10,... | collective-permute-start | bytes 1105928 | tf_op jit(solution)/shard_map/ppermute | solution.py:288
  6.6 9.1 %collective-permute-start.1 = (bf16[160,1152]{1,0:T(8,128)(2,1)S(1)}, bf16[160,1152]{1,0:T(8,128)(2,1)S(1)}, u32[]{:S(2)}, u32[]{:S(2)}) collective-permute-start(bf16[160,1152]{1,0:T(8,128)(2,1)S(1)} %get-tuple-element.23.text), channel_id=1, source_target_pairs={{0,2},{1,3},{2,0},{3,1},{4,6},{5,7},{6,4},{7,5},{8,10},{9,11},{10,... | collective-permute-start | bytes 1105928 | tf_op jit(solution)/shard_map/ppermute | solution.py:288
  16.7 2.3 %collective-permute-start.4 = (bf16[2,160,1152]{2,1,0:T(8,128)(2,1)S(1)}, bf16[2,160,1152]{2,1,0:T(8,128)(2,1)S(1)}, u32[]{:S(2)}, u32[]{:S(2)}) collective-permute-start(bf16[2,160,1152]{2,1,0:T(8,128)(2,1)S(1)} %get-tuple-element.26.got), channel_id=1, source_target_pairs={{0,2},{1,3},{2,0},{3,1},{4,6},{5,7},{6,4},{7,5},{8,10},{9,11},{10,... | collective-permute-start | bytes 2211848 | tf_op jit(solution)/shard_map/ppermute | solution.py:288
  16.8 9.0 %collective-permute-start.5 = (bf16[160,1152]{1,0:T(8,128)(2,1)S(1)}, bf16[160,1152]{1,0:T(8,128)(2,1)S(1)}, u32[]{:S(2)}, u32[]{:S(2)}) collective-permute-start(bf16[160,1152]{1,0:T(8,128)(2,1)S(1)} %bitcast.8), channel_id=1, source_target_pairs={{0,28},{1,29},{2,3},{3,2},{4,0},{5,1},{6,7},{7,6},{8,4},{9,5},{10,... | collective-permute-start | bytes 1105928 | tf_op jit(solution)/shard_map/ppermute | solution.py:288
  19.9 7.9 %collective-permute-start.6 = (bf16[160,1152]{1,0:T(8,128)(2,1)S(1)}, bf16[160,1152]{1,0:T(8,128)(2,1)S(1)}, u32[]{:S(2)}, u32[]{:S(2)}) collective-permute-start(bf16[160,1152]{1,0:T(8,128)(2,1)S(1)} %bitcast.7), channel_id=1, source_target_pairs={{0,1},{1,0},{2,30},{3,31},{4,5},{5,4},{6,2},{7,3},{8,9},{9,8},{10,... | collective-permute-start | bytes 1105928 | tf_op jit(solution)/shard_map/ppermute | solution.py:288

commit v15 on v14

--- a/solution.py
+++ b/solution.py
@@ -121,16 +121,15 @@
     targets[...] = turned.astype(jnp.int32)
 
 
-def visit_kernel(raw, after, half):
-    half[...] = half_rows(raw)
+def halves_kernel(count, *refs):
+    raws, halves = refs[:count], refs[-count:]
+    for raw, half in zip(raws, halves):
+        half[...] = half_rows(raw)
 
 
 def first_kernel(far, params, row_targets, image, text, mate_image, mate_text, visit, *refs):
-    far_raw, got, back = refs[:far], refs[far], refs[far + 1]
-    far_text = [got.at[k + 1] for k in range(far)]
-    got[0] = visit[...]
-    for k in range(far):
-        far_text[k][...] = half_rows(far_raw[k])
+    far_text, mate_far = refs[:far], refs[far : 2 * far]
+    back, later = refs[2 * far :]
 
     def on_first(node):
         back[0] = drawn(params, visit, [text, *far_text]).astype(HALF)
@@ -140,17 +139,14 @@
             pairs = text_pairs(row_targets, lax.rem(node + k + 1, far + 1))
             images = [image, mate_image, visit]
             back[k] = drawn(params, far_text[k], images, pairs).astype(HALF)
+        texts = [text, *far_text, mate_text, *mate_far]
+        later[...] = drawn(params, visit, texts).astype(HALF)
 
     by_role(on_first, on_second)
 
 
-def parted(far, got):
-    return got.at[0], [got.at[k + 1] for k in range(far)]
-
-
-def second_kernel(far, params, row_targets, image, text, mate_text, got, mate_got, back):
-    visit, far_text = parted(far, got)
-    mate_visit, mate_far = parted(far, mate_got)
+def second_kernel(far, params, row_targets, image, visit, mate_visit, later, *refs):
+    far_text, back = refs[:far], refs[far]
 
     def on_first(node):
         for k in range(far):
@@ -159,8 +155,7 @@
             back[k] = drawn(params, far_text[k], images, pairs).astype(HALF)
 
     def on_second(node):
-        texts = [text, *far_text, mate_text, *mate_far]
-        back[0] = drawn(params, visit, texts).astype(HALF)
+        back[0] = later[...]
 
     by_role(on_first, on_second)
 
@@ -173,11 +168,10 @@
 
 
 def third_kernel(
-    far, params, row_targets, targets, image, text, mate_image, mate_text, got, mate_got,
-    image_raw, image_inv, text_raw, text_inv, image_part, text_part,
+    far, params, row_targets, targets, image, text, mate_image, mate_text, visit, mate_visit, *refs
 ):
-    visit, far_text = parted(far, got)
-    mate_visit, mate_far = parted(far, mate_got)
+    far_text, mate_far = refs[:far], refs[far : 2 * far]
+    image_raw, image_inv, text_raw, text_inv, image_part, text_part = refs[2 * far :]
     nodes = far + 1
 
     def on_first(node):
@@ -200,41 +194,47 @@
     by_role(on_first, on_second)
 
 
-def finished(far, received, own, count):
+def finish(received, own, count, out, start, stop):
     raw, inverse, part = own
-    gradient = received[0][...].astype(FULL)
-    for k in range(1, count):
-        gradient += received[k][...].astype(FULL)
-    inv = inverse[...]
-    values = raw[...].astype(FULL)
-    along = jnp.sum(values * gradient, axis=1, keepdims=True) * (inv * inv * inv)
-    return gradient * inv - values * along + part[...]
+    step = 16 if (stop - start) % 16 == 0 else stop - start
+    for at in range(start, stop, step):
+        piece = pl.ds(at, step)
+        gradient = received[0][piece, :].astype(FULL)
+        for k in range(1, count):
+            gradient += received[k][piece, :].astype(FULL)
+        inv = inverse[piece, :]
+        values = raw[piece, :].astype(FULL)
+        along = jnp.sum(values * gradient, axis=1, keepdims=True) * (inv * inv * inv)
+        out[piece, :] = gradient * inv - values * along + part[piece, :]
 
 
 def fourth_kernel(far, *refs):
     image, text, received, ready = refs[0:3], refs[3:6], refs[6 : 6 + far], refs[6 + far]
 
-    def on_first(node):
-        ready[...] = finished(far, received, image, 1)
-
-    def on_second(node):
-        ready[...] = finished(far, received, text, far)
-
-    by_role(on_first, on_second)
+    def run(own, count, node):
+        finish(received, own, count, ready, 0, ready.shape[0])
+
+    by_role(functools.partial(run, image, 1), functools.partial(run, text, far))
 
 
 def last_kernel(far, ready, *refs):
     image, text, received = refs[0:3], refs[3:6], refs[6 : 6 + far]
     image_grads, text_grads, held, sems = refs[6 + far :]
+    rows = held.shape[0]
+    part = rows // 2 if rows % 32 == 0 else rows
 
     def run(own, count, ready_out, out, node):
-        early = pltpu.make_async_copy(ready, ready_out, sems.at[0])
-        early.start()
-        held[...] = finished(far, received, own, count)
-        late = pltpu.make_async_copy(held, out, sems.at[1])
-        late.start()
-        early.wait()
-        late.wait()
+        copies = [pltpu.make_async_copy(ready, ready_out, sems.at[0])]
+        copies[0].start()
+        for i, at in enumerate(range(0, rows, part)):
+            finish(received, own, count, held, at, at + part)
+            piece = pl.ds(at, part)
+            copies.append(
+                pltpu.make_async_copy(held.at[piece], out.at[piece], sems.at[i + 1])
+            )
+            copies[-1].start()
+        for copy in copies:
+            copy.wait()
 
     by_role(
         functools.partial(run, text, far, image_grads, text_grads),
@@ -267,7 +267,7 @@
         out_shape=[jax.ShapeDtypeStruct(*block)] * 2,
         in_specs=[pl.BlockSpec(memory_space=pltpu.VMEM)] * len(operands),
         out_specs=[anywhere] * 2,
-        scratch_shapes=[pltpu.VMEM(*block), pltpu.SemaphoreType.DMA((2,))],
+        scratch_shapes=[pltpu.VMEM(*block), pltpu.SemaphoreType.DMA((3,))],
         compiler_params=pltpu.CompilerParams(vmem_limit_bytes=VMEM_LIMIT),
     )(*operands)
 
@@ -297,8 +297,8 @@
     column = ((rows, 1), FULL)
     returns = ((far, rows, width), HALF)
 
+    far_raw = [send(text_embeds, (0, -k), (0, -k)) for k in range(1, node_count)]
     visit_raw = send(image_embeds, ahead, ahead)
-    far_raw = [send(text_embeds, (0, -k), (0, -k)) for k in range(1, node_count)]
 
     image_raw, text_raw, image, text, image_inv, text_inv = call(
         unit_kernel,
@@ -319,28 +319,33 @@
         anywhere=1,
         scratch=[pltpu.VMEM(names.shape, jnp.int32), pltpu.SemaphoreType.DMA((1,))],
     )
-    (visit,) = call(visit_kernel, "visit", [visit_raw, params], [block_h])
-    *far_raw, visit = lax.optimization_barrier((*far_raw, visit))
-    got, back = call(
+    far_text = call(
+        functools.partial(halves_kernel, far), "far", [*far_raw, params], [block_h] * far
+    )
+    mate_far = [swap(block) for block in far_text]
+    visit_raw, *far_text = lax.optimization_barrier((visit_raw, *far_text))
+    (visit,) = call(functools.partial(halves_kernel, 1), "visit", [visit_raw], [block_h])
+    back, later = call(
         functools.partial(first_kernel, far),
         "first",
-        [params, row_targets, image, text, mate_image, mate_text, visit, *far_raw],
-        [((node_count, rows, width), HALF), returns],
+        [params, row_targets, image, text, mate_image, mate_text, visit, *far_text, *mate_far],
+        [returns, block_h],
     )
     one = [send(back[k], behind if k == 0 else stay, (0, k + 1)) for k in range(far)]
-    mate_got = swap(got)
+    visit, later = lax.optimization_barrier((visit, later))
+    mate_visit = swap(visit)
     (back,) = call(
         functools.partial(second_kernel, far),
         "second",
-        [params, row_targets, image, text, mate_text, got, mate_got],
+        [params, row_targets, image, visit, mate_visit, later, *far_text],
         [returns],
     )
     two = [send(back[k], (0, k + 1), behind if k == 0 else stay) for k in range(far)]
     image_part, text_part = call(
         functools.partial(third_kernel, far),
         "third",
-        [params, row_targets, targets, image, text, mate_image, mate_text, got, mate_got]
-        + [image_raw, image_inv, text_raw, text_inv],
+        [params, row_targets, targets, image, text, mate_image, mate_text, visit, mate_visit]
+        + [*far_text, *mate_far, image_raw, image_inv, text_raw, text_inv],
         [block_f, block_f],
     )
     own = [image_raw, image_inv, image_part, text_raw, text_inv, text_part]

time: 29.2 us -> 31.1 us (1.065)
  starting transfers between devices: 8.52 us -> 10 us
    ppermute x7 -> x8, starting transfers between devices: 8.52 us -> 10 us  [send(): return lax.ppermute(block, ('blk', 'node'), route)]
    ppermute x7 -> x8, waiting for transfers between devices: 10.4 us -> 10.7 us  [send(): return lax.ppermute(block, ('blk', 'node'), route)]
    pallas_call x7 -> x8, Pallas kernels: 6.86 us -> 6.88 us  [call(): pl.pallas_call(kernel, name=name, out_shape=[pltpu.VMEM(s, d) for s, d in...]
  transfers between devices with their start and end apart: 7 -> 8, of which waited for: 4 -> 3; matrix products, arithmetic and copies ran while one was open for 0% -> 0% of each run, Pallas kernels for 20% -> 19%
where the time goes in v15:
time: 31.1 us; the launch traced here: 30.9 us
  waiting for transfers between devices  10.7 us (34%)
  starting transfers between devices  10 us (32%)
  Pallas kernels  8.05 us (26%)
  between operations  2.04 us (7%)
    ppermute x8, waiting for transfers between devices, send(): return lax.ppermute(block, ('blk', 'node'), route)  10.7 us
    ppermute x8, starting transfers between devices, send(): return lax.ppermute(block, ('blk', 'node'), route)  10 us
    pallas_call x8, Pallas kernels, call(): pl.pallas_call(kernel, name=name, out_shape=[pltpu.VMEM(s, d) for s, d in...  6.88 us
    pallas_call x1, Pallas kernels, last(): pl.pallas_call(functools.partial(last_kernel, far), name='last', out_shap...  1.17 us
  transfers between devices with their start and end apart: 8, of which 3 were waited for; matrix products, arithmetic and copies ran while one was open for 0% of the time, Pallas kernels for 19%

profile of v15, /device:TPU:0, one launch (start us, length us, event | category | flops | bytes accessed | tf_op | source)
XLA Modules:
  0.0 30.9 jit_solution(3064250302572806014)
XLA Ops:
  0.6 3.0 %collective-permute-start.3 = (bf16[160,1152]{1,0:T(8,128)(2,1)}, bf16[160,1152]{1,0:T(8,128)(2,1)S(1)}, u32[]{:S(2)}, u32[]{:S(2)}) collective-permute-start(bf16[160,1152]{1,0:T(8,128)(2,1)} %text.1), channel_id=1, source_target_pairs={{0,1},{1,0},{2,3},{3,2},{4,5},{5,4},{6,7},{7,6},{8,9},{9,8},{10,11... | collective-permute-start | bytes 1105928 | tf_op jit(solution)/shard_map/ppermute | solution.py:288
  3.7 1.5 %collective-permute-start.2 = (bf16[160,1152]{1,0:T(8,128)(2,1)}, bf16[160,1152]{1,0:T(8,128)(2,1)S(1)}, u32[]{:S(2)}, u32[]{:S(2)}) collective-permute-start(bf16[160,1152]{1,0:T(8,128)(2,1)} %image.1), channel_id=1, source_target_pairs={{0,4},{1,5},{2,6},{3,7},{4,8},{5,9},{6,10},{7,11},{8,12},{9,13},{1... | collective-permute-start | bytes 1105928 | tf_op jit(solution)/shard_map/ppermute | solution.py:288
  5.2 1.4 %unit.1 = (bf16[160,1152]{1,0:T(8,128)(2,1)S(1)}, bf16[160,1152]{1,0:T(8,128)(2,1)S(1)}, bf16[160,1152]{1,0:T(8,128)(2,1)S(1)}, bf16[160,1152]{1,0:T(8,128)(2,1)...) custom-call(bf16[160,1152]{1,0:T(8,128)(2,1)} %image.1, bf16[160,1152]{1,0:T(8,128)(2,1)} %text.1), custom_call_target="tpu_custom_call" | custom-call | tf_op jit(solution)/shard_map/unit/pallas_call | solution.py:250
  6.5 0.1 collective-permute-start.1
  6.6 0.5 %collective-permute-start = (bf16[160,1152]{1,0:T(8,128)(2,1)S(1)}, bf16[160,1152]{1,0:T(8,128)(2,1)S(1)}, u32[]{:S(2)}, u32[]{:S(2)}) collective-permute-start(bf16[160,1152]{1,0:T(8,128)(2,1)S(1)} %get-tuple-element.24.image), channel_id=1, source_target_pairs={{0,2},{1,3},{2,0},{3,1},{4,6},{5,7},{6,4},{7,5},{8,10},{9,11},{10,... | collective-permute-start | bytes 1105928 | tf_op jit(solution)/shard_map/ppermute | solution.py:288
  8.4 1.1 %prep.1 = (f32[8,128]{1,0:T(8,128)S(1)}, s32[1,480]{1,0:T(1,128)S(1)}, s32[160,1]{1,0:T(8,128)S(1)}) custom-call(s32[40,128]{1,0:T(8,128)} %bitcast.9, f32[1,1]{1,0:T(1,128)} %bitcast.5.scale, f32[1,1]{1,0:T(1,128)} %bitcast.6.bias, f32[160,1]{1,0:T(8,128)S(1)} %get-tuple-element.20.after.refs_3_.refs_1_), custom_call_target="tpu_custom_call" | custom-call | tf_op jit(solution)/shard_map/prep/pallas_call | solution.py:250
  9.5 2.9 %collective-permute-done.3.refs_0_ = bf16[160,1152]{1,0:T(8,128)(2,1)S(1)} collective-permute-done((bf16[160,1152]{1,0:T(8,128)(2,1)}, bf16[160,1152]{1,0:T(8,128)(2,1)S(1)}, u32[]{:S(2)}, u32[]{:S(2)}) %collective-permute-start.3) | collective-permute-done | bytes 368672 | tf_op jit(solution)/shard_map/ppermute | solution.py:288
  12.5 0.2 far.1.refs_0_
  12.6 0.1 collective-permute-start.4
  12.7 4.0 %collective-permute-done.2.refs_0_ = bf16[160,1152]{1,0:T(8,128)(2,1)S(1)} collective-permute-done((bf16[160,1152]{1,0:T(8,128)(2,1)}, bf16[160,1152]{1,0:T(8,128)(2,1)S(1)}, u32[]{:S(2)}, u32[]{:S(2)}) %collective-permute-start.2) | collective-permute-done | bytes 368672 | tf_op jit(solution)/shard_map/ppermute | solution.py:288
  16.7 0.2 visit.1
  16.9 0.0 collective-permute-done.mate_image
  16.9 0.0 collective-permute-done.4.refs_1_
  16.9 0.9 %first.1 = (bf16[1,160,1152]{2,1,0:T(8,128)(2,1)S(1)}, bf16[160,1152]{1,0:T(8,128)(2,1)S(1)}) custom-call(f32[8,128]{1,0:T(8,128)S(1)} %get-tuple-element.21.refs_1_.params, s32[1,480]{1,0:T(1,128)S(1)} %get-tuple-element.22.row_targets, bf16[160,1152]{1,0:T(8,128)(2,1)S(1)} %get-tuple-element.24.image, bf16[160,1152]{1,0:T(8,128)(2,1)S(1)} %get-tuple-element.25.text, ...), custom_call_target="tpu_custom_call" | custom-call | tf_op jit(solution)/shard_map/first/pallas_call | solution.py:250
  17.8 0.1 collective-permute-start.5
  17.9 3.2 %collective-permute-start.6 = (bf16[160,1152]{1,0:T(8,128)(2,1)S(1)}, bf16[160,1152]{1,0:T(8,128)(2,1)S(1)}, u32[]{:S(2)}, u32[]{:S(2)}) collective-permute-start(bf16[160,1152]{1,0:T(8,128)(2,1)S(1)} %bitcast.8), channel_id=1, source_target_pairs={{0,28},{1,29},{2,3},{3,2},{4,0},{5,1},{6,7},{7,6},{8,4},{9,5},{10,... | collective-permute-start | bytes 1105928 | tf_op jit(solution)/shard_map/ppermute | solution.py:288
  21.1 0.0 collective-permute-done.5.mate_visit
  21.1 0.9 %second.1 = bf16[1,160,1152]{2,1,0:T(8,128)(2,1)S(1)} custom-call(f32[8,128]{1,0:T(8,128)S(1)} %get-tuple-element.21.refs_1_.params, s32[1,480]{1,0:T(1,128)S(1)} %get-tuple-element.22.row_targets, bf16[160,1152]{1,0:T(8,128)(2,1)S(1)} %get-tuple-element.24.image, bf16[160,1152]{1,0:T(8,128)(2,1)S(1)} %visit.1, ...), custom_call_target="tpu_custom_call" | custom-call | tf_op jit(solution)/shard_map/second/pallas_call | solution.py:250
  22.0 1.6 %collective-permute-start.7 = (bf16[160,1152]{1,0:T(8,128)(2,1)S(1)}, bf16[160,1152]{1,0:T(8,128)(2,1)S(1)}, u32[]{:S(2)}, u32[]{:S(2)}) collective-permute-start(bf16[160,1152]{1,0:T(8,128)(2,1)S(1)} %bitcast.7), channel_id=1, source_target_pairs={{0,1},{1,0},{2,30},{3,31},{4,5},{5,4},{6,2},{7,3},{8,9},{9,8},{10,... | collective-permute-start | bytes 1105928 | tf_op jit(solution)/shard_map/ppermute | solution.py:288
  23.6 2.0 %third.1 = (f32[160,1152]{1,0:T(8,128)S(1)}, f32[160,1152]{1,0:T(8,128)S(1)}) custom-call(f32[8,128]{1,0:T(8,128)S(1)} %get-tuple-element.21.refs_1_.params, s32[1,480]{1,0:T(1,128)S(1)} %get-tuple-element.22.row_targets, s32[160,1]{1,0:T(8,128)S(1)} %get-tuple-element.23.targets, bf16[160,1152]{1,0:T(8,128)(2,1)S(1)} %get-tuple-element.24.image, ...), custom_call_target="tpu_custom_call" | custom-call | tf_op jit(solution)/shard_map/third/pallas_call | solution.py:250
  25.6 3.8 %collective-permute-done.6.refs_6_ = bf16[160,1152]{1,0:T(8,128)(2,1)S(1)} collective-permute-done((bf16[160,1152]{1,0:T(8,128)(2,1)S(1)}, bf16[160,1152]{1,0:T(8,128)(2,1)S(1)}, u32[]{:S(2)}, u32[]{:S(2)}) %collective-permute-start.6) | collective-permute-done | bytes 368672 | tf_op jit(solution)/shard_map/ppermute | solution.py:288
  29.3 0.3 %fourth.1.ready = f32[160,1152]{1,0:T(8,128)S(1)} custom-call(bf16[160,1152]{1,0:T(8,128)(2,1)S(1)} %get-tuple-element.19.refs_2_.refs_0_, f32[160,1]{1,0:T(8,128)S(1)} %get-tuple-element.20.after.refs_3_.refs_1_, f32[160,1152]{1,0:T(8,128)S(1)} %get-tuple-element.32.refs_2_, bf16[160,1152]{1,0:T(8,128)(2,1)S(1)} %get-tuple-element.30.refs_4_.refs_3_, ...), custom_call_target="tpu_custom_call" | custom-call | tf_op jit(solution)/shard_map/fourth/pallas_call | solution.py:250
  29.7 0.0 collective-permute-done.7.refs_6_
  29.7 1.2 %last.1 = (f32[160,1152]{1,0:T(8,128)}, f32[160,1152]{1,0:T(8,128)}) custom-call(f32[160,1152]{1,0:T(8,128)S(1)} %fourth.1.ready, bf16[160,1152]{1,0:T(8,128)(2,1)S(1)} %get-tuple-element.19.refs_2_.refs_0_, f32[160,1]{1,0:T(8,128)S(1)} %get-tuple-element.20.after.refs_3_.refs_1_, f32[160,1152]{1,0:T(8,128)S(1)} %get-tuple-element.32.refs_2_, ...), custom_call_target="tpu_custom_call" | custom-call | tf_op jit(solution)/shard_map/last/pallas_call | solution.py:264
  (1 shorter events, 0.0 us)
Async XLA Ops:
  0.6 11.8 %collective-permute-start.3 = (bf16[160,1152]{1,0:T(8,128)(2,1)}, bf16[160,1152]{1,0:T(8,128)(2,1)S(1)}, u32[]{:S(2)}, u32[]{:S(2)}) collective-permute-start(bf16[160,1152]{1,0:T(8,128)(2,1)} %text.1), channel_id=1, source_target_pairs={{0,1},{1,0},{2,3},{3,2},{4,5},{5,4},{6,7},{7,6},{8,9},{9,8},{10,11... | collective-permute-start | bytes 1105928 | tf_op jit(solution)/shard_map/ppermute | solution.py:288
  3.7 13.0 %collective-permute-start.2 = (bf16[160,1152]{1,0:T(8,128)(2,1)}, bf16[160,1152]{1,0:T(8,128)(2,1)S(1)}, u32[]{:S(2)}, u32[]{:S(2)}) collective-permute-start(bf16[160,1152]{1,0:T(8,128)(2,1)} %image.1), channel_id=1, source_target_pairs={{0,4},{1,5},{2,6},{3,7},{4,8},{5,9},{6,10},{7,11},{8,12},{9,13},{1... | collective-permute-start | bytes 1105928 | tf_op jit(solution)/shard_map/ppermute | solution.py:288
  6.5 10.4 %collective-permute-start.1 = (bf16[160,1152]{1,0:T(8,128)(2,1)S(1)}, bf16[160,1152]{1,0:T(8,128)(2,1)S(1)}, u32[]{:S(2)}, u32[]{:S(2)}) collective-permute-start(bf16[160,1152]{1,0:T(8,128)(2,1)S(1)} %get-tuple-element.25.text), channel_id=1, source_target_pairs={{0,2},{1,3},{2,0},{3,1},{4,6},{5,7},{6,4},{7,5},{8,10},{9,11},{10,... | collective-permute-start | bytes 1105928 | tf_op jit(solution)/shard_map/ppermute | solution.py:288
  6.6 10.3 %collective-permute-start = (bf16[160,1152]{1,0:T(8,128)(2,1)S(1)}, bf16[160,1152]{1,0:T(8,128)(2,1)S(1)}, u32[]{:S(2)}, u32[]{:S(2)}) collective-permute-start(bf16[160,1152]{1,0:T(8,128)(2,1)S(1)} %get-tuple-element.24.image), channel_id=1, source_target_pairs={{0,2},{1,3},{2,0},{3,1},{4,6},{5,7},{6,4},{7,5},{8,10},{9,11},{10,... | collective-permute-start | bytes 1105928 | tf_op jit(solution)/shard_map/ppermute | solution.py:288
  12.6 4.3 %collective-permute-start.4 = (bf16[160,1152]{1,0:T(8,128)(2,1)S(1)}, bf16[160,1152]{1,0:T(8,128)(2,1)S(1)}, u32[]{:S(2)}, u32[]{:S(2)}) collective-permute-start(bf16[160,1152]{1,0:T(8,128)(2,1)S(1)} %far.1.refs_0_), channel_id=1, source_target_pairs={{0,2},{1,3},{2,0},{3,1},{4,6},{5,7},{6,4},{7,5},{8,10},{9,11},{10,... | collective-permute-start | bytes 1105928 | tf_op jit(solution)/shard_map/ppermute | solution.py:288
  17.8 3.3 %collective-permute-start.5 = (bf16[160,1152]{1,0:T(8,128)(2,1)S(1)}, bf16[160,1152]{1,0:T(8,128)(2,1)S(1)}, u32[]{:S(2)}, u32[]{:S(2)}) collective-permute-start(bf16[160,1152]{1,0:T(8,128)(2,1)S(1)} %visit.1), channel_id=1, source_target_pairs={{0,2},{1,3},{2,0},{3,1},{4,6},{5,7},{6,4},{7,5},{8,10},{9,11},{10,... | collective-permute-start | bytes 1105928 | tf_op jit(solution)/shard_map/ppermute | solution.py:288
  17.9 11.5 %collective-permute-start.6 = (bf16[160,1152]{1,0:T(8,128)(2,1)S(1)}, bf16[160,1152]{1,0:T(8,128)(2,1)S(1)}, u32[]{:S(2)}, u32[]{:S(2)}) collective-permute-start(bf16[160,1152]{1,0:T(8,128)(2,1)S(1)} %bitcast.8), channel_id=1, source_target_pairs={{0,28},{1,29},{2,3},{3,2},{4,0},{5,1},{6,7},{7,6},{8,4},{9,5},{10,... | collective-permute-start | bytes 1105928 | tf_op jit(solution)/shard_map/ppermute | solution.py:288
  22.0 7.7 %collective-permute-start.7 = (bf16[160,1152]{1,0:T(8,128)(2,1)S(1)}, bf16[160,1152]{1,0:T(8,128)(2,1)S(1)}, u32[]{:S(2)}, u32[]{:S(2)}) collective-permute-start(bf16[160,1152]{1,0:T(8,128)(2,1)S(1)} %bitcast.7), channel_id=1, source_target_pairs={{0,1},{1,0},{2,30},{3,31},{4,5},{5,4},{6,2},{7,3},{8,9},{9,8},{10,... | collective-permute-start | bytes 1105928 | tf_op jit(solution)/shard_map/ppermute | solution.py:288

commit v16 on v15

--- a/solution.py
+++ b/solution.py
@@ -121,15 +121,23 @@
     targets[...] = turned.astype(jnp.int32)
 
 
-def halves_kernel(count, *refs):
-    raws, halves = refs[:count], refs[-count:]
-    for raw, half in zip(raws, halves):
-        half[...] = half_rows(raw)
-
-
-def first_kernel(far, params, row_targets, image, text, mate_image, mate_text, visit, *refs):
-    far_text, mate_far = refs[:far], refs[far : 2 * far]
-    back, later = refs[2 * far :]
+def visit_kernel(raw, after, half):
+    half[...] = half_rows(raw)
+
+
+def got_kernel(far, visit, *refs):
+    got = refs[-1]
+    got[0] = visit[...]
+    for k in range(far):
+        got[k + 1] = half_rows(refs[k])
+
+
+def parted(far, got):
+    return got.at[0], [got.at[k + 1] for k in range(far)]
+
+
+def first_kernel(far, params, row_targets, image, text, mate_image, mate_text, got, back):
+    visit, far_text = parted(far, got)
 
     def on_first(node):
         back[0] = drawn(params, visit, [text, *far_text]).astype(HALF)
@@ -139,14 +147,13 @@
             pairs = text_pairs(row_targets, lax.rem(node + k + 1, far + 1))
             images = [image, mate_image, visit]
             back[k] = drawn(params, far_text[k], images, pairs).astype(HALF)
-        texts = [text, *far_text, mate_text, *mate_far]
-        later[...] = drawn(params, visit, texts).astype(HALF)
 
     by_role(on_first, on_second)
 
 
-def second_kernel(far, params, row_targets, image, visit, mate_visit, later, *refs):
-    far_text, back = refs[:far], refs[far]
+def second_kernel(far, params, row_targets, image, text, mate_text, got, mate_got, back):
+    visit, far_text = parted(far, got)
+    mate_visit, mate_far = parted(far, mate_got)
 
     def on_first(node):
         for k in range(far):
@@ -155,7 +162,8 @@
             back[k] = drawn(params, far_text[k], images, pairs).astype(HALF)
 
     def on_second(node):
-        back[0] = later[...]
+        texts = [text, *far_text, mate_text, *mate_far]
+        back[0] = drawn(params, visit, texts).astype(HALF)
 
     by_role(on_first, on_second)
 
@@ -168,10 +176,11 @@
 
 
 def third_kernel(
-    far, params, row_targets, targets, image, text, mate_image, mate_text, visit, mate_visit, *refs
+    far, params, row_targets, targets, image, text, mate_image, mate_text, got, mate_got,
+    image_raw, image_inv, text_raw, text_inv, image_part, text_part,
 ):
-    far_text, mate_far = refs[:far], refs[far : 2 * far]
-    image_raw, image_inv, text_raw, text_inv, image_part, text_part = refs[2 * far :]
+    visit, far_text = parted(far, got)
+    mate_visit, mate_far = parted(far, mate_got)
     nodes = far + 1
 
     def on_first(node):
@@ -297,8 +306,8 @@
     column = ((rows, 1), FULL)
     returns = ((far, rows, width), HALF)
 
+    visit_raw = send(image_embeds, ahead, ahead)
     far_raw = [send(text_embeds, (0, -k), (0, -k)) for k in range(1, node_count)]
-    visit_raw = send(image_embeds, ahead, ahead)
 
     image_raw, text_raw, image, text, image_inv, text_inv = call(
         unit_kernel,
@@ -319,33 +328,34 @@
         anywhere=1,
         scratch=[pltpu.VMEM(names.shape, jnp.int32), pltpu.SemaphoreType.DMA((1,))],
     )
-    far_text = call(
-        functools.partial(halves_kernel, far), "far", [*far_raw, params], [block_h] * far
-    )
-    mate_far = [swap(block) for block in far_text]
-    visit_raw, *far_text = lax.optimization_barrier((visit_raw, *far_text))
-    (visit,) = call(functools.partial(halves_kernel, 1), "visit", [visit_raw], [block_h])
-    back, later = call(
+    (visit,) = call(visit_kernel, "visit", [visit_raw, params], [block_h])
+    *far_raw, visit = lax.optimization_barrier((*far_raw, visit))
+    (got,) = call(
+        functools.partial(got_kernel, far),
+        "got",
+        [visit, *far_raw, mate_image, mate_text],
+        [((node_count, rows, width), HALF)],
+    )
+    (back,) = call(
         functools.partial(first_kernel, far),
         "first",
-        [params, row_targets, image, text, mate_image, mate_text, visit, *far_text, *mate_far],
-        [returns, block_h],
+        [params, row_targets, image, text, mate_image, mate_text, got],
+        [returns],
     )
     one = [send(back[k], behind if k == 0 else stay, (0, k + 1)) for k in range(far)]
-    visit, later = lax.optimization_barrier((visit, later))
-    mate_visit = swap(visit)
+    mate_got = swap(got)
     (back,) = call(
         functools.partial(second_kernel, far),
         "second",
-        [params, row_targets, image, visit, mate_visit, later, *far_text],
+        [params, row_targets, image, text, mate_text, got, mate_got],
         [returns],
     )
     two = [send(back[k], (0, k + 1), behind if k == 0 else stay) for k in range(far)]
     image_part, text_part = call(
         functools.partial(third_kernel, far),
         "third",
-        [params, row_targets, targets, image, text, mate_image, mate_text, visit, mate_visit]
-        + [*far_text, *mate_far, image_raw, image_inv, text_raw, text_inv],
+        [params, row_targets, targets, image, text, mate_image, mate_text, got, mate_got]
+        + [image_raw, image_inv, text_raw, text_inv],
         [block_f, block_f],
     )
     own = [image_raw, image_inv, image_part, text_raw, text_inv, text_part]

time: 31.1 us -> 29.2 us (0.939)
  starting transfers between devices: 10 us -> 8.51 us
    ppermute x8 -> x7, starting transfers between devices: 10 us -> 8.51 us  [send(): return lax.ppermute(block, ('blk', 'node'), route)]
    ppermute x8 -> x7, waiting for transfers between devices: 10.7 us -> 10.4 us  [send(): return lax.ppermute(block, ('blk', 'node'), route)]
  transfers between devices with their start and end apart: 8 -> 7, of which waited for: 3 -> 3; matrix products, arithmetic and copies ran while one was open for 0% -> 0% of each run, Pallas kernels for 19% -> 23%
where the time goes in v16:
time: 29.2 us; the launch traced here: 29 us
  waiting for transfers between devices  10.4 us (36%)
  starting transfers between devices  8.51 us (29%)
  Pallas kernels  8 us (27%)
  between operations  2.03 us (7%)
    ppermute x7, waiting for transfers between devices, send(): return lax.ppermute(block, ('blk', 'node'), route)  10.4 us
    ppermute x7, starting transfers between devices, send(): return lax.ppermute(block, ('blk', 'node'), route)  8.51 us
    pallas_call x8, Pallas kernels, call(): pl.pallas_call(kernel, name=name, out_shape=[pltpu.VMEM(s, d) for s, d in...  6.85 us
    pallas_call x1, Pallas kernels, last(): pl.pallas_call(functools.partial(last_kernel, far), name='last', out_shap...  1.16 us
  transfers between devices with their start and end apart: 7, of which 3 were waited for; matrix products, arithmetic and copies ran while one was open for 0% of the time, Pallas kernels for 23%

profile of v16, /device:TPU:0, one launch (start us, length us, event | category | flops | bytes accessed | tf_op | source)
XLA Modules:
  0.0 29.0 jit_solution(5826686969568280784)
XLA Ops:
  0.6 3.0 %collective-permute-start.3 = (bf16[160,1152]{1,0:T(8,128)(2,1)}, bf16[160,1152]{1,0:T(8,128)(2,1)S(1)}, u32[]{:S(2)}, u32[]{:S(2)}) collective-permute-start(bf16[160,1152]{1,0:T(8,128)(2,1)} %image.1), channel_id=1, source_target_pairs={{0,4},{1,5},{2,6},{3,7},{4,8},{5,9},{6,10},{7,11},{8,12},{9,13},{1... | collective-permute-start | bytes 1105928 | tf_op jit(solution)/shard_map/ppermute | solution.py:297
  3.6 1.5 %collective-permute-start.2 = (bf16[160,1152]{1,0:T(8,128)(2,1)}, bf16[160,1152]{1,0:T(8,128)(2,1)S(1)}, u32[]{:S(2)}, u32[]{:S(2)}) collective-permute-start(bf16[160,1152]{1,0:T(8,128)(2,1)} %text.1), channel_id=1, source_target_pairs={{0,1},{1,0},{2,3},{3,2},{4,5},{5,4},{6,7},{7,6},{8,9},{9,8},{10,11... | collective-permute-start | bytes 1105928 | tf_op jit(solution)/shard_map/ppermute | solution.py:297
  5.1 1.3 %unit.1 = (bf16[160,1152]{1,0:T(8,128)(2,1)S(1)}, bf16[160,1152]{1,0:T(8,128)(2,1)S(1)}, bf16[160,1152]{1,0:T(8,128)(2,1)S(1)}, bf16[160,1152]{1,0:T(8,128)(2,1)...) custom-call(bf16[160,1152]{1,0:T(8,128)(2,1)} %image.1, bf16[160,1152]{1,0:T(8,128)(2,1)} %text.1), custom_call_target="tpu_custom_call" | custom-call | tf_op jit(solution)/shard_map/unit/pallas_call | solution.py:259
  6.5 0.1 collective-permute-start
  6.6 0.5 %collective-permute-start.1 = (bf16[160,1152]{1,0:T(8,128)(2,1)S(1)}, bf16[160,1152]{1,0:T(8,128)(2,1)S(1)}, u32[]{:S(2)}, u32[]{:S(2)}) collective-permute-start(bf16[160,1152]{1,0:T(8,128)(2,1)S(1)} %get-tuple-element.21.text), channel_id=1, source_target_pairs={{0,2},{1,3},{2,0},{3,1},{4,6},{5,7},{6,4},{7,5},{8,10},{9,11},{10,... | collective-permute-start | bytes 1105928 | tf_op jit(solution)/shard_map/ppermute | solution.py:297
  8.3 1.1 %prep.1 = (f32[8,128]{1,0:T(8,128)S(1)}, s32[1,480]{1,0:T(1,128)S(1)}, s32[160,1]{1,0:T(8,128)S(1)}) custom-call(s32[40,128]{1,0:T(8,128)} %bitcast.9, f32[1,1]{1,0:T(1,128)} %bitcast.5.scale, f32[1,1]{1,0:T(1,128)} %bitcast.6.bias, f32[160,1]{1,0:T(8,128)S(1)} %get-tuple-element.16.after.image_inv.refs_1_), custom_call_target="tpu_custom_call" | custom-call | tf_op jit(solution)/shard_map/prep/pallas_call | solution.py:259
  9.5 6.0 %collective-permute-done.3.raw = bf16[160,1152]{1,0:T(8,128)(2,1)S(1)} collective-permute-done((bf16[160,1152]{1,0:T(8,128)(2,1)}, bf16[160,1152]{1,0:T(8,128)(2,1)S(1)}, u32[]{:S(2)}, u32[]{:S(2)}) %collective-permute-start.3) | collective-permute-done | bytes 368672 | tf_op jit(solution)/shard_map/ppermute | solution.py:297
  15.5 0.2 visit.1
  15.6 0.0 collective-permute-done.2.refs_0_
  15.6 0.0 collective-permute-done.refs_1_.mate_image
  15.6 0.0 collective-permute-done.1.refs_2_.mate_text
  15.7 0.2 got.1
  15.8 0.1 collective-permute-start.4
  15.9 0.9 %first.1 = bf16[1,160,1152]{2,1,0:T(8,128)(2,1)S(1)} custom-call(f32[8,128]{1,0:T(8,128)S(1)} %get-tuple-element.17.after.params, s32[1,480]{1,0:T(1,128)S(1)} %get-tuple-element.18.row_targets, bf16[160,1152]{1,0:T(8,128)(2,1)S(1)} %get-tuple-element.20.image, bf16[160,1152]{1,0:T(8,128)(2,1)S(1)} %get-tuple-element.21.text, ...), custom_call_target="tpu_custom_call" | custom-call | tf_op jit(solution)/shard_map/first/pallas_call | solution.py:259
  16.8 1.8 %collective-permute-start.5 = (bf16[160,1152]{1,0:T(8,128)(2,1)S(1)}, bf16[160,1152]{1,0:T(8,128)(2,1)S(1)}, u32[]{:S(2)}, u32[]{:S(2)}) collective-permute-start(bf16[160,1152]{1,0:T(8,128)(2,1)S(1)} %bitcast.8), channel_id=1, source_target_pairs={{0,28},{1,29},{2,3},{3,2},{4,0},{5,1},{6,7},{7,6},{8,4},{9,5},{10,... | collective-permute-start | bytes 1105928 | tf_op jit(solution)/shard_map/ppermute | solution.py:297
  18.6 0.0 collective-permute-done.4.mate_got
  18.6 0.9 %second.1 = bf16[1,160,1152]{2,1,0:T(8,128)(2,1)S(1)} custom-call(f32[8,128]{1,0:T(8,128)S(1)} %get-tuple-element.17.after.params, s32[1,480]{1,0:T(1,128)S(1)} %get-tuple-element.18.row_targets, bf16[160,1152]{1,0:T(8,128)(2,1)S(1)} %get-tuple-element.20.image, bf16[160,1152]{1,0:T(8,128)(2,1)S(1)} %get-tuple-element.21.text, ...), custom_call_target="tpu_custom_call" | custom-call | tf_op jit(solution)/shard_map/second/pallas_call | solution.py:259
  19.5 1.6 %collective-permute-start.6 = (bf16[160,1152]{1,0:T(8,128)(2,1)S(1)}, bf16[160,1152]{1,0:T(8,128)(2,1)S(1)}, u32[]{:S(2)}, u32[]{:S(2)}) collective-permute-start(bf16[160,1152]{1,0:T(8,128)(2,1)S(1)} %bitcast.7), channel_id=1, source_target_pairs={{0,1},{1,0},{2,30},{3,31},{4,5},{5,4},{6,2},{7,3},{8,9},{9,8},{10,... | collective-permute-start | bytes 1105928 | tf_op jit(solution)/shard_map/ppermute | solution.py:297
  21.1 2.0 %third.1 = (f32[160,1152]{1,0:T(8,128)S(1)}, f32[160,1152]{1,0:T(8,128)S(1)}) custom-call(f32[8,128]{1,0:T(8,128)S(1)} %get-tuple-element.17.after.params, s32[1,480]{1,0:T(1,128)S(1)} %get-tuple-element.18.row_targets, s32[160,1]{1,0:T(8,128)S(1)} %get-tuple-element.19.targets, bf16[160,1152]{1,0:T(8,128)(2,1)S(1)} %get-tuple-element.20.image, ...), custom_call_target="tpu_custom_call" | custom-call | tf_op jit(solution)/shard_map/third/pallas_call | solution.py:259
  23.0 3.3 %collective-permute-done.5.refs_6_ = bf16[160,1152]{1,0:T(8,128)(2,1)S(1)} collective-permute-done((bf16[160,1152]{1,0:T(8,128)(2,1)S(1)}, bf16[160,1152]{1,0:T(8,128)(2,1)S(1)}, u32[]{:S(2)}, u32[]{:S(2)}) %collective-permute-start.5) | collective-permute-done | bytes 368672 | tf_op jit(solution)/shard_map/ppermute | solution.py:297
  26.3 0.3 %fourth.1.ready = f32[160,1152]{1,0:T(8,128)S(1)} custom-call(bf16[160,1152]{1,0:T(8,128)(2,1)S(1)} %get-tuple-element.15.image_raw.refs_0_, f32[160,1]{1,0:T(8,128)S(1)} %get-tuple-element.16.after.image_inv.refs_1_, f32[160,1152]{1,0:T(8,128)S(1)} %get-tuple-element.26.refs_2_, bf16[160,1152]{1,0:T(8,128)(2,1)S(1)} %get-tuple-element.24.text_raw.refs_3_, ...), custom_call_target="tpu_custom_call" | custom-call | tf_op jit(solution)/shard_map/fourth/pallas_call | solution.py:259
  26.7 1.1 %collective-permute-done.6.refs_6_ = bf16[160,1152]{1,0:T(8,128)(2,1)S(1)} collective-permute-done((bf16[160,1152]{1,0:T(8,128)(2,1)S(1)}, bf16[160,1152]{1,0:T(8,128)(2,1)S(1)}, u32[]{:S(2)}, u32[]{:S(2)}) %collective-permute-start.6) | collective-permute-done | bytes 368672 | tf_op jit(solution)/shard_map/ppermute | solution.py:297
  27.8 1.2 %last.1 = (f32[160,1152]{1,0:T(8,128)}, f32[160,1152]{1,0:T(8,128)}) custom-call(f32[160,1152]{1,0:T(8,128)S(1)} %fourth.1.ready, bf16[160,1152]{1,0:T(8,128)(2,1)S(1)} %get-tuple-element.15.image_raw.refs_0_, f32[160,1]{1,0:T(8,128)S(1)} %get-tuple-element.16.after.image_inv.refs_1_, f32[160,1152]{1,0:T(8,128)S(1)} %get-tuple-element.26.refs_2_, ...), custom_call_target="tpu_custom_call" | custom-call | tf_op jit(solution)/shard_map/last/pallas_call | solution.py:273
Async XLA Ops:
  0.6 14.8 %collective-permute-start.3 = (bf16[160,1152]{1,0:T(8,128)(2,1)}, bf16[160,1152]{1,0:T(8,128)(2,1)S(1)}, u32[]{:S(2)}, u32[]{:S(2)}) collective-permute-start(bf16[160,1152]{1,0:T(8,128)(2,1)} %image.1), channel_id=1, source_target_pairs={{0,4},{1,5},{2,6},{3,7},{4,8},{5,9},{6,10},{7,11},{8,12},{9,13},{1... | collective-permute-start | bytes 1105928 | tf_op jit(solution)/shard_map/ppermute | solution.py:297
  3.6 12.0 %collective-permute-start.2 = (bf16[160,1152]{1,0:T(8,128)(2,1)}, bf16[160,1152]{1,0:T(8,128)(2,1)S(1)}, u32[]{:S(2)}, u32[]{:S(2)}) collective-permute-start(bf16[160,1152]{1,0:T(8,128)(2,1)} %text.1), channel_id=1, source_target_pairs={{0,1},{1,0},{2,3},{3,2},{4,5},{5,4},{6,7},{7,6},{8,9},{9,8},{10,11... | collective-permute-start | bytes 1105928 | tf_op jit(solution)/shard_map/ppermute | solution.py:297
  6.5 9.2 %collective-permute-start = (bf16[160,1152]{1,0:T(8,128)(2,1)S(1)}, bf16[160,1152]{1,0:T(8,128)(2,1)S(1)}, u32[]{:S(2)}, u32[]{:S(2)}) collective-permute-start(bf16[160,1152]{1,0:T(8,128)(2,1)S(1)} %get-tuple-element.20.image), channel_id=1, source_target_pairs={{0,2},{1,3},{2,0},{3,1},{4,6},{5,7},{6,4},{7,5},{8,10},{9,11},{10,... | collective-permute-start | bytes 1105928 | tf_op jit(solution)/shard_map/ppermute | solution.py:297
  6.6 9.1 %collective-permute-start.1 = (bf16[160,1152]{1,0:T(8,128)(2,1)S(1)}, bf16[160,1152]{1,0:T(8,128)(2,1)S(1)}, u32[]{:S(2)}, u32[]{:S(2)}) collective-permute-start(bf16[160,1152]{1,0:T(8,128)(2,1)S(1)} %get-tuple-element.21.text), channel_id=1, source_target_pairs={{0,2},{1,3},{2,0},{3,1},{4,6},{5,7},{6,4},{7,5},{8,10},{9,11},{10,... | collective-permute-start | bytes 1105928 | tf_op jit(solution)/shard_map/ppermute | solution.py:297
  15.8 2.8 %collective-permute-start.4 = (bf16[2,160,1152]{2,1,0:T(8,128)(2,1)S(1)}, bf16[2,160,1152]{2,1,0:T(8,128)(2,1)S(1)}, u32[]{:S(2)}, u32[]{:S(2)}) collective-permute-start(bf16[2,160,1152]{2,1,0:T(8,128)(2,1)S(1)} %got.1), channel_id=1, source_target_pairs={{0,2},{1,3},{2,0},{3,1},{4,6},{5,7},{6,4},{7,5},{8,10},{9,11},{10,... | collective-permute-start | bytes 2211848 | tf_op jit(solution)/shard_map/ppermute | solution.py:297
  16.8 9.5 %collective-permute-start.5 = (bf16[160,1152]{1,0:T(8,128)(2,1)S(1)}, bf16[160,1152]{1,0:T(8,128)(2,1)S(1)}, u32[]{:S(2)}, u32[]{:S(2)}) collective-permute-start(bf16[160,1152]{1,0:T(8,128)(2,1)S(1)} %bitcast.8), channel_id=1, source_target_pairs={{0,28},{1,29},{2,3},{3,2},{4,0},{5,1},{6,7},{7,6},{8,4},{9,5},{10,... | collective-permute-start | bytes 1105928 | tf_op jit(solution)/shard_map/ppermute | solution.py:297
  19.5 8.3 %collective-permute-start.6 = (bf16[160,1152]{1,0:T(8,128)(2,1)S(1)}, bf16[160,1152]{1,0:T(8,128)(2,1)S(1)}, u32[]{:S(2)}, u32[]{:S(2)}) collective-permute-start(bf16[160,1152]{1,0:T(8,128)(2,1)S(1)} %bitcast.7), channel_id=1, source_target_pairs={{0,1},{1,0},{2,30},{3,31},{4,5},{5,4},{6,2},{7,3},{8,9},{9,8},{10,... | collective-permute-start | bytes 1105928 | tf_op jit(solution)/shard_map/ppermute | solution.py:297

commit v17 on v16

--- a/solution.py
+++ b/solution.py
@@ -23,44 +23,39 @@
     pl.when(jnp.logical_not(first))(functools.partial(on_second, node))
 
 
-def drawn(params, rows, partners, paired=None):
-    vectors = jnp.concatenate([partner[...] for partner in partners], axis=0)
-    dots = lax.dot_general(
-        rows[...], vectors, (((1,), (1,)), ((), ())), preferred_element_type=FULL
-    )
+def drawn(params, rows, partners, paired=()):
     scale, bias = params[0:1, 0:1], params[1:2, 0:1]
-    logits = scale * dots + bias
-    if paired is None:
-        weights = scale * jax.nn.sigmoid(logits)
-    else:
-        pairs = paired(logits.shape)
-        weights = jnp.where(pairs, -scale, scale) * jax.nn.sigmoid(
-            jnp.where(pairs, -logits, logits)
+    total = None
+    for i, partner in enumerate(partners):
+        dots = lax.dot_general(
+            rows[...], partner[...], (((1,), (1,)), ((), ())), preferred_element_type=FULL
         )
-    return jnp.dot(weights.astype(HALF), vectors, preferred_element_type=FULL)
+        logits = scale * dots + bias
+        if i < len(paired):
+            pairs = paired[i](logits.shape)
+            weights = jnp.where(pairs, -scale, scale) * jax.nn.sigmoid(
+                jnp.where(pairs, -logits, logits)
+            )
+        else:
+            weights = scale * jax.nn.sigmoid(logits)
+        term = jnp.dot(weights.astype(HALF), partner[...], preferred_element_type=FULL)
+        total = term if total is None else total + term
+    return total
 
 
 def text_pairs(targets, node):
     def paired(shape):
-        rows = shape[0]
-        names = lax.broadcasted_iota(jnp.int32, shape, 0) + node * rows
-        return names == targets[:, : shape[1]]
-
-    return paired
+        return lax.broadcasted_iota(jnp.int32, shape, 0) + node * shape[0] == targets[...]
+
+    return [paired]
 
 
 def image_pairs(targets, node, nodes):
-    def paired(shape):
-        rows = shape[0]
-        columns = lax.broadcasted_iota(jnp.int32, shape, 1)
-        names = jnp.where(columns < nodes * rows, columns, -1 - nodes * rows)
-        for k in range(nodes):
-            here = jnp.logical_and(columns >= k * rows, columns < (k + 1) * rows)
-            shift = (lax.rem(node + k, nodes) - k) * rows
-            names = jnp.where(here, columns + shift, names)
+    def one(other, shape):
+        names = lax.broadcasted_iota(jnp.int32, shape, 1) + other * shape[1]
         return names == targets[...]
 
-    return paired
+    return [functools.partial(one, lax.rem(node + k, nodes)) for k in range(nodes)]
 
 
 def inverse_of(values):
@@ -111,8 +106,7 @@
     for at in range(step, 128, step):
         mine = jnp.where(lax.rem(start, 128) == at, window[:, at : at + rows], mine)
     mine = mine - group * nodes * rows
-    row_targets[...] = jnp.full(row_targets.shape, -1, jnp.int32)
-    row_targets[:, :rows] = mine
+    row_targets[...] = mine
     square = (rows, rows)
     same = lax.broadcasted_iota(jnp.int32, square, 0) == lax.broadcasted_iota(
         jnp.int32, square, 1
@@ -324,7 +318,7 @@
         prep_kernel,
         "prep",
         [names, similarity_scale[:, None], logit_bias[:, None], image_inv],
-        [((8, 128), FULL), ((1, 3 * rows), jnp.int32), ((rows, 1), jnp.int32)],
+        [((8, 128), FULL), ((1, rows), jnp.int32), ((rows, 1), jnp.int32)],
         anywhere=1,
         scratch=[pltpu.VMEM(names.shape, jnp.int32), pltpu.SemaphoreType.DMA((1,))],
     )

time: 29.2 us -> 29.5 us (1.010)
  Pallas kernels: 8 us -> 8.96 us
  waiting for transfers between devices: 10.4 us -> 9.8 us
    pallas_call x8, Pallas kernels: 6.85 us -> 7.8 us  [call(): pl.pallas_call(kernel, name=name, out_shape=[pltpu.VMEM(s, d) for s, d in...]
    ppermute x7, waiting for transfers between devices: 10.4 us -> 9.8 us  [send(): return lax.ppermute(block, ('blk', 'node'), route)]
  transfers between devices with their start and end apart: 7 -> 7, of which waited for: 3 -> 3; matrix products, arithmetic and copies ran while one was open for 0% -> 0% of each run, Pallas kernels for 23% -> 26%
where the time goes in v17:
time: 29.5 us; the launch traced here: 29.3 us
  waiting for transfers between devices  9.8 us (33%)
  Pallas kernels  8.96 us (30%)
  starting transfers between devices  8.51 us (29%)
  between operations  2.03 us (7%)
    ppermute x7, waiting for transfers between devices, send(): return lax.ppermute(block, ('blk', 'node'), route)  9.8 us
    ppermute x7, starting transfers between devices, send(): return lax.ppermute(block, ('blk', 'node'), route)  8.51 us
    pallas_call x8, Pallas kernels, call(): pl.pallas_call(kernel, name=name, out_shape=[pltpu.VMEM(s, d) for s, d in...  7.8 us
    pallas_call x1, Pallas kernels, last(): pl.pallas_call(functools.partial(last_kernel, far), name='last', out_shap...  1.16 us
  transfers between devices with their start and end apart: 7, of which 3 were waited for; matrix products, arithmetic and copies ran while one was open for 0% of the time, Pallas kernels for 26%

profile of v17, /device:TPU:0, one launch (start us, length us, event | category | flops | bytes accessed | tf_op | source)
XLA Modules:
  0.0 29.3 jit_solution(12195778868403989391)
XLA Ops:
  0.6 3.0 %collective-permute-start.3 = (bf16[160,1152]{1,0:T(8,128)(2,1)}, bf16[160,1152]{1,0:T(8,128)(2,1)S(1)}, u32[]{:S(2)}, u32[]{:S(2)}) collective-permute-start(bf16[160,1152]{1,0:T(8,128)(2,1)} %image.1), channel_id=1, source_target_pairs={{0,4},{1,5},{2,6},{3,7},{4,8},{5,9},{6,10},{7,11},{8,12},{9,13},{1... | collective-permute-start | bytes 1105928 | tf_op jit(solution)/shard_map/ppermute | solution.py:291
  3.6 1.5 %collective-permute-start.2 = (bf16[160,1152]{1,0:T(8,128)(2,1)}, bf16[160,1152]{1,0:T(8,128)(2,1)S(1)}, u32[]{:S(2)}, u32[]{:S(2)}) collective-permute-start(bf16[160,1152]{1,0:T(8,128)(2,1)} %text.1), channel_id=1, source_target_pairs={{0,1},{1,0},{2,3},{3,2},{4,5},{5,4},{6,7},{7,6},{8,9},{9,8},{10,11... | collective-permute-start | bytes 1105928 | tf_op jit(solution)/shard_map/ppermute | solution.py:291
  5.1 1.3 %unit.1 = (bf16[160,1152]{1,0:T(8,128)(2,1)S(1)}, bf16[160,1152]{1,0:T(8,128)(2,1)S(1)}, bf16[160,1152]{1,0:T(8,128)(2,1)S(1)}, bf16[160,1152]{1,0:T(8,128)(2,1)...) custom-call(bf16[160,1152]{1,0:T(8,128)(2,1)} %image.1, bf16[160,1152]{1,0:T(8,128)(2,1)} %text.1), custom_call_target="tpu_custom_call" | custom-call | tf_op jit(solution)/shard_map/unit/pallas_call | solution.py:253
  6.5 0.1 collective-permute-start
  6.6 0.5 %collective-permute-start.1 = (bf16[160,1152]{1,0:T(8,128)(2,1)S(1)}, bf16[160,1152]{1,0:T(8,128)(2,1)S(1)}, u32[]{:S(2)}, u32[]{:S(2)}) collective-permute-start(bf16[160,1152]{1,0:T(8,128)(2,1)S(1)} %get-tuple-element.21.text), channel_id=1, source_target_pairs={{0,2},{1,3},{2,0},{3,1},{4,6},{5,7},{6,4},{7,5},{8,10},{9,11},{10,... | collective-permute-start | bytes 1105928 | tf_op jit(solution)/shard_map/ppermute | solution.py:291
  8.3 1.1 %prep.1 = (f32[8,128]{1,0:T(8,128)S(1)}, s32[1,160]{1,0:T(1,128)S(1)}, s32[160,1]{1,0:T(8,128)S(1)}) custom-call(s32[40,128]{1,0:T(8,128)} %bitcast.9, f32[1,1]{1,0:T(1,128)} %bitcast.5.scale, f32[1,1]{1,0:T(1,128)} %bitcast.6.bias, f32[160,1]{1,0:T(8,128)S(1)} %get-tuple-element.16.after.image_inv.refs_1_), custom_call_target="tpu_custom_call" | custom-call | tf_op jit(solution)/shard_map/prep/pallas_call | solution.py:253
  9.5 6.0 %collective-permute-done.3.raw = bf16[160,1152]{1,0:T(8,128)(2,1)S(1)} collective-permute-done((bf16[160,1152]{1,0:T(8,128)(2,1)}, bf16[160,1152]{1,0:T(8,128)(2,1)S(1)}, u32[]{:S(2)}, u32[]{:S(2)}) %collective-permute-start.3) | collective-permute-done | bytes 368672 | tf_op jit(solution)/shard_map/ppermute | solution.py:291
  15.5 0.2 visit.1
  15.6 0.0 collective-permute-done.2.refs_0_
  15.6 0.0 collective-permute-done.refs_1_.mate_image
  15.6 0.0 collective-permute-done.1.refs_2_.mate_text
  15.7 0.2 got.1
  15.8 0.1 collective-permute-start.4
  15.9 0.8 %first.1 = bf16[1,160,1152]{2,1,0:T(8,128)(2,1)S(1)} custom-call(f32[8,128]{1,0:T(8,128)S(1)} %get-tuple-element.17.after.params, s32[1,160]{1,0:T(1,128)S(1)} %get-tuple-element.18.row_targets, bf16[160,1152]{1,0:T(8,128)(2,1)S(1)} %get-tuple-element.20.image, bf16[160,1152]{1,0:T(8,128)(2,1)S(1)} %get-tuple-element.21.text, ...), custom_call_target="tpu_custom_call" | custom-call | tf_op jit(solution)/shard_map/first/pallas_call | solution.py:253
  16.7 1.8 %collective-permute-start.5 = (bf16[160,1152]{1,0:T(8,128)(2,1)S(1)}, bf16[160,1152]{1,0:T(8,128)(2,1)S(1)}, u32[]{:S(2)}, u32[]{:S(2)}) collective-permute-start(bf16[160,1152]{1,0:T(8,128)(2,1)S(1)} %bitcast.7), channel_id=1, source_target_pairs={{0,28},{1,29},{2,3},{3,2},{4,0},{5,1},{6,7},{7,6},{8,4},{9,5},{10,... | collective-permute-start | bytes 1105928 | tf_op jit(solution)/shard_map/ppermute | solution.py:291
  18.5 0.0 collective-permute-done.4.mate_got
  18.5 1.2 %second.1 = bf16[1,160,1152]{2,1,0:T(8,128)(2,1)S(1)} custom-call(f32[8,128]{1,0:T(8,128)S(1)} %get-tuple-element.17.after.params, s32[1,160]{1,0:T(1,128)S(1)} %get-tuple-element.18.row_targets, bf16[160,1152]{1,0:T(8,128)(2,1)S(1)} %get-tuple-element.20.image, bf16[160,1152]{1,0:T(8,128)(2,1)S(1)} %get-tuple-element.21.text, ...), custom_call_target="tpu_custom_call" | custom-call | tf_op jit(solution)/shard_map/second/pallas_call | solution.py:253
  19.7 1.6 %collective-permute-start.6 = (bf16[160,1152]{1,0:T(8,128)(2,1)S(1)}, bf16[160,1152]{1,0:T(8,128)(2,1)S(1)}, u32[]{:S(2)}, u32[]{:S(2)}) collective-permute-start(bf16[160,1152]{1,0:T(8,128)(2,1)S(1)} %bitcast.8), channel_id=1, source_target_pairs={{0,1},{1,0},{2,30},{3,31},{4,5},{5,4},{6,2},{7,3},{8,9},{9,8},{10,... | collective-permute-start | bytes 1105928 | tf_op jit(solution)/shard_map/ppermute | solution.py:291
  21.3 2.7 %third.1 = (f32[160,1152]{1,0:T(8,128)S(1)}, f32[160,1152]{1,0:T(8,128)S(1)}) custom-call(f32[8,128]{1,0:T(8,128)S(1)} %get-tuple-element.17.after.params, s32[1,160]{1,0:T(1,128)S(1)} %get-tuple-element.18.row_targets, s32[160,1]{1,0:T(8,128)S(1)} %get-tuple-element.19.targets, bf16[160,1152]{1,0:T(8,128)(2,1)S(1)} %get-tuple-element.20.image, ...), custom_call_target="tpu_custom_call" | custom-call | tf_op jit(solution)/shard_map/third/pallas_call | solution.py:253
  24.0 1.4 %collective-permute-done.5.refs_6_ = bf16[160,1152]{1,0:T(8,128)(2,1)S(1)} collective-permute-done((bf16[160,1152]{1,0:T(8,128)(2,1)S(1)}, bf16[160,1152]{1,0:T(8,128)(2,1)S(1)}, u32[]{:S(2)}, u32[]{:S(2)}) %collective-permute-start.5) | collective-permute-done | bytes 368672 | tf_op jit(solution)/shard_map/ppermute | solution.py:291
  25.3 0.3 %fourth.1.ready = f32[160,1152]{1,0:T(8,128)S(1)} custom-call(bf16[160,1152]{1,0:T(8,128)(2,1)S(1)} %get-tuple-element.15.image_raw.refs_0_, f32[160,1]{1,0:T(8,128)S(1)} %get-tuple-element.16.after.image_inv.refs_1_, f32[160,1152]{1,0:T(8,128)S(1)} %get-tuple-element.26.refs_2_, bf16[160,1152]{1,0:T(8,128)(2,1)S(1)} %get-tuple-element.24.text_raw.refs_3_, ...), custom_call_target="tpu_custom_call" | custom-call | tf_op jit(solution)/shard_map/fourth/pallas_call | solution.py:253
  25.7 2.5 %collective-permute-done.6.refs_6_ = bf16[160,1152]{1,0:T(8,128)(2,1)S(1)} collective-permute-done((bf16[160,1152]{1,0:T(8,128)(2,1)S(1)}, bf16[160,1152]{1,0:T(8,128)(2,1)S(1)}, u32[]{:S(2)}, u32[]{:S(2)}) %collective-permute-start.6) | collective-permute-done | bytes 368672 | tf_op jit(solution)/shard_map/ppermute | solution.py:291
  28.1 1.2 %last.1 = (f32[160,1152]{1,0:T(8,128)}, f32[160,1152]{1,0:T(8,128)}) custom-call(f32[160,1152]{1,0:T(8,128)S(1)} %fourth.1.ready, bf16[160,1152]{1,0:T(8,128)(2,1)S(1)} %get-tuple-element.15.image_raw.refs_0_, f32[160,1]{1,0:T(8,128)S(1)} %get-tuple-element.16.after.image_inv.refs_1_, f32[160,1152]{1,0:T(8,128)S(1)} %get-tuple-element.26.refs_2_, ...), custom_call_target="tpu_custom_call" | custom-call | tf_op jit(solution)/shard_map/last/pallas_call | solution.py:267
Async XLA Ops:
  0.6 14.8 %collective-permute-start.3 = (bf16[160,1152]{1,0:T(8,128)(2,1)}, bf16[160,1152]{1,0:T(8,128)(2,1)S(1)}, u32[]{:S(2)}, u32[]{:S(2)}) collective-permute-start(bf16[160,1152]{1,0:T(8,128)(2,1)} %image.1), channel_id=1, source_target_pairs={{0,4},{1,5},{2,6},{3,7},{4,8},{5,9},{6,10},{7,11},{8,12},{9,13},{1... | collective-permute-start | bytes 1105928 | tf_op jit(solution)/shard_map/ppermute | solution.py:291
  3.6 12.0 %collective-permute-start.2 = (bf16[160,1152]{1,0:T(8,128)(2,1)}, bf16[160,1152]{1,0:T(8,128)(2,1)S(1)}, u32[]{:S(2)}, u32[]{:S(2)}) collective-permute-start(bf16[160,1152]{1,0:T(8,128)(2,1)} %text.1), channel_id=1, source_target_pairs={{0,1},{1,0},{2,3},{3,2},{4,5},{5,4},{6,7},{7,6},{8,9},{9,8},{10,11... | collective-permute-start | bytes 1105928 | tf_op jit(solution)/shard_map/ppermute | solution.py:291
  6.5 9.2 %collective-permute-start = (bf16[160,1152]{1,0:T(8,128)(2,1)S(1)}, bf16[160,1152]{1,0:T(8,128)(2,1)S(1)}, u32[]{:S(2)}, u32[]{:S(2)}) collective-permute-start(bf16[160,1152]{1,0:T(8,128)(2,1)S(1)} %get-tuple-element.20.image), channel_id=1, source_target_pairs={{0,2},{1,3},{2,0},{3,1},{4,6},{5,7},{6,4},{7,5},{8,10},{9,11},{10,... | collective-permute-start | bytes 1105928 | tf_op jit(solution)/shard_map/ppermute | solution.py:291
  6.6 9.1 %collective-permute-start.1 = (bf16[160,1152]{1,0:T(8,128)(2,1)S(1)}, bf16[160,1152]{1,0:T(8,128)(2,1)S(1)}, u32[]{:S(2)}, u32[]{:S(2)}) collective-permute-start(bf16[160,1152]{1,0:T(8,128)(2,1)S(1)} %get-tuple-element.21.text), channel_id=1, source_target_pairs={{0,2},{1,3},{2,0},{3,1},{4,6},{5,7},{6,4},{7,5},{8,10},{9,11},{10,... | collective-permute-start | bytes 1105928 | tf_op jit(solution)/shard_map/ppermute | solution.py:291
  15.8 2.7 %collective-permute-start.4 = (bf16[2,160,1152]{2,1,0:T(8,128)(2,1)S(1)}, bf16[2,160,1152]{2,1,0:T(8,128)(2,1)S(1)}, u32[]{:S(2)}, u32[]{:S(2)}) collective-permute-start(bf16[2,160,1152]{2,1,0:T(8,128)(2,1)S(1)} %got.1), channel_id=1, source_target_pairs={{0,2},{1,3},{2,0},{3,1},{4,6},{5,7},{6,4},{7,5},{8,10},{9,11},{10,... | collective-permute-start | bytes 2211848 | tf_op jit(solution)/shard_map/ppermute | solution.py:291
  16.7 8.6 %collective-permute-start.5 = (bf16[160,1152]{1,0:T(8,128)(2,1)S(1)}, bf16[160,1152]{1,0:T(8,128)(2,1)S(1)}, u32[]{:S(2)}, u32[]{:S(2)}) collective-permute-start(bf16[160,1152]{1,0:T(8,128)(2,1)S(1)} %bitcast.7), channel_id=1, source_target_pairs={{0,28},{1,29},{2,3},{3,2},{4,0},{5,1},{6,7},{7,6},{8,4},{9,5},{10,... | collective-permute-start | bytes 1105928 | tf_op jit(solution)/shard_map/ppermute | solution.py:291
  19.7 8.4 %collective-permute-start.6 = (bf16[160,1152]{1,0:T(8,128)(2,1)S(1)}, bf16[160,1152]{1,0:T(8,128)(2,1)S(1)}, u32[]{:S(2)}, u32[]{:S(2)}) collective-permute-start(bf16[160,1152]{1,0:T(8,128)(2,1)S(1)} %bitcast.8), channel_id=1, source_target_pairs={{0,1},{1,0},{2,30},{3,31},{4,5},{5,4},{6,2},{7,3},{8,9},{9,8},{10,... | collective-permute-start | bytes 1105928 | tf_op jit(solution)/shard_map/ppermute | solution.py:291

commit v18 on v16

--- a/solution.py
+++ b/solution.py
@@ -140,7 +140,10 @@
     visit, far_text = parted(far, got)
 
     def on_first(node):
-        back[0] = drawn(params, visit, [text, *far_text]).astype(HALF)
+        total = drawn(params, visit, [text])
+        for k in range(far):
+            total += drawn(params, visit, [far_text[k]])
+        back[0] = total.astype(HALF)
 
     def on_second(node):
         for k in range(far):
@@ -307,7 +310,6 @@
     returns = ((far, rows, width), HALF)
 
     visit_raw = send(image_embeds, ahead, ahead)
-    far_raw = [send(text_embeds, (0, -k), (0, -k)) for k in range(1, node_count)]
 
     image_raw, text_raw, image, text, image_inv, text_inv = call(
         unit_kernel,
@@ -317,6 +319,8 @@
         anywhere=2,
         scratch=[pltpu.SemaphoreType.DMA((2,))],
     )
+    reports, image_inv = lax.optimization_barrier((text_embeds, image_inv))
+    far_raw = [send(reports, (0, -k), (0, -k)) for k in range(1, node_count)]
     mate_image = swap(image)
     mate_text = swap(text)
     names = pair_text.reshape(-1, 128)

time: 29.2 us -> 29.6 us (1.014)
  starting transfers between devices: 8.51 us -> 9.61 us
  waiting for transfers between devices: 10.4 us -> 9.61 us
    ppermute x7, starting transfers between devices: 8.51 us -> 9.61 us  [send(): return lax.ppermute(block, ('blk', 'node'), route)]
    ppermute x7, waiting for transfers between devices: 10.4 us -> 9.61 us  [send(): return lax.ppermute(block, ('blk', 'node'), route)]
where the time goes in v18:
time: 29.6 us; the launch traced here: 29.2 us
  starting transfers between devices  9.61 us (32%)
  waiting for transfers between devices  9.61 us (32%)
  Pallas kernels  7.96 us (27%)
  between operations  2.03 us (7%)
    ppermute x7, starting transfers between devices, send(): return lax.ppermute(block, ('blk', 'node'), route)  9.61 us
    ppermute x7, waiting for transfers between devices, send(): return lax.ppermute(block, ('blk', 'node'), route)  9.61 us
    pallas_call x8, Pallas kernels, call(): pl.pallas_call(kernel, name=name, out_shape=[pltpu.VMEM(s, d) for s, d in...  6.81 us
    pallas_call x1, Pallas kernels, last(): pl.pallas_call(functools.partial(last_kernel, far), name='last', out_shap...  1.16 us
  transfers between devices with their start and end apart: 7, of which 3 were waited for; matrix products, arithmetic and copies ran while one was open for 0% of the time, Pallas kernels for 23%

profile of v18, /device:TPU:0, one launch (start us, length us, event | category | flops | bytes accessed | tf_op | source)
XLA Modules:
  0.0 29.2 jit_solution(177050374651874359)
XLA Ops:
  0.6 0.0 copy-start
  0.6 3.0 %collective-permute-start.3 = (bf16[160,1152]{1,0:T(8,128)(2,1)}, bf16[160,1152]{1,0:T(8,128)(2,1)S(1)}, u32[]{:S(2)}, u32[]{:S(2)}) collective-permute-start(bf16[160,1152]{1,0:T(8,128)(2,1)} %image.1), channel_id=1, source_target_pairs={{0,4},{1,5},{2,6},{3,7},{4,8},{5,9},{6,10},{7,11},{8,12},{9,13},{1... | collective-permute-start | bytes 1105928 | tf_op jit(solution)/shard_map/ppermute | solution.py:300
  3.6 1.4 %unit.1 = (bf16[160,1152]{1,0:T(8,128)(2,1)S(1)}, bf16[160,1152]{1,0:T(8,128)(2,1)S(1)}, bf16[160,1152]{1,0:T(8,128)(2,1)S(1)}, bf16[160,1152]{1,0:T(8,128)(2,1)...) custom-call(bf16[160,1152]{1,0:T(8,128)(2,1)} %image.1, bf16[160,1152]{1,0:T(8,128)(2,1)} %text.1), custom_call_target="tpu_custom_call" | custom-call | tf_op jit(solution)/shard_map/unit/pallas_call | solution.py:262
  5.0 1.6 %collective-permute-start.2 = (bf16[160,1152]{1,0:T(8,128)(2,1)S(1)}, bf16[160,1152]{1,0:T(8,128)(2,1)S(1)}, u32[]{:S(2)}, u32[]{:S(2)}) collective-permute-start(bf16[160,1152]{1,0:T(8,128)(2,1)S(1)} %copy-done), channel_id=1, source_target_pairs={{0,1},{1,0},{2,3},{3,2},{4,5},{5,4},{6,7},{7,6},{8,9},{9,8},{10,11... | collective-permute-start | bytes 1105928 | tf_op jit(solution)/shard_map/ppermute | solution.py:300
  6.6 0.0 collective-permute-start
  6.6 0.5 %collective-permute-start.1 = (bf16[160,1152]{1,0:T(8,128)(2,1)S(1)}, bf16[160,1152]{1,0:T(8,128)(2,1)S(1)}, u32[]{:S(2)}, u32[]{:S(2)}) collective-permute-start(bf16[160,1152]{1,0:T(8,128)(2,1)S(1)} %get-tuple-element.24.text), channel_id=1, source_target_pairs={{0,2},{1,3},{2,0},{3,1},{4,6},{5,7},{6,4},{7,5},{8,10},{9,11},{10,... | collective-permute-start | bytes 1105928 | tf_op jit(solution)/shard_map/ppermute | solution.py:300
  8.4 1.1 %prep.1 = (f32[8,128]{1,0:T(8,128)S(1)}, s32[1,480]{1,0:T(1,128)S(1)}, s32[160,1]{1,0:T(8,128)S(1)}) custom-call(s32[40,128]{1,0:T(8,128)} %bitcast.9, f32[1,1]{1,0:T(1,128)} %bitcast.5.scale, f32[1,1]{1,0:T(1,128)} %bitcast.6.bias, f32[160,1]{1,0:T(8,128)S(1)} %get-tuple-element.19.after.image_inv.refs_1_), custom_call_target="tpu_custom_call" | custom-call | tf_op jit(solution)/shard_map/prep/pallas_call | solution.py:262
  9.5 5.9 %collective-permute-done.3.raw = bf16[160,1152]{1,0:T(8,128)(2,1)S(1)} collective-permute-done((bf16[160,1152]{1,0:T(8,128)(2,1)}, bf16[160,1152]{1,0:T(8,128)(2,1)S(1)}, u32[]{:S(2)}, u32[]{:S(2)}) %collective-permute-start.3) | collective-permute-done | bytes 368672 | tf_op jit(solution)/shard_map/ppermute | solution.py:300
  15.5 0.2 visit.1
  15.6 0.0 collective-permute-done.2.refs_0_
  15.6 0.0 collective-permute-done.refs_1_.mate_image
  15.7 0.0 collective-permute-done.1.refs_2_.mate_text
  15.7 0.2 got.1
  15.8 0.1 collective-permute-start.4
  15.9 0.8 %first.1 = bf16[1,160,1152]{2,1,0:T(8,128)(2,1)S(1)} custom-call(f32[8,128]{1,0:T(8,128)S(1)} %get-tuple-element.20.after.params, s32[1,480]{1,0:T(1,128)S(1)} %get-tuple-element.21.row_targets, bf16[160,1152]{1,0:T(8,128)(2,1)S(1)} %get-tuple-element.23.image, bf16[160,1152]{1,0:T(8,128)(2,1)S(1)} %get-tuple-element.24.text, ...), custom_call_target="tpu_custom_call" | custom-call | tf_op jit(solution)/shard_map/first/pallas_call | solution.py:262
  16.7 2.9 %collective-permute-start.5 = (bf16[160,1152]{1,0:T(8,128)(2,1)S(1)}, bf16[160,1152]{1,0:T(8,128)(2,1)S(1)}, u32[]{:S(2)}, u32[]{:S(2)}) collective-permute-start(bf16[160,1152]{1,0:T(8,128)(2,1)S(1)} %bitcast.8), channel_id=1, source_target_pairs={{0,28},{1,29},{2,3},{3,2},{4,0},{5,1},{6,7},{7,6},{8,4},{9,5},{10,... | collective-permute-start | bytes 1105928 | tf_op jit(solution)/shard_map/ppermute | solution.py:300
  19.6 0.0 collective-permute-done.4.mate_got
  19.6 0.9 %second.1 = bf16[1,160,1152]{2,1,0:T(8,128)(2,1)S(1)} custom-call(f32[8,128]{1,0:T(8,128)S(1)} %get-tuple-element.20.after.params, s32[1,480]{1,0:T(1,128)S(1)} %get-tuple-element.21.row_targets, bf16[160,1152]{1,0:T(8,128)(2,1)S(1)} %get-tuple-element.23.image, bf16[160,1152]{1,0:T(8,128)(2,1)S(1)} %get-tuple-element.24.text, ...), custom_call_target="tpu_custom_call" | custom-call | tf_op jit(solution)/shard_map/second/pallas_call | solution.py:262
  20.5 1.6 %collective-permute-start.6 = (bf16[160,1152]{1,0:T(8,128)(2,1)S(1)}, bf16[160,1152]{1,0:T(8,128)(2,1)S(1)}, u32[]{:S(2)}, u32[]{:S(2)}) collective-permute-start(bf16[160,1152]{1,0:T(8,128)(2,1)S(1)} %bitcast.7), channel_id=1, source_target_pairs={{0,1},{1,0},{2,30},{3,31},{4,5},{5,4},{6,2},{7,3},{8,9},{9,8},{10,... | collective-permute-start | bytes 1105928 | tf_op jit(solution)/shard_map/ppermute | solution.py:300
  22.1 2.0 %third.1 = (f32[160,1152]{1,0:T(8,128)S(1)}, f32[160,1152]{1,0:T(8,128)S(1)}) custom-call(f32[8,128]{1,0:T(8,128)S(1)} %get-tuple-element.20.after.params, s32[1,480]{1,0:T(1,128)S(1)} %get-tuple-element.21.row_targets, s32[160,1]{1,0:T(8,128)S(1)} %get-tuple-element.22.targets, bf16[160,1152]{1,0:T(8,128)(2,1)S(1)} %get-tuple-element.23.image, ...), custom_call_target="tpu_custom_call" | custom-call | tf_op jit(solution)/shard_map/third/pallas_call | solution.py:262
  24.1 2.5 %collective-permute-done.5.refs_6_ = bf16[160,1152]{1,0:T(8,128)(2,1)S(1)} collective-permute-done((bf16[160,1152]{1,0:T(8,128)(2,1)S(1)}, bf16[160,1152]{1,0:T(8,128)(2,1)S(1)}, u32[]{:S(2)}, u32[]{:S(2)}) %collective-permute-start.5) | collective-permute-done | bytes 368672 | tf_op jit(solution)/shard_map/ppermute | solution.py:300
  26.5 0.3 %fourth.1.ready = f32[160,1152]{1,0:T(8,128)S(1)} custom-call(bf16[160,1152]{1,0:T(8,128)(2,1)S(1)} %get-tuple-element.17.image_raw.refs_0_, f32[160,1]{1,0:T(8,128)S(1)} %get-tuple-element.19.after.image_inv.refs_1_, f32[160,1152]{1,0:T(8,128)S(1)} %get-tuple-element.30.refs_2_, bf16[160,1152]{1,0:T(8,128)(2,1)S(1)} %get-tuple-element.28.text_raw.refs_3_, ...), custom_call_target="tpu_custom_call" | custom-call | tf_op jit(solution)/shard_map/fourth/pallas_call | solution.py:262
  26.9 1.2 %collective-permute-done.6.refs_6_ = bf16[160,1152]{1,0:T(8,128)(2,1)S(1)} collective-permute-done((bf16[160,1152]{1,0:T(8,128)(2,1)S(1)}, bf16[160,1152]{1,0:T(8,128)(2,1)S(1)}, u32[]{:S(2)}, u32[]{:S(2)}) %collective-permute-start.6) | collective-permute-done | bytes 368672 | tf_op jit(solution)/shard_map/ppermute | solution.py:300
  28.1 1.2 %last.1 = (f32[160,1152]{1,0:T(8,128)}, f32[160,1152]{1,0:T(8,128)}) custom-call(f32[160,1152]{1,0:T(8,128)S(1)} %fourth.1.ready, bf16[160,1152]{1,0:T(8,128)(2,1)S(1)} %get-tuple-element.17.image_raw.refs_0_, f32[160,1]{1,0:T(8,128)S(1)} %get-tuple-element.19.after.image_inv.refs_1_, f32[160,1152]{1,0:T(8,128)S(1)} %get-tuple-element.30.refs_2_, ...), custom_call_target="tpu_custom_call" | custom-call | tf_op jit(solution)/shard_map/last/pallas_call | solution.py:276
  (1 shorter events, 0.0 us)
Async XLA Ops:
  0.6 4.4 %copy-start = (bf16[160,1152]{1,0:T(8,128)(2,1)S(1)}, bf16[160,1152]{1,0:T(8,128)(2,1)}, u32[]{:S(2)}) copy-start(bf16[160,1152]{1,0:T(8,128)(2,1)} %text.1) | copy-start | bytes 1105924
  0.6 14.8 %collective-permute-start.3 = (bf16[160,1152]{1,0:T(8,128)(2,1)}, bf16[160,1152]{1,0:T(8,128)(2,1)S(1)}, u32[]{:S(2)}, u32[]{:S(2)}) collective-permute-start(bf16[160,1152]{1,0:T(8,128)(2,1)} %image.1), channel_id=1, source_target_pairs={{0,4},{1,5},{2,6},{3,7},{4,8},{5,9},{6,10},{7,11},{8,12},{9,13},{1... | collective-permute-start | bytes 1105928 | tf_op jit(solution)/shard_map/ppermute | solution.py:300
  5.0 10.6 %collective-permute-start.2 = (bf16[160,1152]{1,0:T(8,128)(2,1)S(1)}, bf16[160,1152]{1,0:T(8,128)(2,1)S(1)}, u32[]{:S(2)}, u32[]{:S(2)}) collective-permute-start(bf16[160,1152]{1,0:T(8,128)(2,1)S(1)} %copy-done), channel_id=1, source_target_pairs={{0,1},{1,0},{2,3},{3,2},{4,5},{5,4},{6,7},{7,6},{8,9},{9,8},{10,11... | collective-permute-start | bytes 1105928 | tf_op jit(solution)/shard_map/ppermute | solution.py:300
  6.6 9.1 %collective-permute-start = (bf16[160,1152]{1,0:T(8,128)(2,1)S(1)}, bf16[160,1152]{1,0:T(8,128)(2,1)S(1)}, u32[]{:S(2)}, u32[]{:S(2)}) collective-permute-start(bf16[160,1152]{1,0:T(8,128)(2,1)S(1)} %get-tuple-element.23.image), channel_id=1, source_target_pairs={{0,2},{1,3},{2,0},{3,1},{4,6},{5,7},{6,4},{7,5},{8,10},{9,11},{10,... | collective-permute-start | bytes 1105928 | tf_op jit(solution)/shard_map/ppermute | solution.py:300
  6.6 9.1 %collective-permute-start.1 = (bf16[160,1152]{1,0:T(8,128)(2,1)S(1)}, bf16[160,1152]{1,0:T(8,128)(2,1)S(1)}, u32[]{:S(2)}, u32[]{:S(2)}) collective-permute-start(bf16[160,1152]{1,0:T(8,128)(2,1)S(1)} %get-tuple-element.24.text), channel_id=1, source_target_pairs={{0,2},{1,3},{2,0},{3,1},{4,6},{5,7},{6,4},{7,5},{8,10},{9,11},{10,... | collective-permute-start | bytes 1105928 | tf_op jit(solution)/shard_map/ppermute | solution.py:300
  15.8 3.8 %collective-permute-start.4 = (bf16[2,160,1152]{2,1,0:T(8,128)(2,1)S(1)}, bf16[2,160,1152]{2,1,0:T(8,128)(2,1)S(1)}, u32[]{:S(2)}, u32[]{:S(2)}) collective-permute-start(bf16[2,160,1152]{2,1,0:T(8,128)(2,1)S(1)} %got.1), channel_id=1, source_target_pairs={{0,2},{1,3},{2,0},{3,1},{4,6},{5,7},{6,4},{7,5},{8,10},{9,11},{10,... | collective-permute-start | bytes 2211848 | tf_op jit(solution)/shard_map/ppermute | solution.py:300
  16.7 9.8 %collective-permute-start.5 = (bf16[160,1152]{1,0:T(8,128)(2,1)S(1)}, bf16[160,1152]{1,0:T(8,128)(2,1)S(1)}, u32[]{:S(2)}, u32[]{:S(2)}) collective-permute-start(bf16[160,1152]{1,0:T(8,128)(2,1)S(1)} %bitcast.8), channel_id=1, source_target_pairs={{0,28},{1,29},{2,3},{3,2},{4,0},{5,1},{6,7},{7,6},{8,4},{9,5},{10,... | collective-permute-start | bytes 1105928 | tf_op jit(solution)/shard_map/ppermute | solution.py:300
  20.5 7.6 %collective-permute-start.6 = (bf16[160,1152]{1,0:T(8,128)(2,1)S(1)}, bf16[160,1152]{1,0:T(8,128)(2,1)S(1)}, u32[]{:S(2)}, u32[]{:S(2)}) collective-permute-start(bf16[160,1152]{1,0:T(8,128)(2,1)S(1)} %bitcast.7), channel_id=1, source_target_pairs={{0,1},{1,0},{2,30},{3,31},{4,5},{5,4},{6,2},{7,3},{8,9},{9,8},{10,... | collective-permute-start | bytes 1105928 | tf_op jit(solution)/shard_map/ppermute | solution.py:300

commit v19 on v16

--- a/solution.py
+++ b/solution.py
@@ -136,22 +136,40 @@
     return got.at[0], [got.at[k + 1] for k in range(far)]
 
 
-def first_kernel(far, params, row_targets, image, text, mate_image, mate_text, got, back):
+def ahead_kernel(
+    far, params, row_targets, image, text, mate_image, mate_text, got, back, part
+):
     visit, far_text = parted(far, got)
 
     def on_first(node):
-        back[0] = drawn(params, visit, [text, *far_text]).astype(HALF)
+        pass
 
     def on_second(node):
         for k in range(far):
             pairs = text_pairs(row_targets, lax.rem(node + k + 1, far + 1))
             images = [image, mate_image, visit]
             back[k] = drawn(params, far_text[k], images, pairs).astype(HALF)
+        part[...] = drawn(params, visit, [text, *far_text, mate_text])
 
     by_role(on_first, on_second)
 
 
-def second_kernel(far, params, row_targets, image, text, mate_text, got, mate_got, back):
+def first_kernel(far, params, text, got, early, back):
+    visit, far_text = parted(far, got)
+
+    def on_first(node):
+        total = drawn(params, visit, [text])
+        for k in range(far):
+            total += drawn(params, visit, [far_text[k]])
+        back[0] = total.astype(HALF)
+
+    def on_second(node):
+        back[...] = early[...]
+
+    by_role(on_first, on_second)
+
+
+def second_kernel(far, params, row_targets, image, got, mate_got, part, back):
     visit, far_text = parted(far, got)
     mate_visit, mate_far = parted(far, mate_got)
 
@@ -162,8 +180,7 @@
             back[k] = drawn(params, far_text[k], images, pairs).astype(HALF)
 
     def on_second(node):
-        texts = [text, *far_text, mate_text, *mate_far]
-        back[0] = drawn(params, visit, texts).astype(HALF)
+        back[0] = (part[...] + drawn(params, visit, mate_far)).astype(HALF)
 
     by_role(on_first, on_second)
 
@@ -336,18 +353,22 @@
         [visit, *far_raw, mate_image, mate_text],
         [((node_count, rows, width), HALF)],
     )
+    early, part = call(
+        functools.partial(ahead_kernel, far),
+        "ahead",
+        [params, row_targets, image, text, mate_image, mate_text, got],
+        [returns, block_f],
+    )
+    got, early = lax.optimization_barrier((got, early))
+    mate_got = swap(got)
     (back,) = call(
-        functools.partial(first_kernel, far),
-        "first",
-        [params, row_targets, image, text, mate_image, mate_text, got],
-        [returns],
+        functools.partial(first_kernel, far), "first", [params, text, got, early], [returns]
     )
     one = [send(back[k], behind if k == 0 else stay, (0, k + 1)) for k in range(far)]
-    mate_got = swap(got)
     (back,) = call(
         functools.partial(second_kernel, far),
         "second",
-        [params, row_targets, image, text, mate_text, got, mate_got],
+        [params, row_targets, image, got, mate_got, part],
         [returns],
     )
     two = [send(back[k], (0, k + 1), behind if k == 0 else stay) for k in range(far)]

time: 29.2 us -> 29.8 us (1.021)
  starting transfers between devices: 8.51 us -> 9.02 us
    ppermute x7, starting transfers between devices: 8.51 us -> 9.02 us  [send(): return lax.ppermute(block, ('blk', 'node'), route)]
    pallas_call x8 -> x9, Pallas kernels: 6.85 us -> 6.77 us  [call(): pl.pallas_call(kernel, name=name, out_shape=[pltpu.VMEM(s, d) for s, d in...]
  transfers between devices with their start and end apart: 7 -> 7, of which waited for: 3 -> 2; matrix products, arithmetic and copies ran while one was open for 0% -> 0% of each run, Pallas kernels for 23% -> 22%
where the time goes in v19:
time: 29.8 us; the launch traced here: 29.5 us
  waiting for transfers between devices  10.5 us (35%)
  starting transfers between devices  9.02 us (30%)
  Pallas kernels  7.95 us (27%)
  between operations  2.03 us (7%)
    ppermute x7, waiting for transfers between devices, send(): return lax.ppermute(block, ('blk', 'node'), route)  10.5 us
    ppermute x7, starting transfers between devices, send(): return lax.ppermute(block, ('blk', 'node'), route)  9.02 us
    pallas_call x9, Pallas kernels, call(): pl.pallas_call(kernel, name=name, out_shape=[pltpu.VMEM(s, d) for s, d in...  6.77 us
    pallas_call x1, Pallas kernels, last(): pl.pallas_call(functools.partial(last_kernel, far), name='last', out_shap...  1.18 us
  transfers between devices with their start and end apart: 7, of which 2 were waited for; matrix products, arithmetic and copies ran while one was open for 0% of the time, Pallas kernels for 22%

profile of v19, /device:TPU:0, one launch (start us, length us, event | category | flops | bytes accessed | tf_op | source)
XLA Modules:
  0.0 29.5 jit_solution(13178707983377166588)
XLA Ops:
  0.6 3.0 %collective-permute-start.3 = (bf16[160,1152]{1,0:T(8,128)(2,1)}, bf16[160,1152]{1,0:T(8,128)(2,1)S(1)}, u32[]{:S(2)}, u32[]{:S(2)}) collective-permute-start(bf16[160,1152]{1,0:T(8,128)(2,1)} %image.1), channel_id=1, source_target_pairs={{0,4},{1,5},{2,6},{3,7},{4,8},{5,9},{6,10},{7,11},{8,12},{9,13},{1... | collective-permute-start | bytes 1105928 | tf_op jit(solution)/shard_map/ppermute | solution.py:314
  3.6 1.5 %collective-permute-start.2 = (bf16[160,1152]{1,0:T(8,128)(2,1)}, bf16[160,1152]{1,0:T(8,128)(2,1)S(1)}, u32[]{:S(2)}, u32[]{:S(2)}) collective-permute-start(bf16[160,1152]{1,0:T(8,128)(2,1)} %text.1), channel_id=1, source_target_pairs={{0,1},{1,0},{2,3},{3,2},{4,5},{5,4},{6,7},{7,6},{8,9},{9,8},{10,11... | collective-permute-start | bytes 1105928 | tf_op jit(solution)/shard_map/ppermute | solution.py:314
  5.1 1.3 %unit.1 = (bf16[160,1152]{1,0:T(8,128)(2,1)S(1)}, bf16[160,1152]{1,0:T(8,128)(2,1)S(1)}, bf16[160,1152]{1,0:T(8,128)(2,1)S(1)}, bf16[160,1152]{1,0:T(8,128)(2,1)...) custom-call(bf16[160,1152]{1,0:T(8,128)(2,1)} %image.1, bf16[160,1152]{1,0:T(8,128)(2,1)} %text.1), custom_call_target="tpu_custom_call" | custom-call | tf_op jit(solution)/shard_map/unit/pallas_call | solution.py:276
  6.5 0.1 collective-permute-start
  6.6 0.5 %collective-permute-start.1 = (bf16[160,1152]{1,0:T(8,128)(2,1)S(1)}, bf16[160,1152]{1,0:T(8,128)(2,1)S(1)}, u32[]{:S(2)}, u32[]{:S(2)}) collective-permute-start(bf16[160,1152]{1,0:T(8,128)(2,1)S(1)} %get-tuple-element.25.text), channel_id=1, source_target_pairs={{0,2},{1,3},{2,0},{3,1},{4,6},{5,7},{6,4},{7,5},{8,10},{9,11},{10,... | collective-permute-start | bytes 1105928 | tf_op jit(solution)/shard_map/ppermute | solution.py:314
  8.3 1.1 %prep.1 = (f32[8,128]{1,0:T(8,128)S(1)}, s32[1,480]{1,0:T(1,128)S(1)}, s32[160,1]{1,0:T(8,128)S(1)}) custom-call(s32[40,128]{1,0:T(8,128)} %bitcast.9, f32[1,1]{1,0:T(1,128)} %bitcast.5.scale, f32[1,1]{1,0:T(1,128)} %bitcast.6.bias, f32[160,1]{1,0:T(8,128)S(1)} %get-tuple-element.20.after.image_inv.refs_1_), custom_call_target="tpu_custom_call" | custom-call | tf_op jit(solution)/shard_map/prep/pallas_call | solution.py:276
  9.5 6.0 %collective-permute-done.3.raw = bf16[160,1152]{1,0:T(8,128)(2,1)S(1)} collective-permute-done((bf16[160,1152]{1,0:T(8,128)(2,1)}, bf16[160,1152]{1,0:T(8,128)(2,1)S(1)}, u32[]{:S(2)}, u32[]{:S(2)}) %collective-permute-start.3) | collective-permute-done | bytes 368672 | tf_op jit(solution)/shard_map/ppermute | solution.py:314
  15.5 0.2 visit.1
  15.6 0.0 collective-permute-done.2.refs_0_
  15.6 0.0 collective-permute-done.refs_1_.mate_image
  15.6 0.0 collective-permute-done.1.refs_2_.mate_text
  15.7 0.2 got.1
  15.8 0.9 %collective-permute-start.4 = (bf16[2,160,1152]{2,1,0:T(8,128)(2,1)S(1)}, bf16[2,160,1152]{2,1,0:T(8,128)(2,1)S(1)}, u32[]{:S(2)}, u32[]{:S(2)}) collective-permute-start(bf16[2,160,1152]{2,1,0:T(8,128)(2,1)S(1)} %got.1), channel_id=1, source_target_pairs={{0,2},{1,3},{2,0},{3,1},{4,6},{5,7},{6,4},{7,5},{8,10},{9,11},{10,... | collective-permute-start | bytes 2211848 | tf_op jit(solution)/shard_map/ppermute | solution.py:314
  16.7 0.8 %first.1 = bf16[1,160,1152]{2,1,0:T(8,128)(2,1)S(1)} custom-call(f32[8,128]{1,0:T(8,128)S(1)} %get-tuple-element.21.after.params, bf16[160,1152]{1,0:T(8,128)(2,1)S(1)} %get-tuple-element.25.text, bf16[2,160,1152]{2,1,0:T(8,128)(2,1)S(1)} %got.1, bf16[1,160,1152]{2,1,0:T(8,128)(2,1)S(1)} %get-tuple-element.34.early), custom_call_target="tpu_custom_call" | custom-call | tf_op jit(solution)/shard_map/first/pallas_call | solution.py:276
  17.5 1.5 %collective-permute-start.5 = (bf16[160,1152]{1,0:T(8,128)(2,1)S(1)}, bf16[160,1152]{1,0:T(8,128)(2,1)S(1)}, u32[]{:S(2)}, u32[]{:S(2)}) collective-permute-start(bf16[160,1152]{1,0:T(8,128)(2,1)S(1)} %bitcast.8), channel_id=1, source_target_pairs={{0,28},{1,29},{2,3},{3,2},{4,0},{5,1},{6,7},{7,6},{8,4},{9,5},{10,... | collective-permute-start | bytes 1105928 | tf_op jit(solution)/shard_map/ppermute | solution.py:314
  19.0 0.0 collective-permute-done.4.mate_got
  19.0 0.9 %second.1 = bf16[1,160,1152]{2,1,0:T(8,128)(2,1)S(1)} custom-call(f32[8,128]{1,0:T(8,128)S(1)} %get-tuple-element.21.after.params, s32[1,480]{1,0:T(1,128)S(1)} %get-tuple-element.22.row_targets, bf16[160,1152]{1,0:T(8,128)(2,1)S(1)} %get-tuple-element.24.image, bf16[2,160,1152]{2,1,0:T(8,128)(2,1)S(1)} %got.1, ...), custom_call_target="tpu_custom_call" | custom-call | tf_op jit(solution)/shard_map/second/pallas_call | solution.py:276
  19.9 1.6 %collective-permute-start.6 = (bf16[160,1152]{1,0:T(8,128)(2,1)S(1)}, bf16[160,1152]{1,0:T(8,128)(2,1)S(1)}, u32[]{:S(2)}, u32[]{:S(2)}) collective-permute-start(bf16[160,1152]{1,0:T(8,128)(2,1)S(1)} %bitcast.7), channel_id=1, source_target_pairs={{0,1},{1,0},{2,30},{3,31},{4,5},{5,4},{6,2},{7,3},{8,9},{9,8},{10,... | collective-permute-start | bytes 1105928 | tf_op jit(solution)/shard_map/ppermute | solution.py:314
  21.5 2.0 %third.1 = (f32[160,1152]{1,0:T(8,128)S(1)}, f32[160,1152]{1,0:T(8,128)S(1)}) custom-call(f32[8,128]{1,0:T(8,128)S(1)} %get-tuple-element.21.after.params, s32[1,480]{1,0:T(1,128)S(1)} %get-tuple-element.22.row_targets, s32[160,1]{1,0:T(8,128)S(1)} %get-tuple-element.23.targets, bf16[160,1152]{1,0:T(8,128)(2,1)S(1)} %get-tuple-element.24.image, ...), custom_call_target="tpu_custom_call" | custom-call | tf_op jit(solution)/shard_map/third/pallas_call | solution.py:276
  23.5 4.5 %collective-permute-done.5.refs_6_ = bf16[160,1152]{1,0:T(8,128)(2,1)S(1)} collective-permute-done((bf16[160,1152]{1,0:T(8,128)(2,1)S(1)}, bf16[160,1152]{1,0:T(8,128)(2,1)S(1)}, u32[]{:S(2)}, u32[]{:S(2)}) %collective-permute-start.5) | collective-permute-done | bytes 368672 | tf_op jit(solution)/shard_map/ppermute | solution.py:314
  27.9 0.3 %fourth.1.ready = f32[160,1152]{1,0:T(8,128)S(1)} custom-call(bf16[160,1152]{1,0:T(8,128)(2,1)S(1)} %get-tuple-element.19.image_raw.refs_0_, f32[160,1]{1,0:T(8,128)S(1)} %get-tuple-element.20.after.image_inv.refs_1_, f32[160,1152]{1,0:T(8,128)S(1)} %get-tuple-element.32.refs_2_, bf16[160,1152]{1,0:T(8,128)(2,1)S(1)} %get-tuple-element.30.text_raw.refs_3_, ...), custom_call_target="tpu_custom_call" | custom-call | tf_op jit(solution)/shard_map/fourth/pallas_call | solution.py:276
  28.3 0.0 collective-permute-done.6.refs_6_
  28.3 1.2 %last.1 = (f32[160,1152]{1,0:T(8,128)}, f32[160,1152]{1,0:T(8,128)}) custom-call(f32[160,1152]{1,0:T(8,128)S(1)} %fourth.1.ready, bf16[160,1152]{1,0:T(8,128)(2,1)S(1)} %get-tuple-element.19.image_raw.refs_0_, f32[160,1]{1,0:T(8,128)S(1)} %get-tuple-element.20.after.image_inv.refs_1_, f32[160,1152]{1,0:T(8,128)S(1)} %get-tuple-element.32.refs_2_, ...), custom_call_target="tpu_custom_call" | custom-call | tf_op jit(solution)/shard_map/last/pallas_call | solution.py:290
  (1 shorter events, 0.0 us)
Async XLA Ops:
  0.6 14.8 %collective-permute-start.3 = (bf16[160,1152]{1,0:T(8,128)(2,1)}, bf16[160,1152]{1,0:T(8,128)(2,1)S(1)}, u32[]{:S(2)}, u32[]{:S(2)}) collective-permute-start(bf16[160,1152]{1,0:T(8,128)(2,1)} %image.1), channel_id=1, source_target_pairs={{0,4},{1,5},{2,6},{3,7},{4,8},{5,9},{6,10},{7,11},{8,12},{9,13},{1... | collective-permute-start | bytes 1105928 | tf_op jit(solution)/shard_map/ppermute | solution.py:314
  3.6 12.0 %collective-permute-start.2 = (bf16[160,1152]{1,0:T(8,128)(2,1)}, bf16[160,1152]{1,0:T(8,128)(2,1)S(1)}, u32[]{:S(2)}, u32[]{:S(2)}) collective-permute-start(bf16[160,1152]{1,0:T(8,128)(2,1)} %text.1), channel_id=1, source_target_pairs={{0,1},{1,0},{2,3},{3,2},{4,5},{5,4},{6,7},{7,6},{8,9},{9,8},{10,11... | collective-permute-start | bytes 1105928 | tf_op jit(solution)/shard_map/ppermute | solution.py:314
  6.5 9.2 %collective-permute-start = (bf16[160,1152]{1,0:T(8,128)(2,1)S(1)}, bf16[160,1152]{1,0:T(8,128)(2,1)S(1)}, u32[]{:S(2)}, u32[]{:S(2)}) collective-permute-start(bf16[160,1152]{1,0:T(8,128)(2,1)S(1)} %get-tuple-element.24.image), channel_id=1, source_target_pairs={{0,2},{1,3},{2,0},{3,1},{4,6},{5,7},{6,4},{7,5},{8,10},{9,11},{10,... | collective-permute-start | bytes 1105928 | tf_op jit(solution)/shard_map/ppermute | solution.py:314
  6.6 9.1 %collective-permute-start.1 = (bf16[160,1152]{1,0:T(8,128)(2,1)S(1)}, bf16[160,1152]{1,0:T(8,128)(2,1)S(1)}, u32[]{:S(2)}, u32[]{:S(2)}) collective-permute-start(bf16[160,1152]{1,0:T(8,128)(2,1)S(1)} %get-tuple-element.25.text), channel_id=1, source_target_pairs={{0,2},{1,3},{2,0},{3,1},{4,6},{5,7},{6,4},{7,5},{8,10},{9,11},{10,... | collective-permute-start | bytes 1105928 | tf_op jit(solution)/shard_map/ppermute | solution.py:314
  15.8 3.2 %collective-permute-start.4 = (bf16[2,160,1152]{2,1,0:T(8,128)(2,1)S(1)}, bf16[2,160,1152]{2,1,0:T(8,128)(2,1)S(1)}, u32[]{:S(2)}, u32[]{:S(2)}) collective-permute-start(bf16[2,160,1152]{2,1,0:T(8,128)(2,1)S(1)} %got.1), channel_id=1, source_target_pairs={{0,2},{1,3},{2,0},{3,1},{4,6},{5,7},{6,4},{7,5},{8,10},{9,11},{10,... | collective-permute-start | bytes 2211848 | tf_op jit(solution)/shard_map/ppermute | solution.py:314
  17.5 10.4 %collective-permute-start.5 = (bf16[160,1152]{1,0:T(8,128)(2,1)S(1)}, bf16[160,1152]{1,0:T(8,128)(2,1)S(1)}, u32[]{:S(2)}, u32[]{:S(2)}) collective-permute-start(bf16[160,1152]{1,0:T(8,128)(2,1)S(1)} %bitcast.8), channel_id=1, source_target_pairs={{0,28},{1,29},{2,3},{3,2},{4,0},{5,1},{6,7},{7,6},{8,4},{9,5},{10,... | collective-permute-start | bytes 1105928 | tf_op jit(solution)/shard_map/ppermute | solution.py:314
  19.9 8.4 %collective-permute-start.6 = (bf16[160,1152]{1,0:T(8,128)(2,1)S(1)}, bf16[160,1152]{1,0:T(8,128)(2,1)S(1)}, u32[]{:S(2)}, u32[]{:S(2)}) collective-permute-start(bf16[160,1152]{1,0:T(8,128)(2,1)S(1)} %bitcast.7), channel_id=1, source_target_pairs={{0,1},{1,0},{2,30},{3,31},{4,5},{5,4},{6,2},{7,3},{8,9},{9,8},{10,... | collective-permute-start | bytes 1105928 | tf_op jit(solution)/shard_map/ppermute | solution.py:314

commit v20 on v18

--- a/solution.py
+++ b/solution.py
@@ -136,7 +136,9 @@
     return got.at[0], [got.at[k + 1] for k in range(far)]
 
 
-def first_kernel(far, params, row_targets, image, text, mate_image, mate_text, got, back):
+def first_kernel(
+    far, params, row_targets, image, text, mate_image, mate_text, got, back, part
+):
     visit, far_text = parted(far, got)
 
     def on_first(node):
@@ -150,11 +152,12 @@
             pairs = text_pairs(row_targets, lax.rem(node + k + 1, far + 1))
             images = [image, mate_image, visit]
             back[k] = drawn(params, far_text[k], images, pairs).astype(HALF)
+        part[...] = drawn(params, visit, [text, *far_text, mate_text])
 
     by_role(on_first, on_second)
 
 
-def second_kernel(far, params, row_targets, image, text, mate_text, got, mate_got, back):
+def second_kernel(far, params, row_targets, image, got, mate_got, part, back):
     visit, far_text = parted(far, got)
     mate_visit, mate_far = parted(far, mate_got)
 
@@ -165,8 +168,7 @@
             back[k] = drawn(params, far_text[k], images, pairs).astype(HALF)
 
     def on_second(node):
-        texts = [text, *far_text, mate_text, *mate_far]
-        back[0] = drawn(params, visit, texts).astype(HALF)
+        back[0] = (part[...] + drawn(params, visit, mate_far)).astype(HALF)
 
     by_role(on_first, on_second)
 
@@ -233,7 +235,7 @@
     image, text, received = refs[0:3], refs[3:6], refs[6 : 6 + far]
     image_grads, text_grads, held, sems = refs[6 + far :]
     rows = held.shape[0]
-    part = rows // 2 if rows % 32 == 0 else rows
+    part = rows // 5 if rows % 80 == 0 else rows
 
     def run(own, count, ready_out, out, node):
         copies = [pltpu.make_async_copy(ready, ready_out, sems.at[0])]
@@ -279,7 +281,7 @@
         out_shape=[jax.ShapeDtypeStruct(*block)] * 2,
         in_specs=[pl.BlockSpec(memory_space=pltpu.VMEM)] * len(operands),
         out_specs=[anywhere] * 2,
-        scratch_shapes=[pltpu.VMEM(*block), pltpu.SemaphoreType.DMA((3,))],
+        scratch_shapes=[pltpu.VMEM(*block), pltpu.SemaphoreType.DMA((6,))],
         compiler_params=pltpu.CompilerParams(vmem_limit_bytes=VMEM_LIMIT),
     )(*operands)
 
@@ -310,6 +312,7 @@
     returns = ((far, rows, width), HALF)
 
     visit_raw = send(image_embeds, ahead, ahead)
+    far_raw = [send(text_embeds, (0, -k), (0, -k)) for k in range(1, node_count)]
 
     image_raw, text_raw, image, text, image_inv, text_inv = call(
         unit_kernel,
@@ -319,8 +322,6 @@
         anywhere=2,
         scratch=[pltpu.SemaphoreType.DMA((2,))],
     )
-    reports, image_inv = lax.optimization_barrier((text_embeds, image_inv))
-    far_raw = [send(reports, (0, -k), (0, -k)) for k in range(1, node_count)]
     mate_image = swap(image)
     mate_text = swap(text)
     names = pair_text.reshape(-1, 128)
@@ -340,18 +341,19 @@
         [visit, *far_raw, mate_image, mate_text],
         [((node_count, rows, width), HALF)],
     )
-    (back,) = call(
+    back, part = call(
         functools.partial(first_kernel, far),
         "first",
         [params, row_targets, image, text, mate_image, mate_text, got],
-        [returns],
-    )
+        [returns, block_f],
+    )
+    got, part = lax.optimization_barrier((got, part))
+    mate_got = swap(got)
     one = [send(back[k], behind if k == 0 else stay, (0, k + 1)) for k in range(far)]
-    mate_got = swap(got)
     (back,) = call(
         functools.partial(second_kernel, far),
         "second",
-        [params, row_targets, image, text, mate_text, got, mate_got],
+        [params, row_targets, image, got, mate_got, part],
         [returns],
     )
     two = [send(back[k], (0, k + 1), behind if k == 0 else stay) for k in range(far)]

time: 29.6 us -> 29.1 us (0.983)
  starting transfers between devices: 9.61 us -> 8.52 us
  waiting for transfers between devices: 9.61 us -> 10.4 us
    ppermute x7, starting transfers between devices: 9.61 us -> 8.52 us  [send(): return lax.ppermute(block, ('blk', 'node'), route)]
    ppermute x7, waiting for transfers between devices: 9.61 us -> 10.4 us  [send(): return lax.ppermute(block, ('blk', 'node'), route)]
  transfers between devices with their start and end apart: 7 -> 7, of which waited for: 3 -> 4; matrix products, arithmetic and copies ran while one was open for 0% -> 0% of each run, Pallas kernels for 23% -> 20%
where the time goes in v20:
time: 29.1 us; the launch traced here: 28.9 us
  waiting for transfers between devices  10.4 us (36%)
  starting transfers between devices  8.52 us (29%)
  Pallas kernels  7.93 us (27%)
  between operations  2.02 us (7%)
    ppermute x7, waiting for transfers between devices, send(): return lax.ppermute(block, ('blk', 'node'), route)  10.4 us
    ppermute x7, starting transfers between devices, send(): return lax.ppermute(block, ('blk', 'node'), route)  8.52 us
    pallas_call x8, Pallas kernels, call(): pl.pallas_call(kernel, name=name, out_shape=[pltpu.VMEM(s, d) for s, d in...  6.78 us
    pallas_call x1, Pallas kernels, last(): pl.pallas_call(functools.partial(last_kernel, far), name='last', out_shap...  1.15 us
  transfers between devices with their start and end apart: 7, of which 4 were waited for; matrix products, arithmetic and copies ran while one was open for 0% of the time, Pallas kernels for 20%

profile of v20, /device:TPU:0, one launch (start us, length us, event | category | flops | bytes accessed | tf_op | source)
XLA Modules:
  0.0 28.9 jit_solution(2237309431640653623)
XLA Ops:
  0.6 3.0 %collective-permute-start.3 = (bf16[160,1152]{1,0:T(8,128)(2,1)}, bf16[160,1152]{1,0:T(8,128)(2,1)S(1)}, u32[]{:S(2)}, u32[]{:S(2)}) collective-permute-start(bf16[160,1152]{1,0:T(8,128)(2,1)} %image.1), channel_id=1, source_target_pairs={{0,4},{1,5},{2,6},{3,7},{4,8},{5,9},{6,10},{7,11},{8,12},{9,13},{1... | collective-permute-start | bytes 1105928 | tf_op jit(solution)/shard_map/ppermute | solution.py:302
  3.6 1.5 %collective-permute-start.2 = (bf16[160,1152]{1,0:T(8,128)(2,1)}, bf16[160,1152]{1,0:T(8,128)(2,1)S(1)}, u32[]{:S(2)}, u32[]{:S(2)}) collective-permute-start(bf16[160,1152]{1,0:T(8,128)(2,1)} %text.1), channel_id=1, source_target_pairs={{0,1},{1,0},{2,3},{3,2},{4,5},{5,4},{6,7},{7,6},{8,9},{9,8},{10,11... | collective-permute-start | bytes 1105928 | tf_op jit(solution)/shard_map/ppermute | solution.py:302
  5.1 1.3 %unit.1 = (bf16[160,1152]{1,0:T(8,128)(2,1)S(1)}, bf16[160,1152]{1,0:T(8,128)(2,1)S(1)}, bf16[160,1152]{1,0:T(8,128)(2,1)S(1)}, bf16[160,1152]{1,0:T(8,128)(2,1)...) custom-call(bf16[160,1152]{1,0:T(8,128)(2,1)} %image.1, bf16[160,1152]{1,0:T(8,128)(2,1)} %text.1), custom_call_target="tpu_custom_call" | custom-call | tf_op jit(solution)/shard_map/unit/pallas_call | solution.py:264
  6.5 0.1 collective-permute-start.1
  6.6 0.5 %collective-permute-start = (bf16[160,1152]{1,0:T(8,128)(2,1)S(1)}, bf16[160,1152]{1,0:T(8,128)(2,1)S(1)}, u32[]{:S(2)}, u32[]{:S(2)}) collective-permute-start(bf16[160,1152]{1,0:T(8,128)(2,1)S(1)} %get-tuple-element.24.image), channel_id=1, source_target_pairs={{0,2},{1,3},{2,0},{3,1},{4,6},{5,7},{6,4},{7,5},{8,10},{9,11},{10,... | collective-permute-start | bytes 1105928 | tf_op jit(solution)/shard_map/ppermute | solution.py:302
  8.3 1.1 %prep.1 = (f32[8,128]{1,0:T(8,128)S(1)}, s32[1,480]{1,0:T(1,128)S(1)}, s32[160,1]{1,0:T(8,128)S(1)}) custom-call(s32[40,128]{1,0:T(8,128)} %bitcast.9, f32[1,1]{1,0:T(1,128)} %bitcast.5.scale, f32[1,1]{1,0:T(1,128)} %bitcast.6.bias, f32[160,1]{1,0:T(8,128)S(1)} %get-tuple-element.20.after.image_inv.refs_1_), custom_call_target="tpu_custom_call" | custom-call | tf_op jit(solution)/shard_map/prep/pallas_call | solution.py:264
  9.5 6.0 %collective-permute-done.3.raw = bf16[160,1152]{1,0:T(8,128)(2,1)S(1)} collective-permute-done((bf16[160,1152]{1,0:T(8,128)(2,1)}, bf16[160,1152]{1,0:T(8,128)(2,1)S(1)}, u32[]{:S(2)}, u32[]{:S(2)}) %collective-permute-start.3) | collective-permute-done | bytes 368672 | tf_op jit(solution)/shard_map/ppermute | solution.py:302
  15.5 0.2 visit.1
  15.6 0.0 collective-permute-done.2.refs_0_
  15.6 0.0 collective-permute-done.1.refs_2_.mate_text
  15.6 0.0 collective-permute-done.refs_1_.mate_image
  15.7 0.2 got.1
  15.8 0.8 %first.1 = (bf16[1,160,1152]{2,1,0:T(8,128)(2,1)S(1)}, f32[160,1152]{1,0:T(8,128)S(1)}) custom-call(f32[8,128]{1,0:T(8,128)S(1)} %get-tuple-element.21.after.params, s32[1,480]{1,0:T(1,128)S(1)} %get-tuple-element.22.row_targets, bf16[160,1152]{1,0:T(8,128)(2,1)S(1)} %get-tuple-element.24.image, bf16[160,1152]{1,0:T(8,128)(2,1)S(1)} %get-tuple-element.25.text, ...), custom_call_target="tpu_custom_call" | custom-call | tf_op jit(solution)/shard_map/first/pallas_call | solution.py:264
  16.7 0.1 collective-permute-start.4
  16.7 1.8 %collective-permute-start.5 = (bf16[160,1152]{1,0:T(8,128)(2,1)S(1)}, bf16[160,1152]{1,0:T(8,128)(2,1)S(1)}, u32[]{:S(2)}, u32[]{:S(2)}) collective-permute-start(bf16[160,1152]{1,0:T(8,128)(2,1)S(1)} %bitcast.8), channel_id=1, source_target_pairs={{0,28},{1,29},{2,3},{3,2},{4,0},{5,1},{6,7},{7,6},{8,4},{9,5},{10,... | collective-permute-start | bytes 1105928 | tf_op jit(solution)/shard_map/ppermute | solution.py:302
  18.5 0.4 %collective-permute-done.4.mate_got = bf16[2,160,1152]{2,1,0:T(8,128)(2,1)S(1)} collective-permute-done((bf16[2,160,1152]{2,1,0:T(8,128)(2,1)S(1)}, bf16[2,160,1152]{2,1,0:T(8,128)(2,1)S(1)}, u32[]{:S(2)}, u32[]{:S(2)}) %collective-permute-start.4) | collective-permute-done | bytes 737312 | tf_op jit(solution)/shard_map/ppermute | solution.py:302
  18.9 0.9 %second.1 = bf16[1,160,1152]{2,1,0:T(8,128)(2,1)S(1)} custom-call(f32[8,128]{1,0:T(8,128)S(1)} %get-tuple-element.21.after.params, s32[1,480]{1,0:T(1,128)S(1)} %get-tuple-element.22.row_targets, bf16[160,1152]{1,0:T(8,128)(2,1)S(1)} %get-tuple-element.24.image, bf16[2,160,1152]{2,1,0:T(8,128)(2,1)S(1)} %got.1, ...), custom_call_target="tpu_custom_call" | custom-call | tf_op jit(solution)/shard_map/second/pallas_call | solution.py:264
  19.8 1.6 %collective-permute-start.6 = (bf16[160,1152]{1,0:T(8,128)(2,1)S(1)}, bf16[160,1152]{1,0:T(8,128)(2,1)S(1)}, u32[]{:S(2)}, u32[]{:S(2)}) collective-permute-start(bf16[160,1152]{1,0:T(8,128)(2,1)S(1)} %bitcast.7), channel_id=1, source_target_pairs={{0,1},{1,0},{2,30},{3,31},{4,5},{5,4},{6,2},{7,3},{8,9},{9,8},{10,... | collective-permute-start | bytes 1105928 | tf_op jit(solution)/shard_map/ppermute | solution.py:302
  21.4 2.0 %third.1 = (f32[160,1152]{1,0:T(8,128)S(1)}, f32[160,1152]{1,0:T(8,128)S(1)}) custom-call(f32[8,128]{1,0:T(8,128)S(1)} %get-tuple-element.21.after.params, s32[1,480]{1,0:T(1,128)S(1)} %get-tuple-element.22.row_targets, s32[160,1]{1,0:T(8,128)S(1)} %get-tuple-element.23.targets, bf16[160,1152]{1,0:T(8,128)(2,1)S(1)} %get-tuple-element.24.image, ...), custom_call_target="tpu_custom_call" | custom-call | tf_op jit(solution)/shard_map/third/pallas_call | solution.py:264
  23.4 2.8 %collective-permute-done.5.refs_6_ = bf16[160,1152]{1,0:T(8,128)(2,1)S(1)} collective-permute-done((bf16[160,1152]{1,0:T(8,128)(2,1)S(1)}, bf16[160,1152]{1,0:T(8,128)(2,1)S(1)}, u32[]{:S(2)}, u32[]{:S(2)}) %collective-permute-start.5) | collective-permute-done | bytes 368672 | tf_op jit(solution)/shard_map/ppermute | solution.py:302
  26.1 0.3 %fourth.1.ready = f32[160,1152]{1,0:T(8,128)S(1)} custom-call(bf16[160,1152]{1,0:T(8,128)(2,1)S(1)} %get-tuple-element.19.image_raw.refs_0_, f32[160,1]{1,0:T(8,128)S(1)} %get-tuple-element.20.after.image_inv.refs_1_, f32[160,1152]{1,0:T(8,128)S(1)} %get-tuple-element.32.refs_2_, bf16[160,1152]{1,0:T(8,128)(2,1)S(1)} %get-tuple-element.30.text_raw.refs_3_, ...), custom_call_target="tpu_custom_call" | custom-call | tf_op jit(solution)/shard_map/fourth/pallas_call | solution.py:264
  26.5 1.2 %collective-permute-done.6.refs_6_ = bf16[160,1152]{1,0:T(8,128)(2,1)S(1)} collective-permute-done((bf16[160,1152]{1,0:T(8,128)(2,1)S(1)}, bf16[160,1152]{1,0:T(8,128)(2,1)S(1)}, u32[]{:S(2)}, u32[]{:S(2)}) %collective-permute-start.6) | collective-permute-done | bytes 368672 | tf_op jit(solution)/shard_map/ppermute | solution.py:302
  27.7 1.1 %last.1 = (f32[160,1152]{1,0:T(8,128)}, f32[160,1152]{1,0:T(8,128)}) custom-call(f32[160,1152]{1,0:T(8,128)S(1)} %fourth.1.ready, bf16[160,1152]{1,0:T(8,128)(2,1)S(1)} %get-tuple-element.19.image_raw.refs_0_, f32[160,1]{1,0:T(8,128)S(1)} %get-tuple-element.20.after.image_inv.refs_1_, f32[160,1152]{1,0:T(8,128)S(1)} %get-tuple-element.32.refs_2_, ...), custom_call_target="tpu_custom_call" | custom-call | tf_op jit(solution)/shard_map/last/pallas_call | solution.py:278
Async XLA Ops:
  0.6 14.8 %collective-permute-start.3 = (bf16[160,1152]{1,0:T(8,128)(2,1)}, bf16[160,1152]{1,0:T(8,128)(2,1)S(1)}, u32[]{:S(2)}, u32[]{:S(2)}) collective-permute-start(bf16[160,1152]{1,0:T(8,128)(2,1)} %image.1), channel_id=1, source_target_pairs={{0,4},{1,5},{2,6},{3,7},{4,8},{5,9},{6,10},{7,11},{8,12},{9,13},{1... | collective-permute-start | bytes 1105928 | tf_op jit(solution)/shard_map/ppermute | solution.py:302
  3.6 12.0 %collective-permute-start.2 = (bf16[160,1152]{1,0:T(8,128)(2,1)}, bf16[160,1152]{1,0:T(8,128)(2,1)S(1)}, u32[]{:S(2)}, u32[]{:S(2)}) collective-permute-start(bf16[160,1152]{1,0:T(8,128)(2,1)} %text.1), channel_id=1, source_target_pairs={{0,1},{1,0},{2,3},{3,2},{4,5},{5,4},{6,7},{7,6},{8,9},{9,8},{10,11... | collective-permute-start | bytes 1105928 | tf_op jit(solution)/shard_map/ppermute | solution.py:302
  6.5 9.2 %collective-permute-start.1 = (bf16[160,1152]{1,0:T(8,128)(2,1)S(1)}, bf16[160,1152]{1,0:T(8,128)(2,1)S(1)}, u32[]{:S(2)}, u32[]{:S(2)}) collective-permute-start(bf16[160,1152]{1,0:T(8,128)(2,1)S(1)} %get-tuple-element.25.text), channel_id=1, source_target_pairs={{0,2},{1,3},{2,0},{3,1},{4,6},{5,7},{6,4},{7,5},{8,10},{9,11},{10,... | collective-permute-start | bytes 1105928 | tf_op jit(solution)/shard_map/ppermute | solution.py:302
  6.6 9.1 %collective-permute-start = (bf16[160,1152]{1,0:T(8,128)(2,1)S(1)}, bf16[160,1152]{1,0:T(8,128)(2,1)S(1)}, u32[]{:S(2)}, u32[]{:S(2)}) collective-permute-start(bf16[160,1152]{1,0:T(8,128)(2,1)S(1)} %get-tuple-element.24.image), channel_id=1, source_target_pairs={{0,2},{1,3},{2,0},{3,1},{4,6},{5,7},{6,4},{7,5},{8,10},{9,11},{10,... | collective-permute-start | bytes 1105928 | tf_op jit(solution)/shard_map/ppermute | solution.py:302
  16.7 2.3 %collective-permute-start.4 = (bf16[2,160,1152]{2,1,0:T(8,128)(2,1)S(1)}, bf16[2,160,1152]{2,1,0:T(8,128)(2,1)S(1)}, u32[]{:S(2)}, u32[]{:S(2)}) collective-permute-start(bf16[2,160,1152]{2,1,0:T(8,128)(2,1)S(1)} %got.1), channel_id=1, source_target_pairs={{0,2},{1,3},{2,0},{3,1},{4,6},{5,7},{6,4},{7,5},{8,10},{9,11},{10,... | collective-permute-start | bytes 2211848 | tf_op jit(solution)/shard_map/ppermute | solution.py:302
  16.7 9.4 %collective-permute-start.5 = (bf16[160,1152]{1,0:T(8,128)(2,1)S(1)}, bf16[160,1152]{1,0:T(8,128)(2,1)S(1)}, u32[]{:S(2)}, u32[]{:S(2)}) collective-permute-start(bf16[160,1152]{1,0:T(8,128)(2,1)S(1)} %bitcast.8), channel_id=1, source_target_pairs={{0,28},{1,29},{2,3},{3,2},{4,0},{5,1},{6,7},{7,6},{8,4},{9,5},{10,... | collective-permute-start | bytes 1105928 | tf_op jit(solution)/shard_map/ppermute | solution.py:302
  19.8 7.9 %collective-permute-start.6 = (bf16[160,1152]{1,0:T(8,128)(2,1)S(1)}, bf16[160,1152]{1,0:T(8,128)(2,1)S(1)}, u32[]{:S(2)}, u32[]{:S(2)}) collective-permute-start(bf16[160,1152]{1,0:T(8,128)(2,1)S(1)} %bitcast.7), channel_id=1, source_target_pairs={{0,1},{1,0},{2,30},{3,31},{4,5},{5,4},{6,2},{7,3},{8,9},{9,8},{10,... | collective-permute-start | bytes 1105928 | tf_op jit(solution)/shard_map/ppermute | solution.py:302

commit v21 on v20

--- a/solution.py
+++ b/solution.py
@@ -38,6 +38,22 @@
             jnp.where(pairs, -logits, logits)
         )
     return jnp.dot(weights.astype(HALF), vectors, preferred_element_type=FULL)
+
+
+def drawn_apart(params, rows, partners):
+    scale, bias = params[0:1, 0:1], params[1:2, 0:1]
+    dots = [
+        lax.dot_general(
+            rows[...], partner[...], (((1,), (1,)), ((), ())), preferred_element_type=FULL
+        )
+        for partner in partners
+    ]
+    weights = [(scale * jax.nn.sigmoid(scale * dot + bias)).astype(HALF) for dot in dots]
+    total = None
+    for weight, partner in zip(weights, partners):
+        term = jnp.dot(weight, partner[...], preferred_element_type=FULL)
+        total = term if total is None else total + term
+    return total
 
 
 def text_pairs(targets, node):
@@ -142,10 +158,7 @@
     visit, far_text = parted(far, got)
 
     def on_first(node):
-        total = drawn(params, visit, [text])
-        for k in range(far):
-            total += drawn(params, visit, [far_text[k]])
-        back[0] = total.astype(HALF)
+        back[0] = drawn_apart(params, visit, [text, *far_text]).astype(HALF)
 
     def on_second(node):
         for k in range(far):
@@ -222,38 +235,28 @@
         out[piece, :] = gradient * inv - values * along + part[piece, :]
 
 
-def fourth_kernel(far, *refs):
-    image, text, received, ready = refs[0:3], refs[3:6], refs[6 : 6 + far], refs[6 + far]
-
-    def run(own, count, node):
-        finish(received, own, count, ready, 0, ready.shape[0])
-
-    by_role(functools.partial(run, image, 1), functools.partial(run, text, far))
-
-
-def last_kernel(far, ready, *refs):
+def out_kernel(far, image_on_first, *refs):
     image, text, received = refs[0:3], refs[3:6], refs[6 : 6 + far]
-    image_grads, text_grads, held, sems = refs[6 + far :]
+    image_grads, text_grads, held, sems = refs[-4:]
     rows = held.shape[0]
     part = rows // 5 if rows % 80 == 0 else rows
 
-    def run(own, count, ready_out, out, node):
-        copies = [pltpu.make_async_copy(ready, ready_out, sems.at[0])]
-        copies[0].start()
+    def run(own, count, out, node):
+        copies = []
         for i, at in enumerate(range(0, rows, part)):
             finish(received, own, count, held, at, at + part)
             piece = pl.ds(at, part)
-            copies.append(
-                pltpu.make_async_copy(held.at[piece], out.at[piece], sems.at[i + 1])
-            )
+            copies.append(pltpu.make_async_copy(held.at[piece], out.at[piece], sems.at[i]))
             copies[-1].start()
         for copy in copies:
             copy.wait()
 
-    by_role(
-        functools.partial(run, text, far, image_grads, text_grads),
-        functools.partial(run, image, 1, text_grads, image_grads),
-    )
+    on_images = functools.partial(run, image, 1, image_grads)
+    on_texts = functools.partial(run, text, far, text_grads)
+    if image_on_first:
+        by_role(on_images, on_texts)
+    else:
+        by_role(on_texts, on_images)
 
 
 def call(kernel, name, operands, shapes, anywhere=0, scratch=()):
@@ -273,17 +276,19 @@
     )(*operands)
 
 
-def last(far, operands, block):
+def write_out(far, image_on_first, operands, grads, block):
     anywhere = pl.BlockSpec(memory_space=pl.ANY)
+    count = len(operands)
     return pl.pallas_call(
-        functools.partial(last_kernel, far),
-        name="last",
+        functools.partial(out_kernel, far, image_on_first),
+        name="out",
         out_shape=[jax.ShapeDtypeStruct(*block)] * 2,
-        in_specs=[pl.BlockSpec(memory_space=pltpu.VMEM)] * len(operands),
+        in_specs=[pl.BlockSpec(memory_space=pltpu.VMEM)] * count + [anywhere] * len(grads),
         out_specs=[anywhere] * 2,
-        scratch_shapes=[pltpu.VMEM(*block), pltpu.SemaphoreType.DMA((6,))],
+        scratch_shapes=[pltpu.VMEM(*block), pltpu.SemaphoreType.DMA((5,))],
+        input_output_aliases={count + i: i for i in range(len(grads))},
         compiler_params=pltpu.CompilerParams(vmem_limit_bytes=VMEM_LIMIT),
-    )(*operands)
+    )(*operands, *grads)
 
 
 def local(image_embeds, text_embeds, pair_text, similarity_scale, logit_bias):
@@ -365,10 +370,8 @@
         [block_f, block_f],
     )
     own = [image_raw, image_inv, image_part, text_raw, text_inv, text_part]
-    (ready,) = call(
-        functools.partial(fourth_kernel, far), "fourth", [*own, *one], [block_f]
-    )
-    return tuple(last(far, [ready, *own, *two], block_f))
+    grads = write_out(far, True, [*own, *one], [], block_f)
+    return tuple(write_out(far, False, [*own, *two], grads, block_f))
 
 
 def solution(mesh):

time: 29.1 us -> 29.1 us (level)
  waiting for transfers between devices: 10.4 us -> 9.62 us
  Pallas kernels: 7.93 us -> 8.69 us
    pallas_call x1 -> x2, Pallas kernels: 1.15 us -> 2.25 us  [write_out(): pl.pallas_call(functools.partial(out_kernel, far, image_on_first), name='...]
    ppermute x7, waiting for transfers between devices: 10.4 us -> 9.62 us  [send(): return lax.ppermute(block, ('blk', 'node'), route)]
    pallas_call x8 -> x7, Pallas kernels: 6.78 us -> 6.45 us  [call(): pl.pallas_call(kernel, name=name, out_shape=[pltpu.VMEM(s, d) for s, d in...]
  transfers between devices with their start and end apart: 7 -> 7, of which waited for: 4 -> 4; matrix products, arithmetic and copies ran while one was open for 0% -> 0% of each run, Pallas kernels for 20% -> 23%
where the time goes in v21:
time: 29.1 us; the launch traced here: 28.8 us
  waiting for transfers between devices  9.62 us (33%)
  Pallas kernels  8.69 us (30%)
  starting transfers between devices  8.52 us (29%)
  between operations  2.02 us (7%)
    ppermute x7, waiting for transfers between devices, send(): return lax.ppermute(block, ('blk', 'node'), route)  9.62 us
    ppermute x7, starting transfers between devices, send(): return lax.ppermute(block, ('blk', 'node'), route)  8.52 us
    pallas_call x7, Pallas kernels, call(): pl.pallas_call(kernel, name=name, out_shape=[pltpu.VMEM(s, d) for s, d in...  6.45 us
    pallas_call x2, Pallas kernels, write_out(): pl.pallas_call(functools.partial(out_kernel, far, image_on_first), name='...  2.25 us
  transfers between devices with their start and end apart: 7, of which 4 were waited for; matrix products, arithmetic and copies ran while one was open for 0% of the time, Pallas kernels for 23%

profile of v21, /device:TPU:0, one launch (start us, length us, event | category | flops | bytes accessed | tf_op | source)
XLA Modules:
  0.0 28.8 jit_solution(9794343857685335204)
XLA Ops:
  0.6 3.0 %collective-permute-start.3 = (bf16[160,1152]{1,0:T(8,128)(2,1)}, bf16[160,1152]{1,0:T(8,128)(2,1)S(1)}, u32[]{:S(2)}, u32[]{:S(2)}) collective-permute-start(bf16[160,1152]{1,0:T(8,128)(2,1)} %image.1), channel_id=1, source_target_pairs={{0,4},{1,5},{2,6},{3,7},{4,8},{5,9},{6,10},{7,11},{8,12},{9,13},{1... | collective-permute-start | bytes 1105928 | tf_op jit(solution)/shard_map/ppermute | solution.py:307
  3.6 1.5 %collective-permute-start.2 = (bf16[160,1152]{1,0:T(8,128)(2,1)}, bf16[160,1152]{1,0:T(8,128)(2,1)S(1)}, u32[]{:S(2)}, u32[]{:S(2)}) collective-permute-start(bf16[160,1152]{1,0:T(8,128)(2,1)} %text.1), channel_id=1, source_target_pairs={{0,1},{1,0},{2,3},{3,2},{4,5},{5,4},{6,7},{7,6},{8,9},{9,8},{10,11... | collective-permute-start | bytes 1105928 | tf_op jit(solution)/shard_map/ppermute | solution.py:307
  5.1 1.3 %unit.1 = (bf16[160,1152]{1,0:T(8,128)(2,1)S(1)}, bf16[160,1152]{1,0:T(8,128)(2,1)S(1)}, bf16[160,1152]{1,0:T(8,128)(2,1)S(1)}, bf16[160,1152]{1,0:T(8,128)(2,1)...) custom-call(bf16[160,1152]{1,0:T(8,128)(2,1)} %image.1, bf16[160,1152]{1,0:T(8,128)(2,1)} %text.1), custom_call_target="tpu_custom_call" | custom-call | tf_op jit(solution)/shard_map/unit/pallas_call | solution.py:267
  6.5 0.1 collective-permute-start.1
  6.6 0.5 %collective-permute-start = (bf16[160,1152]{1,0:T(8,128)(2,1)S(1)}, bf16[160,1152]{1,0:T(8,128)(2,1)S(1)}, u32[]{:S(2)}, u32[]{:S(2)}) collective-permute-start(bf16[160,1152]{1,0:T(8,128)(2,1)S(1)} %get-tuple-element.26.image), channel_id=1, source_target_pairs={{0,2},{1,3},{2,0},{3,1},{4,6},{5,7},{6,4},{7,5},{8,10},{9,11},{10,... | collective-permute-start | bytes 1105928 | tf_op jit(solution)/shard_map/ppermute | solution.py:307
  8.3 1.1 %prep.1 = (f32[8,128]{1,0:T(8,128)S(1)}, s32[1,480]{1,0:T(1,128)S(1)}, s32[160,1]{1,0:T(8,128)S(1)}) custom-call(s32[40,128]{1,0:T(8,128)} %bitcast.9, f32[1,1]{1,0:T(1,128)} %bitcast.5.scale, f32[1,1]{1,0:T(1,128)} %bitcast.6.bias, f32[160,1]{1,0:T(8,128)S(1)} %get-tuple-element.22.after.image_inv.refs_1_), custom_call_target="tpu_custom_call" | custom-call | tf_op jit(solution)/shard_map/prep/pallas_call | solution.py:267
  9.5 6.0 %collective-permute-done.3.raw = bf16[160,1152]{1,0:T(8,128)(2,1)S(1)} collective-permute-done((bf16[160,1152]{1,0:T(8,128)(2,1)}, bf16[160,1152]{1,0:T(8,128)(2,1)S(1)}, u32[]{:S(2)}, u32[]{:S(2)}) %collective-permute-start.3) | collective-permute-done | bytes 368672 | tf_op jit(solution)/shard_map/ppermute | solution.py:307
  15.5 0.2 visit.1
  15.6 0.0 collective-permute-done.2.refs_0_
  15.6 0.0 collective-permute-done.1.refs_2_.mate_text
  15.6 0.0 collective-permute-done.refs_1_.mate_image
  15.7 0.2 got.1
  15.8 0.8 %first.1 = (bf16[1,160,1152]{2,1,0:T(8,128)(2,1)S(1)}, f32[160,1152]{1,0:T(8,128)S(1)}) custom-call(f32[8,128]{1,0:T(8,128)S(1)} %get-tuple-element.23.after.params, s32[1,480]{1,0:T(1,128)S(1)} %get-tuple-element.24.row_targets, bf16[160,1152]{1,0:T(8,128)(2,1)S(1)} %get-tuple-element.26.image, bf16[160,1152]{1,0:T(8,128)(2,1)S(1)} %get-tuple-element.27.text, ...), custom_call_target="tpu_custom_call" | custom-call | tf_op jit(solution)/shard_map/first/pallas_call | solution.py:267
  16.7 0.1 collective-permute-start.4
  16.7 1.8 %collective-permute-start.6 = (bf16[160,1152]{1,0:T(8,128)(2,1)S(1)}, bf16[160,1152]{1,0:T(8,128)(2,1)S(1)}, u32[]{:S(2)}, u32[]{:S(2)}) collective-permute-start(bf16[160,1152]{1,0:T(8,128)(2,1)S(1)} %bitcast.8), channel_id=1, source_target_pairs={{0,28},{1,29},{2,3},{3,2},{4,0},{5,1},{6,7},{7,6},{8,4},{9,5},{10,... | collective-permute-start | bytes 1105928 | tf_op jit(solution)/shard_map/ppermute | solution.py:307
  18.5 0.4 %collective-permute-done.4.mate_got = bf16[2,160,1152]{2,1,0:T(8,128)(2,1)S(1)} collective-permute-done((bf16[2,160,1152]{2,1,0:T(8,128)(2,1)S(1)}, bf16[2,160,1152]{2,1,0:T(8,128)(2,1)S(1)}, u32[]{:S(2)}, u32[]{:S(2)}) %collective-permute-start.4) | collective-permute-done | bytes 737312 | tf_op jit(solution)/shard_map/ppermute | solution.py:307
  18.9 0.9 %second.1 = bf16[1,160,1152]{2,1,0:T(8,128)(2,1)S(1)} custom-call(f32[8,128]{1,0:T(8,128)S(1)} %get-tuple-element.23.after.params, s32[1,480]{1,0:T(1,128)S(1)} %get-tuple-element.24.row_targets, bf16[160,1152]{1,0:T(8,128)(2,1)S(1)} %get-tuple-element.26.image, bf16[2,160,1152]{2,1,0:T(8,128)(2,1)S(1)} %got.1, ...), custom_call_target="tpu_custom_call" | custom-call | tf_op jit(solution)/shard_map/second/pallas_call | solution.py:267
  19.8 1.6 %collective-permute-start.5 = (bf16[160,1152]{1,0:T(8,128)(2,1)S(1)}, bf16[160,1152]{1,0:T(8,128)(2,1)S(1)}, u32[]{:S(2)}, u32[]{:S(2)}) collective-permute-start(bf16[160,1152]{1,0:T(8,128)(2,1)S(1)} %bitcast.7), channel_id=1, source_target_pairs={{0,1},{1,0},{2,30},{3,31},{4,5},{5,4},{6,2},{7,3},{8,9},{9,8},{10,... | collective-permute-start | bytes 1105928 | tf_op jit(solution)/shard_map/ppermute | solution.py:307
  21.4 2.0 %third.1 = (f32[160,1152]{1,0:T(8,128)S(1)}, f32[160,1152]{1,0:T(8,128)S(1)}) custom-call(f32[8,128]{1,0:T(8,128)S(1)} %get-tuple-element.23.after.params, s32[1,480]{1,0:T(1,128)S(1)} %get-tuple-element.24.row_targets, s32[160,1]{1,0:T(8,128)S(1)} %get-tuple-element.25.targets, bf16[160,1152]{1,0:T(8,128)(2,1)S(1)} %get-tuple-element.26.image, ...), custom_call_target="tpu_custom_call" | custom-call | tf_op jit(solution)/shard_map/third/pallas_call | solution.py:267
  23.4 2.8 %collective-permute-done.6.refs_6_ = bf16[160,1152]{1,0:T(8,128)(2,1)S(1)} collective-permute-done((bf16[160,1152]{1,0:T(8,128)(2,1)S(1)}, bf16[160,1152]{1,0:T(8,128)(2,1)S(1)}, u32[]{:S(2)}, u32[]{:S(2)}) %collective-permute-start.6) | collective-permute-done | bytes 368672 | tf_op jit(solution)/shard_map/ppermute | solution.py:307
  26.1 1.1 %out.2 = (f32[160,1152]{1,0:T(8,128)}, f32[160,1152]{1,0:T(8,128)}) custom-call(bf16[160,1152]{1,0:T(8,128)(2,1)S(1)} %get-tuple-element.21.image_raw.refs_0_, f32[160,1]{1,0:T(8,128)S(1)} %get-tuple-element.22.after.image_inv.refs_1_, f32[160,1152]{1,0:T(8,128)S(1)} %get-tuple-element.34.refs_2_, bf16[160,1152]{1,0:T(8,128)(2,1)S(1)} %get-tuple-element.32.text_raw.refs_3_, ...), custom_call_target="tpu_custom_call" | custom-call | tf_op jit(solution)/shard_map/out/pallas_call | solution.py:282
  27.3 0.5 %collective-permute-done.5.refs_6_ = bf16[160,1152]{1,0:T(8,128)(2,1)S(1)} collective-permute-done((bf16[160,1152]{1,0:T(8,128)(2,1)S(1)}, bf16[160,1152]{1,0:T(8,128)(2,1)S(1)}, u32[]{:S(2)}, u32[]{:S(2)}) %collective-permute-start.5) | collective-permute-done | bytes 368672 | tf_op jit(solution)/shard_map/ppermute | solution.py:307
  27.7 1.1 %out.3 = (f32[160,1152]{1,0:T(8,128)}, f32[160,1152]{1,0:T(8,128)}) custom-call(bf16[160,1152]{1,0:T(8,128)(2,1)S(1)} %get-tuple-element.21.image_raw.refs_0_, f32[160,1]{1,0:T(8,128)S(1)} %get-tuple-element.22.after.image_inv.refs_1_, f32[160,1152]{1,0:T(8,128)S(1)} %get-tuple-element.34.refs_2_, ...), custom_call_target="tpu_custom_call", output_to_operand_aliasing={{0}: (7, {}), {1}: (8, {})} | custom-call | tf_op jit(solution)/shard_map/out/pallas_call | solution.py:282
Async XLA Ops:
  0.6 14.8 %collective-permute-start.3 = (bf16[160,1152]{1,0:T(8,128)(2,1)}, bf16[160,1152]{1,0:T(8,128)(2,1)S(1)}, u32[]{:S(2)}, u32[]{:S(2)}) collective-permute-start(bf16[160,1152]{1,0:T(8,128)(2,1)} %image.1), channel_id=1, source_target_pairs={{0,4},{1,5},{2,6},{3,7},{4,8},{5,9},{6,10},{7,11},{8,12},{9,13},{1... | collective-permute-start | bytes 1105928 | tf_op jit(solution)/shard_map/ppermute | solution.py:307
  3.6 12.0 %collective-permute-start.2 = (bf16[160,1152]{1,0:T(8,128)(2,1)}, bf16[160,1152]{1,0:T(8,128)(2,1)S(1)}, u32[]{:S(2)}, u32[]{:S(2)}) collective-permute-start(bf16[160,1152]{1,0:T(8,128)(2,1)} %text.1), channel_id=1, source_target_pairs={{0,1},{1,0},{2,3},{3,2},{4,5},{5,4},{6,7},{7,6},{8,9},{9,8},{10,11... | collective-permute-start | bytes 1105928 | tf_op jit(solution)/shard_map/ppermute | solution.py:307
  6.5 9.2 %collective-permute-start.1 = (bf16[160,1152]{1,0:T(8,128)(2,1)S(1)}, bf16[160,1152]{1,0:T(8,128)(2,1)S(1)}, u32[]{:S(2)}, u32[]{:S(2)}) collective-permute-start(bf16[160,1152]{1,0:T(8,128)(2,1)S(1)} %get-tuple-element.27.text), channel_id=1, source_target_pairs={{0,2},{1,3},{2,0},{3,1},{4,6},{5,7},{6,4},{7,5},{8,10},{9,11},{10,... | collective-permute-start | bytes 1105928 | tf_op jit(solution)/shard_map/ppermute | solution.py:307
  6.6 9.1 %collective-permute-start = (bf16[160,1152]{1,0:T(8,128)(2,1)S(1)}, bf16[160,1152]{1,0:T(8,128)(2,1)S(1)}, u32[]{:S(2)}, u32[]{:S(2)}) collective-permute-start(bf16[160,1152]{1,0:T(8,128)(2,1)S(1)} %get-tuple-element.26.image), channel_id=1, source_target_pairs={{0,2},{1,3},{2,0},{3,1},{4,6},{5,7},{6,4},{7,5},{8,10},{9,11},{10,... | collective-permute-start | bytes 1105928 | tf_op jit(solution)/shard_map/ppermute | solution.py:307
  16.7 2.3 %collective-permute-start.4 = (bf16[2,160,1152]{2,1,0:T(8,128)(2,1)S(1)}, bf16[2,160,1152]{2,1,0:T(8,128)(2,1)S(1)}, u32[]{:S(2)}, u32[]{:S(2)}) collective-permute-start(bf16[2,160,1152]{2,1,0:T(8,128)(2,1)S(1)} %got.1), channel_id=1, source_target_pairs={{0,2},{1,3},{2,0},{3,1},{4,6},{5,7},{6,4},{7,5},{8,10},{9,11},{10,... | collective-permute-start | bytes 2211848 | tf_op jit(solution)/shard_map/ppermute | solution.py:307
  16.7 9.4 %collective-permute-start.6 = (bf16[160,1152]{1,0:T(8,128)(2,1)S(1)}, bf16[160,1152]{1,0:T(8,128)(2,1)S(1)}, u32[]{:S(2)}, u32[]{:S(2)}) collective-permute-start(bf16[160,1152]{1,0:T(8,128)(2,1)S(1)} %bitcast.8), channel_id=1, source_target_pairs={{0,28},{1,29},{2,3},{3,2},{4,0},{5,1},{6,7},{7,6},{8,4},{9,5},{10,... | collective-permute-start | bytes 1105928 | tf_op jit(solution)/shard_map/ppermute | solution.py:307
  19.8 7.9 %collective-permute-start.5 = (bf16[160,1152]{1,0:T(8,128)(2,1)S(1)}, bf16[160,1152]{1,0:T(8,128)(2,1)S(1)}, u32[]{:S(2)}, u32[]{:S(2)}) collective-permute-start(bf16[160,1152]{1,0:T(8,128)(2,1)S(1)} %bitcast.7), channel_id=1, source_target_pairs={{0,1},{1,0},{2,30},{3,31},{4,5},{5,4},{6,2},{7,3},{8,9},{9,8},{10,... | collective-permute-start | bytes 1105928 | tf_op jit(solution)/shard_map/ppermute | solution.py:307

commit v22 on v21

--- a/solution.py
+++ b/solution.py
@@ -40,20 +40,36 @@
     return jnp.dot(weights.astype(HALF), vectors, preferred_element_type=FULL)
 
 
-def drawn_apart(params, rows, partners):
+def drawn_apart(params, rows, partners, paired=()):
     scale, bias = params[0:1, 0:1], params[1:2, 0:1]
-    dots = [
-        lax.dot_general(
+    weights = []
+    for i, partner in enumerate(partners):
+        dots = lax.dot_general(
             rows[...], partner[...], (((1,), (1,)), ((), ())), preferred_element_type=FULL
         )
-        for partner in partners
-    ]
-    weights = [(scale * jax.nn.sigmoid(scale * dot + bias)).astype(HALF) for dot in dots]
+        logits = scale * dots + bias
+        if i < len(paired):
+            pairs = paired[i](logits.shape)
+            weight = jnp.where(pairs, -scale, scale) * jax.nn.sigmoid(
+                jnp.where(pairs, -logits, logits)
+            )
+        else:
+            weight = scale * jax.nn.sigmoid(logits)
+        weights.append(weight.astype(HALF))
     total = None
     for weight, partner in zip(weights, partners):
         term = jnp.dot(weight, partner[...], preferred_element_type=FULL)
         total = term if total is None else total + term
     return total
+
+
+def own_pairs(targets, node):
+    def paired(shape):
+        return lax.broadcasted_iota(jnp.int32, shape, 0) + node * shape[0] == (
+            targets[:, : shape[1]]
+        )
+
+    return [paired]
 
 
 def text_pairs(targets, node):
@@ -170,18 +186,31 @@
     by_role(on_first, on_second)
 
 
-def second_kernel(far, params, row_targets, image, got, mate_got, part, back):
+def middle_kernel(far, params, row_targets, image, got, begun, sums):
+    visit, far_text = parted(far, got)
+
+    def on_first(node):
+        for k in range(far):
+            pairs = own_pairs(row_targets, lax.rem(node + k + 1, far + 1))
+            sums[k] = drawn_apart(params, far_text[k], [image, visit], pairs)
+
+    def on_second(node):
+        pass
+
+    by_role(on_first, on_second)
+
+
+def second_kernel(far, params, got, mate_got, part, sums, back):
     visit, far_text = parted(far, got)
     mate_visit, mate_far = parted(far, mate_got)
 
     def on_first(node):
         for k in range(far):
-            pairs = text_pairs(row_targets, lax.rem(node + k + 1, far + 1))
-            images = [image, visit, mate_visit]
-            back[k] = drawn(params, far_text[k], images, pairs).astype(HALF)
+            total = sums[k] + drawn_apart(params, far_text[k], [mate_visit])
+            back[k] = total.astype(HALF)
 
     def on_second(node):
-        back[0] = (part[...] + drawn(params, visit, mate_far)).astype(HALF)
+        back[0] = (part[...] + drawn_apart(params, visit, mate_far)).astype(HALF)
 
     by_role(on_first, on_second)
 
@@ -355,10 +384,16 @@
     got, part = lax.optimization_barrier((got, part))
     mate_got = swap(got)
     one = [send(back[k], behind if k == 0 else stay, (0, k + 1)) for k in range(far)]
+    (sums,) = call(
+        functools.partial(middle_kernel, far),
+        "middle",
+        [params, row_targets, image, got, part],
+        [((far, rows, width), FULL)],
+    )
     (back,) = call(
         functools.partial(second_kernel, far),
         "second",
-        [params, row_targets, image, got, mate_got, part],
+        [params, got, mate_got, part, sums],
         [returns],
     )
     two = [send(back[k], (0, k + 1), behind if k == 0 else stay) for k in range(far)]

time: 29.1 us -> 29 us (level)
  waiting for transfers between devices: 9.62 us -> 8.99 us
  Pallas kernels: 8.69 us -> 9.28 us
    ppermute x7, waiting for transfers between devices: 9.62 us -> 8.99 us  [send(): return lax.ppermute(block, ('blk', 'node'), route)]
    pallas_call x7 -> x8, Pallas kernels: 6.45 us -> 7.04 us  [call(): pl.pallas_call(kernel, name=name, out_shape=[pltpu.VMEM(s, d) for s, d in...]
  transfers between devices with their start and end apart: 7 -> 7, of which waited for: 4 -> 3; matrix products, arithmetic and copies ran while one was open for 0% -> 0% of each run, Pallas kernels for 23% -> 25%
where the time goes in v22:
time: 29 us; the launch traced here: 28.8 us
  Pallas kernels  9.28 us (32%)
  waiting for transfers between devices  8.99 us (31%)
  starting transfers between devices  8.54 us (29%)
  between operations  2.03 us (7%)
    ppermute x7, waiting for transfers between devices, send(): return lax.ppermute(block, ('blk', 'node'), route)  8.99 us
    ppermute x7, starting transfers between devices, send(): return lax.ppermute(block, ('blk', 'node'), route)  8.54 us
    pallas_call x8, Pallas kernels, call(): pl.pallas_call(kernel, name=name, out_shape=[pltpu.VMEM(s, d) for s, d in...  7.04 us
    pallas_call x2, Pallas kernels, write_out(): pl.pallas_call(functools.partial(out_kernel, far, image_on_first), name='...  2.23 us
  transfers between devices with their start and end apart: 7, of which 3 were waited for; matrix products, arithmetic and copies ran while one was open for 0% of the time, Pallas kernels for 25%

profile of v22, /device:TPU:0, one launch (start us, length us, event | category | flops | bytes accessed | tf_op | source)
XLA Modules:
  0.0 28.8 jit_solution(14894120361241819832)
XLA Ops:
  0.6 3.0 %collective-permute-start.3 = (bf16[160,1152]{1,0:T(8,128)(2,1)}, bf16[160,1152]{1,0:T(8,128)(2,1)S(1)}, u32[]{:S(2)}, u32[]{:S(2)}) collective-permute-start(bf16[160,1152]{1,0:T(8,128)(2,1)} %image.1), channel_id=1, source_target_pairs={{0,4},{1,5},{2,6},{3,7},{4,8},{5,9},{6,10},{7,11},{8,12},{9,13},{1... | collective-permute-start | bytes 1105928 | tf_op jit(solution)/shard_map/ppermute | solution.py:336
  3.6 1.5 %collective-permute-start.2 = (bf16[160,1152]{1,0:T(8,128)(2,1)}, bf16[160,1152]{1,0:T(8,128)(2,1)S(1)}, u32[]{:S(2)}, u32[]{:S(2)}) collective-permute-start(bf16[160,1152]{1,0:T(8,128)(2,1)} %text.1), channel_id=1, source_target_pairs={{0,1},{1,0},{2,3},{3,2},{4,5},{5,4},{6,7},{7,6},{8,9},{9,8},{10,11... | collective-permute-start | bytes 1105928 | tf_op jit(solution)/shard_map/ppermute | solution.py:336
  5.1 1.3 %unit.1 = (bf16[160,1152]{1,0:T(8,128)(2,1)S(1)}, bf16[160,1152]{1,0:T(8,128)(2,1)S(1)}, bf16[160,1152]{1,0:T(8,128)(2,1)S(1)}, bf16[160,1152]{1,0:T(8,128)(2,1)...) custom-call(bf16[160,1152]{1,0:T(8,128)(2,1)} %image.1, bf16[160,1152]{1,0:T(8,128)(2,1)} %text.1), custom_call_target="tpu_custom_call" | custom-call | tf_op jit(solution)/shard_map/unit/pallas_call | solution.py:296
  6.5 0.1 collective-permute-start.1
  6.6 0.5 %collective-permute-start = (bf16[160,1152]{1,0:T(8,128)(2,1)S(1)}, bf16[160,1152]{1,0:T(8,128)(2,1)S(1)}, u32[]{:S(2)}, u32[]{:S(2)}) collective-permute-start(bf16[160,1152]{1,0:T(8,128)(2,1)S(1)} %get-tuple-element.26.image), channel_id=1, source_target_pairs={{0,2},{1,3},{2,0},{3,1},{4,6},{5,7},{6,4},{7,5},{8,10},{9,11},{10,... | collective-permute-start | bytes 1105928 | tf_op jit(solution)/shard_map/ppermute | solution.py:336
  8.3 1.1 %prep.1 = (f32[8,128]{1,0:T(8,128)S(1)}, s32[1,480]{1,0:T(1,128)S(1)}, s32[160,1]{1,0:T(8,128)S(1)}) custom-call(s32[40,128]{1,0:T(8,128)} %bitcast.9, f32[1,1]{1,0:T(1,128)} %bitcast.5.scale, f32[1,1]{1,0:T(1,128)} %bitcast.6.bias, f32[160,1]{1,0:T(8,128)S(1)} %get-tuple-element.22.after.image_inv.refs_1_), custom_call_target="tpu_custom_call" | custom-call | tf_op jit(solution)/shard_map/prep/pallas_call | solution.py:296
  9.5 6.0 %collective-permute-done.3.raw = bf16[160,1152]{1,0:T(8,128)(2,1)S(1)} collective-permute-done((bf16[160,1152]{1,0:T(8,128)(2,1)}, bf16[160,1152]{1,0:T(8,128)(2,1)S(1)}, u32[]{:S(2)}, u32[]{:S(2)}) %collective-permute-start.3) | collective-permute-done | bytes 368672 | tf_op jit(solution)/shard_map/ppermute | solution.py:336
  15.5 0.2 visit.1
  15.6 0.0 collective-permute-done.2.refs_0_
  15.6 0.0 collective-permute-done.1.refs_2_.mate_text
  15.6 0.0 collective-permute-done.refs_1_.mate_image
  15.7 0.2 got.1
  15.8 0.8 %first.1 = (bf16[1,160,1152]{2,1,0:T(8,128)(2,1)S(1)}, f32[160,1152]{1,0:T(8,128)S(1)}) custom-call(f32[8,128]{1,0:T(8,128)S(1)} %get-tuple-element.23.after.params, s32[1,480]{1,0:T(1,128)S(1)} %get-tuple-element.24.row_targets, bf16[160,1152]{1,0:T(8,128)(2,1)S(1)} %get-tuple-element.26.image, bf16[160,1152]{1,0:T(8,128)(2,1)S(1)} %get-tuple-element.27.text, ...), custom_call_target="tpu_custom_call" | custom-call | tf_op jit(solution)/shard_map/first/pallas_call | solution.py:296
  16.6 0.1 collective-permute-start.4
  16.7 1.8 %collective-permute-start.6 = (bf16[160,1152]{1,0:T(8,128)(2,1)S(1)}, bf16[160,1152]{1,0:T(8,128)(2,1)S(1)}, u32[]{:S(2)}, u32[]{:S(2)}) collective-permute-start(bf16[160,1152]{1,0:T(8,128)(2,1)S(1)} %bitcast.8), channel_id=1, source_target_pairs={{0,28},{1,29},{2,3},{3,2},{4,0},{5,1},{6,7},{7,6},{8,4},{9,5},{10,... | collective-permute-start | bytes 1105928 | tf_op jit(solution)/shard_map/ppermute | solution.py:336
  18.5 0.8 %middle.1.sums = f32[1,160,1152]{2,1,0:T(8,128)S(1)} custom-call(f32[8,128]{1,0:T(8,128)S(1)} %get-tuple-element.23.after.params, s32[1,480]{1,0:T(1,128)S(1)} %get-tuple-element.24.row_targets, bf16[160,1152]{1,0:T(8,128)(2,1)S(1)} %get-tuple-element.26.image, bf16[2,160,1152]{2,1,0:T(8,128)(2,1)S(1)} %got.1, f32[160,1152]{1,0:T(8,128)S(1)} %get-tuple-element.36.begun.part), custom_call_target="tpu_custom_call" | custom-call | tf_op jit(solution)/shard_map/middle/pallas_call | solution.py:296
  19.3 0.0 collective-permute-done.4.mate_got
  19.3 0.7 %second.1 = bf16[1,160,1152]{2,1,0:T(8,128)(2,1)S(1)} custom-call(f32[8,128]{1,0:T(8,128)S(1)} %get-tuple-element.23.after.params, bf16[2,160,1152]{2,1,0:T(8,128)(2,1)S(1)} %got.1, bf16[2,160,1152]{2,1,0:T(8,128)(2,1)S(1)} %collective-permute-done.4.mate_got, f32[160,1152]{1,0:T(8,128)S(1)} %get-tuple-element.36.begun.part, f32[1,160,1152]{2,1,0:T(8,128)S(1)} %middle.1.sums), custom_call_target="tpu_custom_call" | custom-call | tf_op jit(solution)/shard_map/second/pallas_call | solution.py:296
  20.0 1.6 %collective-permute-start.5 = (bf16[160,1152]{1,0:T(8,128)(2,1)S(1)}, bf16[160,1152]{1,0:T(8,128)(2,1)S(1)}, u32[]{:S(2)}, u32[]{:S(2)}) collective-permute-start(bf16[160,1152]{1,0:T(8,128)(2,1)S(1)} %bitcast.7), channel_id=1, source_target_pairs={{0,1},{1,0},{2,30},{3,31},{4,5},{5,4},{6,2},{7,3},{8,9},{9,8},{10,... | collective-permute-start | bytes 1105928 | tf_op jit(solution)/shard_map/ppermute | solution.py:336
  21.6 2.0 %third.1 = (f32[160,1152]{1,0:T(8,128)S(1)}, f32[160,1152]{1,0:T(8,128)S(1)}) custom-call(f32[8,128]{1,0:T(8,128)S(1)} %get-tuple-element.23.after.params, s32[1,480]{1,0:T(1,128)S(1)} %get-tuple-element.24.row_targets, s32[160,1]{1,0:T(8,128)S(1)} %get-tuple-element.25.targets, bf16[160,1152]{1,0:T(8,128)(2,1)S(1)} %get-tuple-element.26.image, ...), custom_call_target="tpu_custom_call" | custom-call | tf_op jit(solution)/shard_map/third/pallas_call | solution.py:296
  23.6 2.5 %collective-permute-done.6.refs_6_ = bf16[160,1152]{1,0:T(8,128)(2,1)S(1)} collective-permute-done((bf16[160,1152]{1,0:T(8,128)(2,1)S(1)}, bf16[160,1152]{1,0:T(8,128)(2,1)S(1)}, u32[]{:S(2)}, u32[]{:S(2)}) %collective-permute-start.6) | collective-permute-done | bytes 368672 | tf_op jit(solution)/shard_map/ppermute | solution.py:336
  26.1 1.1 %out.2 = (f32[160,1152]{1,0:T(8,128)}, f32[160,1152]{1,0:T(8,128)}) custom-call(bf16[160,1152]{1,0:T(8,128)(2,1)S(1)} %get-tuple-element.21.image_raw.refs_0_, f32[160,1]{1,0:T(8,128)S(1)} %get-tuple-element.22.after.image_inv.refs_1_, f32[160,1152]{1,0:T(8,128)S(1)} %get-tuple-element.34.refs_2_, bf16[160,1152]{1,0:T(8,128)(2,1)S(1)} %get-tuple-element.32.text_raw.refs_3_, ...), custom_call_target="tpu_custom_call" | custom-call | tf_op jit(solution)/shard_map/out/pallas_call | solution.py:311
  27.3 0.5 %collective-permute-done.5.refs_6_ = bf16[160,1152]{1,0:T(8,128)(2,1)S(1)} collective-permute-done((bf16[160,1152]{1,0:T(8,128)(2,1)S(1)}, bf16[160,1152]{1,0:T(8,128)(2,1)S(1)}, u32[]{:S(2)}, u32[]{:S(2)}) %collective-permute-start.5) | collective-permute-done | bytes 368672 | tf_op jit(solution)/shard_map/ppermute | solution.py:336
  27.7 1.1 %out.3 = (f32[160,1152]{1,0:T(8,128)}, f32[160,1152]{1,0:T(8,128)}) custom-call(bf16[160,1152]{1,0:T(8,128)(2,1)S(1)} %get-tuple-element.21.image_raw.refs_0_, f32[160,1]{1,0:T(8,128)S(1)} %get-tuple-element.22.after.image_inv.refs_1_, f32[160,1152]{1,0:T(8,128)S(1)} %get-tuple-element.34.refs_2_, ...), custom_call_target="tpu_custom_call", output_to_operand_aliasing={{0}: (7, {}), {1}: (8, {})} | custom-call | tf_op jit(solution)/shard_map/out/pallas_call | solution.py:311
Async XLA Ops:
  0.6 14.8 %collective-permute-start.3 = (bf16[160,1152]{1,0:T(8,128)(2,1)}, bf16[160,1152]{1,0:T(8,128)(2,1)S(1)}, u32[]{:S(2)}, u32[]{:S(2)}) collective-permute-start(bf16[160,1152]{1,0:T(8,128)(2,1)} %image.1), channel_id=1, source_target_pairs={{0,4},{1,5},{2,6},{3,7},{4,8},{5,9},{6,10},{7,11},{8,12},{9,13},{1... | collective-permute-start | bytes 1105928 | tf_op jit(solution)/shard_map/ppermute | solution.py:336
  3.6 12.0 %collective-permute-start.2 = (bf16[160,1152]{1,0:T(8,128)(2,1)}, bf16[160,1152]{1,0:T(8,128)(2,1)S(1)}, u32[]{:S(2)}, u32[]{:S(2)}) collective-permute-start(bf16[160,1152]{1,0:T(8,128)(2,1)} %text.1), channel_id=1, source_target_pairs={{0,1},{1,0},{2,3},{3,2},{4,5},{5,4},{6,7},{7,6},{8,9},{9,8},{10,11... | collective-permute-start | bytes 1105928 | tf_op jit(solution)/shard_map/ppermute | solution.py:336
  6.5 9.2 %collective-permute-start.1 = (bf16[160,1152]{1,0:T(8,128)(2,1)S(1)}, bf16[160,1152]{1,0:T(8,128)(2,1)S(1)}, u32[]{:S(2)}, u32[]{:S(2)}) collective-permute-start(bf16[160,1152]{1,0:T(8,128)(2,1)S(1)} %get-tuple-element.27.text), channel_id=1, source_target_pairs={{0,2},{1,3},{2,0},{3,1},{4,6},{5,7},{6,4},{7,5},{8,10},{9,11},{10,... | collective-permute-start | bytes 1105928 | tf_op jit(solution)/shard_map/ppermute | solution.py:336
  6.6 9.1 %collective-permute-start = (bf16[160,1152]{1,0:T(8,128)(2,1)S(1)}, bf16[160,1152]{1,0:T(8,128)(2,1)S(1)}, u32[]{:S(2)}, u32[]{:S(2)}) collective-permute-start(bf16[160,1152]{1,0:T(8,128)(2,1)S(1)} %get-tuple-element.26.image), channel_id=1, source_target_pairs={{0,2},{1,3},{2,0},{3,1},{4,6},{5,7},{6,4},{7,5},{8,10},{9,11},{10,... | collective-permute-start | bytes 1105928 | tf_op jit(solution)/shard_map/ppermute | solution.py:336
  16.6 2.7 %collective-permute-start.4 = (bf16[2,160,1152]{2,1,0:T(8,128)(2,1)S(1)}, bf16[2,160,1152]{2,1,0:T(8,128)(2,1)S(1)}, u32[]{:S(2)}, u32[]{:S(2)}) collective-permute-start(bf16[2,160,1152]{2,1,0:T(8,128)(2,1)S(1)} %got.1), channel_id=1, source_target_pairs={{0,2},{1,3},{2,0},{3,1},{4,6},{5,7},{6,4},{7,5},{8,10},{9,11},{10,... | collective-permute-start | bytes 2211848 | tf_op jit(solution)/shard_map/ppermute | solution.py:336
  16.7 9.4 %collective-permute-start.6 = (bf16[160,1152]{1,0:T(8,128)(2,1)S(1)}, bf16[160,1152]{1,0:T(8,128)(2,1)S(1)}, u32[]{:S(2)}, u32[]{:S(2)}) collective-permute-start(bf16[160,1152]{1,0:T(8,128)(2,1)S(1)} %bitcast.8), channel_id=1, source_target_pairs={{0,28},{1,29},{2,3},{3,2},{4,0},{5,1},{6,7},{7,6},{8,4},{9,5},{10,... | collective-permute-start | bytes 1105928 | tf_op jit(solution)/shard_map/ppermute | solution.py:336
  20.0 7.7 %collective-permute-start.5 = (bf16[160,1152]{1,0:T(8,128)(2,1)S(1)}, bf16[160,1152]{1,0:T(8,128)(2,1)S(1)}, u32[]{:S(2)}, u32[]{:S(2)}) collective-permute-start(bf16[160,1152]{1,0:T(8,128)(2,1)S(1)} %bitcast.7), channel_id=1, source_target_pairs={{0,1},{1,0},{2,30},{3,31},{4,5},{5,4},{6,2},{7,3},{8,9},{9,8},{10,... | collective-permute-start | bytes 1105928 | tf_op jit(solution)/shard_map/ppermute | solution.py:336

commit v23 on v21

--- a/solution.py
+++ b/solution.py
@@ -141,21 +141,15 @@
     half[...] = half_rows(raw)
 
 
-def got_kernel(far, visit, *refs):
-    got = refs[-1]
-    got[0] = visit[...]
-    for k in range(far):
-        got[k + 1] = half_rows(refs[k])
-
-
 def parted(far, got):
     return got.at[0], [got.at[k + 1] for k in range(far)]
 
 
-def first_kernel(
-    far, params, row_targets, image, text, mate_image, mate_text, got, back, part
-):
-    visit, far_text = parted(far, got)
+def first_kernel(far, params, row_targets, image, text, mate_image, mate_text, visit, *refs):
+    far_raw, (got, back, part) = refs[:far], refs[far:]
+    _, far_text = parted(far, got)
+    for k in range(far):
+        far_text[k][...] = half_rows(far_raw[k])
 
     def on_first(node):
         back[0] = drawn_apart(params, visit, [text, *far_text]).astype(HALF)
@@ -168,6 +162,7 @@
         part[...] = drawn(params, visit, [text, *far_text, mate_text])
 
     by_role(on_first, on_second)
+    got[0] = visit[...]
 
 
 def second_kernel(far, params, row_targets, image, got, mate_got, part, back):
@@ -340,17 +335,11 @@
     )
     (visit,) = call(visit_kernel, "visit", [visit_raw, params], [block_h])
     *far_raw, visit = lax.optimization_barrier((*far_raw, visit))
-    (got,) = call(
-        functools.partial(got_kernel, far),
-        "got",
-        [visit, *far_raw, mate_image, mate_text],
-        [((node_count, rows, width), HALF)],
-    )
-    back, part = call(
+    got, back, part = call(
         functools.partial(first_kernel, far),
         "first",
-        [params, row_targets, image, text, mate_image, mate_text, got],
-        [returns, block_f],
+        [params, row_targets, image, text, mate_image, mate_text, visit, *far_raw],
+        [((node_count, rows, width), HALF), returns, block_f],
     )
     got, part = lax.optimization_barrier((got, part))
     mate_got = swap(got)

time: 29.1 us -> 29.1 us (level)
    pallas_call x7 -> x6, Pallas kernels: 6.45 us -> 6.45 us  [call(): pl.pallas_call(kernel, name=name, out_shape=[pltpu.VMEM(s, d) for s, d in...]
where the time goes in v23:
time: 29.1 us; the launch traced here: 28.8 us
  waiting for transfers between devices  9.6 us (33%)
  Pallas kernels  8.69 us (30%)
  starting transfers between devices  8.54 us (29%)
  between operations  2.02 us (7%)
    ppermute x7, waiting for transfers between devices, send(): return lax.ppermute(block, ('blk', 'node'), route)  9.6 us
    ppermute x7, starting transfers between devices, send(): return lax.ppermute(block, ('blk', 'node'), route)  8.54 us
    pallas_call x6, Pallas kernels, call(): pl.pallas_call(kernel, name=name, out_shape=[pltpu.VMEM(s, d) for s, d in...  6.45 us
    pallas_call x2, Pallas kernels, write_out(): pl.pallas_call(functools.partial(out_kernel, far, image_on_first), name='...  2.24 us
  transfers between devices with their start and end apart: 7, of which 4 were waited for; matrix products, arithmetic and copies ran while one was open for 0% of the time, Pallas kernels for 23%

profile of v23, /device:TPU:0, one launch (start us, length us, event | category | flops | bytes accessed | tf_op | source)
XLA Modules:
  0.0 28.8 jit_solution(8632372882552359047)
XLA Ops:
  0.6 3.0 %collective-permute-start.3 = (bf16[160,1152]{1,0:T(8,128)(2,1)}, bf16[160,1152]{1,0:T(8,128)(2,1)S(1)}, u32[]{:S(2)}, u32[]{:S(2)}) collective-permute-start(bf16[160,1152]{1,0:T(8,128)(2,1)} %image.1), channel_id=1, source_target_pairs={{0,4},{1,5},{2,6},{3,7},{4,8},{5,9},{6,10},{7,11},{8,12},{9,13},{1... | collective-permute-start | bytes 1105928 | tf_op jit(solution)/shard_map/ppermute | solution.py:302
  3.6 1.5 %collective-permute-start.2 = (bf16[160,1152]{1,0:T(8,128)(2,1)}, bf16[160,1152]{1,0:T(8,128)(2,1)S(1)}, u32[]{:S(2)}, u32[]{:S(2)}) collective-permute-start(bf16[160,1152]{1,0:T(8,128)(2,1)} %text.1), channel_id=1, source_target_pairs={{0,1},{1,0},{2,3},{3,2},{4,5},{5,4},{6,7},{7,6},{8,9},{9,8},{10,11... | collective-permute-start | bytes 1105928 | tf_op jit(solution)/shard_map/ppermute | solution.py:302
  5.1 1.3 %unit.1 = (bf16[160,1152]{1,0:T(8,128)(2,1)S(1)}, bf16[160,1152]{1,0:T(8,128)(2,1)S(1)}, bf16[160,1152]{1,0:T(8,128)(2,1)S(1)}, bf16[160,1152]{1,0:T(8,128)(2,1)...) custom-call(bf16[160,1152]{1,0:T(8,128)(2,1)} %image.1, bf16[160,1152]{1,0:T(8,128)(2,1)} %text.1), custom_call_target="tpu_custom_call" | custom-call | tf_op jit(solution)/shard_map/unit/pallas_call | solution.py:262
  6.5 0.1 collective-permute-start.1
  6.6 0.5 %collective-permute-start = (bf16[160,1152]{1,0:T(8,128)(2,1)S(1)}, bf16[160,1152]{1,0:T(8,128)(2,1)S(1)}, u32[]{:S(2)}, u32[]{:S(2)}) collective-permute-start(bf16[160,1152]{1,0:T(8,128)(2,1)S(1)} %get-tuple-element.27.image), channel_id=1, source_target_pairs={{0,2},{1,3},{2,0},{3,1},{4,6},{5,7},{6,4},{7,5},{8,10},{9,11},{10,... | collective-permute-start | bytes 1105928 | tf_op jit(solution)/shard_map/ppermute | solution.py:302
  8.3 1.1 %prep.1 = (f32[8,128]{1,0:T(8,128)S(1)}, s32[1,480]{1,0:T(1,128)S(1)}, s32[160,1]{1,0:T(8,128)S(1)}) custom-call(s32[40,128]{1,0:T(8,128)} %bitcast.9, f32[1,1]{1,0:T(1,128)} %bitcast.5.scale, f32[1,1]{1,0:T(1,128)} %bitcast.6.bias, f32[160,1]{1,0:T(8,128)S(1)} %get-tuple-element.23.after.image_inv.refs_1_), custom_call_target="tpu_custom_call" | custom-call | tf_op jit(solution)/shard_map/prep/pallas_call | solution.py:262
  9.5 6.0 %collective-permute-done.3.raw = bf16[160,1152]{1,0:T(8,128)(2,1)S(1)} collective-permute-done((bf16[160,1152]{1,0:T(8,128)(2,1)}, bf16[160,1152]{1,0:T(8,128)(2,1)S(1)}, u32[]{:S(2)}, u32[]{:S(2)}) %collective-permute-start.3) | collective-permute-done | bytes 368672 | tf_op jit(solution)/shard_map/ppermute | solution.py:302
  15.5 0.2 visit.1
  15.6 0.0 collective-permute-done.2.refs_0_
  15.6 0.0 collective-permute-done.1.mate_text
  15.6 0.0 collective-permute-done.mate_image
  15.7 1.0 %first.1 = (bf16[2,160,1152]{2,1,0:T(8,128)(2,1)S(1)}, bf16[1,160,1152]{2,1,0:T(8,128)(2,1)S(1)}, f32[160,1152]{1,0:T(8,128)S(1)}) custom-call(f32[8,128]{1,0:T(8,128)S(1)} %get-tuple-element.24.after.params, s32[1,480]{1,0:T(1,128)S(1)} %get-tuple-element.25.row_targets, bf16[160,1152]{1,0:T(8,128)(2,1)S(1)} %get-tuple-element.27.image, ...), custom_call_target="tpu_custom_call" | custom-call | tf_op jit(solution)/shard_map/first/pallas_call | solution.py:262
  16.7 0.1 collective-permute-start.4
  16.8 1.7 %collective-permute-start.6 = (bf16[160,1152]{1,0:T(8,128)(2,1)S(1)}, bf16[160,1152]{1,0:T(8,128)(2,1)S(1)}, u32[]{:S(2)}, u32[]{:S(2)}) collective-permute-start(bf16[160,1152]{1,0:T(8,128)(2,1)S(1)} %bitcast.8), channel_id=1, source_target_pairs={{0,28},{1,29},{2,3},{3,2},{4,0},{5,1},{6,7},{7,6},{8,4},{9,5},{10,... | collective-permute-start | bytes 1105928 | tf_op jit(solution)/shard_map/ppermute | solution.py:302
  18.5 0.4 %collective-permute-done.4.mate_got = bf16[2,160,1152]{2,1,0:T(8,128)(2,1)S(1)} collective-permute-done((bf16[2,160,1152]{2,1,0:T(8,128)(2,1)S(1)}, bf16[2,160,1152]{2,1,0:T(8,128)(2,1)S(1)}, u32[]{:S(2)}, u32[]{:S(2)}) %collective-permute-start.4) | collective-permute-done | bytes 737312 | tf_op jit(solution)/shard_map/ppermute | solution.py:302
  18.9 0.9 %second.1 = bf16[1,160,1152]{2,1,0:T(8,128)(2,1)S(1)} custom-call(f32[8,128]{1,0:T(8,128)S(1)} %get-tuple-element.24.after.params, s32[1,480]{1,0:T(1,128)S(1)} %get-tuple-element.25.row_targets, bf16[160,1152]{1,0:T(8,128)(2,1)S(1)} %get-tuple-element.27.image, bf16[2,160,1152]{2,1,0:T(8,128)(2,1)S(1)} %get-tuple-element.33.got, ...), custom_call_target="tpu_custom_call" | custom-call | tf_op jit(solution)/shard_map/second/pallas_call | solution.py:262
  19.8 1.6 %collective-permute-start.5 = (bf16[160,1152]{1,0:T(8,128)(2,1)S(1)}, bf16[160,1152]{1,0:T(8,128)(2,1)S(1)}, u32[]{:S(2)}, u32[]{:S(2)}) collective-permute-start(bf16[160,1152]{1,0:T(8,128)(2,1)S(1)} %bitcast.7), channel_id=1, source_target_pairs={{0,1},{1,0},{2,30},{3,31},{4,5},{5,4},{6,2},{7,3},{8,9},{9,8},{10,... | collective-permute-start | bytes 1105928 | tf_op jit(solution)/shard_map/ppermute | solution.py:302
  21.4 2.0 %third.1 = (f32[160,1152]{1,0:T(8,128)S(1)}, f32[160,1152]{1,0:T(8,128)S(1)}) custom-call(f32[8,128]{1,0:T(8,128)S(1)} %get-tuple-element.24.after.params, s32[1,480]{1,0:T(1,128)S(1)} %get-tuple-element.25.row_targets, s32[160,1]{1,0:T(8,128)S(1)} %get-tuple-element.26.targets, bf16[160,1152]{1,0:T(8,128)(2,1)S(1)} %get-tuple-element.27.image, ...), custom_call_target="tpu_custom_call" | custom-call | tf_op jit(solution)/shard_map/third/pallas_call | solution.py:262
  23.4 2.7 %collective-permute-done.6.refs_6_ = bf16[160,1152]{1,0:T(8,128)(2,1)S(1)} collective-permute-done((bf16[160,1152]{1,0:T(8,128)(2,1)S(1)}, bf16[160,1152]{1,0:T(8,128)(2,1)S(1)}, u32[]{:S(2)}, u32[]{:S(2)}) %collective-permute-start.6) | collective-permute-done | bytes 368672 | tf_op jit(solution)/shard_map/ppermute | solution.py:302
  26.1 1.1 %out.2 = (f32[160,1152]{1,0:T(8,128)}, f32[160,1152]{1,0:T(8,128)}) custom-call(bf16[160,1152]{1,0:T(8,128)(2,1)S(1)} %get-tuple-element.22.image_raw.refs_0_, f32[160,1]{1,0:T(8,128)S(1)} %get-tuple-element.23.after.image_inv.refs_1_, f32[160,1152]{1,0:T(8,128)S(1)} %get-tuple-element.36.refs_2_, bf16[160,1152]{1,0:T(8,128)(2,1)S(1)} %get-tuple-element.34.text_raw.refs_3_, ...), custom_call_target="tpu_custom_call" | custom-call | tf_op jit(solution)/shard_map/out/pallas_call | solution.py:277
  27.3 0.5 %collective-permute-done.5.refs_6_ = bf16[160,1152]{1,0:T(8,128)(2,1)S(1)} collective-permute-done((bf16[160,1152]{1,0:T(8,128)(2,1)S(1)}, bf16[160,1152]{1,0:T(8,128)(2,1)S(1)}, u32[]{:S(2)}, u32[]{:S(2)}) %collective-permute-start.5) | collective-permute-done | bytes 368672 | tf_op jit(solution)/shard_map/ppermute | solution.py:302
  27.7 1.1 %out.3 = (f32[160,1152]{1,0:T(8,128)}, f32[160,1152]{1,0:T(8,128)}) custom-call(bf16[160,1152]{1,0:T(8,128)(2,1)S(1)} %get-tuple-element.22.image_raw.refs_0_, f32[160,1]{1,0:T(8,128)S(1)} %get-tuple-element.23.after.image_inv.refs_1_, f32[160,1152]{1,0:T(8,128)S(1)} %get-tuple-element.36.refs_2_, ...), custom_call_target="tpu_custom_call", output_to_operand_aliasing={{0}: (7, {}), {1}: (8, {})} | custom-call | tf_op jit(solution)/shard_map/out/pallas_call | solution.py:277
Async XLA Ops:
  0.6 14.8 %collective-permute-start.3 = (bf16[160,1152]{1,0:T(8,128)(2,1)}, bf16[160,1152]{1,0:T(8,128)(2,1)S(1)}, u32[]{:S(2)}, u32[]{:S(2)}) collective-permute-start(bf16[160,1152]{1,0:T(8,128)(2,1)} %image.1), channel_id=1, source_target_pairs={{0,4},{1,5},{2,6},{3,7},{4,8},{5,9},{6,10},{7,11},{8,12},{9,13},{1... | collective-permute-start | bytes 1105928 | tf_op jit(solution)/shard_map/ppermute | solution.py:302
  3.6 12.0 %collective-permute-start.2 = (bf16[160,1152]{1,0:T(8,128)(2,1)}, bf16[160,1152]{1,0:T(8,128)(2,1)S(1)}, u32[]{:S(2)}, u32[]{:S(2)}) collective-permute-start(bf16[160,1152]{1,0:T(8,128)(2,1)} %text.1), channel_id=1, source_target_pairs={{0,1},{1,0},{2,3},{3,2},{4,5},{5,4},{6,7},{7,6},{8,9},{9,8},{10,11... | collective-permute-start | bytes 1105928 | tf_op jit(solution)/shard_map/ppermute | solution.py:302
  6.5 9.2 %collective-permute-start.1 = (bf16[160,1152]{1,0:T(8,128)(2,1)S(1)}, bf16[160,1152]{1,0:T(8,128)(2,1)S(1)}, u32[]{:S(2)}, u32[]{:S(2)}) collective-permute-start(bf16[160,1152]{1,0:T(8,128)(2,1)S(1)} %get-tuple-element.28.text), channel_id=1, source_target_pairs={{0,2},{1,3},{2,0},{3,1},{4,6},{5,7},{6,4},{7,5},{8,10},{9,11},{10,... | collective-permute-start | bytes 1105928 | tf_op jit(solution)/shard_map/ppermute | solution.py:302
  6.6 9.1 %collective-permute-start = (bf16[160,1152]{1,0:T(8,128)(2,1)S(1)}, bf16[160,1152]{1,0:T(8,128)(2,1)S(1)}, u32[]{:S(2)}, u32[]{:S(2)}) collective-permute-start(bf16[160,1152]{1,0:T(8,128)(2,1)S(1)} %get-tuple-element.27.image), channel_id=1, source_target_pairs={{0,2},{1,3},{2,0},{3,1},{4,6},{5,7},{6,4},{7,5},{8,10},{9,11},{10,... | collective-permute-start | bytes 1105928 | tf_op jit(solution)/shard_map/ppermute | solution.py:302
  16.7 2.3 %collective-permute-start.4 = (bf16[2,160,1152]{2,1,0:T(8,128)(2,1)S(1)}, bf16[2,160,1152]{2,1,0:T(8,128)(2,1)S(1)}, u32[]{:S(2)}, u32[]{:S(2)}) collective-permute-start(bf16[2,160,1152]{2,1,0:T(8,128)(2,1)S(1)} %get-tuple-element.33.got), channel_id=1, source_target_pairs={{0,2},{1,3},{2,0},{3,1},{4,6},{5,7},{6,4},{7,5},{8,10},{9,11},{10,... | collective-permute-start | bytes 2211848 | tf_op jit(solution)/shard_map/ppermute | solution.py:302
  16.8 9.4 %collective-permute-start.6 = (bf16[160,1152]{1,0:T(8,128)(2,1)S(1)}, bf16[160,1152]{1,0:T(8,128)(2,1)S(1)}, u32[]{:S(2)}, u32[]{:S(2)}) collective-permute-start(bf16[160,1152]{1,0:T(8,128)(2,1)S(1)} %bitcast.8), channel_id=1, source_target_pairs={{0,28},{1,29},{2,3},{3,2},{4,0},{5,1},{6,7},{7,6},{8,4},{9,5},{10,... | collective-permute-start | bytes 1105928 | tf_op jit(solution)/shard_map/ppermute | solution.py:302
  19.8 7.9 %collective-permute-start.5 = (bf16[160,1152]{1,0:T(8,128)(2,1)S(1)}, bf16[160,1152]{1,0:T(8,128)(2,1)S(1)}, u32[]{:S(2)}, u32[]{:S(2)}) collective-permute-start(bf16[160,1152]{1,0:T(8,128)(2,1)S(1)} %bitcast.7), channel_id=1, source_target_pairs={{0,1},{1,0},{2,30},{3,31},{4,5},{5,4},{6,2},{7,3},{8,9},{9,8},{10,... | collective-permute-start | bytes 1105928 | tf_op jit(solution)/shard_map/ppermute | solution.py:302

commit v24 on v21

--- a/solution.py
+++ b/solution.py
@@ -239,7 +239,7 @@
     image, text, received = refs[0:3], refs[3:6], refs[6 : 6 + far]
     image_grads, text_grads, held, sems = refs[-4:]
     rows = held.shape[0]
-    part = rows // 5 if rows % 80 == 0 else rows
+    part = rows // 10 if rows % 160 == 0 else rows
 
     def run(own, count, out, node):
         copies = []
@@ -285,7 +285,7 @@
         out_shape=[jax.ShapeDtypeStruct(*block)] * 2,
         in_specs=[pl.BlockSpec(memory_space=pltpu.VMEM)] * count + [anywhere] * len(grads),
         out_specs=[anywhere] * 2,
-        scratch_shapes=[pltpu.VMEM(*block), pltpu.SemaphoreType.DMA((5,))],
+        scratch_shapes=[pltpu.VMEM(*block), pltpu.SemaphoreType.DMA((10,))],
         input_output_aliases={count + i: i for i in range(len(grads))},
         compiler_params=pltpu.CompilerParams(vmem_limit_bytes=VMEM_LIMIT),
     )(*operands, *grads)

time: 29.1 us -> 29.1 us (level)
  no operation moved by 1% of the time
where the time goes in v24:
time: 29.1 us; the launch traced here: 28.9 us
  waiting for transfers between devices  9.59 us (33%)
  Pallas kernels  8.75 us (30%)
  starting transfers between devices  8.52 us (29%)
  between operations  2.02 us (7%)
    ppermute x7, waiting for transfers between devices, send(): return lax.ppermute(block, ('blk', 'node'), route)  9.59 us
    ppermute x7, starting transfers between devices, send(): return lax.ppermute(block, ('blk', 'node'), route)  8.52 us
    pallas_call x7, Pallas kernels, call(): pl.pallas_call(kernel, name=name, out_shape=[pltpu.VMEM(s, d) for s, d in...  6.45 us
    pallas_call x2, Pallas kernels, write_out(): pl.pallas_call(functools.partial(out_kernel, far, image_on_first), name='...  2.31 us
  transfers between devices with their start and end apart: 7, of which 4 were waited for; matrix products, arithmetic and copies ran while one was open for 0% of the time, Pallas kernels for 23%

profile of v24, /device:TPU:0, one launch (start us, length us, event | category | flops | bytes accessed | tf_op | source)
XLA Modules:
  0.0 28.9 jit_solution(8406839691419101222)
XLA Ops:
  0.6 3.0 %collective-permute-start.3 = (bf16[160,1152]{1,0:T(8,128)(2,1)}, bf16[160,1152]{1,0:T(8,128)(2,1)S(1)}, u32[]{:S(2)}, u32[]{:S(2)}) collective-permute-start(bf16[160,1152]{1,0:T(8,128)(2,1)} %image.1), channel_id=1, source_target_pairs={{0,4},{1,5},{2,6},{3,7},{4,8},{5,9},{6,10},{7,11},{8,12},{9,13},{1... | collective-permute-start | bytes 1105928 | tf_op jit(solution)/shard_map/ppermute | solution.py:307
  3.6 1.5 %collective-permute-start.2 = (bf16[160,1152]{1,0:T(8,128)(2,1)}, bf16[160,1152]{1,0:T(8,128)(2,1)S(1)}, u32[]{:S(2)}, u32[]{:S(2)}) collective-permute-start(bf16[160,1152]{1,0:T(8,128)(2,1)} %text.1), channel_id=1, source_target_pairs={{0,1},{1,0},{2,3},{3,2},{4,5},{5,4},{6,7},{7,6},{8,9},{9,8},{10,11... | collective-permute-start | bytes 1105928 | tf_op jit(solution)/shard_map/ppermute | solution.py:307
  5.1 1.3 %unit.1 = (bf16[160,1152]{1,0:T(8,128)(2,1)S(1)}, bf16[160,1152]{1,0:T(8,128)(2,1)S(1)}, bf16[160,1152]{1,0:T(8,128)(2,1)S(1)}, bf16[160,1152]{1,0:T(8,128)(2,1)...) custom-call(bf16[160,1152]{1,0:T(8,128)(2,1)} %image.1, bf16[160,1152]{1,0:T(8,128)(2,1)} %text.1), custom_call_target="tpu_custom_call" | custom-call | tf_op jit(solution)/shard_map/unit/pallas_call | solution.py:267
  6.5 0.1 collective-permute-start.1
  6.6 0.5 %collective-permute-start = (bf16[160,1152]{1,0:T(8,128)(2,1)S(1)}, bf16[160,1152]{1,0:T(8,128)(2,1)S(1)}, u32[]{:S(2)}, u32[]{:S(2)}) collective-permute-start(bf16[160,1152]{1,0:T(8,128)(2,1)S(1)} %get-tuple-element.26.image), channel_id=1, source_target_pairs={{0,2},{1,3},{2,0},{3,1},{4,6},{5,7},{6,4},{7,5},{8,10},{9,11},{10,... | collective-permute-start | bytes 1105928 | tf_op jit(solution)/shard_map/ppermute | solution.py:307
  8.3 1.1 %prep.1 = (f32[8,128]{1,0:T(8,128)S(1)}, s32[1,480]{1,0:T(1,128)S(1)}, s32[160,1]{1,0:T(8,128)S(1)}) custom-call(s32[40,128]{1,0:T(8,128)} %bitcast.9, f32[1,1]{1,0:T(1,128)} %bitcast.5.scale, f32[1,1]{1,0:T(1,128)} %bitcast.6.bias, f32[160,1]{1,0:T(8,128)S(1)} %get-tuple-element.22.after.image_inv.refs_1_), custom_call_target="tpu_custom_call" | custom-call | tf_op jit(solution)/shard_map/prep/pallas_call | solution.py:267
  9.5 6.0 %collective-permute-done.3.raw = bf16[160,1152]{1,0:T(8,128)(2,1)S(1)} collective-permute-done((bf16[160,1152]{1,0:T(8,128)(2,1)}, bf16[160,1152]{1,0:T(8,128)(2,1)S(1)}, u32[]{:S(2)}, u32[]{:S(2)}) %collective-permute-start.3) | collective-permute-done | bytes 368672 | tf_op jit(solution)/shard_map/ppermute | solution.py:307
  15.5 0.2 visit.1
  15.6 0.0 collective-permute-done.2.refs_0_
  15.6 0.0 collective-permute-done.1.refs_2_.mate_text
  15.6 0.0 collective-permute-done.refs_1_.mate_image
  15.7 0.2 got.1
  15.8 0.8 %first.1 = (bf16[1,160,1152]{2,1,0:T(8,128)(2,1)S(1)}, f32[160,1152]{1,0:T(8,128)S(1)}) custom-call(f32[8,128]{1,0:T(8,128)S(1)} %get-tuple-element.23.after.params, s32[1,480]{1,0:T(1,128)S(1)} %get-tuple-element.24.row_targets, bf16[160,1152]{1,0:T(8,128)(2,1)S(1)} %get-tuple-element.26.image, bf16[160,1152]{1,0:T(8,128)(2,1)S(1)} %get-tuple-element.27.text, ...), custom_call_target="tpu_custom_call" | custom-call | tf_op jit(solution)/shard_map/first/pallas_call | solution.py:267
  16.7 0.1 collective-permute-start.4
  16.7 1.8 %collective-permute-start.6 = (bf16[160,1152]{1,0:T(8,128)(2,1)S(1)}, bf16[160,1152]{1,0:T(8,128)(2,1)S(1)}, u32[]{:S(2)}, u32[]{:S(2)}) collective-permute-start(bf16[160,1152]{1,0:T(8,128)(2,1)S(1)} %bitcast.8), channel_id=1, source_target_pairs={{0,28},{1,29},{2,3},{3,2},{4,0},{5,1},{6,7},{7,6},{8,4},{9,5},{10,... | collective-permute-start | bytes 1105928 | tf_op jit(solution)/shard_map/ppermute | solution.py:307
  18.5 0.4 %collective-permute-done.4.mate_got = bf16[2,160,1152]{2,1,0:T(8,128)(2,1)S(1)} collective-permute-done((bf16[2,160,1152]{2,1,0:T(8,128)(2,1)S(1)}, bf16[2,160,1152]{2,1,0:T(8,128)(2,1)S(1)}, u32[]{:S(2)}, u32[]{:S(2)}) %collective-permute-start.4) | collective-permute-done | bytes 737312 | tf_op jit(solution)/shard_map/ppermute | solution.py:307
  18.9 0.9 %second.1 = bf16[1,160,1152]{2,1,0:T(8,128)(2,1)S(1)} custom-call(f32[8,128]{1,0:T(8,128)S(1)} %get-tuple-element.23.after.params, s32[1,480]{1,0:T(1,128)S(1)} %get-tuple-element.24.row_targets, bf16[160,1152]{1,0:T(8,128)(2,1)S(1)} %get-tuple-element.26.image, bf16[2,160,1152]{2,1,0:T(8,128)(2,1)S(1)} %got.1, ...), custom_call_target="tpu_custom_call" | custom-call | tf_op jit(solution)/shard_map/second/pallas_call | solution.py:267
  19.8 1.6 %collective-permute-start.5 = (bf16[160,1152]{1,0:T(8,128)(2,1)S(1)}, bf16[160,1152]{1,0:T(8,128)(2,1)S(1)}, u32[]{:S(2)}, u32[]{:S(2)}) collective-permute-start(bf16[160,1152]{1,0:T(8,128)(2,1)S(1)} %bitcast.7), channel_id=1, source_target_pairs={{0,1},{1,0},{2,30},{3,31},{4,5},{5,4},{6,2},{7,3},{8,9},{9,8},{10,... | collective-permute-start | bytes 1105928 | tf_op jit(solution)/shard_map/ppermute | solution.py:307
  21.4 2.0 %third.1 = (f32[160,1152]{1,0:T(8,128)S(1)}, f32[160,1152]{1,0:T(8,128)S(1)}) custom-call(f32[8,128]{1,0:T(8,128)S(1)} %get-tuple-element.23.after.params, s32[1,480]{1,0:T(1,128)S(1)} %get-tuple-element.24.row_targets, s32[160,1]{1,0:T(8,128)S(1)} %get-tuple-element.25.targets, bf16[160,1152]{1,0:T(8,128)(2,1)S(1)} %get-tuple-element.26.image, ...), custom_call_target="tpu_custom_call" | custom-call | tf_op jit(solution)/shard_map/third/pallas_call | solution.py:267
  23.4 2.8 %collective-permute-done.6.refs_6_ = bf16[160,1152]{1,0:T(8,128)(2,1)S(1)} collective-permute-done((bf16[160,1152]{1,0:T(8,128)(2,1)S(1)}, bf16[160,1152]{1,0:T(8,128)(2,1)S(1)}, u32[]{:S(2)}, u32[]{:S(2)}) %collective-permute-start.6) | collective-permute-done | bytes 368672 | tf_op jit(solution)/shard_map/ppermute | solution.py:307
  26.1 1.2 %out.2 = (f32[160,1152]{1,0:T(8,128)}, f32[160,1152]{1,0:T(8,128)}) custom-call(bf16[160,1152]{1,0:T(8,128)(2,1)S(1)} %get-tuple-element.21.image_raw.refs_0_, f32[160,1]{1,0:T(8,128)S(1)} %get-tuple-element.22.after.image_inv.refs_1_, f32[160,1152]{1,0:T(8,128)S(1)} %get-tuple-element.34.refs_2_, bf16[160,1152]{1,0:T(8,128)(2,1)S(1)} %get-tuple-element.32.text_raw.refs_3_, ...), custom_call_target="tpu_custom_call" | custom-call | tf_op jit(solution)/shard_map/out/pallas_call | solution.py:282
  27.3 0.4 %collective-permute-done.5.refs_6_ = bf16[160,1152]{1,0:T(8,128)(2,1)S(1)} collective-permute-done((bf16[160,1152]{1,0:T(8,128)(2,1)S(1)}, bf16[160,1152]{1,0:T(8,128)(2,1)S(1)}, u32[]{:S(2)}, u32[]{:S(2)}) %collective-permute-start.5) | collective-permute-done | bytes 368672 | tf_op jit(solution)/shard_map/ppermute | solution.py:307
  27.7 1.2 %out.3 = (f32[160,1152]{1,0:T(8,128)}, f32[160,1152]{1,0:T(8,128)}) custom-call(bf16[160,1152]{1,0:T(8,128)(2,1)S(1)} %get-tuple-element.21.image_raw.refs_0_, f32[160,1]{1,0:T(8,128)S(1)} %get-tuple-element.22.after.image_inv.refs_1_, f32[160,1152]{1,0:T(8,128)S(1)} %get-tuple-element.34.refs_2_, ...), custom_call_target="tpu_custom_call", output_to_operand_aliasing={{0}: (7, {}), {1}: (8, {})} | custom-call | tf_op jit(solution)/shard_map/out/pallas_call | solution.py:282
Async XLA Ops:
  0.6 14.8 %collective-permute-start.3 = (bf16[160,1152]{1,0:T(8,128)(2,1)}, bf16[160,1152]{1,0:T(8,128)(2,1)S(1)}, u32[]{:S(2)}, u32[]{:S(2)}) collective-permute-start(bf16[160,1152]{1,0:T(8,128)(2,1)} %image.1), channel_id=1, source_target_pairs={{0,4},{1,5},{2,6},{3,7},{4,8},{5,9},{6,10},{7,11},{8,12},{9,13},{1... | collective-permute-start | bytes 1105928 | tf_op jit(solution)/shard_map/ppermute | solution.py:307
  3.6 12.0 %collective-permute-start.2 = (bf16[160,1152]{1,0:T(8,128)(2,1)}, bf16[160,1152]{1,0:T(8,128)(2,1)S(1)}, u32[]{:S(2)}, u32[]{:S(2)}) collective-permute-start(bf16[160,1152]{1,0:T(8,128)(2,1)} %text.1), channel_id=1, source_target_pairs={{0,1},{1,0},{2,3},{3,2},{4,5},{5,4},{6,7},{7,6},{8,9},{9,8},{10,11... | collective-permute-start | bytes 1105928 | tf_op jit(solution)/shard_map/ppermute | solution.py:307
  6.5 9.2 %collective-permute-start.1 = (bf16[160,1152]{1,0:T(8,128)(2,1)S(1)}, bf16[160,1152]{1,0:T(8,128)(2,1)S(1)}, u32[]{:S(2)}, u32[]{:S(2)}) collective-permute-start(bf16[160,1152]{1,0:T(8,128)(2,1)S(1)} %get-tuple-element.27.text), channel_id=1, source_target_pairs={{0,2},{1,3},{2,0},{3,1},{4,6},{5,7},{6,4},{7,5},{8,10},{9,11},{10,... | collective-permute-start | bytes 1105928 | tf_op jit(solution)/shard_map/ppermute | solution.py:307
  6.6 9.1 %collective-permute-start = (bf16[160,1152]{1,0:T(8,128)(2,1)S(1)}, bf16[160,1152]{1,0:T(8,128)(2,1)S(1)}, u32[]{:S(2)}, u32[]{:S(2)}) collective-permute-start(bf16[160,1152]{1,0:T(8,128)(2,1)S(1)} %get-tuple-element.26.image), channel_id=1, source_target_pairs={{0,2},{1,3},{2,0},{3,1},{4,6},{5,7},{6,4},{7,5},{8,10},{9,11},{10,... | collective-permute-start | bytes 1105928 | tf_op jit(solution)/shard_map/ppermute | solution.py:307
  16.7 2.3 %collective-permute-start.4 = (bf16[2,160,1152]{2,1,0:T(8,128)(2,1)S(1)}, bf16[2,160,1152]{2,1,0:T(8,128)(2,1)S(1)}, u32[]{:S(2)}, u32[]{:S(2)}) collective-permute-start(bf16[2,160,1152]{2,1,0:T(8,128)(2,1)S(1)} %got.1), channel_id=1, source_target_pairs={{0,2},{1,3},{2,0},{3,1},{4,6},{5,7},{6,4},{7,5},{8,10},{9,11},{10,... | collective-permute-start | bytes 2211848 | tf_op jit(solution)/shard_map/ppermute | solution.py:307
  16.7 9.4 %collective-permute-start.6 = (bf16[160,1152]{1,0:T(8,128)(2,1)S(1)}, bf16[160,1152]{1,0:T(8,128)(2,1)S(1)}, u32[]{:S(2)}, u32[]{:S(2)}) collective-permute-start(bf16[160,1152]{1,0:T(8,128)(2,1)S(1)} %bitcast.8), channel_id=1, source_target_pairs={{0,28},{1,29},{2,3},{3,2},{4,0},{5,1},{6,7},{7,6},{8,4},{9,5},{10,... | collective-permute-start | bytes 1105928 | tf_op jit(solution)/shard_map/ppermute | solution.py:307
  19.8 7.9 %collective-permute-start.5 = (bf16[160,1152]{1,0:T(8,128)(2,1)S(1)}, bf16[160,1152]{1,0:T(8,128)(2,1)S(1)}, u32[]{:S(2)}, u32[]{:S(2)}) collective-permute-start(bf16[160,1152]{1,0:T(8,128)(2,1)S(1)} %bitcast.7), channel_id=1, source_target_pairs={{0,1},{1,0},{2,30},{3,31},{4,5},{5,4},{6,2},{7,3},{8,9},{9,8},{10,... | collective-permute-start | bytes 1105928 | tf_op jit(solution)/shard_map/ppermute | solution.py:307

commit v25 on v24

--- a/solution.py
+++ b/solution.py
@@ -239,7 +239,7 @@
     image, text, received = refs[0:3], refs[3:6], refs[6 : 6 + far]
     image_grads, text_grads, held, sems = refs[-4:]
     rows = held.shape[0]
-    part = rows // 10 if rows % 160 == 0 else rows
+    part = rows // 2 if rows % 32 == 0 else rows
 
     def run(own, count, out, node):
         copies = []
@@ -285,7 +285,7 @@
         out_shape=[jax.ShapeDtypeStruct(*block)] * 2,
         in_specs=[pl.BlockSpec(memory_space=pltpu.VMEM)] * count + [anywhere] * len(grads),
         out_specs=[anywhere] * 2,
-        scratch_shapes=[pltpu.VMEM(*block), pltpu.SemaphoreType.DMA((10,))],
+        scratch_shapes=[pltpu.VMEM(*block), pltpu.SemaphoreType.DMA((2,))],
         input_output_aliases={count + i: i for i in range(len(grads))},
         compiler_params=pltpu.CompilerParams(vmem_limit_bytes=VMEM_LIMIT),
     )(*operands, *grads)

time: 29.1 us -> 29.1 us (level)
  no operation moved by 1% of the time
where the time goes in v25:
time: 29.1 us; the launch traced here: 28.9 us
  waiting for transfers between devices  9.59 us (33%)
  Pallas kernels  8.75 us (30%)
  starting transfers between devices  8.52 us (29%)
  between operations  2.02 us (7%)
    ppermute x7, waiting for transfers between devices, send(): return lax.ppermute(block, ('blk', 'node'), route)  9.59 us
    ppermute x7, starting transfers between devices, send(): return lax.ppermute(block, ('blk', 'node'), route)  8.52 us
    pallas_call x7, Pallas kernels, call(): pl.pallas_call(kernel, name=name, out_shape=[pltpu.VMEM(s, d) for s, d in...  6.45 us
    pallas_call x2, Pallas kernels, write_out(): pl.pallas_call(functools.partial(out_kernel, far, image_on_first), name='...  2.3 us
  transfers between devices with their start and end apart: 7, of which 4 were waited for; matrix products, arithmetic and copies ran while one was open for 0% of the time, Pallas kernels for 23%

profile of v25, /device:TPU:0, one launch (start us, length us, event | category | flops | bytes accessed | tf_op | source)
XLA Modules:
  0.0 28.9 jit_solution(16959149529891457306)
XLA Ops:
  0.6 3.0 %collective-permute-start.3 = (bf16[160,1152]{1,0:T(8,128)(2,1)}, bf16[160,1152]{1,0:T(8,128)(2,1)S(1)}, u32[]{:S(2)}, u32[]{:S(2)}) collective-permute-start(bf16[160,1152]{1,0:T(8,128)(2,1)} %image.1), channel_id=1, source_target_pairs={{0,4},{1,5},{2,6},{3,7},{4,8},{5,9},{6,10},{7,11},{8,12},{9,13},{1... | collective-permute-start | bytes 1105928 | tf_op jit(solution)/shard_map/ppermute | solution.py:307
  3.6 1.5 %collective-permute-start.2 = (bf16[160,1152]{1,0:T(8,128)(2,1)}, bf16[160,1152]{1,0:T(8,128)(2,1)S(1)}, u32[]{:S(2)}, u32[]{:S(2)}) collective-permute-start(bf16[160,1152]{1,0:T(8,128)(2,1)} %text.1), channel_id=1, source_target_pairs={{0,1},{1,0},{2,3},{3,2},{4,5},{5,4},{6,7},{7,6},{8,9},{9,8},{10,11... | collective-permute-start | bytes 1105928 | tf_op jit(solution)/shard_map/ppermute | solution.py:307
  5.1 1.3 %unit.1 = (bf16[160,1152]{1,0:T(8,128)(2,1)S(1)}, bf16[160,1152]{1,0:T(8,128)(2,1)S(1)}, bf16[160,1152]{1,0:T(8,128)(2,1)S(1)}, bf16[160,1152]{1,0:T(8,128)(2,1)...) custom-call(bf16[160,1152]{1,0:T(8,128)(2,1)} %image.1, bf16[160,1152]{1,0:T(8,128)(2,1)} %text.1), custom_call_target="tpu_custom_call" | custom-call | tf_op jit(solution)/shard_map/unit/pallas_call | solution.py:267
  6.5 0.1 collective-permute-start.1
  6.6 0.5 %collective-permute-start = (bf16[160,1152]{1,0:T(8,128)(2,1)S(1)}, bf16[160,1152]{1,0:T(8,128)(2,1)S(1)}, u32[]{:S(2)}, u32[]{:S(2)}) collective-permute-start(bf16[160,1152]{1,0:T(8,128)(2,1)S(1)} %get-tuple-element.26.image), channel_id=1, source_target_pairs={{0,2},{1,3},{2,0},{3,1},{4,6},{5,7},{6,4},{7,5},{8,10},{9,11},{10,... | collective-permute-start | bytes 1105928 | tf_op jit(solution)/shard_map/ppermute | solution.py:307
  8.3 1.1 %prep.1 = (f32[8,128]{1,0:T(8,128)S(1)}, s32[1,480]{1,0:T(1,128)S(1)}, s32[160,1]{1,0:T(8,128)S(1)}) custom-call(s32[40,128]{1,0:T(8,128)} %bitcast.9, f32[1,1]{1,0:T(1,128)} %bitcast.5.scale, f32[1,1]{1,0:T(1,128)} %bitcast.6.bias, f32[160,1]{1,0:T(8,128)S(1)} %get-tuple-element.22.after.image_inv.refs_1_), custom_call_target="tpu_custom_call" | custom-call | tf_op jit(solution)/shard_map/prep/pallas_call | solution.py:267
  9.5 6.0 %collective-permute-done.3.raw = bf16[160,1152]{1,0:T(8,128)(2,1)S(1)} collective-permute-done((bf16[160,1152]{1,0:T(8,128)(2,1)}, bf16[160,1152]{1,0:T(8,128)(2,1)S(1)}, u32[]{:S(2)}, u32[]{:S(2)}) %collective-permute-start.3) | collective-permute-done | bytes 368672 | tf_op jit(solution)/shard_map/ppermute | solution.py:307
  15.5 0.2 visit.1
  15.6 0.0 collective-permute-done.2.refs_0_
  15.6 0.0 collective-permute-done.1.refs_2_.mate_text
  15.6 0.0 collective-permute-done.refs_1_.mate_image
  15.7 0.2 got.1
  15.8 0.8 %first.1 = (bf16[1,160,1152]{2,1,0:T(8,128)(2,1)S(1)}, f32[160,1152]{1,0:T(8,128)S(1)}) custom-call(f32[8,128]{1,0:T(8,128)S(1)} %get-tuple-element.23.after.params, s32[1,480]{1,0:T(1,128)S(1)} %get-tuple-element.24.row_targets, bf16[160,1152]{1,0:T(8,128)(2,1)S(1)} %get-tuple-element.26.image, bf16[160,1152]{1,0:T(8,128)(2,1)S(1)} %get-tuple-element.27.text, ...), custom_call_target="tpu_custom_call" | custom-call | tf_op jit(solution)/shard_map/first/pallas_call | solution.py:267
  16.7 0.1 collective-permute-start.4
  16.7 1.8 %collective-permute-start.6 = (bf16[160,1152]{1,0:T(8,128)(2,1)S(1)}, bf16[160,1152]{1,0:T(8,128)(2,1)S(1)}, u32[]{:S(2)}, u32[]{:S(2)}) collective-permute-start(bf16[160,1152]{1,0:T(8,128)(2,1)S(1)} %bitcast.8), channel_id=1, source_target_pairs={{0,28},{1,29},{2,3},{3,2},{4,0},{5,1},{6,7},{7,6},{8,4},{9,5},{10,... | collective-permute-start | bytes 1105928 | tf_op jit(solution)/shard_map/ppermute | solution.py:307
  18.5 0.4 %collective-permute-done.4.mate_got = bf16[2,160,1152]{2,1,0:T(8,128)(2,1)S(1)} collective-permute-done((bf16[2,160,1152]{2,1,0:T(8,128)(2,1)S(1)}, bf16[2,160,1152]{2,1,0:T(8,128)(2,1)S(1)}, u32[]{:S(2)}, u32[]{:S(2)}) %collective-permute-start.4) | collective-permute-done | bytes 737312 | tf_op jit(solution)/shard_map/ppermute | solution.py:307
  18.9 0.9 %second.1 = bf16[1,160,1152]{2,1,0:T(8,128)(2,1)S(1)} custom-call(f32[8,128]{1,0:T(8,128)S(1)} %get-tuple-element.23.after.params, s32[1,480]{1,0:T(1,128)S(1)} %get-tuple-element.24.row_targets, bf16[160,1152]{1,0:T(8,128)(2,1)S(1)} %get-tuple-element.26.image, bf16[2,160,1152]{2,1,0:T(8,128)(2,1)S(1)} %got.1, ...), custom_call_target="tpu_custom_call" | custom-call | tf_op jit(solution)/shard_map/second/pallas_call | solution.py:267
  19.8 1.6 %collective-permute-start.5 = (bf16[160,1152]{1,0:T(8,128)(2,1)S(1)}, bf16[160,1152]{1,0:T(8,128)(2,1)S(1)}, u32[]{:S(2)}, u32[]{:S(2)}) collective-permute-start(bf16[160,1152]{1,0:T(8,128)(2,1)S(1)} %bitcast.7), channel_id=1, source_target_pairs={{0,1},{1,0},{2,30},{3,31},{4,5},{5,4},{6,2},{7,3},{8,9},{9,8},{10,... | collective-permute-start | bytes 1105928 | tf_op jit(solution)/shard_map/ppermute | solution.py:307
  21.4 2.0 %third.1 = (f32[160,1152]{1,0:T(8,128)S(1)}, f32[160,1152]{1,0:T(8,128)S(1)}) custom-call(f32[8,128]{1,0:T(8,128)S(1)} %get-tuple-element.23.after.params, s32[1,480]{1,0:T(1,128)S(1)} %get-tuple-element.24.row_targets, s32[160,1]{1,0:T(8,128)S(1)} %get-tuple-element.25.targets, bf16[160,1152]{1,0:T(8,128)(2,1)S(1)} %get-tuple-element.26.image, ...), custom_call_target="tpu_custom_call" | custom-call | tf_op jit(solution)/shard_map/third/pallas_call | solution.py:267
  23.4 2.8 %collective-permute-done.6.refs_6_ = bf16[160,1152]{1,0:T(8,128)(2,1)S(1)} collective-permute-done((bf16[160,1152]{1,0:T(8,128)(2,1)S(1)}, bf16[160,1152]{1,0:T(8,128)(2,1)S(1)}, u32[]{:S(2)}, u32[]{:S(2)}) %collective-permute-start.6) | collective-permute-done | bytes 368672 | tf_op jit(solution)/shard_map/ppermute | solution.py:307
  26.1 1.1 %out.2 = (f32[160,1152]{1,0:T(8,128)}, f32[160,1152]{1,0:T(8,128)}) custom-call(bf16[160,1152]{1,0:T(8,128)(2,1)S(1)} %get-tuple-element.21.image_raw.refs_0_, f32[160,1]{1,0:T(8,128)S(1)} %get-tuple-element.22.after.image_inv.refs_1_, f32[160,1152]{1,0:T(8,128)S(1)} %get-tuple-element.34.refs_2_, bf16[160,1152]{1,0:T(8,128)(2,1)S(1)} %get-tuple-element.32.text_raw.refs_3_, ...), custom_call_target="tpu_custom_call" | custom-call | tf_op jit(solution)/shard_map/out/pallas_call | solution.py:282
  27.3 0.4 %collective-permute-done.5.refs_6_ = bf16[160,1152]{1,0:T(8,128)(2,1)S(1)} collective-permute-done((bf16[160,1152]{1,0:T(8,128)(2,1)S(1)}, bf16[160,1152]{1,0:T(8,128)(2,1)S(1)}, u32[]{:S(2)}, u32[]{:S(2)}) %collective-permute-start.5) | collective-permute-done | bytes 368672 | tf_op jit(solution)/shard_map/ppermute | solution.py:307
  27.7 1.2 %out.3 = (f32[160,1152]{1,0:T(8,128)}, f32[160,1152]{1,0:T(8,128)}) custom-call(bf16[160,1152]{1,0:T(8,128)(2,1)S(1)} %get-tuple-element.21.image_raw.refs_0_, f32[160,1]{1,0:T(8,128)S(1)} %get-tuple-element.22.after.image_inv.refs_1_, f32[160,1152]{1,0:T(8,128)S(1)} %get-tuple-element.34.refs_2_, ...), custom_call_target="tpu_custom_call", output_to_operand_aliasing={{0}: (7, {}), {1}: (8, {})} | custom-call | tf_op jit(solution)/shard_map/out/pallas_call | solution.py:282
Async XLA Ops:
  0.6 14.8 %collective-permute-start.3 = (bf16[160,1152]{1,0:T(8,128)(2,1)}, bf16[160,1152]{1,0:T(8,128)(2,1)S(1)}, u32[]{:S(2)}, u32[]{:S(2)}) collective-permute-start(bf16[160,1152]{1,0:T(8,128)(2,1)} %image.1), channel_id=1, source_target_pairs={{0,4},{1,5},{2,6},{3,7},{4,8},{5,9},{6,10},{7,11},{8,12},{9,13},{1... | collective-permute-start | bytes 1105928 | tf_op jit(solution)/shard_map/ppermute | solution.py:307
  3.6 12.0 %collective-permute-start.2 = (bf16[160,1152]{1,0:T(8,128)(2,1)}, bf16[160,1152]{1,0:T(8,128)(2,1)S(1)}, u32[]{:S(2)}, u32[]{:S(2)}) collective-permute-start(bf16[160,1152]{1,0:T(8,128)(2,1)} %text.1), channel_id=1, source_target_pairs={{0,1},{1,0},{2,3},{3,2},{4,5},{5,4},{6,7},{7,6},{8,9},{9,8},{10,11... | collective-permute-start | bytes 1105928 | tf_op jit(solution)/shard_map/ppermute | solution.py:307
  6.5 9.2 %collective-permute-start.1 = (bf16[160,1152]{1,0:T(8,128)(2,1)S(1)}, bf16[160,1152]{1,0:T(8,128)(2,1)S(1)}, u32[]{:S(2)}, u32[]{:S(2)}) collective-permute-start(bf16[160,1152]{1,0:T(8,128)(2,1)S(1)} %get-tuple-element.27.text), channel_id=1, source_target_pairs={{0,2},{1,3},{2,0},{3,1},{4,6},{5,7},{6,4},{7,5},{8,10},{9,11},{10,... | collective-permute-start | bytes 1105928 | tf_op jit(solution)/shard_map/ppermute | solution.py:307
  6.6 9.1 %collective-permute-start = (bf16[160,1152]{1,0:T(8,128)(2,1)S(1)}, bf16[160,1152]{1,0:T(8,128)(2,1)S(1)}, u32[]{:S(2)}, u32[]{:S(2)}) collective-permute-start(bf16[160,1152]{1,0:T(8,128)(2,1)S(1)} %get-tuple-element.26.image), channel_id=1, source_target_pairs={{0,2},{1,3},{2,0},{3,1},{4,6},{5,7},{6,4},{7,5},{8,10},{9,11},{10,... | collective-permute-start | bytes 1105928 | tf_op jit(solution)/shard_map/ppermute | solution.py:307
  16.7 2.3 %collective-permute-start.4 = (bf16[2,160,1152]{2,1,0:T(8,128)(2,1)S(1)}, bf16[2,160,1152]{2,1,0:T(8,128)(2,1)S(1)}, u32[]{:S(2)}, u32[]{:S(2)}) collective-permute-start(bf16[2,160,1152]{2,1,0:T(8,128)(2,1)S(1)} %got.1), channel_id=1, source_target_pairs={{0,2},{1,3},{2,0},{3,1},{4,6},{5,7},{6,4},{7,5},{8,10},{9,11},{10,... | collective-permute-start | bytes 2211848 | tf_op jit(solution)/shard_map/ppermute | solution.py:307
  16.7 9.4 %collective-permute-start.6 = (bf16[160,1152]{1,0:T(8,128)(2,1)S(1)}, bf16[160,1152]{1,0:T(8,128)(2,1)S(1)}, u32[]{:S(2)}, u32[]{:S(2)}) collective-permute-start(bf16[160,1152]{1,0:T(8,128)(2,1)S(1)} %bitcast.8), channel_id=1, source_target_pairs={{0,28},{1,29},{2,3},{3,2},{4,0},{5,1},{6,7},{7,6},{8,4},{9,5},{10,... | collective-permute-start | bytes 1105928 | tf_op jit(solution)/shard_map/ppermute | solution.py:307
  19.8 7.9 %collective-permute-start.5 = (bf16[160,1152]{1,0:T(8,128)(2,1)S(1)}, bf16[160,1152]{1,0:T(8,128)(2,1)S(1)}, u32[]{:S(2)}, u32[]{:S(2)}) collective-permute-start(bf16[160,1152]{1,0:T(8,128)(2,1)S(1)} %bitcast.7), channel_id=1, source_target_pairs={{0,1},{1,0},{2,30},{3,31},{4,5},{5,4},{6,2},{7,3},{8,9},{9,8},{10,... | collective-permute-start | bytes 1105928 | tf_op jit(solution)/shard_map/ppermute | solution.py:307
